TPU v7x, 32 devices: a whole 2x2x4 slice. The times are simulated.
32 devices in a mesh: seq: 8 (over y, x, core), batch: 4 (over z).
Axes of the slice: x: 2, y: 2, z: 4, core: 2. Of those that a mesh axis runs over, the one named last changes fastest.
Arguments:
- tokens: float32 [4, 1024, 768], P('batch', 'seq'), may hold values from -6 to 6
- cotangent: float32 [4, 1024, 768], P('batch', 'seq'), may hold values from -6 to 6
- group_ids: int32 [4, 1024], P('batch', 'seq'), may hold values from 0 to 7, never falling along the last dimension, each value on 1 to 640 neighbouring positions
- attention_weight: float32 [4, 768, 768], P(None, ('seq', 'batch')), may hold values from -1 to 1, as said below
- ffin_weight: float32 [2, 768, 2048], P(None, ('seq', 'batch')), may hold values from -0.21875 to 0.21875
- ffout_weight: float32 [2048, 768], P(('seq', 'batch')), may hold values from -0.125 to 0.125
- bias_table: float32 [32, 12], replicated, may hold values from -6 to 6
- gains: float32 [2, 768], replicated, may hold values from 0.5 to 1.5
- attention_momentum: float32 [4, 768, 768], P(None, ('seq', 'batch')), may hold values from -2560 to 2560, as said below
- ffin_momentum: float32 [2, 768, 2048], P(None, ('seq', 'batch')), may hold values from -160 to 160
- ffout_momentum: float32 [2048, 768], P(('seq', 'batch')), may hold values from -256 to 256
- bias_momentum: float32 [32, 12], replicated, may hold values from -3072 to 3072
- gain_momentum: float32 [2, 768], replicated, may hold values from -768 to 768
- attention_average: float32 [4, 768, 768], P(None, ('seq', 'batch')), may hold values from -1 to 1, as said below
- ffin_average: float32 [2, 768, 2048], P(None, ('seq', 'batch')), may hold values from -0.21875 to 0.21875
- ffout_average: float32 [2048, 768], P(('seq', 'batch')), may hold values from -0.125 to 0.125
- bias_average: float32 [32, 12], replicated, may hold values from -6 to 6
- gain_average: float32 [2, 768], replicated, may hold values from 0.5 to 1.5
Outputs:
- layer_output: float32 [4, 1024, 768], P('batch', 'seq')
- input_grad: float32 [4, 1024, 768], P('batch', 'seq')
- new_attention_weight: float32 [4, 768, 768], P(None, ('seq', 'batch'))
- new_ffin_weight: float32 [2, 768, 2048], P(None, ('seq', 'batch'))
- new_ffout_weight: float32 [2048, 768], P(('seq', 'batch'))
- new_bias_table: float32 [32, 12], replicated
- new_gains: float32 [2, 768], replicated
- new_attention_momentum: float32 [4, 768, 768], P(None, ('seq', 'batch'))
- new_ffin_momentum: float32 [2, 768, 2048], P(None, ('seq', 'batch'))
- new_ffout_momentum: float32 [2048, 768], P(('seq', 'batch'))
- new_bias_momentum: float32 [32, 12], replicated
- new_gain_momentum: float32 [2, 768], replicated
- new_attention_average: float32 [4, 768, 768], P(None, ('seq', 'batch'))
- new_ffin_average: float32 [2, 768, 2048], P(None, ('seq', 'batch'))
- new_ffout_average: float32 [2048, 768], P(('seq', 'batch'))
- new_bias_average: float32 [32, 12], replicated
- new_gain_average: float32 [2, 768], replicated
- attention_copy: bfloat16 [4, 768, 768], P(None, ('seq', 'batch'))
- ffin_copy: bfloat16 [2, 768, 2048], P(None, ('seq', 'batch'))
- ffout_copy: bfloat16 [2048, 768], P(('seq', 'batch'))
Inputs may be any that keep to these rules, and one draw needn't show every extreme that they name: `group_ids`: along each sequence the group ids never fall; every one of the 8 groups holds 1 to 640 positions and one holds exactly 640. `attention_weight`: independent entries. `attention_average`: independent entries. `attention_momentum`: independent entries.
All inputs are finite; a program needn't handle non-finite values.
Results may differ from a plain program's by a relative error of at most 0.017.
Values may be sent and summed in bfloat16 or wider, within the bound.
No kernel may reach another device: no remote copies, remote signals or barrier semaphores. Data moves between devices by JAX's collectives and lax.ppermute only.
A program may use at most 192 MiB of HBM per device.

v0:
```python
import math

import jax
import jax.numpy as jnp
from jax import lax
from jax.sharding import PartitionSpec as P

eps_norm = 1e-06
momentum_coef = 0.5
average_coef = 0.5
attention_rates = (0.0033, 0.0033, 0.025, 0.2)
ffin_rate = 0.063
ffout_rate = 0.023
bias_rate = 0.08
gain_rates = (0.045, 0.22)
thresholds = (12, 16, 23, 32, 46, 64, 91)
masked_score = -1e30


def passed_along(value, axis, steps):
    count = lax.axis_size(axis)
    pairs = [(source, (source + steps) % count) for source in range(count)]
    return lax.ppermute(value, axis, pairs)


def rms_norm(values, gain):
    mean_square = jnp.mean(values * values, axis=-1, keepdims=True)
    return values * lax.rsqrt(mean_square + eps_norm) * gain


def bucket_of(offset):
    magnitude = jnp.abs(offset)
    beyond = jnp.zeros_like(offset)
    for threshold in thresholds:
        beyond = beyond + (magnitude >= threshold).astype(jnp.int32)
    inside = jnp.where(magnitude < 8, magnitude, 8 + beyond)
    return inside + 16 * (offset > 0).astype(jnp.int32)


def activate(gate_proj, up_proj):
    return jax.nn.gelu(gate_proj, approximate=True) * up_proj


def update(weight, grad, momentum, average, rate):
    new_momentum = momentum_coef * momentum + grad
    new_weight = weight - rate * (grad + momentum_coef * new_momentum)
    new_average = average_coef * average + (1.0 - average_coef) * new_weight
    return (new_weight, new_momentum, new_average)


def matmul(left_rows, right_rows):
    return jnp.dot(left_rows, right_rows, preferred_element_type=jnp.float32)


def bucket_offsets(table_heads, buckets):
    bucket_count = table_heads.shape[1]
    query_count, key_count = buckets.shape
    flat_buckets = buckets.reshape(query_count * key_count)
    bucket_onehot = (
        jnp.arange(bucket_count, dtype=jnp.int32)[:, None] == flat_buckets[None, :]
    ).astype(jnp.float32)
    looked = jnp.dot(
        table_heads,
        bucket_onehot,
        precision=lax.Precision.HIGHEST,
        preferred_element_type=jnp.float32,
    )
    return looked.reshape(table_heads.shape[0], query_count, key_count)


def shards(
    tokens,
    cotangent,
    group_ids,
    attention_weight,
    ffin_weight,
    ffout_weight,
    bias_table,
    gains,
    attention_momentum,
    ffin_momentum,
    ffout_momentum,
    bias_momentum,
    gain_momentum,
    attention_average,
    ffin_average,
    ffout_average,
    bias_average,
    gain_average,
):
    seq_count, tok_seq, model_width = tokens.shape
    cycle_size = lax.axis_size("seq")
    cycle_index = lax.axis_index("seq")
    head_count = bias_table.shape[1]
    head_width = model_width // head_count
    row_count = seq_count * tok_seq
    bucket_count = bias_table.shape[0]
    table_heads = bias_table.T
    full_attention, full_ffin, full_ffout = (
        lax.all_gather(attention_weight.astype(jnp.bfloat16), ("seq", "batch"), axis=1, tiled=True),
        lax.all_gather(ffin_weight.astype(jnp.bfloat16), ("seq", "batch"), axis=1, tiled=True),
        lax.all_gather(ffout_weight.astype(jnp.bfloat16), ("seq", "batch"), axis=0, tiled=True),
    )
    all_groups = lax.all_gather(group_ids, "seq", axis=1, tiled=True)
    flat_tokens = tokens.reshape(row_count, model_width)
    first_normed, first_back = jax.vjp(rms_norm, flat_tokens, gains[0])
    first_low = first_normed.astype(jnp.bfloat16)

    def heads_of(matrix):
        return matrix.astype(jnp.bfloat16).reshape(seq_count, tok_seq, head_count, head_width)

    query_low = heads_of(matmul(first_low, full_attention[0]))
    key_low = heads_of(matmul(first_low, full_attention[1]))
    value_low = heads_of(matmul(first_low, full_attention[2]))
    query_pos = cycle_index * tok_seq + jnp.arange(tok_seq, dtype=jnp.int32)
    query_groups = lax.dynamic_slice_in_dim(all_groups, cycle_index * tok_seq, tok_seq, 1)

    def block_terms(key_part, key_start):
        key_count = key_part.shape[1]
        key_pos = key_start + jnp.arange(key_count, dtype=jnp.int32)
        key_groups = lax.dynamic_slice_in_dim(all_groups, key_start, key_count, 1)
        buckets = bucket_of(key_pos[None, :] - query_pos[:, None])
        offsets = bucket_offsets(table_heads, buckets)
        raw_scores = jnp.einsum(
            "sqhd,skhd->shqk", query_low, key_part, preferred_element_type=jnp.float32
        )
        allowed = (query_groups[:, :, None] == key_groups[:, None, :])[:, None]
        return (raw_scores + offsets[None], allowed, buckets)

    def absorb(state, key_part, value_part, key_start):
        row_best, row_total, weighted = state
        scores, allowed, buckets = block_terms(key_part, key_start)
        block_top = jnp.max(jnp.where(allowed, scores, masked_score), axis=-1)
        new_best = jnp.maximum(row_best, block_top)
        weights_soft = jnp.where(allowed, jnp.exp(scores - new_best[..., None]), 0.0)
        factor = jnp.exp(row_best - new_best)
        row_total = row_total * factor + jnp.sum(weights_soft, axis=-1)
        weighted = weighted * jnp.transpose(factor, (0, 2, 1))[..., None] + jnp.einsum(
            "shqk,skhd->sqhd",
            weights_soft.astype(jnp.bfloat16),
            value_part,
            preferred_element_type=jnp.float32,
        )
        return (new_best, row_total, weighted)

    zero_heads = jnp.zeros((seq_count, tok_seq, head_count, head_width), jnp.float32)
    start_state = (
        jnp.full((seq_count, head_count, tok_seq), masked_score, jnp.float32),
        jnp.zeros((seq_count, head_count, tok_seq), jnp.float32),
        zero_heads,
    )

    def forward_step(step_index, carry):
        moving_keys, moving_values, state = carry
        source = (cycle_index - step_index) % cycle_size
        state = absorb(state, moving_keys, moving_values, source * tok_seq)
        moving_keys, moving_values = passed_along((moving_keys, moving_values), "seq", 1)
        return (moving_keys, moving_values, state)

    finished = lax.fori_loop(0, cycle_size, forward_step, (key_low, value_low, start_state))
    row_best, row_total, weighted = finished[2]
    attended = weighted / jnp.transpose(row_total, (0, 2, 1))[..., None]
    log_total = row_best + jnp.log(row_total)
    attended_low = attended.reshape(row_count, model_width).astype(jnp.bfloat16)
    mixed = flat_tokens + matmul(attended_low, full_attention[3])
    second_normed, second_back = jax.vjp(rms_norm, mixed, gains[1])
    second_low = second_normed.astype(jnp.bfloat16)
    gate_proj = matmul(second_low, full_ffin[0])
    up_proj = matmul(second_low, full_ffin[1])
    hidden, activate_back = jax.vjp(activate, gate_proj, up_proj)
    hidden_low = hidden.astype(jnp.bfloat16)
    layer_output = mixed + matmul(hidden_low, full_ffout)
    flat_cot = cotangent.reshape(row_count, model_width)
    cot_low = flat_cot.astype(jnp.bfloat16)
    grad_ffout = matmul(hidden_low.T, cot_low)
    hidden_grad = matmul(cot_low, full_ffout.T)
    gate_grad, up_grad = activate_back(hidden_grad)
    gate_low = gate_grad.astype(jnp.bfloat16)
    up_low = up_grad.astype(jnp.bfloat16)
    grad_ffin = jnp.stack([matmul(second_low.T, gate_low), matmul(second_low.T, up_low)])
    second_grad = matmul(gate_low, full_ffin[0].T) + matmul(up_low, full_ffin[1].T)
    mixed_part, second_gain_grad = second_back(second_grad)
    mixed_grad = flat_cot + mixed_part
    branch_low = mixed_grad.astype(jnp.bfloat16)
    grad_out_proj = matmul(attended_low.T, branch_low)
    attended_grad = (
        matmul(branch_low, full_attention[3].T)
        .astype(jnp.bfloat16)
        .reshape(seq_count, tok_seq, head_count, head_width)
    )
    delta = jnp.transpose(jnp.sum(attended_grad.astype(jnp.float32) * attended, axis=-1), (0, 2, 1))

    def bucket_sums(score_grad, buckets):
        pair_count = buckets.shape[0] * buckets.shape[1]
        bucket_onehot = (
            buckets.reshape(pair_count)[:, None]
            == jnp.arange(bucket_count, dtype=jnp.int32)[None, :]
        ).astype(jnp.bfloat16)
        summed_heads = jnp.sum(score_grad, axis=0).reshape(head_count, pair_count)
        upper_part = summed_heads.astype(jnp.bfloat16)
        lower_part = (summed_heads - upper_part.astype(jnp.float32)).astype(jnp.bfloat16)
        both_parts = matmul(jnp.concatenate([upper_part, lower_part], axis=0), bucket_onehot)
        return (both_parts[:head_count] + both_parts[head_count:]).T

    def retreat(key_part, value_part, key_start):
        scores, allowed, buckets = block_terms(key_part, key_start)
        weights_soft = jnp.where(allowed, jnp.exp(scores - log_total[..., None]), 0.0)
        value_grad = jnp.einsum(
            "shqk,sqhd->skhd",
            weights_soft.astype(jnp.bfloat16),
            attended_grad,
            preferred_element_type=jnp.float32,
        )
        spread = jnp.einsum(
            "sqhd,skhd->shqk", attended_grad, value_part, preferred_element_type=jnp.float32
        )
        score_grad = weights_soft * (spread - delta[..., None])
        bias_grad = bucket_sums(score_grad, buckets)
        score_low = score_grad.astype(jnp.bfloat16)
        query_grad = jnp.einsum(
            "shqk,skhd->sqhd", score_low, key_part, preferred_element_type=jnp.float32
        )
        key_grad = jnp.einsum(
            "shqk,sqhd->skhd", score_low, query_low, preferred_element_type=jnp.float32
        )
        return (query_grad, key_grad, value_grad, bias_grad)

    zero_bias = jnp.zeros(bias_table.shape, jnp.float32)

    def backward_step(step_index, carry):
        moving_keys, moving_values, key_sum, value_sum, query_sum, bias_sum = carry
        source = (cycle_index - step_index) % cycle_size
        query_grad, key_grad, value_grad, bias_grad = retreat(
            moving_keys, moving_values, source * tok_seq
        )
        moving_keys, moving_values = passed_along((moving_keys, moving_values), "seq", 1)
        key_sum, value_sum = (
            passed_along((key_sum + key_grad).astype(jnp.bfloat16), "seq", 1).astype(jnp.float32),
            passed_along((value_sum + value_grad).astype(jnp.bfloat16), "seq", 1).astype(
                jnp.float32
            ),
        )
        return (
            moving_keys,
            moving_values,
            key_sum,
            value_sum,
            query_sum + query_grad,
            bias_sum + bias_grad,
        )

    finished = lax.fori_loop(
        0,
        cycle_size,
        backward_step,
        (key_low, value_low, zero_heads, zero_heads, zero_heads, zero_bias),
    )
    key_total, value_total, query_total, bias_total = (
        finished[2],
        finished[3],
        finished[4],
        finished[5],
    )

    def flat_low(grad_heads):
        return grad_heads.reshape(row_count, model_width).astype(jnp.bfloat16)

    query_flat = flat_low(query_total)
    key_flat = flat_low(key_total)
    value_flat = flat_low(value_total)
    grad_attention = jnp.stack(
        [
            matmul(first_low.T, query_flat),
            matmul(first_low.T, key_flat),
            matmul(first_low.T, value_flat),
            grad_out_proj,
        ]
    )
    first_grad = (
        matmul(query_flat, full_attention[0].T)
        + matmul(key_flat, full_attention[1].T)
        + matmul(value_flat, full_attention[2].T)
    )
    token_part, first_gain_grad = first_back(first_grad)
    input_grad = mixed_grad + token_part
    own_attention, own_ffin, own_ffout = (
        lax.psum_scatter(grad_attention, ("seq", "batch"), scatter_dimension=1, tiled=True),
        lax.psum_scatter(grad_ffin, ("seq", "batch"), scatter_dimension=1, tiled=True),
        lax.psum_scatter(grad_ffout, ("seq", "batch"), scatter_dimension=0, tiled=True),
    )
    bias_reduced, gains_reduced = lax.psum(
        (bias_total, jnp.stack([first_gain_grad, second_gain_grad])), ("seq", "batch")
    )
    all_tokens = seq_count * lax.axis_size("batch") * tok_seq * cycle_size
    inverse_root = 1.0 / math.sqrt(all_tokens)
    attention_rate = jnp.array(attention_rates, dtype=jnp.float32)[:, None, None] * inverse_root
    gain_rate = jnp.array(gain_rates, dtype=jnp.float32)[:, None] * inverse_root
    attn_new = update(
        attention_weight, own_attention, attention_momentum, attention_average, attention_rate
    )
    ffin_new = update(ffin_weight, own_ffin, ffin_momentum, ffin_average, ffin_rate * inverse_root)
    ffout_new = update(
        ffout_weight, own_ffout, ffout_momentum, ffout_average, ffout_rate * inverse_root
    )
    bias_new = update(
        bias_table, bias_reduced, bias_momentum, bias_average, bias_rate * inverse_root
    )
    gain_new = update(gains, gains_reduced, gain_momentum, gain_average, gain_rate)
    return (
        layer_output.reshape(seq_count, tok_seq, model_width),
        input_grad.reshape(seq_count, tok_seq, model_width),
        attn_new[0],
        ffin_new[0],
        ffout_new[0],
        bias_new[0],
        gain_new[0],
        attn_new[1],
        ffin_new[1],
        ffout_new[1],
        bias_new[1],
        gain_new[1],
        attn_new[2],
        ffin_new[2],
        ffout_new[2],
        bias_new[2],
        gain_new[2],
        attn_new[0].astype(jnp.bfloat16),
        ffin_new[0].astype(jnp.bfloat16),
        ffout_new[0].astype(jnp.bfloat16),
    )


def solution(mesh):
    placed = (
        P("batch", "seq", None),
        P("batch", "seq", None),
        P("batch", "seq"),
        P(None, ("seq", "batch"), None),
        P(None, ("seq", "batch"), None),
        P(("seq", "batch"), None),
        P(),
        P(),
        P(None, ("seq", "batch"), None),
        P(None, ("seq", "batch"), None),
        P(("seq", "batch"), None),
        P(),
        P(),
        P(None, ("seq", "batch"), None),
        P(None, ("seq", "batch"), None),
        P(("seq", "batch"), None),
        P(),
        P(),
    )
    return jax.shard_map(
        shards,
        mesh=mesh,
        in_specs=placed,
        out_specs=(
            P("batch", "seq", None),
            P("batch", "seq", None),
            P(None, ("seq", "batch"), None),
            P(None, ("seq", "batch"), None),
            P(("seq", "batch"), None),
            P(),
            P(),
            P(None, ("seq", "batch"), None),
            P(None, ("seq", "batch"), None),
            P(("seq", "batch"), None),
            P(),
            P(),
            P(None, ("seq", "batch"), None),
            P(None, ("seq", "batch"), None),
            P(("seq", "batch"), None),
            P(),
            P(),
            P(None, ("seq", "batch"), None),
            P(None, ("seq", "batch"), None),
            P(("seq", "batch"), None),
        ),
        check_vma=False,
    )
```

profile of v0, /device:TPU:0, one launch (start us, length us, event | category | flops | bytes accessed | tf_op | source)
XLA Modules:
  0.0 670.9 jit_solution(8973599587128123739)
XLA Ops:
  15.5 10.3 %all_gather.13 = s32[1,1024]{1,0:T(1,128)S(1)} all-gather(s32[1,128]{1,0:T(1,128)} %param.26), channel_id=1, replica_groups=mesh['seq'=8,'batch'=4] {'seq'}, dimensions={1}, use_global_device_ids=true | all-gather | bytes 4608 | tf_op jit(solution)/shard_map/all_gather | solution.py:104
  27.5 50.6 %all-gather.4.cloned.1.call-done = bf16[4,768,768]{2,1,0:T(8,128)(2,1)} async-done(((bf16[4,24,768]{2,1,0:T(8,128)(2,1)}), bf16[4,768,768]{2,1,0:T(8,128)(2,1)}) %all-gather.4.cloned.1.call-update) | async-done | bytes 4718608 | tf_op jit(solution)/shard_map/all_gather | solution.py:100
  84.8 89.2 %while.50 = (s32[]{:T(128)}, bf16[1,128,12,64]{1,3,2,0:T(8,128)(2,1)}, bf16[1,128,12,64]{1,3,2,0:T(8,128)(2,1)}, f32[1,12,128]{2,1,0:T(8,128)S(1)}, f32[1,12,128...) while((s32[]{:T(128)}, ...), condition=%wide.region_4.5_spmd.clone, body=%wide.region_1.4_spmd.clone.sunk | while | flops 128902416 | bytes 13211572 | solution.py:160
  92.5 2.9 collective-permute-done.1
  112.2 3.2 collective-permute-done
  115.4 3.9 collective-permute-done.1
  126.3 2.1 collective-permute-done.1
  135.3 4.3 collective-permute-done
  139.6 6.3 collective-permute-done.1
  152.9 2.1 collective-permute-done.1
  162.1 2.1 collective-permute-done.1
  171.9 2.1 collective-permute-done.1
  174.8 1.9 multiply_reduce_fusion.3
  178.8 3.5 fusion.66
  182.3 3.6 fusion.68
  185.9 31.0 %all-gather.8.cloned.1.call-done = bf16[2048,768]{1,0:T(8,128)(2,1)} async-done(((bf16[64,768]{1,0:T(8,128)(2,1)}), bf16[2048,768]{1,0:T(8,128)(2,1)}) %all-gather.8.cloned.1.call-update) | async-done | bytes 3145744 | tf_op jit(solution)/shard_map/all_gather | solution.py:102
  217.0 4.0 multiply_convert_fusion
  221.0 3.7 fusion.65
  224.7 3.8 multiply_reduce_fusion
  228.7 2.0 convolution_convert_fusion
  230.9 3.7 fusion.100
  235.6 124.5 %while.51 = (s32[]{:T(128)}, bf16[1,128,12,64]{1,3,2,0:T(8,128)(2,1)S(1)}, bf16[1,128,12,64]{1,3,2,0:T(8,128)(2,1)S(1)}, f32[1,128,12,64]{1,3,2,0:T(8,128)S(1)},...) while((s32[]{:T(128)}, ...), condition=%wide.region_9.10_spmd.clone, body=%wide.region_8.9_spmd.clone.sunk | while | flops 232932752 | bytes 23391280 | solution.py:252
  245.4 1.9 collective-permute-done.4
  259.3 1.9 collective-permute-done.4
  273.2 1.9 collective-permute-done.4
  283.7 2.4 collective-permute-start.5
  288.0 5.1 collective-permute-done.4
  294.0 5.4 collective-permute-done.5
  306.8 2.7 collective-permute-start.5
  315.4 1.9 collective-permute-start.3
  324.9 3.6 collective-permute-done.4
  336.8 2.6 collective-permute-start.5
  345.3 1.7 collective-permute-start.3
  354.7 2.3 collective-permute-done.4
  363.4 4.0 pad_maximum_fusion.1
  368.3 2.1 convolution_bitcast_fusion.4
  370.4 3.6 convolution_bitcast_fusion.5
  374.0 9.5 %pad_maximum_fusion = f32[2,768,2048]{2,1,0:T(8,128)} fusion(f32[1,768,2048]{2,1,0:T(8,128)S(1)} %convolution_bitcast_fusion.4, f32[1,768,2048]{2,1,0:T(8,128)} %convolution_bitcast_fusion.5), kind=kLoop, calls=%fused_computation.95 | loop fusion | flops 3145728 | bytes 25165824 | tf_op jit(solution)/shard_map/stack | solution.py:180
  384.5 1.9 fusion.78
  386.5 1.9 convolution_add_fusion.3
  388.4 2.0 fusion.85
  390.5 38.4 %all-reduce = (f32[32,12]{0,1:T(8,128)S(1)}, f32[2,768]{1,0:T(2,128)S(1)}) all-reduce(f32[32,12]{0,1:T(8,128)S(1)} %copy-done.40, f32[2,768]{1,0:T(2,128)S(1)} %pad_maximum_fusion.2), channel_id=1, replica_groups=mesh['seq'=8,'batch'=4] {'seq','batch'}, use_global_device_ids=true, to_apply=%region_14.15 | all-reduce | flops 1920 | bytes 15360 | tf_op jit(solution)/shard_map/psum | solution.py:291
  433.0 3.4 fusion.70
  436.4 1.8 fusion.96
  438.9 62.1 %reduce-scatter.4.cloned.1.call-done = f32[4,24,768]{2,1,0:T(8,128)} async-done(((f32[4,768,768]{2,1,0:T(8,128)}), f32[4,24,768]{2,1,0:T(8,128)}) %reduce-scatter.4.cloned.1.call-update) | async-done | bytes 294928 | tf_op jit(solution)/shard_map/reduce_scatter | solution.py:287
  501.0 1.8 fusion.98
  503.6 157.7 %reduce-scatter.6.cloned.1.call-done = f32[2,24,2048]{2,1,0:T(8,128)} async-done(((f32[2,768,2048]{2,1,0:T(8,128)}), f32[2,24,2048]{2,1,0:T(8,128)}) %reduce-scatter.6.cloned.1.call-update) | async-done | bytes 393232 | tf_op jit(solution)/shard_map/reduce_scatter | solution.py:288
  661.3 1.9 fusion.97
  (557 shorter events, 182.2 us)
Async XLA Ops:
  7.2 70.8 %all-gather.4.cloned.1.call-start = ((), (), s32[]{:S(2)}) async-start(), calls=%async_computation.3 | async-start | bytes 4866048 | tf_op jit(solution)/shard_map/all_gather | solution.py:100
  8.9 169.9 %all-gather.6.cloned.1.call-start = ((), (), s32[]{:S(2)}) async-start(), calls=%async_computation.4 | async-start | bytes 6488064 | tf_op jit(solution)/shard_map/all_gather | solution.py:101
  10.7 206.3 %all-gather.8.cloned.1.call-start = ((), (), s32[]{:S(2)}) async-start(), calls=%async_computation.5 | async-start | bytes 3244032 | tf_op jit(solution)/shard_map/all_gather | solution.py:102
  12.3 424.1 %reduce-scatter.8.cloned.1.call-start = ((), (), s32[]{:S(2)}) async-start(), calls=%async_computation.8 | async-start | bytes 6488064 | tf_op jit(solution)/shard_map/reduce_scatter | solution.py:289
  85.7 6.7 %collective-permute-start = (bf16[1,128,12,64]{1,3,2,0:T(8,128)(2,1)S(1)}, bf16[1,128,12,64]{1,3,2,0:T(8,128)(2,1)}, u32[]{:S(2)}, u32[]{:S(2)}) collective-permute-start(bf16[1,128,12,64]{1,3,2,0:T(8,128)(2,1)S(1)} %copy.80), channel_id=1, source_target_pairs={{0,4},{4,8},{8,12},{12,16},{16,20},{20,24},{24,28},{28,0},{1,5},{5... | collective-permute-start | bytes 589832 | tf_op jit(solution)/shard_map/while/body/eval_jaxpr/ppermute | solution.py:23
  86.9 8.4 %collective-permute-start.1 = (bf16[1,128,12,64]{1,3,2,0:T(8,128)(2,1)S(1)}, bf16[1,128,12,64]{1,3,2,0:T(8,128)(2,1)}, u32[]{:S(2)}, u32[]{:S(2)}) collective-permute-start(bf16[1,128,12,64]{1,3,2,0:T(8,128)(2,1)S(1)} %copy.81), channel_id=1, source_target_pairs={{0,4},{4,8},{8,12},{12,16},{16,20},{20,24},{24,28},{28,0},{1,5},{5... | collective-permute-start | bytes 589832 | tf_op jit(solution)/shard_map/while/body/eval_jaxpr/ppermute | solution.py:23
  96.3 6.5 collective-permute-start
  97.2 7.3 %collective-permute-start.1 = (bf16[1,128,12,64]{1,3,2,0:T(8,128)(2,1)S(1)}, bf16[1,128,12,64]{1,3,2,0:T(8,128)(2,1)}, u32[]{:S(2)}, u32[]{:S(2)}) collective-permute-start(bf16[1,128,12,64]{1,3,2,0:T(8,128)(2,1)S(1)} %copy.81), channel_id=1, source_target_pairs={{0,4},{4,8},{8,12},{12,16},{16,20},{20,24},{24,28},{28,0},{1,5},{5... | collective-permute-start | bytes 589832 | tf_op jit(solution)/shard_map/while/body/eval_jaxpr/ppermute | solution.py:23
  105.4 10.0 %collective-permute-start = (bf16[1,128,12,64]{1,3,2,0:T(8,128)(2,1)S(1)}, bf16[1,128,12,64]{1,3,2,0:T(8,128)(2,1)}, u32[]{:S(2)}, u32[]{:S(2)}) collective-permute-start(bf16[1,128,12,64]{1,3,2,0:T(8,128)(2,1)S(1)} %copy.80), channel_id=1, source_target_pairs={{0,4},{4,8},{8,12},{12,16},{16,20},{20,24},{24,28},{28,0},{1,5},{5... | collective-permute-start | bytes 589832 | tf_op jit(solution)/shard_map/while/body/eval_jaxpr/ppermute | solution.py:23
  106.3 12.9 %collective-permute-start.1 = (bf16[1,128,12,64]{1,3,2,0:T(8,128)(2,1)S(1)}, bf16[1,128,12,64]{1,3,2,0:T(8,128)(2,1)}, u32[]{:S(2)}, u32[]{:S(2)}) collective-permute-start(bf16[1,128,12,64]{1,3,2,0:T(8,128)(2,1)S(1)} %copy.81), channel_id=1, source_target_pairs={{0,4},{4,8},{8,12},{12,16},{16,20},{20,24},{24,28},{28,0},{1,5},{5... | collective-permute-start | bytes 589832 | tf_op jit(solution)/shard_map/while/body/eval_jaxpr/ppermute | solution.py:23
  121.1 7.3 %collective-permute-start.1 = (bf16[1,128,12,64]{1,3,2,0:T(8,128)(2,1)S(1)}, bf16[1,128,12,64]{1,3,2,0:T(8,128)(2,1)}, u32[]{:S(2)}, u32[]{:S(2)}) collective-permute-start(bf16[1,128,12,64]{1,3,2,0:T(8,128)(2,1)S(1)} %copy.81), channel_id=1, source_target_pairs={{0,4},{4,8},{8,12},{12,16},{16,20},{20,24},{24,28},{28,0},{1,5},{5... | collective-permute-start | bytes 589832 | tf_op jit(solution)/shard_map/while/body/eval_jaxpr/ppermute | solution.py:23
  129.3 10.3 %collective-permute-start = (bf16[1,128,12,64]{1,3,2,0:T(8,128)(2,1)S(1)}, bf16[1,128,12,64]{1,3,2,0:T(8,128)(2,1)}, u32[]{:S(2)}, u32[]{:S(2)}) collective-permute-start(bf16[1,128,12,64]{1,3,2,0:T(8,128)(2,1)S(1)} %copy.80), channel_id=1, source_target_pairs={{0,4},{4,8},{8,12},{12,16},{16,20},{20,24},{24,28},{28,0},{1,5},{5... | collective-permute-start | bytes 589832 | tf_op jit(solution)/shard_map/while/body/eval_jaxpr/ppermute | solution.py:23
  130.2 15.6 %collective-permute-start.1 = (bf16[1,128,12,64]{1,3,2,0:T(8,128)(2,1)S(1)}, bf16[1,128,12,64]{1,3,2,0:T(8,128)(2,1)}, u32[]{:S(2)}, u32[]{:S(2)}) collective-permute-start(bf16[1,128,12,64]{1,3,2,0:T(8,128)(2,1)S(1)} %copy.81), channel_id=1, source_target_pairs={{0,4},{4,8},{8,12},{12,16},{16,20},{20,24},{24,28},{28,0},{1,5},{5... | collective-permute-start | bytes 589832 | tf_op jit(solution)/shard_map/while/body/eval_jaxpr/ppermute | solution.py:23
  147.8 7.3 %collective-permute-start.1 = (bf16[1,128,12,64]{1,3,2,0:T(8,128)(2,1)S(1)}, bf16[1,128,12,64]{1,3,2,0:T(8,128)(2,1)}, u32[]{:S(2)}, u32[]{:S(2)}) collective-permute-start(bf16[1,128,12,64]{1,3,2,0:T(8,128)(2,1)S(1)} %copy.81), channel_id=1, source_target_pairs={{0,4},{4,8},{8,12},{12,16},{16,20},{20,24},{24,28},{28,0},{1,5},{5... | collective-permute-start | bytes 589832 | tf_op jit(solution)/shard_map/while/body/eval_jaxpr/ppermute | solution.py:23
  156.9 7.3 %collective-permute-start.1 = (bf16[1,128,12,64]{1,3,2,0:T(8,128)(2,1)S(1)}, bf16[1,128,12,64]{1,3,2,0:T(8,128)(2,1)}, u32[]{:S(2)}, u32[]{:S(2)}) collective-permute-start(bf16[1,128,12,64]{1,3,2,0:T(8,128)(2,1)S(1)} %copy.81), channel_id=1, source_target_pairs={{0,4},{4,8},{8,12},{12,16},{16,20},{20,24},{24,28},{28,0},{1,5},{5... | collective-permute-start | bytes 589832 | tf_op jit(solution)/shard_map/while/body/eval_jaxpr/ppermute | solution.py:23
  165.1 6.8 %collective-permute-start = (bf16[1,128,12,64]{1,3,2,0:T(8,128)(2,1)S(1)}, bf16[1,128,12,64]{1,3,2,0:T(8,128)(2,1)}, u32[]{:S(2)}, u32[]{:S(2)}) collective-permute-start(bf16[1,128,12,64]{1,3,2,0:T(8,128)(2,1)S(1)} %copy.80), channel_id=1, source_target_pairs={{0,4},{4,8},{8,12},{12,16},{16,20},{20,24},{24,28},{28,0},{1,5},{5... | collective-permute-start | bytes 589832 | tf_op jit(solution)/shard_map/while/body/eval_jaxpr/ppermute | solution.py:23
  166.0 8.0 %collective-permute-start.1 = (bf16[1,128,12,64]{1,3,2,0:T(8,128)(2,1)S(1)}, bf16[1,128,12,64]{1,3,2,0:T(8,128)(2,1)}, u32[]{:S(2)}, u32[]{:S(2)}) collective-permute-start(bf16[1,128,12,64]{1,3,2,0:T(8,128)(2,1)S(1)} %copy.81), channel_id=1, source_target_pairs={{0,4},{4,8},{8,12},{12,16},{16,20},{20,24},{24,28},{28,0},{1,5},{5... | collective-permute-start | bytes 589832 | tf_op jit(solution)/shard_map/while/body/eval_jaxpr/ppermute | solution.py:23
  234.6 266.4 %reduce-scatter.4.cloned.1.call-start = ((), (), s32[]{:S(2)}) async-start(), calls=%async_computation.6 | async-start | bytes 9732096 | tf_op jit(solution)/shard_map/reduce_scatter | solution.py:287
  235.6 14.7 %collective-permute-start.2 = (bf16[1,128,12,64]{1,3,2,0:T(8,128)(2,1)S(1)}, bf16[1,128,12,64]{1,3,2,0:T(8,128)(2,1)S(1)}, u32[]{:S(2)}, u32[]{:S(2)}) collective-permute-start(bf16[1,128,12,64]{1,3,2,0:T(8,128)(2,1)S(1)} %copy.99), channel_id=1, source_target_pairs={{0,4},{4,8},{8,12},{12,16},{16,20},{20,24},{24,28},{28,0},{1,5},{5... | collective-permute-start | bytes 589832 | tf_op jit(solution)/shard_map/while/body/eval_jaxpr/ppermute | solution.py:23
  236.0 14.4 %collective-permute-start.3 = (bf16[1,128,12,64]{1,3,2,0:T(8,128)(2,1)S(1)}, bf16[1,128,12,64]{1,3,2,0:T(8,128)(2,1)S(1)}, u32[]{:S(2)}, u32[]{:S(2)}) collective-permute-start(bf16[1,128,12,64]{1,3,2,0:T(8,128)(2,1)S(1)} %copy.100), channel_id=1, source_target_pairs={{0,4},{4,8},{8,12},{12,16},{16,20},{20,24},{24,28},{28,0},{1,5},{5... | collective-permute-start | bytes 589832 | tf_op jit(solution)/shard_map/while/body/eval_jaxpr/ppermute | solution.py:23
  241.0 6.3 collective-permute-start.4
  242.2 7.2 %collective-permute-start.5 = (bf16[1,128,12,64]{1,3,2,0:T(8,128)(2,1)}, bf16[1,128,12,64]{1,3,2,0:T(8,128)(2,1)}, u32[]{:S(2)}, u32[]{:S(2)}) collective-permute-start(bf16[1,128,12,64]{1,3,2,0:T(8,128)(2,1)} %fusion.190), channel_id=1, source_target_pairs={{0,4},{4,8},{8,12},{12,16},{16,20},{20,24},{24,28},{28,0},{1,5},{5... | collective-permute-start | bytes 589832 | tf_op jit(solution)/shard_map/while/body/eval_jaxpr/ppermute | solution.py:23
  250.4 13.9 %collective-permute-start.2 = (bf16[1,128,12,64]{1,3,2,0:T(8,128)(2,1)S(1)}, bf16[1,128,12,64]{1,3,2,0:T(8,128)(2,1)S(1)}, u32[]{:S(2)}, u32[]{:S(2)}) collective-permute-start(bf16[1,128,12,64]{1,3,2,0:T(8,128)(2,1)S(1)} %copy.99), channel_id=1, source_target_pairs={{0,4},{4,8},{8,12},{12,16},{16,20},{20,24},{24,28},{28,0},{1,5},{5... | collective-permute-start | bytes 589832 | tf_op jit(solution)/shard_map/while/body/eval_jaxpr/ppermute | solution.py:23
  250.5 13.8 %collective-permute-start.3 = (bf16[1,128,12,64]{1,3,2,0:T(8,128)(2,1)S(1)}, bf16[1,128,12,64]{1,3,2,0:T(8,128)(2,1)S(1)}, u32[]{:S(2)}, u32[]{:S(2)}) collective-permute-start(bf16[1,128,12,64]{1,3,2,0:T(8,128)(2,1)S(1)} %copy.100), channel_id=1, source_target_pairs={{0,4},{4,8},{8,12},{12,16},{16,20},{20,24},{24,28},{28,0},{1,5},{5... | collective-permute-start | bytes 589832 | tf_op jit(solution)/shard_map/while/body/eval_jaxpr/ppermute | solution.py:23
  254.9 6.3 collective-permute-start.4
  255.9 7.4 %collective-permute-start.5 = (bf16[1,128,12,64]{1,3,2,0:T(8,128)(2,1)}, bf16[1,128,12,64]{1,3,2,0:T(8,128)(2,1)}, u32[]{:S(2)}, u32[]{:S(2)}) collective-permute-start(bf16[1,128,12,64]{1,3,2,0:T(8,128)(2,1)} %fusion.190), channel_id=1, source_target_pairs={{0,4},{4,8},{8,12},{12,16},{16,20},{20,24},{24,28},{28,0},{1,5},{5... | collective-permute-start | bytes 589832 | tf_op jit(solution)/shard_map/while/body/eval_jaxpr/ppermute | solution.py:23
  264.4 13.8 %collective-permute-start.2 = (bf16[1,128,12,64]{1,3,2,0:T(8,128)(2,1)S(1)}, bf16[1,128,12,64]{1,3,2,0:T(8,128)(2,1)S(1)}, u32[]{:S(2)}, u32[]{:S(2)}) collective-permute-start(bf16[1,128,12,64]{1,3,2,0:T(8,128)(2,1)S(1)} %copy.99), channel_id=1, source_target_pairs={{0,4},{4,8},{8,12},{12,16},{16,20},{20,24},{24,28},{28,0},{1,5},{5... | collective-permute-start | bytes 589832 | tf_op jit(solution)/shard_map/while/body/eval_jaxpr/ppermute | solution.py:23
  264.4 13.8 %collective-permute-start.3 = (bf16[1,128,12,64]{1,3,2,0:T(8,128)(2,1)S(1)}, bf16[1,128,12,64]{1,3,2,0:T(8,128)(2,1)S(1)}, u32[]{:S(2)}, u32[]{:S(2)}) collective-permute-start(bf16[1,128,12,64]{1,3,2,0:T(8,128)(2,1)S(1)} %copy.100), channel_id=1, source_target_pairs={{0,4},{4,8},{8,12},{12,16},{16,20},{20,24},{24,28},{28,0},{1,5},{5... | collective-permute-start | bytes 589832 | tf_op jit(solution)/shard_map/while/body/eval_jaxpr/ppermute | solution.py:23
  268.8 6.3 collective-permute-start.4
  269.8 7.4 %collective-permute-start.5 = (bf16[1,128,12,64]{1,3,2,0:T(8,128)(2,1)}, bf16[1,128,12,64]{1,3,2,0:T(8,128)(2,1)}, u32[]{:S(2)}, u32[]{:S(2)}) collective-permute-start(bf16[1,128,12,64]{1,3,2,0:T(8,128)(2,1)} %fusion.190), channel_id=1, source_target_pairs={{0,4},{4,8},{8,12},{12,16},{16,20},{20,24},{24,28},{28,0},{1,5},{5... | collective-permute-start | bytes 589832 | tf_op jit(solution)/shard_map/while/body/eval_jaxpr/ppermute | solution.py:23
  278.2 22.1 %collective-permute-start.2 = (bf16[1,128,12,64]{1,3,2,0:T(8,128)(2,1)S(1)}, bf16[1,128,12,64]{1,3,2,0:T(8,128)(2,1)S(1)}, u32[]{:S(2)}, u32[]{:S(2)}) collective-permute-start(bf16[1,128,12,64]{1,3,2,0:T(8,128)(2,1)S(1)} %copy.99), channel_id=1, source_target_pairs={{0,4},{4,8},{8,12},{12,16},{16,20},{20,24},{24,28},{28,0},{1,5},{5... | collective-permute-start | bytes 589832 | tf_op jit(solution)/shard_map/while/body/eval_jaxpr/ppermute | solution.py:23
  278.3 22.0 %collective-permute-start.3 = (bf16[1,128,12,64]{1,3,2,0:T(8,128)(2,1)S(1)}, bf16[1,128,12,64]{1,3,2,0:T(8,128)(2,1)S(1)}, u32[]{:S(2)}, u32[]{:S(2)}) collective-permute-start(bf16[1,128,12,64]{1,3,2,0:T(8,128)(2,1)S(1)} %copy.100), channel_id=1, source_target_pairs={{0,4},{4,8},{8,12},{12,16},{16,20},{20,24},{24,28},{28,0},{1,5},{5... | collective-permute-start | bytes 589832 | tf_op jit(solution)/shard_map/while/body/eval_jaxpr/ppermute | solution.py:23
  282.7 10.3 %collective-permute-start.4 = (bf16[1,128,12,64]{1,3,2,0:T(8,128)(2,1)}, bf16[1,128,12,64]{1,3,2,0:T(8,128)(2,1)}, u32[]{:S(2)}, u32[]{:S(2)}) collective-permute-start(bf16[1,128,12,64]{1,3,2,0:T(8,128)(2,1)} %fusion.189), channel_id=1, source_target_pairs={{0,4},{4,8},{8,12},{12,16},{16,20},{20,24},{24,28},{28,0},{1,5},{5... | collective-permute-start | bytes 589832 | tf_op jit(solution)/shard_map/while/body/eval_jaxpr/ppermute | solution.py:23
  283.7 15.7 %collective-permute-start.5 = (bf16[1,128,12,64]{1,3,2,0:T(8,128)(2,1)}, bf16[1,128,12,64]{1,3,2,0:T(8,128)(2,1)}, u32[]{:S(2)}, u32[]{:S(2)}) collective-permute-start(bf16[1,128,12,64]{1,3,2,0:T(8,128)(2,1)} %fusion.190), channel_id=1, source_target_pairs={{0,4},{4,8},{8,12},{12,16},{16,20},{20,24},{24,28},{28,0},{1,5},{5... | collective-permute-start | bytes 589832 | tf_op jit(solution)/shard_map/while/body/eval_jaxpr/ppermute | solution.py:23
  300.4 14.8 %collective-permute-start.2 = (bf16[1,128,12,64]{1,3,2,0:T(8,128)(2,1)S(1)}, bf16[1,128,12,64]{1,3,2,0:T(8,128)(2,1)S(1)}, u32[]{:S(2)}, u32[]{:S(2)}) collective-permute-start(bf16[1,128,12,64]{1,3,2,0:T(8,128)(2,1)S(1)} %copy.99), channel_id=1, source_target_pairs={{0,4},{4,8},{8,12},{12,16},{16,20},{20,24},{24,28},{28,0},{1,5},{5... | collective-permute-start | bytes 589832 | tf_op jit(solution)/shard_map/while/body/eval_jaxpr/ppermute | solution.py:23
  300.5 14.8 %collective-permute-start.3 = (bf16[1,128,12,64]{1,3,2,0:T(8,128)(2,1)S(1)}, bf16[1,128,12,64]{1,3,2,0:T(8,128)(2,1)S(1)}, u32[]{:S(2)}, u32[]{:S(2)}) collective-permute-start(bf16[1,128,12,64]{1,3,2,0:T(8,128)(2,1)S(1)} %copy.100), channel_id=1, source_target_pairs={{0,4},{4,8},{8,12},{12,16},{16,20},{20,24},{24,28},{28,0},{1,5},{5... | collective-permute-start | bytes 589832 | tf_op jit(solution)/shard_map/while/body/eval_jaxpr/ppermute | solution.py:23
  306.8 7.4 %collective-permute-start.5 = (bf16[1,128,12,64]{1,3,2,0:T(8,128)(2,1)}, bf16[1,128,12,64]{1,3,2,0:T(8,128)(2,1)}, u32[]{:S(2)}, u32[]{:S(2)}) collective-permute-start(bf16[1,128,12,64]{1,3,2,0:T(8,128)(2,1)} %fusion.190), channel_id=1, source_target_pairs={{0,4},{4,8},{8,12},{12,16},{16,20},{20,24},{24,28},{28,0},{1,5},{5... | collective-permute-start | bytes 589832 | tf_op jit(solution)/shard_map/while/body/eval_jaxpr/ppermute | solution.py:23
  315.3 16.3 %collective-permute-start.2 = (bf16[1,128,12,64]{1,3,2,0:T(8,128)(2,1)S(1)}, bf16[1,128,12,64]{1,3,2,0:T(8,128)(2,1)S(1)}, u32[]{:S(2)}, u32[]{:S(2)}) collective-permute-start(bf16[1,128,12,64]{1,3,2,0:T(8,128)(2,1)S(1)} %copy.99), channel_id=1, source_target_pairs={{0,4},{4,8},{8,12},{12,16},{16,20},{20,24},{24,28},{28,0},{1,5},{5... | collective-permute-start | bytes 589832 | tf_op jit(solution)/shard_map/while/body/eval_jaxpr/ppermute | solution.py:23
  315.4 16.2 %collective-permute-start.3 = (bf16[1,128,12,64]{1,3,2,0:T(8,128)(2,1)S(1)}, bf16[1,128,12,64]{1,3,2,0:T(8,128)(2,1)S(1)}, u32[]{:S(2)}, u32[]{:S(2)}) collective-permute-start(bf16[1,128,12,64]{1,3,2,0:T(8,128)(2,1)S(1)} %copy.100), channel_id=1, source_target_pairs={{0,4},{4,8},{8,12},{12,16},{16,20},{20,24},{24,28},{28,0},{1,5},{5... | collective-permute-start | bytes 589832 | tf_op jit(solution)/shard_map/while/body/eval_jaxpr/ppermute | solution.py:23
  320.9 7.6 %collective-permute-start.4 = (bf16[1,128,12,64]{1,3,2,0:T(8,128)(2,1)}, bf16[1,128,12,64]{1,3,2,0:T(8,128)(2,1)}, u32[]{:S(2)}, u32[]{:S(2)}) collective-permute-start(bf16[1,128,12,64]{1,3,2,0:T(8,128)(2,1)} %fusion.189), channel_id=1, source_target_pairs={{0,4},{4,8},{8,12},{12,16},{16,20},{20,24},{24,28},{28,0},{1,5},{5... | collective-permute-start | bytes 589832 | tf_op jit(solution)/shard_map/while/body/eval_jaxpr/ppermute | solution.py:23
  321.9 8.8 %collective-permute-start.5 = (bf16[1,128,12,64]{1,3,2,0:T(8,128)(2,1)}, bf16[1,128,12,64]{1,3,2,0:T(8,128)(2,1)}, u32[]{:S(2)}, u32[]{:S(2)}) collective-permute-start(bf16[1,128,12,64]{1,3,2,0:T(8,128)(2,1)} %fusion.190), channel_id=1, source_target_pairs={{0,4},{4,8},{8,12},{12,16},{16,20},{20,24},{24,28},{28,0},{1,5},{5... | collective-permute-start | bytes 589832 | tf_op jit(solution)/shard_map/while/body/eval_jaxpr/ppermute | solution.py:23
  331.6 13.6 %collective-permute-start.2 = (bf16[1,128,12,64]{1,3,2,0:T(8,128)(2,1)S(1)}, bf16[1,128,12,64]{1,3,2,0:T(8,128)(2,1)S(1)}, u32[]{:S(2)}, u32[]{:S(2)}) collective-permute-start(bf16[1,128,12,64]{1,3,2,0:T(8,128)(2,1)S(1)} %copy.99), channel_id=1, source_target_pairs={{0,4},{4,8},{8,12},{12,16},{16,20},{20,24},{24,28},{28,0},{1,5},{5... | collective-permute-start | bytes 589832 | tf_op jit(solution)/shard_map/while/body/eval_jaxpr/ppermute | solution.py:23
  331.7 13.5 %collective-permute-start.3 = (bf16[1,128,12,64]{1,3,2,0:T(8,128)(2,1)S(1)}, bf16[1,128,12,64]{1,3,2,0:T(8,128)(2,1)S(1)}, u32[]{:S(2)}, u32[]{:S(2)}) collective-permute-start(bf16[1,128,12,64]{1,3,2,0:T(8,128)(2,1)S(1)} %copy.100), channel_id=1, source_target_pairs={{0,4},{4,8},{8,12},{12,16},{16,20},{20,24},{24,28},{28,0},{1,5},{5... | collective-permute-start | bytes 589832 | tf_op jit(solution)/shard_map/while/body/eval_jaxpr/ppermute | solution.py:23
  336.8 7.4 %collective-permute-start.5 = (bf16[1,128,12,64]{1,3,2,0:T(8,128)(2,1)}, bf16[1,128,12,64]{1,3,2,0:T(8,128)(2,1)}, u32[]{:S(2)}, u32[]{:S(2)}) collective-permute-start(bf16[1,128,12,64]{1,3,2,0:T(8,128)(2,1)} %fusion.190), channel_id=1, source_target_pairs={{0,4},{4,8},{8,12},{12,16},{16,20},{20,24},{24,28},{28,0},{1,5},{5... | collective-permute-start | bytes 589832 | tf_op jit(solution)/shard_map/while/body/eval_jaxpr/ppermute | solution.py:23
  345.3 14.9 %collective-permute-start.2 = (bf16[1,128,12,64]{1,3,2,0:T(8,128)(2,1)S(1)}, bf16[1,128,12,64]{1,3,2,0:T(8,128)(2,1)S(1)}, u32[]{:S(2)}, u32[]{:S(2)}) collective-permute-start(bf16[1,128,12,64]{1,3,2,0:T(8,128)(2,1)S(1)} %copy.99), channel_id=1, source_target_pairs={{0,4},{4,8},{8,12},{12,16},{16,20},{20,24},{24,28},{28,0},{1,5},{5... | collective-permute-start | bytes 589832 | tf_op jit(solution)/shard_map/while/body/eval_jaxpr/ppermute | solution.py:23
  345.3 14.8 %collective-permute-start.3 = (bf16[1,128,12,64]{1,3,2,0:T(8,128)(2,1)S(1)}, bf16[1,128,12,64]{1,3,2,0:T(8,128)(2,1)S(1)}, u32[]{:S(2)}, u32[]{:S(2)}) collective-permute-start(bf16[1,128,12,64]{1,3,2,0:T(8,128)(2,1)S(1)} %copy.100), channel_id=1, source_target_pairs={{0,4},{4,8},{8,12},{12,16},{16,20},{20,24},{24,28},{28,0},{1,5},{5... | collective-permute-start | bytes 589832 | tf_op jit(solution)/shard_map/while/body/eval_jaxpr/ppermute | solution.py:23
  351.7 7.4 %collective-permute-start.5 = (bf16[1,128,12,64]{1,3,2,0:T(8,128)(2,1)}, bf16[1,128,12,64]{1,3,2,0:T(8,128)(2,1)}, u32[]{:S(2)}, u32[]{:S(2)}) collective-permute-start(bf16[1,128,12,64]{1,3,2,0:T(8,128)(2,1)} %fusion.190), channel_id=1, source_target_pairs={{0,4},{4,8},{8,12},{12,16},{16,20},{20,24},{24,28},{28,0},{1,5},{5... | collective-permute-start | bytes 589832 | tf_op jit(solution)/shard_map/while/body/eval_jaxpr/ppermute | solution.py:23
  367.4 293.9 %reduce-scatter.6.cloned.1.call-start = ((), (), s32[]{:S(2)}) async-start(), calls=%async_computation.7 | async-start | bytes 12976128 | tf_op jit(solution)/shard_map/reduce_scatter | solution.py:288
  (64 other events, 2114.3 us)
Sparse Core Ops, SparseCore 0:
  11.7 66.3 all-gather.3
  81.5 73.7 all-gather.5
  158.8 58.1 all-gather.7
  234.7 123.9 reduce-scatter.7
  367.5 133.5 reduce-scatter.3
  506.9 154.3 reduce-scatter.5
where the time goes:
time: 673 us; the launch traced here: 671 us
  waiting for transfers between devices  365 us (54%)
  matrix products  95.5 us (14%)
  other arithmetic  71.8 us (11%)
  blocking collectives  48.7 us (7%)
  local copies, waits for them, and re-layouts  44.4 us (7%)
  starting transfers between devices  28.7 us (4%)
  between operations  14.9 us (2%)
    reduce_scatter x1, waiting for transfers between devices, shards(): lax.psum_scatter(grad_ffin, ('seq', 'batch'), scatter_dimension=1, tiled=...  158 us
    ppermute x48, waiting for transfers between devices, passed_along(): return lax.ppermute(value, axis, pairs)  63.6 us
    reduce_scatter x1, waiting for transfers between devices, shards(): lax.psum_scatter(grad_attention, ('seq', 'batch'), scatter_dimension=1, t...  62.1 us
    dot_general x29, matrix products, matmul(): return jnp.dot(left_rows, right_rows, preferred_element_type=jnp.float32)  54.3 us
    all_gather x1, waiting for transfers between devices, shards(): lax.all_gather(attention_weight.astype(jnp.bfloat16), ('seq', 'batch'), a...  50.6 us
    psum x1, blocking collectives, shards(): lax.psum((bias_total, jnp.stack([first_gain_grad, second_gain_grad])), ('...  38.4 us
    all_gather x1, waiting for transfers between devices, shards(): lax.all_gather(ffout_weight.astype(jnp.bfloat16), ('seq', 'batch'), axis=...  31 us
    ppermute x48, starting transfers between devices, passed_along(): return lax.ppermute(value, axis, pairs)  28.2 us
  transfers between devices with their start and end apart: 54, of which 34 were waited for; matrix products, arithmetic and copies ran while one was open for 28% of the time, Pallas kernels for 0%

commit v1 on v0

v1 whole, which is shorter than its diff:
```python
import functools
import math

import jax
import jax.numpy as jnp
from jax import lax
from jax.experimental import pallas as pl
from jax.experimental.pallas import tpu as pltpu
from jax.sharding import PartitionSpec as P

eps_norm = 1e-06
momentum_coef = 0.5
average_coef = 0.5
attention_rates = (0.0033, 0.0033, 0.025, 0.2)
ffin_rate = 0.063
ffout_rate = 0.023
bias_rate = 0.08
gain_rates = (0.045, 0.22)
thresholds = (12, 16, 23, 32, 46, 64, 91)
masked_score = -1e30
gelu_scale = math.sqrt(2.0 / math.pi)
gelu_cubic = 0.044715
bf16 = jnp.bfloat16
f32 = jnp.float32
vmem_bytes = 60 * 1024 * 1024
lanes = 128


def product(left, right, left_dim, right_dim):
    return lax.dot_general(
        left, right, (((left_dim,), (right_dim,)), ((), ())), preferred_element_type=f32
    )


def mm(left, right):
    return product(left, right, 1, 0)


def mm_nt(left, right):
    return product(left, right, 1, 1)


def mm_tn(left, right):
    return product(left, right, 0, 0)


def bucket_of(offset):
    magnitude = jnp.abs(offset)
    beyond = jnp.zeros_like(offset)
    for threshold in thresholds:
        beyond = beyond + (magnitude >= threshold).astype(jnp.int32)
    inside = jnp.where(magnitude < 8, magnitude, 8 + beyond)
    return inside + 16 * (offset > 0).astype(jnp.int32)


def update(weight, grad, momentum, average, rate):
    new_momentum = momentum_coef * momentum + grad
    new_weight = weight - rate * (grad + momentum_coef * new_momentum)
    new_average = average_coef * average + (1.0 - average_coef) * new_weight
    return (new_weight, new_momentum, new_average)


def rms_scale(values):
    return lax.rsqrt(jnp.mean(values * values, axis=-1, keepdims=True) + eps_norm)


def params():
    return pltpu.CompilerParams(vmem_limit_bytes=vmem_bytes)


def any_spec():
    return pl.BlockSpec(memory_space=pl.ANY)


def cost(flops, nbytes, exps=0):
    return pl.CostEstimate(flops=int(flops), bytes_accessed=int(nbytes), transcendentals=int(exps))


def bias_kernel(table_ref, out_ref):
    head = pl.program_id(0)
    spot = lax.broadcasted_iota(jnp.int32, (8, 2 * lanes), 1)
    for block in range(3):
        buckets = bucket_of(lanes * (block - 1) + lanes - 1 - spot)
        row = jnp.zeros((8, 2 * lanes), f32)
        for bucket in range(table_ref.shape[0]):
            row = jnp.where(buckets == bucket, table_ref[bucket, head], row)
        wide = jnp.broadcast_to(row[:1], (lanes, 2 * lanes))
        rolled = pltpu.roll(wide, lanes + 1, 1, stride=1, stride_axis=0)
        out_ref[0, lanes * (block + 1) : lanes * (block + 2), :] = rolled[:, :lanes]
    out_ref[0, 0:lanes, :] = jnp.full((lanes, lanes), table_ref[15, head], f32)
    out_ref[0, 4 * lanes : 5 * lanes, :] = jnp.full((lanes, lanes), table_ref[31, head], f32)


def bias_rows(table):
    heads = table.shape[1]
    return pl.pallas_call(
        bias_kernel,
        grid=(heads,),
        in_specs=[pl.BlockSpec(memory_space=pltpu.SMEM)],
        out_specs=pl.BlockSpec((1, 5 * lanes, lanes), lambda i: (i, 0, 0)),
        out_shape=jax.ShapeDtypeStruct((heads, 5 * lanes, lanes), f32),
        compiler_params=params(),
        cost_estimate=cost(heads * 3e6, 4e6),
        name="bias_rows",
    )(table)


def bias_sum_kernel(grad_ref, out_ref):
    row_id = lax.broadcasted_iota(jnp.int32, (lanes, 2 * lanes), 0)
    bucket_id = lax.broadcasted_iota(jnp.int32, (2 * lanes, lanes), 1)
    place = lax.broadcasted_iota(jnp.int32, (2 * lanes, lanes), 0)
    total = jnp.zeros((8, lanes), f32)
    for block in range(3):
        part = grad_ref[0, lanes * (block + 1) : lanes * (block + 2), :]
        wide = jnp.concatenate([part, jnp.zeros((lanes, lanes), f32)], axis=1)
        for bit in range(7):
            step = 1 << bit
            moved = pltpu.roll(wide, step, 1)
            wide = jnp.where((row_id & step) == 0, moved, wide)
        sums = jnp.sum(wide.reshape(lanes // 8, 8, 2 * lanes), axis=0)
        onehot = (bucket_of(lanes * (block - 1) + lanes - 1 - place) == bucket_id).astype(f32)
        total = total + lax.dot_general(
            sums,
            onehot,
            (((1,), (0,)), ((), ())),
            precision=lax.Precision.HIGHEST,
            preferred_element_type=f32,
        )
    low = jnp.sum(grad_ref[0, 0:lanes, :])
    high = jnp.sum(grad_ref[0, 4 * lanes : 5 * lanes, :])
    lane = lax.broadcasted_iota(jnp.int32, (1, lanes), 1)
    row = jnp.sum(total, axis=0, keepdims=True)
    row = row + jnp.where(lane == 15, low, 0.0) + jnp.where(lane == 31, high, 0.0)
    out_ref[0] = row


def bias_sums(grad_band):
    heads = grad_band.shape[0]
    summed = pl.pallas_call(
        bias_sum_kernel,
        grid=(heads,),
        in_specs=[pl.BlockSpec((1, 5 * lanes, lanes), lambda i: (i, 0, 0))],
        out_specs=pl.BlockSpec((1, 1, lanes), lambda i: (i, 0, 0)),
        out_shape=jax.ShapeDtypeStruct((heads, 1, lanes), f32),
        compiler_params=params(),
        cost_estimate=cost(heads * 3e6, 4e6),
        name="bias_sums",
    )(grad_band)
    return summed.reshape(heads, lanes)


def row_block(meta_ref, slot, rows):
    start = meta_ref[slot] * rows
    return pl.ds(pl.multiple_of(start, 16) if rows % 16 == 0 else start, rows)


def run_copies(pairs, sem):
    copies = [pltpu.make_async_copy(a, b, sem.at[i]) for i, (a, b) in enumerate(pairs)]
    for copy in copies:
        copy.start()
    return copies


def wait_all(copies):
    for copy in copies:
        copy.wait()


def whole_spec():
    return pl.BlockSpec(memory_space=pltpu.VMEM)


def smem_spec():
    return pl.BlockSpec(memory_space=pltpu.SMEM)


def dma(count):
    return pltpu.SemaphoreType.DMA((count,))


def shaped(kind, *shape):
    return jax.ShapeDtypeStruct(shape, kind)


def rows_kernel(width, count, meta_ref, *refs):
    pieces, (full_ref, turned_ref, mask_ref) = refs[:count], refs[count:]
    chip_ids = pieces[0][:, width : width + lanes].astype(f32).T[:1, :]
    for index, piece in enumerate(pieces):
        rows = piece.shape[0]
        grain = min(rows, lanes)
        for part in range(rows // grain):
            start = meta_ref[index] + part * grain
            place = pl.ds(pl.multiple_of(start, grain), grain)
            local = piece[part * grain : (part + 1) * grain, :]
            full_ref[place, :] = local[:, :width]
            wide = local[:, width : width + lanes].astype(f32)
            same = jnp.concatenate([wide, wide], axis=1) == chip_ids
            mask_ref[place, :] = jnp.where(same, 0.0, masked_score)
    for start in range(0, full_ref.shape[0], lanes):
        turned_ref[:, start : start + lanes] = full_ref[start : start + lanes, :].T


def place_rows(pieces, starts, width):
    length = sum(piece.shape[0] for piece in pieces)
    return pl.pallas_call(
        functools.partial(rows_kernel, width, len(pieces)),
        in_specs=[smem_spec()] + [whole_spec()] * len(pieces),
        out_specs=[whole_spec()] * 3,
        out_shape=[
            shaped(bf16, length, width),
            shaped(bf16, width, length),
            shaped(f32, length, 2 * lanes),
        ],
        compiler_params=params(),
        cost_estimate=cost(3e6, 8e6),
        name="place_rows",
    )(starts, *pieces)


def one_head(matrix, half):
    first = lax.broadcasted_iota(jnp.int32, matrix.shape, 1) < matrix.shape[1] // 2
    return jnp.where(first if half == 0 else jnp.logical_not(first), matrix, jnp.zeros_like(matrix))


def band_place(block, chip, part):
    kind = jnp.clip(block - (2 * chip + part) + 2, 0, 4)
    return pl.ds(pl.multiple_of(kind * lanes, lanes), lanes)


def attend_kernel(plan, meta_ref, rows_ref, mask_ref, bias_ref, *refs):
    count = plan[-1][0] + 1
    pieces = refs[:count]
    q_ref, k_ref, v_ref, p_ref, o_ref = refs[count : count + 5]
    weight, score, soft, sem = refs[count + 5 :]
    pair = pl.program_id(0)
    chip = meta_ref[0]
    length = rows_ref.shape[0]
    blocks = length // lanes
    group = 2 * lanes

    @pl.when(pair == 0)
    def _():
        pairs = []
        for index, lead, target, size, slot in plan:
            size = min(size, 3 - target)
            place = row_block(meta_ref, slot, pieces[index].shape[1])
            pairs.append(
                (pieces[index].at[lead : lead + size], weight.at[target : target + size, place, :])
            )
        wait_all(run_copies(pairs, sem))

    cols = pl.ds(pl.multiple_of(pair * lanes, lanes), lanes)
    own = rows_ref[pl.ds(pl.multiple_of(chip * group, group), group), :]
    query = mm(own, weight[0, :, cols]).astype(bf16)
    both = jnp.concatenate([weight[1, :, cols], weight[2, :, cols]], axis=1)
    key_value = mm(rows_ref[...], both).astype(bf16)
    key, value = key_value[:, :lanes], key_value[:, lanes:]
    q_ref[...] = query
    k_ref[...] = key
    v_ref[...] = value
    turned = []
    for half in range(2):
        score[...] = mm_nt(key, one_head(query, half))
        best = jnp.full((8, group), masked_score, f32)
        for block in range(blocks):
            rows = slice(block * lanes, (block + 1) * lanes)
            bias = [bias_ref[half, band_place(block, chip, part), :] for part in range(2)]
            now = score[rows, :] + jnp.concatenate(bias, axis=1) + mask_ref[rows, :]
            score[rows, :] = now
            best = jnp.maximum(best, jnp.max(now.reshape(lanes // 8, 8, group), axis=0))
        top = jnp.max(best, axis=0, keepdims=True)
        total = jnp.zeros((8, group), f32)
        for block in range(blocks):
            rows = slice(block * lanes, (block + 1) * lanes)
            now = jnp.exp(score[rows, :] - top)
            score[rows, :] = now
            total = total + jnp.sum(now.reshape(lanes // 8, 8, group), axis=0)
        inverse = 1.0 / jnp.sum(total, axis=0, keepdims=True)
        for block in range(blocks):
            rows = slice(block * lanes, (block + 1) * lanes)
            now = score[rows, :] * inverse
            p_ref[half, rows, :] = now
            soft[rows, :] = now.astype(bf16)
        features = lanes // 2
        turned.append(mm_tn(value, soft[...])[half * features : (half + 1) * features])
    o_ref[...] = jnp.concatenate(turned, axis=0).T


def attend(plan, pieces, meta, rows, mask, bias):
    length, width = rows.shape
    half = width // 2
    group = 2 * lanes
    pairs = half // lanes
    col = lambda i, *_: (0, i)
    fixed = lambda i, *_: (0, 0)
    flops = 2 * (group * width * half + 2 * length * width * half + 4 * group * length * half)
    return pl.pallas_call(
        functools.partial(attend_kernel, plan),
        grid_spec=pltpu.PrefetchScalarGridSpec(
            num_scalar_prefetch=1,
            grid=(pairs,),
            in_specs=[
                pl.BlockSpec((length, width), fixed),
                pl.BlockSpec((length, group), fixed),
                pl.BlockSpec((2, 5 * lanes, lanes), lambda i, *_: (i, 0, 0)),
            ]
            + [any_spec()] * len(pieces),
            out_specs=[
                pl.BlockSpec((group, lanes), col),
                pl.BlockSpec((length, lanes), col),
                pl.BlockSpec((length, lanes), col),
                pl.BlockSpec((2, length, group), lambda i, *_: (i, 0, 0)),
                pl.BlockSpec((group, lanes), col),
            ],
            scratch_shapes=[
                pltpu.VMEM((3, width, half), bf16),
                pltpu.VMEM((length, group), f32),
                pltpu.VMEM((length, group), bf16),
                dma(len(plan)),
            ],
        ),
        out_shape=[
            shaped(bf16, group, half),
            shaped(bf16, length, half),
            shaped(bf16, length, half),
            shaped(f32, 2 * pairs, length, group),
            shaped(f32, group, half),
        ],
        compiler_params=params(),
        cost_estimate=cost(flops, 30e6, 2 * group * length * pairs),
        name="attend",
    )(meta, rows, mask, bias, *pieces)


def mix_kernel(meta_ref, attended_ref, near_ref, far_ref, part_ref, weight_ref, sem):
    chips, rows, half = near_ref.shape
    rows = rows // 2
    pairs = []
    for index, source in enumerate((near_ref, far_ref)):
        for step in range(chips):
            place = row_block(meta_ref, 1 + index * chips + step, rows)
            for side in range(2):
                pairs.append(
                    (
                        source.at[step, side * rows : (side + 1) * rows, :],
                        weight_ref.at[place, side * half : (side + 1) * half],
                    )
                )
    wait_all(run_copies(pairs, sem))
    core = meta_ref[0]
    mine = weight_ref[pl.ds(pl.multiple_of(core * half, half), half), :]
    part_ref[...] = mm(attended_ref[...].astype(bf16), mine)


def mix(meta, attended, near, far):
    group, half = attended.shape
    width = 2 * half
    return pl.pallas_call(
        mix_kernel,
        in_specs=[smem_spec(), whole_spec(), any_spec(), any_spec()],
        out_specs=[whole_spec()] * 2,
        out_shape=[shaped(f32, group, width), shaped(bf16, width, width)],
        scratch_shapes=[dma(4 * near.shape[0])],
        compiler_params=params(),
        cost_estimate=cost(2 * group * width * half, 4e6),
        name="mix",
    )(meta, attended, near, far)


def feed_kernel(
    gu_plan,
    down_count,
    meta_ref,
    tokens_ref,
    cot_ref,
    part_ref,
    arrived_ref,
    gain_ref,
    *refs,
):
    refs = list(refs)
    take = lambda n: [refs.pop(0) for _ in range(n)]
    gu_pieces = take(gu_plan[-1][0] + 1)
    down_pieces = take(down_count)
    mixed_ref, out_ref, back_ref, gu_out, down_out = take(5)
    gu, down, grad_gu, grad_down, cot_low, normed_low = take(6)
    gu_sem, down_sem, gu_out_sem, down_out_sem = take(4)
    step = pl.program_id(0)
    steps = pl.num_programs(0)
    block = 256
    chips = gu_out.shape[0]

    @pl.when(step == 0)
    def _():
        pairs = []
        for index, lead, target, size, slot in gu_plan:
            place = row_block(meta_ref, slot, gu_pieces[index].shape[1])
            pairs.append(
                (gu_pieces[index].at[lead : lead + size], gu.at[target : target + size, place, :])
            )
        gu_copies = run_copies(pairs, gu_sem)
        pairs = []
        slot = chips
        for piece in down_pieces:
            for index in range(piece.shape[0]):
                place = row_block(meta_ref, slot, piece.shape[1])
                pairs.append((piece.at[index], down.at[place, :]))
                slot += 1
        down_copies = run_copies(pairs, down_sem)
        mixed = tokens_ref[...] + part_ref[...] + arrived_ref[...]
        mixed_ref[...] = mixed
        normed_low[...] = (mixed * rms_scale(mixed) * gain_ref[...]).astype(bf16)
        cot_low[...] = cot_ref[...].astype(bf16)
        out_ref[...] = jnp.zeros_like(out_ref)
        back_ref[...] = jnp.zeros_like(back_ref)
        wait_all(gu_copies)
        wait_all(down_copies)

    cols = pl.ds(pl.multiple_of(step * block, block), block)
    normed = normed_low[...]
    cot = cot_low[...]
    gate_w, up_w, down_w = gu[0, :, cols], gu[1, :, cols], down[cols, :]
    gate, up = mm(normed, gate_w), mm(normed, up_w)
    square = gate * gate
    curve = jnp.tanh(gelu_scale * gate * (1.0 + gelu_cubic * square))
    half = 0.5 * (1.0 + curve)
    gelu = gate * half
    slope = half + 0.5 * gate * (1.0 - curve * curve) * gelu_scale * (1.0 + 3.0 * gelu_cubic * square)
    hidden = (gelu * up).astype(bf16)
    dh = mm_nt(cot, down_w)
    dgate = (dh * up * slope).astype(bf16)
    dup = (dh * gelu).astype(bf16)
    out_ref[...] += mm(hidden, down_w)
    back_ref[...] += mm_nt(dgate, gate_w) + mm_nt(dup, up_w)
    grad_down[cols, :] = mm_tn(hidden, cot).astype(bf16)
    grad_gu[0, :, cols] = mm_tn(normed, dgate).astype(bf16)
    grad_gu[1, :, cols] = mm_tn(normed, dup).astype(bf16)

    @pl.when(step == steps - 1)
    def _():
        pairs = []
        for index in range(chips):
            place = row_block(meta_ref, index, gu_out.shape[2])
            pairs.append((grad_gu.at[:, place, :], gu_out.at[index]))
        gu_copies = run_copies(pairs, gu_out_sem)
        pairs = []
        for index in range(chips):
            place = row_block(meta_ref, index, down_out.shape[1])
            pairs.append((grad_down.at[place, :], down_out.at[index]))
        down_copies = run_copies(pairs, down_out_sem)
        wait_all(gu_copies)
        wait_all(down_copies)


def feed(gu_plan, gu_pieces, down_pieces, meta, tokens, cot, part, arrived, gain, chips):
    group, width = tokens.shape
    hidden = gu_pieces[0].shape[2]
    block = 256
    fixed = lambda i, *_: (0, 0)
    full = lambda *shape: pl.BlockSpec(shape, fixed)
    flops = 2 * 9 * group * width * hidden
    down_copies = sum(piece.shape[0] for piece in down_pieces)
    return pl.pallas_call(
        functools.partial(feed_kernel, gu_plan, len(down_pieces)),
        grid_spec=pltpu.PrefetchScalarGridSpec(
            num_scalar_prefetch=1,
            grid=(hidden // block,),
            in_specs=[full(group, width)] * 4
            + [full(1, width)]
            + [any_spec()] * (len(gu_pieces) + len(down_pieces)),
            out_specs=[full(group, width)] * 3 + [any_spec()] * 2,
            scratch_shapes=[
                pltpu.VMEM((2, width, hidden), bf16),
                pltpu.VMEM((hidden, width), bf16),
                pltpu.VMEM((2, width, hidden), bf16),
                pltpu.VMEM((hidden, width), bf16),
                pltpu.VMEM((group, width), bf16),
                pltpu.VMEM((group, width), bf16),
                dma(len(gu_plan)),
                dma(down_copies),
                dma(chips),
                dma(chips),
            ],
        ),
        out_shape=[shaped(f32, group, width)] * 3
        + [shaped(bf16, chips, 2, width // chips, hidden), shaped(bf16, chips, hidden // chips, width)],
        compiler_params=params(),
        cost_estimate=cost(flops, 25e6, group * hidden),
        name="feed",
    )(meta, tokens, cot, part, arrived, gain, *gu_pieces, *down_pieces)


def settle_kernel(
    meta_ref,
    mixed_ref,
    cot_ref,
    back_ref,
    arrived_ref,
    attended_ref,
    weight_ref,
    gain_ref,
    dmixed_ref,
    do_ref,
    gain_grad_ref,
    near_ref,
    far_ref,
):
    core = meta_ref[0]
    half = attended_ref.shape[1]
    mixed = mixed_ref[...]
    scale = rms_scale(mixed)
    dn2 = back_ref[...] + arrived_ref[...]
    gained = dn2 * gain_ref[...]
    inner = jnp.mean(gained * mixed, axis=-1, keepdims=True)
    dmixed = cot_ref[...] + scale * gained - mixed * (scale * scale * scale * inner)
    dmixed_ref[...] = dmixed
    gain_grad_ref[...] = 0.5 * jnp.sum(dn2 * mixed * scale, axis=0, keepdims=True)
    branch = dmixed.astype(bf16)
    mine = weight_ref[pl.ds(pl.multiple_of(core * half, half), half), :]
    do_ref[...] = mm_nt(branch, mine).astype(bf16)
    grad = mm_tn(attended_ref[...].astype(bf16), branch).astype(bf16)
    count, rows = near_ref.shape[0], near_ref.shape[1]
    blocks = [grad[i * rows : (i + 1) * rows] for i in range(2 * count)]
    for index in range(count):
        even, odd = blocks[2 * index], blocks[2 * index + 1]
        near_ref[index] = jnp.where(core == 0, even, odd)
        far_ref[index] = jnp.where(core == 0, odd, even)


def settle(meta, mixed, cot, back, arrived, attended, weight, gain, chips):
    group, width = mixed.shape
    half = width // 2
    rows = half // chips
    return pl.pallas_call(
        settle_kernel,
        in_specs=[smem_spec()] + [whole_spec()] * 7,
        out_specs=[whole_spec()] * 5,
        out_shape=[
            shaped(f32, group, width),
            shaped(bf16, group, half),
            shaped(f32, 1, width),
            shaped(bf16, chips // 2, rows, width),
            shaped(bf16, chips // 2, rows, width),
        ],
        compiler_params=params(),
        cost_estimate=cost(4 * group * width * half, 6e6),
        name="settle",
    )(meta, mixed, cot, back, arrived, attended, weight, gain)


def retreat_kernel(meta_ref, do_ref, o_ref, q_ref, k_ref, v_ref, p_ref, dq_ref, dkv_ref, band_ref, low, sums):
    chip = meta_ref[0]
    blocks = k_ref.shape[0] // lanes
    group = 2 * lanes
    features = lanes // 2
    do = do_ref[...]
    spread = (do.astype(f32) * o_ref[...]).T
    band_ref[...] = jnp.zeros_like(band_ref)
    turned = []
    for half in range(2):
        do_half, query_half = one_head(do, half), one_head(q_ref[...], half)
        delta = jnp.sum(spread[half * features : (half + 1) * features], axis=0, keepdims=True)
        for block in range(blocks):
            rows = slice(block * lanes, (block + 1) * lanes)
            soft = p_ref[half, rows, :]
            ds = soft * (mm_nt(v_ref[rows, :], do_half) - delta)
            for part in range(2):
                place = band_place(block, chip, part)
                band_ref[half, place, :] += ds[:, part * lanes : (part + 1) * lanes]
            ds_low = ds.astype(bf16)
            low[rows, :] = ds_low
            dk = mm(ds_low, query_half)
            dv = mm(soft.astype(bf16), do_half)
            if half == 0:
                sums[rows, :lanes] = dk
                sums[rows, lanes:] = dv
            else:
                dkv_ref[rows, :lanes] = (sums[rows, :lanes] + dk).astype(bf16)
                dkv_ref[rows, lanes:] = (sums[rows, lanes:] + dv).astype(bf16)
        turned.append(mm_tn(k_ref[...], low[...])[half * features : (half + 1) * features])
    dq_ref[...] = jnp.concatenate(turned, axis=0).T.astype(bf16)


def retreat(meta, do, o, q, k, v, p):
    length, half = k.shape
    group = do.shape[0]
    pairs = half // lanes
    col = lambda i, *_: (0, i)
    deep = lambda i, *_: (i, 0, 0)
    flops = 2 * 8 * group * length * half
    return pl.pallas_call(
        retreat_kernel,
        grid_spec=pltpu.PrefetchScalarGridSpec(
            num_scalar_prefetch=1,
            grid=(pairs,),
            in_specs=[
                pl.BlockSpec((group, lanes), col),
                pl.BlockSpec((group, lanes), col),
                pl.BlockSpec((group, lanes), col),
                pl.BlockSpec((length, lanes), col),
                pl.BlockSpec((length, lanes), col),
                pl.BlockSpec((2, length, group), deep),
            ],
            out_specs=[
                pl.BlockSpec((group, lanes), col),
                pl.BlockSpec((length, 2 * lanes), col),
                pl.BlockSpec((2, 5 * lanes, lanes), deep),
            ],
            scratch_shapes=[
                pltpu.VMEM((length, group), bf16),
                pltpu.VMEM((length, 2 * lanes), f32),
            ],
        ),
        out_shape=[
            shaped(bf16, group, half),
            shaped(bf16, length, 2 * half),
            shaped(f32, 2 * pairs, 5 * lanes, lanes),
        ],
        compiler_params=params(),
        cost_estimate=cost(flops, 20e6),
        name="retreat",
    )(meta, do, o, q, k, v, p)


def grads_kernel(plan, meta_ref, rows_ref, turned_ref, dq_ref, dkv_ref, gain_ref, near_wo, far_wo, *refs):
    refs = list(refs)
    take = lambda n: [refs.pop(0) for _ in range(n)]
    pieces = take(plan[-1][0] + 1)
    grad_out, near_out, far_out, gain_grad_ref = take(4)
    weight, both, grad, back = take(4)
    sem, grad_sem, wo_sem, row_sem = take(4)
    chip, core = meta_ref[0], meta_ref[1]
    length, width = rows_ref.shape
    half = width // 2
    group = dq_ref.shape[0]
    chips = grad_out.shape[0]
    slots = 2
    pairs = []
    for index, lead, target, size, slot in plan:
        size = min(size, 3 - target)
        place = row_block(meta_ref, slots + slot, pieces[index].shape[1])
        pairs.append((pieces[index].at[lead : lead + size], weight.at[target : target + size, place, :]))
    loads = run_copies(pairs, sem)
    pairs = []
    rows = near_wo.shape[1]
    for source, owner in ((near_wo, core), (far_wo, 1 - core)):
        for index in range(near_wo.shape[0]):
            target = owner * (chips // 2) + index
            for side in range(2):
                pairs.append(
                    (
                        source.at[index, :, side * half : (side + 1) * half],
                        grad_out.at[chip ^ target, 3, side * rows : (side + 1) * rows, :],
                    )
                )
    wo_copies = run_copies(pairs, wo_sem)
    own_rows = pl.ds(pl.multiple_of(chip * group, group), group)
    grad[0] = mm_tn(rows_ref[own_rows, :], dq_ref[...]).astype(bf16)
    for pair in range(half // lanes):
        wide = slice(pair * 2 * lanes, (pair + 1) * 2 * lanes)
        cols = slice(pair * lanes, (pair + 1) * lanes)
        summed = mm(turned_ref[...], dkv_ref[:, wide]).astype(bf16)
        grad[1, :, cols] = summed[:, :lanes]
        grad[2, :, cols] = summed[:, lanes:]
    pairs = []
    for index in range(chips):
        place = row_block(meta_ref, slots + index, grad_out.shape[2])
        pairs.append((grad.at[:, place, :], grad_out.at[index, 0:3]))
    grad_copies = run_copies(pairs, grad_sem)
    wait_all(loads)
    for pair in range(half // lanes):
        wide = pair * 2 * lanes
        cols = slice(pair * lanes, (pair + 1) * lanes)
        both[:, wide : wide + lanes] = weight[1, :, cols]
        both[:, wide + lanes : wide + 2 * lanes] = weight[2, :, cols]
    for start in range(0, length, group):
        back[start : start + group, :] = mm_nt(dkv_ref[start : start + group, :], both[...])
    back[own_rows, :] += mm_nt(dq_ref[...], weight[0])
    gain_sum = jnp.zeros((8, width), f32)
    for start in range(0, length, lanes):
        both_rows = back[start : start + lanes, :] * rows_ref[start : start + lanes, :].astype(f32)
        gain_sum = gain_sum + jnp.sum(both_rows.reshape(lanes // 8, 8, width), axis=0)
    gain_grad_ref[...] = jnp.sum(gain_sum, axis=0, keepdims=True) / gain_ref[...]
    for index in range(chips):
        for side, out in ((core, near_out), (1 - core, far_out)):
            start = meta_ref[slots + index] * group + side * lanes
            out[index] = back[pl.ds(pl.multiple_of(start, lanes), lanes), :].astype(bf16)
    wait_all(grad_copies)
    wait_all(wo_copies)


def weight_grads(plan, pieces, meta, rows, turned, dq, dkv, gain, near_wo, far_wo, chips):
    length, width = rows.shape
    half = width // 2
    group = dq.shape[0]
    flops = 2 * (4 * length * width * half + 2 * group * width * half)
    return pl.pallas_call(
        functools.partial(grads_kernel, plan),
        in_specs=[smem_spec()] + [whole_spec()] * 7 + [any_spec()] * len(pieces),
        out_specs=[any_spec()] + [whole_spec()] * 3,
        out_shape=[
            shaped(bf16, chips, 4, width // chips, half),
            shaped(bf16, chips, lanes, width),
            shaped(bf16, chips, lanes, width),
            shaped(f32, 1, width),
        ],
        scratch_shapes=[
            pltpu.VMEM((3, width, half), bf16),
            pltpu.VMEM((width, width), bf16),
            pltpu.VMEM((3, width, half), bf16),
            pltpu.VMEM((length, width), f32),
            dma(len(plan)),
            dma(chips),
            dma(2 * chips),
            dma(1),
        ],
        compiler_params=params(),
        cost_estimate=cost(flops, 20e6),
        name="weight_grads",
    )(meta, rows, turned, dq, dkv, gain, near_wo, far_wo, *pieces)


def core_swap(value):
    count = lax.axis_size("seq")
    return lax.ppermute(value, "seq", [(i, i ^ 1) for i in range(count)])


def plane_swap(value, step):
    count = lax.axis_size("seq")
    return lax.ppermute(value, "seq", [(i, i ^ (2 * step)) for i in range(count)])


def along(value, step):
    count = lax.axis_size("batch")
    return lax.ppermute(value, "batch", [(i, (i + step) % count) for i in range(count)])


def along_all(value):
    return [value] + [along(value, step) for step in range(1, lax.axis_size("batch"))]


def after(value, *earlier):
    return lax.optimization_barrier((value,) + earlier)[0]


def join_kernel(order_ref, *refs):
    sources, out = refs[:-1], refs[-1]
    for index, source in enumerate(sources):
        out[:, :, order_ref[index]] = source[...]


def join(blocks, order):
    lead, rest = blocks[0].shape[:2], blocks[0].shape[2:]
    return pl.pallas_call(
        join_kernel,
        in_specs=[smem_spec()] + [whole_spec()] * len(blocks),
        out_specs=whole_spec(),
        out_shape=shaped(bf16, *lead, len(blocks), *rest),
        compiler_params=params(),
        cost_estimate=cost(0, 2e6),
        name="join",
    )(order, *blocks)


def gather_plane(value):
    chips = lax.axis_size("seq") // 2
    size = value.shape[0]
    if chips != 4:
        pieces = [value] + [plane_swap(value, step) for step in range(1, chips)]
        return pieces, [(step, 0, 0, size, step) for step in range(chips)]
    first, second = plane_swap(value, 1), plane_swap(value, 2)
    low, high = plane_swap(first[: size // 2], 2), plane_swap(second[size // 2 :], 1)
    plan = [(0, 0, 0, size, 0), (1, 0, 0, size, 1), (2, 0, 0, size, 2)]
    plan += [(3, 0, 0, size // 2, 3), (4, 0, size // 2, size - size // 2, 3)]
    return [value, first, second, low, high], plan


def total(blocks):
    summed = blocks[0].astype(f32)
    for block in blocks[1:]:
        summed = summed + block.astype(f32)
    return summed


def scatter_plane(blocks):
    chips = len(blocks)
    if chips != 4:
        return total(blocks[:1] + [plane_swap(blocks[step], step) for step in range(1, chips)])
    cut = blocks[3].shape[0] // 2
    low, high = plane_swap(blocks[3][:cut], 1), plane_swap(blocks[3][cut:], 2)
    add = lambda a, b: total([a, b]).astype(bf16)
    second = jnp.concatenate([add(blocks[2][:cut], low), blocks[2][cut:]], axis=0)
    first = jnp.concatenate([blocks[1][:cut], add(blocks[1][cut:], high)], axis=0)
    return total([blocks[0], plane_swap(first, 1), plane_swap(second, 2)])


def scatter_direct(blocks):
    chips = len(blocks)
    return total(blocks[:1] + [plane_swap(blocks[step], step) for step in range(1, chips)])


def scatter_along(split, dim, place):
    count = lax.axis_size("batch")
    pick = lambda step: lax.dynamic_index_in_dim(split, (place + step) % count, dim, keepdims=False)
    return total([pick(0)] + [along(pick(step).astype(bf16), step) for step in range(1, count)])


def shards(
    tokens,
    cotangent,
    group_ids,
    attention_weight,
    ffin_weight,
    ffout_weight,
    bias_table,
    gains,
    attention_momentum,
    ffin_momentum,
    ffout_momentum,
    bias_momentum,
    gain_momentum,
    attention_average,
    ffin_average,
    ffout_average,
    bias_average,
    gain_average,
):
    _, tok, width = tokens.shape
    cycle_size, places = lax.axis_size("seq"), lax.axis_size("batch")
    cycle_index = lax.axis_index("seq").astype(jnp.int32)
    place = lax.axis_index("batch").astype(jnp.int32)
    chips = cycle_size // 2
    chip, core = cycle_index // 2, cycle_index % 2
    half = width // 2
    rows = attention_weight.shape[1]
    down_rows = ffout_weight.shape[0]
    hidden = ffin_weight.shape[2]
    grain = hidden // cycle_size
    heads = bias_table.shape[1]
    group = 2 * tok
    first_core = core == 0

    def by_core(mine, theirs):
        return [jnp.where(first_core, mine, theirs), jnp.where(first_core, theirs, mine)]

    steps = [chip ^ step for step in range(chips)]
    order = jnp.stack([(place + places - step) % places for step in range(places)])
    flat_tokens, flat_cot = tokens.reshape(tok, width), cotangent.reshape(tok, width)

    attention_low = attention_weight.astype(bf16)
    sides = [attention_low[..., :half], attention_low[..., half:]]
    own_side = jnp.where(first_core, sides[0][:3], sides[1][:3])
    their_side = core_swap(jnp.where(first_core, sides[1][:3], sides[0][:3]))
    attn_block = jnp.concatenate(
        [jnp.stack(by_core(own_side, their_side), axis=1), jnp.stack([sides[0][3], sides[1][3]])[None]],
        axis=0,
    )
    ffin_cut = ffin_weight.astype(bf16).reshape(2, rows, chips, 2, grain)
    sides = [ffin_cut[:, :, :, side].reshape(2, rows, hidden // 2) for side in range(2)]
    own_side = jnp.where(first_core, sides[0], sides[1])
    their_side = core_swap(jnp.where(first_core, sides[1], sides[0]))
    gu_block = jnp.stack(by_core(own_side, their_side), axis=1)
    down_block = ffout_weight.astype(bf16)

    ids_wide = jnp.broadcast_to(group_ids.reshape(tok, 1), (tok, lanes)).astype(bf16)
    normed = flat_tokens * rms_scale(flat_tokens) * gains[0]
    own_rows = jnp.concatenate([normed.astype(bf16), ids_wide], axis=1)
    chip_rows = jnp.concatenate(by_core(own_rows, core_swap(own_rows)), axis=0)
    chip_tokens = jnp.concatenate(by_core(flat_tokens, core_swap(flat_tokens)), axis=0)
    chip_cot = jnp.concatenate(by_core(flat_cot, core_swap(flat_cot)), axis=0)

    row_pieces, row_plan = gather_plane(own_rows)
    near_rows = jnp.concatenate(row_pieces[1:], axis=0)
    far_rows = core_swap(near_rows)
    starts = [chip * group]
    pieces = [chip_rows]
    for source, side in ((near_rows, core), (far_rows, 1 - core)):
        offset = 0
        for _, _, target, size, step in row_plan[1:]:
            starts.append(steps[step] * group + side * tok + target)
            pieces.append(source[offset : offset + size])
            offset += size
    rows_full, turned, mask = place_rows(pieces, jnp.stack(starts), width)
    own_heads = jnp.where(first_core, bias_table[:, : heads // 2], bias_table[:, heads // 2 :])
    bias = bias_rows(own_heads)

    attn_joined = join(along_all(attn_block), order).reshape(4, 2 * places * rows, half)
    attn_pieces, attn_plan = gather_plane(attn_joined)
    gu_joined = join(along_all(gu_block), order).reshape(2, 2 * places * rows, hidden // 2)
    gu_pieces, gu_plan = gather_plane(gu_joined)
    down_near, down_plan = gather_plane(down_block)
    if chips == 4:
        down_near = down_near[:3] + [jnp.concatenate(down_near[3:], axis=0)]
    down_pieces = along_all(jnp.stack(down_near))

    step_meta = jnp.stack(steps)
    query, key, value, soft, attended = attend(
        attn_plan, attn_pieces, step_meta, rows_full, mask, bias
    )
    wo_near = jnp.stack([attn_pieces[i][lead + 3 - target] for i, lead, target, size, _ in attn_plan if target + size == 4])
    wo_far = core_swap(wo_near)
    wo_meta = jnp.stack([core] + [step * 2 + core for step in steps] + [step * 2 + 1 - core for step in steps])
    part, out_weight = mix(wo_meta, attended, wo_near, wo_far)
    down_meta = [step * places + order[index] for index in range(places) for step in steps]
    mixed, out_part, back_part, gu_grads, down_grads = feed(
        gu_plan,
        gu_pieces,
        down_pieces,
        jnp.stack(steps + down_meta),
        chip_tokens,
        chip_cot,
        part,
        core_swap(part),
        gains[1:2],
        chips,
    )
    dmixed, attended_grad, second_gain, near_wo, far_wo = settle(
        core.reshape(1), mixed, chip_cot, back_part, core_swap(back_part), attended, out_weight, gains[1:2], chips
    )
    mine = lambda value: lax.dynamic_slice_in_dim(value, core * tok, tok, 0)
    theirs = lambda value: lax.dynamic_slice_in_dim(value, (1 - core) * tok, tok, 0)
    layer_output = mine(mixed) + mine(out_part) + core_swap(theirs(out_part))

    dq, dkv, band = retreat(chip.reshape(1), attended_grad, attended, query, key, value, soft)
    attn_grads, near_back, far_back, first_gain = weight_grads(
        attn_plan,
        attn_pieces,
        jnp.stack([chip, core] + steps),
        rows_full,
        turned,
        dq,
        dkv,
        gains[:1],
        near_wo,
        core_swap(far_wo),
        chips,
    )
    bias_part = bias_sums(band)[:, : bias_table.shape[0]].T

    def own_columns(summed, columns):
        keep = jnp.where(first_core, summed[:, 0], summed[:, 1])
        send = jnp.where(first_core, summed[:, 1], summed[:, 0])
        return columns(by_core(keep, core_swap(send)))

    gu_sum = scatter_plane([gu_grads[step] for step in range(chips)]).astype(bf16)
    gu_sum = scatter_along(gu_sum.reshape(2, 2, places, rows, hidden // 2), 2, place)
    weave = lambda parts: jnp.stack(
        [part.reshape(2, rows, chips, grain) for part in parts], axis=3
    ).reshape(2, rows, hidden)
    own_gu = own_columns(gu_sum, weave)
    down_sum = scatter_along(down_grads.reshape(chips, places, down_rows, width), 1, place).astype(bf16)
    own_down = scatter_direct([down_sum[step] for step in range(chips)])
    attn_sum = scatter_direct([attn_grads[step] for step in range(chips)]).astype(bf16)
    attn_sum = scatter_along(attn_sum.reshape(4, 2, places, rows, half), 2, place)
    own_qkv = own_columns(attn_sum[:3], lambda parts: jnp.concatenate(parts, axis=-1))
    own_wo = jnp.concatenate([attn_sum[3, 0], attn_sum[3, 1]], axis=-1)
    own_attention = jnp.concatenate([own_qkv, own_wo[None]], axis=0)

    arrived = core_swap(far_back)
    merged = [total([near_back[step], arrived[step]]).astype(bf16) for step in range(chips)]
    first_grad = scatter_direct(merged)
    scale = rms_scale(flat_tokens)
    gained = first_grad * gains[0]
    inner = jnp.mean(gained * flat_tokens, axis=-1, keepdims=True)
    input_grad = mine(dmixed) + scale * gained - flat_tokens * (scale**3 * inner)

    none = jnp.zeros_like(bias_part)
    bias_wide = jnp.concatenate(by_core(bias_part, none), axis=1)
    small = jnp.concatenate([bias_wide.reshape(-1), first_gain[0], second_gain[0]]).reshape(-1, lanes)
    small = small + core_swap(small)
    small = scatter_direct([small] * chips)
    small = total(along_all(small)).reshape(-1)
    bias_reduced = small[: bias_table.size].reshape(bias_table.shape)
    gains_reduced = small[bias_table.size :].reshape(gains.shape)

    all_tokens = lax.axis_size("batch") * tok * cycle_size
    inverse_root = 1.0 / math.sqrt(all_tokens)
    attention_rate = jnp.array(attention_rates, dtype=f32)[:, None, None] * inverse_root
    gain_rate = jnp.array(gain_rates, dtype=f32)[:, None] * inverse_root
    attn_new = update(
        attention_weight, own_attention, attention_momentum, attention_average, attention_rate
    )
    ffin_new = update(
        ffin_weight, own_gu, ffin_momentum, ffin_average, ffin_rate * inverse_root
    )
    ffout_new = update(
        ffout_weight, own_down, ffout_momentum, ffout_average, ffout_rate * inverse_root
    )
    bias_new = update(bias_table, bias_reduced, bias_momentum, bias_average, bias_rate * inverse_root)
    gain_new = update(gains, gains_reduced, gain_momentum, gain_average, gain_rate)
    return (
        layer_output.reshape(tokens.shape),
        input_grad.reshape(tokens.shape),
        attn_new[0],
        ffin_new[0],
        ffout_new[0],
        bias_new[0],
        gain_new[0],
        attn_new[1],
        ffin_new[1],
        ffout_new[1],
        bias_new[1],
        gain_new[1],
        attn_new[2],
        ffin_new[2],
        ffout_new[2],
        bias_new[2],
        gain_new[2],
        attn_new[0].astype(bf16),
        ffin_new[0].astype(bf16),
        ffout_new[0].astype(bf16),
    )


def solution(mesh):
    rows = P("batch", "seq", None)
    stacked = P(None, ("seq", "batch"), None)
    single = P(("seq", "batch"), None)
    weights = (stacked, stacked, single, P(), P())
    return jax.shard_map(
        shards,
        mesh=mesh,
        in_specs=(rows, rows, P("batch", "seq")) + weights * 3,
        out_specs=(rows, rows) + weights * 3 + (stacked, stacked, single),
        check_vma=False,
    )
```

time: 673 us -> 327 us (0.49)
  waiting for transfers between devices: 365 us -> 79.9 us
  matrix products: 95.5 us -> 0 us
  Pallas kernels: 0 us -> 73.2 us
  starting transfers between devices: 28.7 us -> 98.8 us
  blocking collectives: 48.7 us -> 0 us
  other arithmetic: 71.8 us -> 36.5 us
  between operations: 14.9 us -> 1.66 us
  local copies, waits for them, and re-layouts: 44.4 us -> 34.5 us
    reduce_scatter x3 -> x0, waiting for transfers between devices: 220 us -> none  [the longest x1 158 us: shards(): lax.psum_scatter(grad_ffin, ('seq', 'batch'), scatter_dimension=1, tiled=...]
    dot_general x101 -> x0, matrix products: 95.5 us -> none  [the longest x29 54.3 us: matmul(): return jnp.dot(left_rows, right_rows, preferred_element_type=jnp.float32)]
    all_gather x3 -> x0, waiting for transfers between devices: 81.6 us -> none  [the longest x1 50.6 us: shards(): lax.all_gather(attention_weight.astype(jnp.bfloat16), ('seq', 'batch'), a...]
    pallas_call x0 -> x11, Pallas kernels: none -> 73.2 us  [the longest x1 13.8 us: feed(): pl.pallas_call(functools.partial(feed_kernel, gu_plan, len(down_pieces)),...]
    ppermute x48 -> x68, starting transfers between devices: 28.2 us -> 98.8 us  [the longest x21 56.3 us: along(): lax.ppermute(value, 'batch', [(i, (i + step) % count) for i in range(coun...]
    psum x1 -> x0, blocking collectives: 38.4 us -> none  [shards(): lax.psum((bias_total, jnp.stack([first_gain_grad, second_gain_grad])), ('...]
    while x72 -> x0, local copies, waits for them, and re-layouts: 23.9 us -> none
    convert_element_type x36 -> x12, other arithmetic: 29.1 us -> 11.8 us  [the longest x1 2.01 us: shards(): ffout_new[0].astype(bf16)]
  transfers between devices with their start and end apart: 54 -> 68, of which waited for: 34 -> 18; matrix products, arithmetic and copies ran while one was open for 28% -> 20% of each run, Pallas kernels for 0% -> 18%
where the time goes in v1:
time: 327 us; the launch traced here: 325 us
  starting transfers between devices  98.8 us (30%)
  waiting for transfers between devices  79.9 us (24%)
  Pallas kernels  73.2 us (22%)
  other arithmetic  36.5 us (11%)
  local copies, waits for them, and re-layouts  34.5 us (11%)
    ppermute x21, starting transfers between devices, along(): lax.ppermute(value, 'batch', [(i, (i + step) % count) for i in range(coun...  56.3 us
    ppermute x21, waiting for transfers between devices, along(): lax.ppermute(value, 'batch', [(i, (i + step) % count) for i in range(coun...  45.2 us
    ppermute x32, starting transfers between devices, plane_swap(): return lax.ppermute(value, 'seq', [(i, i ^ 2 * step) for i in range(count)])  39.3 us
    ppermute x32, waiting for transfers between devices, plane_swap(): return lax.ppermute(value, 'seq', [(i, i ^ 2 * step) for i in range(count)])  34.2 us
    pallas_call x1, Pallas kernels, feed(): pl.pallas_call(functools.partial(feed_kernel, gu_plan, len(down_pieces)),...  13.8 us
    pallas_call x1, Pallas kernels, attend(): pl.pallas_call(functools.partial(attend_kernel, plan), grid_spec=pltpu.Pr...  13 us
    pallas_call x1, Pallas kernels, retreat(): pl.pallas_call(retreat_kernel, grid_spec=pltpu.PrefetchScalarGridSpec(num...  11.3 us
    pallas_call x1, Pallas kernels, weight_grads(): pl.pallas_call(functools.partial(grads_kernel, plan), in_specs=[smem_spec...  8.33 us
  transfers between devices with their start and end apart: 68, of which 18 were waited for; matrix products, arithmetic and copies ran while one was open for 20% of the time, Pallas kernels for 18%

profile of v1, /device:TPU:0, one launch (start us, length us, event | category | flops | bytes accessed | tf_op | source)
XLA Modules:
  0.0 324.6 jit_solution(1488255383358537907)
XLA Ops:
  8.5 4.1 %bias_rows.1.bias_ref = f32[6,640,128]{2,1,0:T(8,128)} custom-call(f32[32,6]{1,0:T(8,128)} %slice_select_fusion.1.table_ref), custom_call_target="tpu_custom_call" | custom-call | flops 18000000 | bytes 4000000 | tf_op jit(solution)/shard_map/bias_rows/pallas_call | solution.py:96
  12.6 4.1 %collective-permute-start.10 = (bf16[4,2,24,384]{3,2,1,0:T(8,128)(2,1)S(1)}, bf16[4,2,24,384]{3,2,1,0:T(8,128)(2,1)S(1)}, u32[]{:S(2)}, u32[]{:S(2)}) collective-permute-start(bf16[4,2,24,384]{3,2,1,0:T(8,128)(2,1)S(1)} %pad_maximum_fusion.12.refs_0_), channel_id=1, source_target_pairs={{0,2},{1,3},{2,0},{3,1},{4,6},{5,7},{6,4},{7,5},{8,10},{9,11},{10,... | collective-permute-start | bytes 442376 | tf_op jit(solution)/shard_map/ppermute | solution.py:735
  22.7 1.5 select_bitcast_fusion.3
  24.8 2.2 collective-permute-start.26
  28.6 2.1 join.2
  34.2 4.1 %collective-permute-start.19 = (bf16[2,2,24,1024]{3,2,1,0:T(8,128)(2,1)S(1)}, bf16[2,2,24,1024]{3,2,1,0:T(8,128)(2,1)S(1)}, u32[]{:S(2)}, u32[]{:S(2)}) collective-permute-start(bf16[2,2,24,1024]{3,2,1,0:T(8,128)(2,1)S(1)} %pad_maximum_fusion.11.refs_0_), channel_id=1, source_target_pairs={{0,1},{1,2},{2,3},{3,0},{4,5},{5,6},{6,7},{7,4},{8,9},{9,10},{10,1... | collective-permute-start | bytes 589832 | tf_op jit(solution)/shard_map/ppermute | solution.py:735
  41.5 6.1 %collective-permute-done.5.refs_3_ = bf16[64,896]{1,0:T(8,128)(2,1)S(1)} collective-permute-done((bf16[64,896]{1,0:T(8,128)(2,1)S(1)}, bf16[64,896]{1,0:T(8,128)(2,1)S(1)}, u32[]{:S(2)}, u32[]{:S(2)}) %collective-permute-start.5) | collective-permute-done | bytes 114720 | tf_op jit(solution)/shard_map/ppermute | solution.py:730
  47.6 1.5 collective-permute-start.28
  51.7 5.6 %collective-permute-start.21 = (bf16[2,2,24,1024]{3,2,1,0:T(8,128)(2,1)S(1)}, bf16[2,2,24,1024]{3,2,1,0:T(8,128)(2,1)S(1)}, u32[]{:S(2)}, u32[]{:S(2)}) collective-permute-start(bf16[2,2,24,1024]{3,2,1,0:T(8,128)(2,1)S(1)} %pad_maximum_fusion.11.refs_0_), channel_id=1, source_target_pairs={{0,3},{1,0},{2,1},{3,2},{4,7},{5,4},{6,5},{7,6},{8,11},{9,8},{10,9... | collective-permute-start | bytes 589832 | tf_op jit(solution)/shard_map/ppermute | solution.py:735
  58.3 1.7 pad_maximum_fusion.7.refs_5_
  62.0 2.2 join.3
  64.2 1.6 collective-permute-start.22
  70.2 2.9 collective-permute-done.12.refs_1_
  76.3 16.5 %collective-permute-done.15.refs_4_ = bf16[2,192,384]{2,1,0:T(8,128)(2,1)S(1)} collective-permute-done((bf16[2,192,384]{2,1,0:T(8,128)(2,1)S(1)}, bf16[2,192,384]{2,1,0:T(8,128)(2,1)S(1)}, u32[]{:S(2)}, u32[]{:S(2)}) %collective-permute-start.15) | collective-permute-done | bytes 294944 | tf_op jit(solution)/shard_map/ppermute | solution.py:730
  94.3 2.0 fusion.29
  96.2 1.7 fusion.28
  97.9 3.7 %place_rows.1 = (bf16[1024,768]{1,0:T(8,128)(2,1)}, bf16[768,1024]{1,0:T(8,128)(2,1)}, f32[1024,256]{1,0:T(8,128)}) custom-call(s32[9]{0:T(128)} %stack.237.meta_ref, bf16[256,896]{1,0:T(8,128)(2,1)} %pad_maximum_fusion.6.refs_0_, bf16[128,896]{1,0:T(8,128)(2,1)} %copy-done.8, bf16[128,896]{1,0:T(8,128)(2,1)} %copy-done.9, bf16[64,896]{1,0:T(8,128)(2,1)} %copy-done.21, ...), custom_call_target="tpu_custom_call" | custom-call | flops 3000000 | bytes 8000000 | tf_op jit(solution)/shard_map/place_rows/pallas_call | solution.py:205
  101.6 13.0 %attend.1 = (bf16[256,384]{1,0:T(8,128)(2,1)}, bf16[1024,384]{1,0:T(8,128)(2,1)}, bf16[1024,384]{1,0:T(8,128)(2,1)}, f32[6,1024,256]{2,1,0:T(8,128)}, f32[256,384]{1,0:T(8,128)}) custom-call(s32[4]{0:T(128)} %pad_add_fusion.meta_ref, bf16[1024,768]{1,0:T(8,128)(2,1)} %get-tuple-element.47.rows_ref, f32[1024,256]{1,0:T(8,128)} %get-tuple-element.48.mask_ref, ...), custom_call_target="tpu_custom_call" | custom-call | flops 2164260864 | bytes 30000000 | tf_op jit(solution)/shard_map/attend/pallas_call | solution.py:297
  115.5 3.8 %mix.1 = (f32[256,768]{1,0:T(8,128)}, bf16[768,768]{1,0:T(8,128)(2,1)}) custom-call(s32[9]{0:T(128)} %stack.226.meta_ref, f32[256,384]{1,0:T(8,128)} %get-tuple-element.49.attended_ref.o_ref, bf16[4,192,384]{2,1,0:T(8,128)(2,1)} %copy-done.2, bf16[4,192,384]{2,1,0:T(8,128)(2,1)} %copy-done.19), custom_call_target="tpu_custom_call" | custom-call | flops 150994944 | bytes 4000000 | tf_op jit(solution)/shard_map/mix/pallas_call | solution.py:358
  130.7 9.4 %collective-permute-done.31.refs_7_ = bf16[4,64,768]{2,1,0:T(8,128)(2,1)S(1)} collective-permute-done((bf16[4,64,768]{2,1,0:T(8,128)(2,1)}, bf16[4,64,768]{2,1,0:T(8,128)(2,1)S(1)}, u32[]{:S(2)}, u32[]{:S(2)}) %collective-permute-start.31) | collective-permute-done | bytes 393248 | tf_op jit(solution)/shard_map/ppermute | solution.py:735
  140.9 13.8 %feed.1 = (f32[256,768]{1,0:T(8,128)}, f32[256,768]{1,0:T(8,128)}, f32[256,768]{1,0:T(8,128)}, bf16[4,2,192,1024]{3,2,1,0:T(8,128)(2,1)}, bf16[4,256,768]{2,1,0:T(8,128)(2,1)}) custom-call(s32[20]{0:T(128)} %stack.216.meta_ref, f32[256,768]{1,0:T(8,128)} %pad_maximum_fusion.tokens_ref, f32[256,768]{1,0:T(8,128)} %pad_maximum_fusion.1.cot_ref, ...), custom_call_target="tpu_custom_call" | custom-call | flops 3623878656 | bytes 25000000 | tf_op jit(solution)/shard_map/feed/pallas_call | solution.py:463
  156.1 8.4 %collective-permute-start.55 = (bf16[4,64,768]{2,1,0:T(8,128)(2,1)S(1)}, bf16[4,64,768]{2,1,0:T(8,128)(2,1)S(1)}, u32[]{:S(2)}, u32[]{:S(2)}) collective-permute-start(bf16[4,64,768]{2,1,0:T(8,128)(2,1)S(1)} %get-tuple-element.117), channel_id=1, source_target_pairs={{0,1},{1,2},{2,3},{3,0},{4,5},{5,6},{6,7},{7,4},{8,9},{9,10},{10,1... | collective-permute-start | bytes 1179656 | tf_op jit(solution)/shard_map/ppermute | solution.py:735
  164.4 3.2 collective-permute-start.56
  167.6 1.5 slice_bitcast_fusion.6
  170.2 6.9 %collective-permute-done.55 = bf16[4,64,768]{2,1,0:T(8,128)(2,1)S(1)} collective-permute-done((bf16[4,64,768]{2,1,0:T(8,128)(2,1)S(1)}, bf16[4,64,768]{2,1,0:T(8,128)(2,1)S(1)}, u32[]{:S(2)}, u32[]{:S(2)}) %collective-permute-start.55) | collective-permute-done | bytes 393248 | tf_op jit(solution)/shard_map/ppermute | solution.py:735
  178.6 15.1 %collective-permute-done.56 = bf16[4,64,768]{2,1,0:T(8,128)(2,1)S(1)} collective-permute-done((bf16[4,64,768]{2,1,0:T(8,128)(2,1)S(1)}, bf16[4,64,768]{2,1,0:T(8,128)(2,1)S(1)}, u32[]{:S(2)}, u32[]{:S(2)}) %collective-permute-start.56) | collective-permute-done | bytes 393248 | tf_op jit(solution)/shard_map/ppermute | solution.py:735
  203.8 4.2 %settle.1 = (f32[256,768]{1,0:T(8,128)}, bf16[256,384]{1,0:T(8,128)(2,1)}, f32[1,768]{1,0:T(1,128)}, bf16[2,96,768]{2,1,0:T(8,128)(2,1)}, bf16[2,96,768]{2,1,0:T(8,128)(2,1)}) custom-call(s32[1]{0:T(128)} %bitcast.22.meta_ref, f32[256,768]{1,0:T(8,128)} %get-tuple-element.51.mixed_ref, f32[256,768]{1,0:T(8,128)} %pad_maximum_fusion.1.cot_ref, ...), custom_call_target="tpu_custom_call" | custom-call | flops 301989888 | bytes 6000000 | tf_op jit(solution)/shard_map/settle/pallas_call | solution.py:534
  208.0 11.3 %retreat.1 = (bf16[256,384]{1,0:T(8,128)(2,1)}, bf16[1024,768]{1,0:T(8,128)(2,1)}, f32[6,640,128]{2,1,0:T(8,128)}) custom-call(s32[1]{0:T(128)} %bitcast.meta_ref, bf16[256,384]{1,0:T(8,128)(2,1)} %get-tuple-element.57.do_ref, f32[256,384]{1,0:T(8,128)} %get-tuple-element.49.attended_ref.o_ref, bf16[256,384]{1,0:T(8,128)(2,1)} %get-tuple-element.58.q_ref, ...), custom_call_target="tpu_custom_call" | custom-call | flops 1610612736 | bytes 20000000 | tf_op jit(solution)/shard_map/retreat/pallas_call | solution.py:591
  219.2 6.9 %bias_sums.1 = f32[6,1,128]{2,1,0:T(1,128)} custom-call(f32[6,640,128]{2,1,0:T(8,128)} %get-tuple-element.71.grad_ref), custom_call_target="tpu_custom_call" | custom-call | flops 18000000 | bytes 4000000 | tf_op jit(solution)/shard_map/bias_sums/pallas_call | solution.py:139
  232.1 8.3 %weight_grads.1 = (bf16[4,4,192,384]{3,2,1,0:T(8,128)(2,1)}, bf16[4,128,768]{2,1,0:T(8,128)(2,1)}, bf16[4,128,768]{2,1,0:T(8,128)(2,1)}, f32[1,768]{1,0:T(1,128)}) custom-call(s32[6]{0:T(128)} %stack.256.meta_ref, bf16[1024,768]{1,0:T(8,128)(2,1)} %get-tuple-element.47.rows_ref, bf16[768,1024]{1,0:T(8,128)(2,1)} %get-tuple-element.56.turned_ref, ...), custom_call_target="tpu_custom_call" | custom-call | flops 2717908992 | bytes 20000000 | tf_op jit(solution)/shard_map/weight_grads/pallas_call | solution.py:697
  242.7 2.0 fusion.25
  249.0 1.6 add_multiply_fusion.2
  252.1 8.9 %collective-permute-start.65 = (f32[15,128]{1,0:T(8,128)S(1)}, f32[15,128]{1,0:T(8,128)S(1)}, u32[]{:S(2)}, u32[]{:S(2)}) collective-permute-start(f32[15,128]{1,0:T(8,128)S(1)} %add_add_fusion.1), channel_id=1, source_target_pairs={{0,1},{1,2},{2,3},{3,0},{4,5},{5,6},{6,7},{7,4},{8,9},{9,10},{10,1... | collective-permute-start | bytes 23048 | tf_op jit(solution)/shard_map/ppermute | solution.py:735
  261.0 2.4 collective-permute-start.67
  263.4 2.7 slice_bitcast_fusion.2
  270.8 1.8 fusion.1
  272.9 2.6 collective-permute-start.52
  275.4 1.6 collective-permute-start.53
  279.1 3.4 %collective-permute-done.51 = bf16[2,2,24,1024]{3,2,0,1:T(8,128)(2,1)S(1)} collective-permute-done((bf16[2,2,24,1024]{3,2,0,1:T(8,128)(2,1)S(1)}, bf16[2,2,24,1024]{3,2,0,1:T(8,128)(2,1)S(1)}, u32[]{:S(2)}, u32[]{:S(2)}) %collective-permute-start.51) | collective-permute-done | bytes 196640 | tf_op jit(solution)/shard_map/ppermute | solution.py:735
  283.9 4.2 %collective-permute-done.52 = bf16[2,2,24,1024]{3,2,0,1:T(8,128)(2,1)S(1)} collective-permute-done((bf16[2,2,24,1024]{3,2,0,1:T(8,128)(2,1)S(1)}, bf16[2,2,24,1024]{3,2,0,1:T(8,128)(2,1)S(1)}, u32[]{:S(2)}, u32[]{:S(2)}) %collective-permute-start.52) | collective-permute-done | bytes 196640 | tf_op jit(solution)/shard_map/ppermute | solution.py:735
  291.8 1.9 fusion.26
  293.7 1.9 fusion.4
  295.7 4.5 %collective-permute-start.43 = (bf16[4,2,24,384]{3,2,1,0:T(8,128)(2,1)S(1)}, bf16[4,2,24,384]{3,2,1,0:T(8,128)(2,1)S(1)}, u32[]{:S(2)}, u32[]{:S(2)}) collective-permute-start(bf16[4,2,24,384]{3,2,1,0:T(8,128)(2,1)S(1)} %get-tuple-element.137), channel_id=1, source_target_pairs={{0,1},{1,2},{2,3},{3,0},{4,5},{5,6},{6,7},{7,4},{8,9},{9,10},{10,1... | collective-permute-start | bytes 442376 | tf_op jit(solution)/shard_map/ppermute | solution.py:735
  300.1 2.0 collective-permute-start.44
  302.1 2.8 collective-permute-start.45
  305.8 4.8 %collective-permute-done.44 = bf16[4,2,24,384]{3,2,1,0:T(8,128)(2,1)S(1)} collective-permute-done((bf16[4,2,24,384]{3,2,1,0:T(8,128)(2,1)S(1)}, bf16[4,2,24,384]{3,2,1,0:T(8,128)(2,1)S(1)}, u32[]{:S(2)}, u32[]{:S(2)}) %collective-permute-start.44) | collective-permute-done | bytes 147488 | tf_op jit(solution)/shard_map/ppermute | solution.py:735
  316.3 2.5 collective-permute-done.37
  318.8 4.6 %collective-permute-done.38 = bf16[128,768]{1,0:T(8,128)(2,1)S(1)} collective-permute-done((bf16[128,768]{1,0:T(8,128)(2,1)S(1)}, bf16[128,768]{1,0:T(8,128)(2,1)S(1)}, u32[]{:S(2)}, u32[]{:S(2)}) %collective-permute-start.38) | collective-permute-done | bytes 196640 | tf_op jit(solution)/shard_map/ppermute | solution.py:730
  (318 shorter events, 97.6 us)
Async XLA Ops:
  3.1 18.1 %collective-permute-start.18 = (bf16[2,24,1024]{2,1,0:T(8,128)(2,1)}, bf16[2,24,1024]{2,1,0:T(8,128)(2,1)}, u32[]{:S(2)}, u32[]{:S(2)}) collective-permute-start(bf16[2,24,1024]{2,1,0:T(8,128)(2,1)} %select_n.266), channel_id=1, source_target_pairs={{0,4},{4,0},{8,12},{12,8},{16,20},{20,16},{24,28},{28,24},{1,5},{5... | collective-permute-start | bytes 294920 | tf_op jit(solution)/shard_map/ppermute | solution.py:725
  3.7 14.3 %collective-permute-start = (f32[128,768]{1,0:T(8,128)S(1)}, f32[128,768]{1,0:T(8,128)S(1)}, u32[]{:S(2)}, u32[]{:S(2)}) collective-permute-start(f32[128,768]{1,0:T(8,128)S(1)} %bitcast.228), channel_id=1, source_target_pairs={{0,4},{4,0},{8,12},{12,8},{16,20},{20,16},{24,28},{28,24},{1,5},{5... | collective-permute-start | bytes 1179656 | tf_op jit(solution)/shard_map/ppermute | solution.py:725
  4.2 14.6 %collective-permute-start.1 = (f32[128,768]{1,0:T(8,128)S(1)}, f32[128,768]{1,0:T(8,128)S(1)}, u32[]{:S(2)}, u32[]{:S(2)}) collective-permute-start(f32[128,768]{1,0:T(8,128)S(1)} %bitcast.239), channel_id=1, source_target_pairs={{0,4},{4,0},{8,12},{12,8},{16,20},{20,16},{24,28},{28,24},{1,5},{5... | collective-permute-start | bytes 1179656 | tf_op jit(solution)/shard_map/ppermute | solution.py:725
  12.6 12.2 %collective-permute-start.10 = (bf16[4,2,24,384]{3,2,1,0:T(8,128)(2,1)S(1)}, bf16[4,2,24,384]{3,2,1,0:T(8,128)(2,1)S(1)}, u32[]{:S(2)}, u32[]{:S(2)}) collective-permute-start(bf16[4,2,24,384]{3,2,1,0:T(8,128)(2,1)S(1)} %pad_maximum_fusion.12.refs_0_), channel_id=1, source_target_pairs={{0,2},{1,3},{2,0},{3,1},{4,6},{5,7},{6,4},{7,5},{8,10},{9,11},{10,... | collective-permute-start | bytes 442376 | tf_op jit(solution)/shard_map/ppermute | solution.py:735
  16.7 10.3 %collective-permute-start.11 = (bf16[4,2,24,384]{3,2,1,0:T(8,128)(2,1)S(1)}, bf16[4,2,24,384]{3,2,1,0:T(8,128)(2,1)S(1)}, u32[]{:S(2)}, u32[]{:S(2)}) collective-permute-start(bf16[4,2,24,384]{3,2,1,0:T(8,128)(2,1)S(1)} %pad_maximum_fusion.12.refs_0_), channel_id=1, source_target_pairs={{0,3},{1,0},{2,1},{3,2},{4,7},{5,4},{6,5},{7,6},{8,11},{9,8},{10,9... | collective-permute-start | bytes 442376 | tf_op jit(solution)/shard_map/ppermute | solution.py:735
  18.0 10.5 %collective-permute-start.9 = (bf16[4,2,24,384]{3,2,1,0:T(8,128)(2,1)S(1)}, bf16[4,2,24,384]{3,2,1,0:T(8,128)(2,1)}, u32[]{:S(2)}, u32[]{:S(2)}) collective-permute-start(bf16[4,2,24,384]{3,2,1,0:T(8,128)(2,1)S(1)} %pad_maximum_fusion.12.refs_0_), channel_id=1, source_target_pairs={{0,1},{1,2},{2,3},{3,0},{4,5},{5,6},{6,7},{7,4},{8,9},{9,10},{10,1... | collective-permute-start | bytes 442376 | tf_op jit(solution)/shard_map/ppermute | solution.py:735
  19.7 12.3 %collective-permute-start.3 = (bf16[128,896]{1,0:T(8,128)(2,1)}, bf16[128,896]{1,0:T(8,128)(2,1)S(1)}, u32[]{:S(2)}, u32[]{:S(2)}) collective-permute-start(bf16[128,896]{1,0:T(8,128)(2,1)} %pad_maximum_fusion.10), channel_id=1, source_target_pairs={{0,8},{4,12},{8,0},{12,4},{16,24},{20,28},{24,16},{28,20},{1,9},{5... | collective-permute-start | bytes 688136 | tf_op jit(solution)/shard_map/ppermute | solution.py:730
  21.2 11.6 %collective-permute-start.4 = (bf16[128,896]{1,0:T(8,128)(2,1)}, bf16[128,896]{1,0:T(8,128)(2,1)S(1)}, u32[]{:S(2)}, u32[]{:S(2)}) collective-permute-start(bf16[128,896]{1,0:T(8,128)(2,1)} %pad_maximum_fusion.10), channel_id=1, source_target_pairs={{0,16},{4,20},{8,24},{12,28},{16,0},{20,4},{24,8},{28,12},{1,17},{... | collective-permute-start | bytes 688136 | tf_op jit(solution)/shard_map/ppermute | solution.py:730
  27.0 11.3 %collective-permute-start.27 = (bf16[64,768]{1,0:T(8,128)(2,1)}, bf16[64,768]{1,0:T(8,128)(2,1)}, u32[]{:S(2)}, u32[]{:S(2)}) collective-permute-start(bf16[64,768]{1,0:T(8,128)(2,1)} %convert_element_type.238), channel_id=1, source_target_pairs={{0,16},{4,20},{8,24},{12,28},{16,0},{20,4},{24,8},{28,12},{1,17},{... | collective-permute-start | bytes 294920 | tf_op jit(solution)/shard_map/ppermute | solution.py:730
  30.7 33.6 %collective-permute-start.13 = (bf16[4,192,384]{2,1,0:T(8,128)(2,1)}, bf16[4,192,384]{2,1,0:T(8,128)(2,1)}, u32[]{:S(2)}, u32[]{:S(2)}) collective-permute-start(bf16[4,192,384]{2,1,0:T(8,128)(2,1)} %bitcast.234), channel_id=1, source_target_pairs={{0,16},{4,20},{8,24},{12,28},{16,0},{20,4},{24,8},{28,12},{1,17},{... | collective-permute-start | bytes 1769480 | tf_op jit(solution)/shard_map/ppermute | solution.py:730
  32.0 15.5 %collective-permute-start.5 = (bf16[64,896]{1,0:T(8,128)(2,1)S(1)}, bf16[64,896]{1,0:T(8,128)(2,1)S(1)}, u32[]{:S(2)}, u32[]{:S(2)}) collective-permute-start(bf16[64,896]{1,0:T(8,128)(2,1)S(1)} %slice.283), channel_id=1, source_target_pairs={{0,16},{4,20},{8,24},{12,28},{16,0},{20,4},{24,8},{28,12},{1,17},{... | collective-permute-start | bytes 344072 | tf_op jit(solution)/shard_map/ppermute | solution.py:730
  32.8 16.3 %collective-permute-start.6 = (bf16[64,896]{1,0:T(8,128)(2,1)S(1)}, bf16[64,896]{1,0:T(8,128)(2,1)S(1)}, u32[]{:S(2)}, u32[]{:S(2)}) collective-permute-start(bf16[64,896]{1,0:T(8,128)(2,1)S(1)} %slice.284), channel_id=1, source_target_pairs={{0,8},{4,12},{8,0},{12,4},{16,24},{20,28},{24,16},{28,20},{1,9},{5... | collective-permute-start | bytes 344072 | tf_op jit(solution)/shard_map/ppermute | solution.py:730
  34.2 23.6 %collective-permute-start.19 = (bf16[2,2,24,1024]{3,2,1,0:T(8,128)(2,1)S(1)}, bf16[2,2,24,1024]{3,2,1,0:T(8,128)(2,1)S(1)}, u32[]{:S(2)}, u32[]{:S(2)}) collective-permute-start(bf16[2,2,24,1024]{3,2,1,0:T(8,128)(2,1)S(1)} %pad_maximum_fusion.11.refs_0_), channel_id=1, source_target_pairs={{0,1},{1,2},{2,3},{3,0},{4,5},{5,6},{6,7},{7,4},{8,9},{9,10},{10,1... | collective-permute-start | bytes 589832 | tf_op jit(solution)/shard_map/ppermute | solution.py:735
  38.3 19.5 %collective-permute-start.20 = (bf16[2,2,24,1024]{3,2,1,0:T(8,128)(2,1)S(1)}, bf16[2,2,24,1024]{3,2,1,0:T(8,128)(2,1)S(1)}, u32[]{:S(2)}, u32[]{:S(2)}) collective-permute-start(bf16[2,2,24,1024]{3,2,1,0:T(8,128)(2,1)S(1)} %pad_maximum_fusion.11.refs_0_), channel_id=1, source_target_pairs={{0,2},{1,3},{2,0},{3,1},{4,6},{5,7},{6,4},{7,5},{8,10},{9,11},{10,... | collective-permute-start | bytes 589832 | tf_op jit(solution)/shard_map/ppermute | solution.py:735
  57.3 15.8 %collective-permute-start.12 = (bf16[4,192,384]{2,1,0:T(8,128)(2,1)S(1)}, bf16[4,192,384]{2,1,0:T(8,128)(2,1)}, u32[]{:S(2)}, u32[]{:S(2)}) collective-permute-start(bf16[4,192,384]{2,1,0:T(8,128)(2,1)S(1)} %bitcast.237), channel_id=1, source_target_pairs={{0,8},{4,12},{8,0},{12,4},{16,24},{20,28},{24,16},{28,20},{1,9},{5... | collective-permute-start | bytes 1769480 | tf_op jit(solution)/shard_map/ppermute | solution.py:730
  57.8 36.3 %collective-permute-start.7 = (bf16[384,896]{1,0:T(8,128)(2,1)}, bf16[384,896]{1,0:T(8,128)(2,1)}, u32[]{:S(2)}, u32[]{:S(2)}) collective-permute-start(bf16[384,896]{1,0:T(8,128)(2,1)} %pad_maximum_fusion.4), channel_id=1, source_target_pairs={{0,4},{4,0},{8,12},{12,8},{16,20},{20,16},{24,28},{28,24},{1,5},{5... | collective-permute-start | bytes 2064392 | tf_op jit(solution)/shard_map/ppermute | solution.py:725
  61.1 63.9 %collective-permute-start.30 = (bf16[4,64,768]{2,1,0:T(8,128)(2,1)}, bf16[4,64,768]{2,1,0:T(8,128)(2,1)}, u32[]{:S(2)}, u32[]{:S(2)}) collective-permute-start(bf16[4,64,768]{2,1,0:T(8,128)(2,1)} %pad_maximum_fusion.7.refs_5_), channel_id=1, source_target_pairs={{0,1},{1,2},{2,3},{3,0},{4,5},{5,6},{6,7},{7,4},{8,9},{9,10},{10,1... | collective-permute-start | bytes 1179656 | tf_op jit(solution)/shard_map/ppermute | solution.py:735
  64.2 56.8 %collective-permute-start.22 = (bf16[2,192,1024]{2,1,0:T(8,128)(2,1)}, bf16[2,192,1024]{2,1,0:T(8,128)(2,1)}, u32[]{:S(2)}, u32[]{:S(2)}) collective-permute-start(bf16[2,192,1024]{2,1,0:T(8,128)(2,1)} %bitcast.53.refs_0_), channel_id=1, source_target_pairs={{0,8},{4,12},{8,0},{12,4},{16,24},{20,28},{24,16},{28,20},{1,9},{5... | collective-permute-start | bytes 2359304 | tf_op jit(solution)/shard_map/ppermute | solution.py:730
  66.8 26.0 %collective-permute-start.15 = (bf16[2,192,384]{2,1,0:T(8,128)(2,1)S(1)}, bf16[2,192,384]{2,1,0:T(8,128)(2,1)S(1)}, u32[]{:S(2)}, u32[]{:S(2)}) collective-permute-start(bf16[2,192,384]{2,1,0:T(8,128)(2,1)S(1)} %slice.296), channel_id=1, source_target_pairs={{0,8},{4,12},{8,0},{12,4},{16,24},{20,28},{24,16},{28,20},{1,9},{5... | collective-permute-start | bytes 884744 | tf_op jit(solution)/shard_map/ppermute | solution.py:730
  73.1 49.9 %collective-permute-start.23 = (bf16[2,192,1024]{2,1,0:T(8,128)(2,1)}, bf16[2,192,1024]{2,1,0:T(8,128)(2,1)}, u32[]{:S(2)}, u32[]{:S(2)}) collective-permute-start(bf16[2,192,1024]{2,1,0:T(8,128)(2,1)} %bitcast.53.refs_0_), channel_id=1, source_target_pairs={{0,16},{4,20},{8,24},{12,28},{16,0},{20,4},{24,8},{28,12},{1,17},{... | collective-permute-start | bytes 2359304 | tf_op jit(solution)/shard_map/ppermute | solution.py:730
  94.2 20.4 %collective-permute-start.16 = (bf16[4,192,384]{2,1,0:T(8,128)(2,1)S(1)}, bf16[4,192,384]{2,1,0:T(8,128)(2,1)S(1)}, u32[]{:S(2)}, u32[]{:S(2)}) collective-permute-start(bf16[4,192,384]{2,1,0:T(8,128)(2,1)S(1)} %pad_maximum_fusion.5.near_ref), channel_id=1, source_target_pairs={{0,4},{4,0},{8,12},{12,8},{16,20},{20,16},{24,28},{28,24},{1,5},{5... | collective-permute-start | bytes 1769480 | tf_op jit(solution)/shard_map/ppermute | solution.py:725
  119.3 21.4 %collective-permute-start.17 = (f32[256,768]{1,0:T(8,128)}, f32[256,768]{1,0:T(8,128)}, u32[]{:S(2)}, u32[]{:S(2)}) collective-permute-start(f32[256,768]{1,0:T(8,128)} %get-tuple-element.50.part_ref), channel_id=1, source_target_pairs={{0,4},{4,0},{8,12},{12,8},{16,20},{20,16},{24,28},{28,24},{1,5},{5... | collective-permute-start | bytes 2359304 | tf_op jit(solution)/shard_map/ppermute | solution.py:725
  119.7 20.4 %collective-permute-start.31 = (bf16[4,64,768]{2,1,0:T(8,128)(2,1)}, bf16[4,64,768]{2,1,0:T(8,128)(2,1)S(1)}, u32[]{:S(2)}, u32[]{:S(2)}) collective-permute-start(bf16[4,64,768]{2,1,0:T(8,128)(2,1)} %pad_maximum_fusion.7.refs_5_), channel_id=1, source_target_pairs={{0,2},{1,3},{2,0},{3,1},{4,6},{5,7},{6,4},{7,5},{8,10},{9,11},{10,... | collective-permute-start | bytes 1179656 | tf_op jit(solution)/shard_map/ppermute | solution.py:735
  121.0 19.6 %collective-permute-start.32 = (bf16[4,64,768]{2,1,0:T(8,128)(2,1)}, bf16[4,64,768]{2,1,0:T(8,128)(2,1)}, u32[]{:S(2)}, u32[]{:S(2)}) collective-permute-start(bf16[4,64,768]{2,1,0:T(8,128)(2,1)} %pad_maximum_fusion.7.refs_5_), channel_id=1, source_target_pairs={{0,3},{1,0},{2,1},{3,2},{4,7},{5,4},{6,5},{7,6},{8,11},{9,8},{10,9... | collective-permute-start | bytes 1179656 | tf_op jit(solution)/shard_map/ppermute | solution.py:735
  123.0 17.6 %collective-permute-start.24 = (bf16[1,192,1024]{2,1,0:T(8,128)(2,1)S(1)}, bf16[1,192,1024]{2,1,0:T(8,128)(2,1)}, u32[]{:S(2)}, u32[]{:S(2)}) collective-permute-start(bf16[1,192,1024]{2,1,0:T(8,128)(2,1)S(1)} %slice.303), channel_id=1, source_target_pairs={{0,16},{4,20},{8,24},{12,28},{16,0},{20,4},{24,8},{28,12},{1,17},{... | collective-permute-start | bytes 1179656 | tf_op jit(solution)/shard_map/ppermute | solution.py:730
  125.0 15.6 %collective-permute-start.25 = (bf16[1,192,1024]{2,1,0:T(8,128)(2,1)S(1)}, bf16[1,192,1024]{2,1,0:T(8,128)(2,1)}, u32[]{:S(2)}, u32[]{:S(2)}) collective-permute-start(bf16[1,192,1024]{2,1,0:T(8,128)(2,1)S(1)} %slice.304), channel_id=1, source_target_pairs={{0,8},{4,12},{8,0},{12,4},{16,24},{20,28},{24,16},{28,20},{1,9},{5... | collective-permute-start | bytes 1179656 | tf_op jit(solution)/shard_map/ppermute | solution.py:730
  154.7 49.1 %collective-permute-start.34 = (f32[256,768]{1,0:T(8,128)}, f32[256,768]{1,0:T(8,128)}, u32[]{:S(2)}, u32[]{:S(2)}) collective-permute-start(f32[256,768]{1,0:T(8,128)} %get-tuple-element.53.back_ref), channel_id=1, source_target_pairs={{0,4},{4,0},{8,12},{12,8},{16,20},{20,16},{24,28},{28,24},{1,5},{5... | collective-permute-start | bytes 2359304 | tf_op jit(solution)/shard_map/ppermute | solution.py:725
  156.1 21.1 %collective-permute-start.55 = (bf16[4,64,768]{2,1,0:T(8,128)(2,1)S(1)}, bf16[4,64,768]{2,1,0:T(8,128)(2,1)S(1)}, u32[]{:S(2)}, u32[]{:S(2)}) collective-permute-start(bf16[4,64,768]{2,1,0:T(8,128)(2,1)S(1)} %get-tuple-element.117), channel_id=1, source_target_pairs={{0,1},{1,2},{2,3},{3,0},{4,5},{5,6},{6,7},{7,4},{8,9},{9,10},{10,1... | collective-permute-start | bytes 1179656 | tf_op jit(solution)/shard_map/ppermute | solution.py:735
  164.4 29.3 %collective-permute-start.56 = (bf16[4,64,768]{2,1,0:T(8,128)(2,1)S(1)}, bf16[4,64,768]{2,1,0:T(8,128)(2,1)S(1)}, u32[]{:S(2)}, u32[]{:S(2)}) collective-permute-start(bf16[4,64,768]{2,1,0:T(8,128)(2,1)S(1)} %get-tuple-element.119), channel_id=1, source_target_pairs={{0,2},{1,3},{2,0},{3,1},{4,6},{5,7},{6,4},{7,5},{8,10},{9,11},{10,... | collective-permute-start | bytes 1179656 | tf_op jit(solution)/shard_map/ppermute | solution.py:735
  167.6 26.2 %collective-permute-start.57 = (bf16[4,64,768]{2,1,0:T(8,128)(2,1)S(1)}, bf16[4,64,768]{2,1,0:T(8,128)(2,1)S(1)}, u32[]{:S(2)}, u32[]{:S(2)}) collective-permute-start(bf16[4,64,768]{2,1,0:T(8,128)(2,1)S(1)} %get-tuple-element.118), channel_id=1, source_target_pairs={{0,3},{1,0},{2,1},{3,2},{4,7},{5,4},{6,5},{7,6},{8,11},{9,8},{10,9... | collective-permute-start | bytes 1179656 | tf_op jit(solution)/shard_map/ppermute | solution.py:735
  169.2 28.1 %collective-permute-start.47 = (bf16[1,192,1024]{2,1,0:T(8,128)(2,1)S(1)}, bf16[1,192,1024]{2,1,0:T(8,128)(2,1)S(1)}, u32[]{:S(2)}, u32[]{:S(2)}) collective-permute-start(bf16[1,192,1024]{2,1,0:T(8,128)(2,1)S(1)} %get-tuple-element.111), channel_id=1, source_target_pairs={{0,16},{4,20},{8,24},{12,28},{16,0},{20,4},{24,8},{28,12},{1,17},{... | collective-permute-start | bytes 1179656 | tf_op jit(solution)/shard_map/ppermute | solution.py:730
  177.1 20.7 %collective-permute-start.49 = (bf16[1,192,1024]{2,1,0:T(8,128)(2,1)S(1)}, bf16[1,192,1024]{2,1,0:T(8,128)(2,1)S(1)}, u32[]{:S(2)}, u32[]{:S(2)}) collective-permute-start(bf16[1,192,1024]{2,1,0:T(8,128)(2,1)S(1)} %get-tuple-element.110), channel_id=1, source_target_pairs={{0,8},{4,12},{8,0},{12,4},{16,24},{20,28},{24,16},{28,20},{1,9},{5... | collective-permute-start | bytes 1179656 | tf_op jit(solution)/shard_map/ppermute | solution.py:730
  195.8 46.7 %collective-permute-start.58 = (bf16[64,768]{1,0:T(8,128)(2,1)}, bf16[64,768]{1,0:T(8,128)(2,1)}, u32[]{:S(2)}, u32[]{:S(2)}) collective-permute-start(bf16[64,768]{1,0:T(8,128)(2,1)} %get-tuple-element.144), channel_id=1, source_target_pairs={{0,8},{4,12},{8,0},{12,4},{16,24},{20,28},{24,16},{28,20},{1,9},{5... | collective-permute-start | bytes 294920 | tf_op jit(solution)/shard_map/ppermute | solution.py:730
  197.2 45.5 %collective-permute-start.59 = (bf16[64,768]{1,0:T(8,128)(2,1)}, bf16[64,768]{1,0:T(8,128)(2,1)}, u32[]{:S(2)}, u32[]{:S(2)}) collective-permute-start(bf16[64,768]{1,0:T(8,128)(2,1)} %get-tuple-element.146), channel_id=1, source_target_pairs={{0,16},{4,20},{8,24},{12,28},{16,0},{20,4},{24,8},{28,12},{1,17},{... | collective-permute-start | bytes 294920 | tf_op jit(solution)/shard_map/ppermute | solution.py:730
  197.8 44.9 %collective-permute-start.60 = (bf16[64,768]{1,0:T(8,128)(2,1)}, bf16[64,768]{1,0:T(8,128)(2,1)}, u32[]{:S(2)}, u32[]{:S(2)}) collective-permute-start(bf16[64,768]{1,0:T(8,128)(2,1)} %get-tuple-element.145), channel_id=1, source_target_pairs={{0,24},{4,28},{8,16},{12,20},{16,8},{20,12},{24,0},{28,4},{1,25},{... | collective-permute-start | bytes 294920 | tf_op jit(solution)/shard_map/ppermute | solution.py:730
  201.5 69.3 %collective-permute-start.48 = (bf16[2,192,1024]{2,1,0:T(8,128)(2,1)}, bf16[2,192,1024]{2,1,0:T(8,128)(2,1)}, u32[]{:S(2)}, u32[]{:S(2)}) collective-permute-start(bf16[2,192,1024]{2,1,0:T(8,128)(2,1)} %pad_maximum_fusion.2), channel_id=1, source_target_pairs={{0,8},{4,12},{8,0},{12,4},{16,24},{20,28},{24,16},{28,20},{1,9},{5... | collective-permute-start | bytes 2359304 | tf_op jit(solution)/shard_map/ppermute | solution.py:730
  231.5 39.3 %collective-permute-start.50 = (bf16[2,192,1024]{2,1,0:T(8,128)(2,1)}, bf16[2,192,1024]{2,1,0:T(8,128)(2,1)}, u32[]{:S(2)}, u32[]{:S(2)}) collective-permute-start(bf16[2,192,1024]{2,1,0:T(8,128)(2,1)} %pad_maximum_fusion.3), channel_id=1, source_target_pairs={{0,16},{4,20},{8,24},{12,28},{16,0},{20,4},{24,8},{28,12},{1,17},{... | collective-permute-start | bytes 2359304 | tf_op jit(solution)/shard_map/ppermute | solution.py:730
  252.1 14.1 %collective-permute-start.65 = (f32[15,128]{1,0:T(8,128)S(1)}, f32[15,128]{1,0:T(8,128)S(1)}, u32[]{:S(2)}, u32[]{:S(2)}) collective-permute-start(f32[15,128]{1,0:T(8,128)S(1)} %add_add_fusion.1), channel_id=1, source_target_pairs={{0,1},{1,2},{2,3},{3,0},{4,5},{5,6},{6,7},{7,4},{8,9},{9,10},{10,1... | collective-permute-start | bytes 23048 | tf_op jit(solution)/shard_map/ppermute | solution.py:735
  266.2 27.5 %collective-permute-start.40 = (bf16[4,192,384]{2,1,0:T(8,128)(2,1)}, bf16[4,192,384]{2,1,0:T(8,128)(2,1)}, u32[]{:S(2)}, u32[]{:S(2)}) collective-permute-start(bf16[4,192,384]{2,1,0:T(8,128)(2,1)} %get-tuple-element.114), channel_id=1, source_target_pairs={{0,8},{4,12},{8,0},{12,4},{16,24},{20,28},{24,16},{28,20},{1,9},{5... | collective-permute-start | bytes 1769480 | tf_op jit(solution)/shard_map/ppermute | solution.py:730
  267.7 26.0 %collective-permute-start.41 = (bf16[4,192,384]{2,1,0:T(8,128)(2,1)}, bf16[4,192,384]{2,1,0:T(8,128)(2,1)}, u32[]{:S(2)}, u32[]{:S(2)}) collective-permute-start(bf16[4,192,384]{2,1,0:T(8,128)(2,1)} %get-tuple-element.116), channel_id=1, source_target_pairs={{0,16},{4,20},{8,24},{12,28},{16,0},{20,4},{24,8},{28,12},{1,17},{... | collective-permute-start | bytes 1769480 | tf_op jit(solution)/shard_map/ppermute | solution.py:730
  272.9 15.3 %collective-permute-start.52 = (bf16[2,2,24,1024]{3,2,0,1:T(8,128)(2,1)S(1)}, bf16[2,2,24,1024]{3,2,0,1:T(8,128)(2,1)S(1)}, u32[]{:S(2)}, u32[]{:S(2)}) collective-permute-start(bf16[2,2,24,1024]{3,2,0,1:T(8,128)(2,1)S(1)} %bitcast.241), channel_id=1, source_target_pairs={{0,2},{1,3},{2,0},{3,1},{4,6},{5,7},{6,4},{7,5},{8,10},{9,11},{10,... | collective-permute-start | bytes 589832 | tf_op jit(solution)/shard_map/ppermute | solution.py:735
  275.4 12.7 %collective-permute-start.53 = (bf16[2,2,24,1024]{3,2,0,1:T(8,128)(2,1)S(1)}, bf16[2,2,24,1024]{3,2,0,1:T(8,128)(2,1)S(1)}, u32[]{:S(2)}, u32[]{:S(2)}) collective-permute-start(bf16[2,2,24,1024]{3,2,0,1:T(8,128)(2,1)S(1)} %bitcast.240), channel_id=1, source_target_pairs={{0,3},{1,0},{2,1},{3,2},{4,7},{5,4},{6,5},{7,6},{8,11},{9,8},{10,9... | collective-permute-start | bytes 589832 | tf_op jit(solution)/shard_map/ppermute | solution.py:735
  282.5 11.2 %collective-permute-start.42 = (bf16[4,192,384]{2,1,0:T(8,128)(2,1)S(1)}, bf16[4,192,384]{2,1,0:T(8,128)(2,1)S(1)}, u32[]{:S(2)}, u32[]{:S(2)}) collective-permute-start(bf16[4,192,384]{2,1,0:T(8,128)(2,1)S(1)} %copy-done.18), channel_id=1, source_target_pairs={{0,24},{4,28},{8,16},{12,20},{16,8},{20,12},{24,0},{28,4},{1,25},{... | collective-permute-start | bytes 1769480 | tf_op jit(solution)/shard_map/ppermute | solution.py:730
  288.2 22.6 %collective-permute-start.36 = (bf16[4,128,768]{2,1,0:T(8,128)(2,1)}, bf16[4,128,768]{2,1,0:T(8,128)(2,1)S(1)}, u32[]{:S(2)}, u32[]{:S(2)}) collective-permute-start(bf16[4,128,768]{2,1,0:T(8,128)(2,1)} %get-tuple-element.67), channel_id=1, source_target_pairs={{0,4},{4,0},{8,12},{12,8},{16,20},{20,16},{24,28},{28,24},{1,5},{5... | collective-permute-start | bytes 2359304 | tf_op jit(solution)/shard_map/ppermute | solution.py:725
  295.7 10.1 %collective-permute-start.43 = (bf16[4,2,24,384]{3,2,1,0:T(8,128)(2,1)S(1)}, bf16[4,2,24,384]{3,2,1,0:T(8,128)(2,1)S(1)}, u32[]{:S(2)}, u32[]{:S(2)}) collective-permute-start(bf16[4,2,24,384]{3,2,1,0:T(8,128)(2,1)S(1)} %get-tuple-element.137), channel_id=1, source_target_pairs={{0,1},{1,2},{2,3},{3,0},{4,5},{5,6},{6,7},{7,4},{8,9},{9,10},{10,1... | collective-permute-start | bytes 442376 | tf_op jit(solution)/shard_map/ppermute | solution.py:735
  300.1 10.4 %collective-permute-start.44 = (bf16[4,2,24,384]{3,2,1,0:T(8,128)(2,1)S(1)}, bf16[4,2,24,384]{3,2,1,0:T(8,128)(2,1)S(1)}, u32[]{:S(2)}, u32[]{:S(2)}) collective-permute-start(bf16[4,2,24,384]{3,2,1,0:T(8,128)(2,1)S(1)} %get-tuple-element.139), channel_id=1, source_target_pairs={{0,2},{1,3},{2,0},{3,1},{4,6},{5,7},{6,4},{7,5},{8,10},{9,11},{10,... | collective-permute-start | bytes 442376 | tf_op jit(solution)/shard_map/ppermute | solution.py:735
  312.1 11.2 %collective-permute-start.38 = (bf16[128,768]{1,0:T(8,128)(2,1)S(1)}, bf16[128,768]{1,0:T(8,128)(2,1)S(1)}, u32[]{:S(2)}, u32[]{:S(2)}) collective-permute-start(bf16[128,768]{1,0:T(8,128)(2,1)S(1)} %get-tuple-element.122), channel_id=1, source_target_pairs={{0,16},{4,20},{8,24},{12,28},{16,0},{20,4},{24,8},{28,12},{1,17},{... | collective-permute-start | bytes 589832 | tf_op jit(solution)/shard_map/ppermute | solution.py:730
  313.1 10.2 %collective-permute-start.39 = (bf16[128,768]{1,0:T(8,128)(2,1)S(1)}, bf16[128,768]{1,0:T(8,128)(2,1)S(1)}, u32[]{:S(2)}, u32[]{:S(2)}) collective-permute-start(bf16[128,768]{1,0:T(8,128)(2,1)S(1)} %get-tuple-element.121), channel_id=1, source_target_pairs={{0,24},{4,28},{8,16},{12,20},{16,8},{20,12},{24,0},{28,4},{1,25},{... | collective-permute-start | bytes 589832 | tf_op jit(solution)/shard_map/ppermute | solution.py:730
  (72 other events, 572.3 us)

commit v2 on v1

--- a/solution.py
+++ b/solution.py
@@ -73,7 +73,7 @@
 
 
 def cost(flops, nbytes, exps=0):
-    return pl.CostEstimate(flops=int(flops), bytes_accessed=int(nbytes), transcendentals=int(exps))
+    return pl.CostEstimate(flops=1, bytes_accessed=1, transcendentals=0)
 
 
 def bias_kernel(table_ref, out_ref):
@@ -105,48 +105,72 @@
     )(table)
 
 
-def bias_sum_kernel(grad_ref, out_ref):
-    row_id = lax.broadcasted_iota(jnp.int32, (lanes, 2 * lanes), 0)
-    bucket_id = lax.broadcasted_iota(jnp.int32, (2 * lanes, lanes), 1)
-    place = lax.broadcasted_iota(jnp.int32, (2 * lanes, lanes), 0)
-    total = jnp.zeros((8, lanes), f32)
-    for block in range(3):
-        part = grad_ref[0, lanes * (block + 1) : lanes * (block + 2), :]
-        wide = jnp.concatenate([part, jnp.zeros((lanes, lanes), f32)], axis=1)
-        for bit in range(7):
-            step = 1 << bit
-            moved = pltpu.roll(wide, step, 1)
-            wide = jnp.where((row_id & step) == 0, moved, wide)
-        sums = jnp.sum(wide.reshape(lanes // 8, 8, 2 * lanes), axis=0)
-        onehot = (bucket_of(lanes * (block - 1) + lanes - 1 - place) == bucket_id).astype(f32)
-        total = total + lax.dot_general(
-            sums,
-            onehot,
-            (((1,), (0,)), ((), ())),
-            precision=lax.Precision.HIGHEST,
-            preferred_element_type=f32,
-        )
-    low = jnp.sum(grad_ref[0, 0:lanes, :])
-    high = jnp.sum(grad_ref[0, 4 * lanes : 5 * lanes, :])
-    lane = lax.broadcasted_iota(jnp.int32, (1, lanes), 1)
-    row = jnp.sum(total, axis=0, keepdims=True)
-    row = row + jnp.where(lane == 15, low, 0.0) + jnp.where(lane == 31, high, 0.0)
-    out_ref[0] = row
-
-
-def bias_sums(grad_band):
-    heads = grad_band.shape[0]
-    summed = pl.pallas_call(
-        bias_sum_kernel,
-        grid=(heads,),
-        in_specs=[pl.BlockSpec((1, 5 * lanes, lanes), lambda i: (i, 0, 0))],
-        out_specs=pl.BlockSpec((1, 1, lanes), lambda i: (i, 0, 0)),
-        out_shape=jax.ShapeDtypeStruct((heads, 1, lanes), f32),
+def ready_kernel(meta_ref, attn_ref, ffin_ref, ffout_ref, tokens_ref, ids_ref, gain_ref, *outs):
+    attn_out, attn_send, gu_out, gu_send, row_out, down_out = outs
+    down_out[...] = ffout_ref[...].astype(bf16)
+    core = meta_ref[0]
+    first = core == 0
+    width = tokens_ref.shape[1]
+    half = width // 2
+    low = attn_ref[...].astype(bf16)
+    left, right = low[..., :half], low[..., half:]
+    attn_out[0:3, core] = jnp.where(first, left[:3], right[:3])
+    attn_send[...] = jnp.where(first, right[:3], left[:3])
+    attn_out[3, 0] = left[3]
+    attn_out[3, 1] = right[3]
+    grain = ffin_ref.shape[2] // (2 * meta_ref.shape[0])
+    for index in range(meta_ref.shape[0]):
+        start = 2 * index * grain
+        even = ffin_ref[:, :, start : start + grain].astype(bf16)
+        odd = ffin_ref[:, :, start + grain : start + 2 * grain].astype(bf16)
+        cols = slice(index * grain, (index + 1) * grain)
+        gu_out[:, core, :, cols] = jnp.where(first, even, odd)
+        gu_send[:, :, cols] = jnp.where(first, odd, even)
+    tok = tokens_ref.shape[0]
+    tokens = tokens_ref[...]
+    row_out[:tok, :] = (tokens * rms_scale(tokens) * gain_ref[0:1, :]).astype(bf16)
+    ids = jnp.broadcast_to(ids_ref[...].astype(f32), (16, tok))
+    ids = jnp.concatenate([ids, jnp.zeros((16, width - tok), f32)], axis=1)
+    row_out[tok:, :] = ids.astype(bf16)
+
+
+def make_ready(core, attention_weight, ffin_weight, ffout_weight, tokens, ids, gain, chips):
+    tok, width = tokens.shape
+    rows, half, hidden = attention_weight.shape[1], width // 2, ffin_weight.shape[2]
+    return pl.pallas_call(
+        ready_kernel,
+        in_specs=[smem_spec()] + [whole_spec()] * 6,
+        out_specs=[whole_spec()] * 6,
+        out_shape=[
+            shaped(bf16, 4, 2, rows, half),
+            shaped(bf16, 3, rows, half),
+            shaped(bf16, 2, 2, rows, hidden // 2),
+            shaped(bf16, 2, rows, hidden // 2),
+            shaped(bf16, tok + 16, width),
+            shaped(bf16, *ffout_weight.shape),
+        ],
         compiler_params=params(),
-        cost_estimate=cost(heads * 3e6, 4e6),
-        name="bias_sums",
-    )(grad_band)
-    return summed.reshape(heads, lanes)
+        cost_estimate=cost(1e6, 2e6),
+        name="make_ready",
+    )(jnp.broadcast_to(core, (chips,)), attention_weight, ffin_weight, ffout_weight, tokens, ids, gain)
+
+
+def fill_kernel(core_ref, kept_ref, arrived_ref, out_ref):
+    count = arrived_ref.shape[0]
+    out_ref[...] = kept_ref[...]
+    out_ref[0:count, 1 - core_ref[0]] = arrived_ref[...]
+
+
+def fill(core, kept, arrived):
+    return pl.pallas_call(
+        fill_kernel,
+        in_specs=[smem_spec(), whole_spec(), whole_spec()],
+        out_specs=whole_spec(),
+        out_shape=shaped(bf16, *kept.shape),
+        compiler_params=params(),
+        cost_estimate=cost(0, 1e6),
+        name="fill",
+    )(core.reshape(1), kept, arrived)
 
 
 def row_block(meta_ref, slot, rows):
@@ -182,29 +206,35 @@
     return jax.ShapeDtypeStruct(shape, kind)
 
 
-def rows_kernel(width, count, meta_ref, *refs):
-    pieces, (full_ref, turned_ref, mask_ref) = refs[:count], refs[count:]
-    chip_ids = pieces[0][:, width : width + lanes].astype(f32).T[:1, :]
-    for index, piece in enumerate(pieces):
-        rows = piece.shape[0]
-        grain = min(rows, lanes)
-        for part in range(rows // grain):
-            start = meta_ref[index] + part * grain
-            place = pl.ds(pl.multiple_of(start, grain), grain)
-            local = piece[part * grain : (part + 1) * grain, :]
-            full_ref[place, :] = local[:, :width]
-            wide = local[:, width : width + lanes].astype(f32)
+def rows_kernel(meta_ref, near_ref, far_ref, full_ref, turned_ref, mask_ref):
+    chips = near_ref.shape[0]
+    core = meta_ref[chips]
+    groups = lambda block: block[lanes : lanes + 16, :lanes].astype(f32)[:1, :]
+    mine, other = groups(near_ref[0]), groups(far_ref[0])
+    chip_ids = jnp.where(
+        core == 0,
+        jnp.concatenate([mine, other], axis=1),
+        jnp.concatenate([other, mine], axis=1),
+    )
+    for source, side in ((near_ref, core), (far_ref, 1 - core)):
+        for step in range(chips):
+            block = source[step]
+            start = (meta_ref[step] * 2 + side) * lanes
+            place = pl.ds(pl.multiple_of(start, lanes), lanes)
+            normed = block[:lanes, :]
+            full_ref[place, :] = normed
+            turned_ref[:, place] = normed.T
+            wide = jnp.broadcast_to(groups(block), (lanes, lanes)).T
             same = jnp.concatenate([wide, wide], axis=1) == chip_ids
             mask_ref[place, :] = jnp.where(same, 0.0, masked_score)
-    for start in range(0, full_ref.shape[0], lanes):
-        turned_ref[:, start : start + lanes] = full_ref[start : start + lanes, :].T
-
-
-def place_rows(pieces, starts, width):
-    length = sum(piece.shape[0] for piece in pieces)
+
+
+def place_rows(meta, near, far):
+    chips, _, width = near.shape
+    length = 2 * chips * lanes
     return pl.pallas_call(
-        functools.partial(rows_kernel, width, len(pieces)),
-        in_specs=[smem_spec()] + [whole_spec()] * len(pieces),
+        rows_kernel,
+        in_specs=[smem_spec()] + [whole_spec()] * 2,
         out_specs=[whole_spec()] * 3,
         out_shape=[
             shaped(bf16, length, width),
@@ -214,7 +244,7 @@
         compiler_params=params(),
         cost_estimate=cost(3e6, 8e6),
         name="place_rows",
-    )(starts, *pieces)
+    )(meta, near, far)
 
 
 def one_head(matrix, half):
@@ -369,7 +399,9 @@
 
 def feed_kernel(
     gu_plan,
-    down_count,
+    chips,
+    gu_count,
+    places,
     meta_ref,
     tokens_ref,
     cot_ref,
@@ -381,14 +413,14 @@
     refs = list(refs)
     take = lambda n: [refs.pop(0) for _ in range(n)]
     gu_pieces = take(gu_plan[-1][0] + 1)
-    down_pieces = take(down_count)
-    mixed_ref, out_ref, back_ref, gu_out, down_out = take(5)
+    (down_full,) = take(1)
+    mixed_ref, out_ref, back_ref = take(3)
+    gu_outs, down_outs = take(gu_count), take(places)
     gu, down, grad_gu, grad_down, cot_low, normed_low = take(6)
     gu_sem, down_sem, gu_out_sem, down_out_sem = take(4)
     step = pl.program_id(0)
     steps = pl.num_programs(0)
     block = 256
-    chips = gu_out.shape[0]
 
     @pl.when(step == 0)
     def _():
@@ -400,12 +432,10 @@
             )
         gu_copies = run_copies(pairs, gu_sem)
         pairs = []
-        slot = chips
-        for piece in down_pieces:
-            for index in range(piece.shape[0]):
-                place = row_block(meta_ref, slot, piece.shape[1])
-                pairs.append((piece.at[index], down.at[place, :]))
-                slot += 1
+        grain = down.shape[0] // chips
+        for index in range(chips):
+            source = down_full.at[row_block(meta_ref, chips + index, grain), :]
+            pairs.append((source, down.at[index * grain : (index + 1) * grain, :]))
         down_copies = run_copies(pairs, down_sem)
         mixed = tokens_ref[...] + part_ref[...] + arrived_ref[...]
         mixed_ref[...] = mixed
@@ -439,36 +469,44 @@
     @pl.when(step == steps - 1)
     def _():
         pairs = []
-        for index in range(chips):
-            place = row_block(meta_ref, index, gu_out.shape[2])
-            pairs.append((grad_gu.at[:, place, :], gu_out.at[index]))
+        for out, (lead, step) in zip(gu_outs, cut_plan(chips, 2)):
+            place = row_block(meta_ref, step, out.shape[1])
+            pairs.append((grad_gu.at[lead : lead + out.shape[0], place, :], out))
         gu_copies = run_copies(pairs, gu_out_sem)
         pairs = []
-        for index in range(chips):
-            place = row_block(meta_ref, index, down_out.shape[1])
-            pairs.append((grad_down.at[place, :], down_out.at[index]))
+        for turn, out in enumerate(down_outs):
+            for spot, step in enumerate(bit_reversed(chips)):
+                place = row_block(meta_ref, 2 * chips + turn * chips + step, out.shape[1])
+                pairs.append((grad_down.at[place, :], out.at[spot]))
         down_copies = run_copies(pairs, down_out_sem)
         wait_all(gu_copies)
         wait_all(down_copies)
 
 
-def feed(gu_plan, gu_pieces, down_pieces, meta, tokens, cot, part, arrived, gain, chips):
+def cut_plan(chips, size):
+    if chips != 4:
+        return [(0, step) for step in range(chips)]
+    return [(0, 0), (0, 1), (0, 2), (0, 3), (size // 2, 3)]
+
+
+def feed(gu_plan, gu_pieces, down_full, meta, tokens, cot, part, arrived, gain, chips, places):
     group, width = tokens.shape
     hidden = gu_pieces[0].shape[2]
     block = 256
     fixed = lambda i, *_: (0, 0)
     full = lambda *shape: pl.BlockSpec(shape, fixed)
     flops = 2 * 9 * group * width * hidden
-    down_copies = sum(piece.shape[0] for piece in down_pieces)
-    return pl.pallas_call(
-        functools.partial(feed_kernel, gu_plan, len(down_pieces)),
+    plan = cut_plan(chips, 2)
+    size = [1 if chips == 4 and step == 3 else 2 for _, step in plan]
+    results = pl.pallas_call(
+        functools.partial(feed_kernel, gu_plan, chips, len(plan), places),
         grid_spec=pltpu.PrefetchScalarGridSpec(
             num_scalar_prefetch=1,
             grid=(hidden // block,),
             in_specs=[full(group, width)] * 4
             + [full(1, width)]
-            + [any_spec()] * (len(gu_pieces) + len(down_pieces)),
-            out_specs=[full(group, width)] * 3 + [any_spec()] * 2,
+            + [any_spec()] * (len(gu_pieces) + 1),
+            out_specs=[full(group, width)] * 3 + [any_spec()] * (len(plan) + places),
             scratch_shapes=[
                 pltpu.VMEM((2, width, hidden), bf16),
                 pltpu.VMEM((hidden, width), bf16),
@@ -477,17 +515,19 @@
                 pltpu.VMEM((group, width), bf16),
                 pltpu.VMEM((group, width), bf16),
                 dma(len(gu_plan)),
-                dma(down_copies),
                 dma(chips),
-                dma(chips),
+                dma(len(plan)),
+                dma(chips * places),
             ],
         ),
         out_shape=[shaped(f32, group, width)] * 3
-        + [shaped(bf16, chips, 2, width // chips, hidden), shaped(bf16, chips, hidden // chips, width)],
+        + [shaped(bf16, lead, width // chips, hidden) for lead in size]
+        + [shaped(bf16, chips, hidden // (chips * places), width)] * places,
         compiler_params=params(),
         cost_estimate=cost(flops, 25e6, group * hidden),
         name="feed",
-    )(meta, tokens, cot, part, arrived, gain, *gu_pieces, *down_pieces)
+    )(meta, tokens, cot, part, arrived, gain, *gu_pieces, down_full)
+    return results[:3], results[3 : 3 + len(plan)], results[3 + len(plan) :]
 
 
 def settle_kernel(
@@ -548,7 +588,25 @@
     )(meta, mixed, cot, back, arrived, attended, weight, gain)
 
 
-def retreat_kernel(meta_ref, do_ref, o_ref, q_ref, k_ref, v_ref, p_ref, dq_ref, dkv_ref, band_ref, low, sums):
+def band_rows(band_ref):
+    line = lax.broadcasted_iota(jnp.int32, (8, 2 * lanes), 0)
+    none = jnp.zeros((8, lanes), f32)
+    found = []
+    for block in range(3):
+        summed = jnp.zeros((8, 2 * lanes), f32)
+        for part in range(lanes // 8):
+            start = lanes * (block + 1) + 8 * part
+            wide = jnp.concatenate([band_ref[start : start + 8, :], none], axis=1)
+            move = lanes - 8 - 8 * part
+            summed = summed + (pltpu.roll(wide, move, 1) if move else wide)
+        for bit in range(3):
+            step = 1 << bit
+            summed = jnp.where((line & step) == 0, pltpu.roll(summed, step, 1), summed)
+        found.append(jnp.sum(summed, axis=0, keepdims=True))
+    return jnp.concatenate(found, axis=1)
+
+
+def retreat_kernel(meta_ref, do_ref, o_ref, q_ref, k_ref, v_ref, p_ref, dq_ref, dkv_ref, bias_ref, low, sums, band_ref, onehot):
     chip = meta_ref[0]
     blocks = k_ref.shape[0] // lanes
     group = 2 * lanes
@@ -556,6 +614,16 @@
     do = do_ref[...]
     spread = (do.astype(f32) * o_ref[...]).T
     band_ref[...] = jnp.zeros_like(band_ref)
+    far = jnp.zeros((8, lanes), f32)
+    rows_of = []
+
+    @pl.when(pl.program_id(0) == 0)
+    def _():
+        bucket = lax.broadcasted_iota(jnp.int32, (6 * lanes, lanes), 1)
+        spot = lax.broadcasted_iota(jnp.int32, (6 * lanes, lanes), 0)
+        offset = lanes * (spot // (2 * lanes)) - 1 - spot % (2 * lanes)
+        onehot[...] = (bucket_of(offset) == bucket).astype(f32)
+
     turned = []
     for half in range(2):
         do_half, query_half = one_head(do, half), one_head(q_ref[...], half)
@@ -566,7 +634,7 @@
             ds = soft * (mm_nt(v_ref[rows, :], do_half) - delta)
             for part in range(2):
                 place = band_place(block, chip, part)
-                band_ref[half, place, :] += ds[:, part * lanes : (part + 1) * lanes]
+                band_ref[place, :] += ds[:, part * lanes : (part + 1) * lanes]
             ds_low = ds.astype(bf16)
             low[rows, :] = ds_low
             dk = mm(ds_low, query_half)
@@ -578,7 +646,25 @@
                 dkv_ref[rows, :lanes] = (sums[rows, :lanes] + dk).astype(bf16)
                 dkv_ref[rows, lanes:] = (sums[rows, lanes:] + dv).astype(bf16)
         turned.append(mm_tn(k_ref[...], low[...])[half * features : (half + 1) * features])
+        rows_of.append(band_rows(band_ref))
+        low_sum = jnp.sum(band_ref[0:lanes, :])
+        high_sum = jnp.sum(band_ref[4 * lanes : 5 * lanes, :])
+        lane = lax.broadcasted_iota(jnp.int32, (8, lanes), 1)
+        line = lax.broadcasted_iota(jnp.int32, (8, lanes), 0)
+        far = far + jnp.where((lane == 15) & (line == half), low_sum, 0.0)
+        far = far + jnp.where((lane == 31) & (line == half), high_sum, 0.0)
+        if half == 0:
+            band_ref[...] = jnp.zeros_like(band_ref)
     dq_ref[...] = jnp.concatenate(turned, axis=0).T.astype(bf16)
+    rows_of.append(jnp.zeros((6, rows_of[0].shape[1]), f32))
+    near = lax.dot_general(
+        jnp.concatenate(rows_of, axis=0),
+        onehot[...],
+        (((1,), (0,)), ((), ())),
+        precision=lax.Precision.HIGHEST,
+        preferred_element_type=f32,
+    )
+    bias_ref[0] = near + far
 
 
 def retreat(meta, do, o, q, k, v, p):
@@ -604,17 +690,19 @@
             out_specs=[
                 pl.BlockSpec((group, lanes), col),
                 pl.BlockSpec((length, 2 * lanes), col),
-                pl.BlockSpec((2, 5 * lanes, lanes), deep),
+                pl.BlockSpec((1, 8, lanes), deep),
             ],
             scratch_shapes=[
                 pltpu.VMEM((length, group), bf16),
                 pltpu.VMEM((length, 2 * lanes), f32),
+                pltpu.VMEM((5 * lanes, lanes), f32),
+                pltpu.VMEM((6 * lanes, lanes), f32),
             ],
         ),
         out_shape=[
             shaped(bf16, group, half),
             shaped(bf16, length, 2 * half),
-            shaped(f32, 2 * pairs, 5 * lanes, lanes),
+            shaped(f32, pairs, 8, lanes),
         ],
         compiler_params=params(),
         cost_estimate=cost(flops, 20e6),
@@ -622,52 +710,123 @@
     )(meta, do, o, q, k, v, p)
 
 
-def grads_kernel(plan, meta_ref, rows_ref, turned_ref, dq_ref, dkv_ref, gain_ref, near_wo, far_wo, *refs):
+small_rows = 16
+
+
+def load_plan(plan, pieces, meta_ref, first, weight):
+    pairs = []
+    for index, lead, target, size, slot in plan:
+        size = min(size, 3 - target)
+        place = row_block(meta_ref, first + slot, pieces[index].shape[1])
+        pairs.append((pieces[index].at[lead : lead + size], weight.at[target : target + size, place, :]))
+    return pairs
+
+
+def grads_kernel(
+    plan, count, meta_ref, rows_ref, turned_ref, dq_ref, dkv_ref, gains_ref, second_ref, bias_ref, near_wo, far_wo, *refs
+):
     refs = list(refs)
     take = lambda n: [refs.pop(0) for _ in range(n)]
     pieces = take(plan[-1][0] + 1)
-    grad_out, near_out, far_out, gain_grad_ref = take(4)
-    weight, both, grad, back = take(4)
-    sem, grad_sem, wo_sem, row_sem = take(4)
+    outs = take(count)
+    weight, grad, wo, small, sem, out_sem = take(6)
     chip, core = meta_ref[0], meta_ref[1]
-    length, width = rows_ref.shape
+    width = rows_ref.shape[1]
     half = width // 2
     group = dq_ref.shape[0]
-    chips = grad_out.shape[0]
-    slots = 2
-    pairs = []
-    for index, lead, target, size, slot in plan:
-        size = min(size, 3 - target)
-        place = row_block(meta_ref, slots + slot, pieces[index].shape[1])
-        pairs.append((pieces[index].at[lead : lead + size], weight.at[target : target + size, place, :]))
-    loads = run_copies(pairs, sem)
-    pairs = []
-    rows = near_wo.shape[1]
-    for source, owner in ((near_wo, core), (far_wo, 1 - core)):
-        for index in range(near_wo.shape[0]):
-            target = owner * (chips // 2) + index
-            for side in range(2):
-                pairs.append(
-                    (
-                        source.at[index, :, side * half : (side + 1) * half],
-                        grad_out.at[chip ^ target, 3, side * rows : (side + 1) * rows, :],
-                    )
-                )
-    wo_copies = run_copies(pairs, wo_sem)
+    chips = wo.shape[0]
+    loads = run_copies(load_plan(plan, pieces, meta_ref, 2, weight), sem)
+    for index in range(chips // 2):
+        wo[core * (chips // 2) + index] = near_wo[index]
+        wo[(1 - core) * (chips // 2) + index] = far_wo[index]
     own_rows = pl.ds(pl.multiple_of(chip * group, group), group)
-    grad[0] = mm_tn(rows_ref[own_rows, :], dq_ref[...]).astype(bf16)
+    query_grad = mm_tn(rows_ref[own_rows, :], dq_ref[...])
+    grad[0] = query_grad.astype(bf16)
+    wait_all(loads)
+    along_row = [query_grad[:, at : at + lanes] * weight[0, :, at : at + lanes].astype(f32) for at in range(0, half, lanes)]
+    along_row = sum(along_row[1:], along_row[0])
     for pair in range(half // lanes):
         wide = slice(pair * 2 * lanes, (pair + 1) * 2 * lanes)
         cols = slice(pair * lanes, (pair + 1) * lanes)
-        summed = mm(turned_ref[...], dkv_ref[:, wide]).astype(bf16)
-        grad[1, :, cols] = summed[:, :lanes]
-        grad[2, :, cols] = summed[:, lanes:]
+        summed = mm(turned_ref[...], dkv_ref[:, wide])
+        low = summed.astype(bf16)
+        grad[1, :, cols] = low[:, :lanes]
+        grad[2, :, cols] = low[:, lanes:]
+        along_row = along_row + summed[:, :lanes] * weight[1, :, cols].astype(f32)
+        along_row = along_row + summed[:, lanes:] * weight[2, :, cols].astype(f32)
+    first_gain = jnp.sum(along_row.T, axis=0, keepdims=True) / gains_ref[...]
+    second_gain = second_ref[...]
+    lines = [first_gain[:, :half], first_gain[:, half:], second_gain[:, :half], second_gain[:, half:]]
+    for pair in range(bias_ref.shape[0]):
+        both = [bias_ref[pair, 0:1, :], bias_ref[pair, 1:2, :]]
+        both.append(jnp.zeros((1, half - 2 * lanes), f32))
+        lines.append(jnp.concatenate(both, axis=1))
+    lines.append(jnp.zeros((small_rows - len(lines), half), f32))
+    small[...] = jnp.concatenate(lines, axis=0).astype(bf16)
+    rows = width // chips
+    side_rows = rows // 2
     pairs = []
-    for index in range(chips):
-        place = row_block(meta_ref, slots + index, grad_out.shape[2])
-        pairs.append((grad.at[:, place, :], grad_out.at[index, 0:3]))
-    grad_copies = run_copies(pairs, grad_sem)
-    wait_all(loads)
+    for out, (matrix, step) in zip(outs, cut_plan(chips, 4)):
+        place = row_block(meta_ref, 2 + step, rows)
+        last = 2 if chips == 4 and step == 3 and matrix == 0 else 4
+        at = 0
+        for index in range(matrix, min(last, 3)):
+            pairs.append((grad.at[index, place, :], out.at[at : at + rows, :]))
+            at += rows
+        if last == 4:
+            target = meta_ref[2 + step]
+            for side in range(2):
+                pairs.append(
+                    (wo.at[target, :, side * half : (side + 1) * half], out.at[at : at + side_rows, :])
+                )
+                at += side_rows
+            pairs.append((small, out.at[at : at + small_rows, :]))
+    wait_all(run_copies(pairs, out_sem))
+
+
+def weight_grads(plan, pieces, meta, rows, turned, dq, dkv, gain, second, bias, near_wo, far_wo, chips):
+    length, width = rows.shape
+    half = width // 2
+    group = dq.shape[0]
+    flops = 2 * (2 * length * width * half + group * width * half)
+    block = width // chips
+    cuts = cut_plan(chips, 4)
+    sizes = []
+    for matrix, step in cuts:
+        whole = 4 * block + small_rows
+        parted = chips == 4 and step == 3
+        sizes.append(whole if not parted else 2 * block if matrix == 0 else whole - 2 * block)
+    return pl.pallas_call(
+        functools.partial(grads_kernel, plan, len(cuts)),
+        in_specs=[smem_spec()] + [whole_spec()] * 9 + [any_spec()] * len(pieces),
+        out_specs=[any_spec()] * len(cuts),
+        out_shape=[shaped(bf16, size, half) for size in sizes],
+        scratch_shapes=[
+            pltpu.VMEM((3, width, half), bf16),
+            pltpu.VMEM((3, width, half), bf16),
+            pltpu.VMEM((chips, block // 2, width), bf16),
+            pltpu.VMEM((small_rows, half), bf16),
+            dma(len(plan)),
+            dma(6 * chips + 1),
+        ],
+        compiler_params=params(),
+        cost_estimate=cost(flops, 12e6),
+        name="weight_grads",
+    )(meta, rows, turned, dq, dkv, gain, second, bias, near_wo, far_wo, *pieces)
+
+
+def back_kernel(plan, meta_ref, dq_ref, dkv_ref, *refs):
+    refs = list(refs)
+    take = lambda n: [refs.pop(0) for _ in range(n)]
+    pieces = take(plan[-1][0] + 1)
+    near_out, far_out = take(2)
+    weight, both, back, sem = take(4)
+    chip, core = meta_ref[0], meta_ref[1]
+    length = dkv_ref.shape[0]
+    half = dq_ref.shape[1]
+    group = dq_ref.shape[0]
+    chips = near_out.shape[0]
+    wait_all(run_copies(load_plan(plan, pieces, meta_ref, 2, weight), sem))
     for pair in range(half // lanes):
         wide = pair * 2 * lanes
         cols = slice(pair * lanes, (pair + 1) * lanes)
@@ -675,49 +834,68 @@
         both[:, wide + lanes : wide + 2 * lanes] = weight[2, :, cols]
     for start in range(0, length, group):
         back[start : start + group, :] = mm_nt(dkv_ref[start : start + group, :], both[...])
+    own_rows = pl.ds(pl.multiple_of(chip * group, group), group)
     back[own_rows, :] += mm_nt(dq_ref[...], weight[0])
-    gain_sum = jnp.zeros((8, width), f32)
-    for start in range(0, length, lanes):
-        both_rows = back[start : start + lanes, :] * rows_ref[start : start + lanes, :].astype(f32)
-        gain_sum = gain_sum + jnp.sum(both_rows.reshape(lanes // 8, 8, width), axis=0)
-    gain_grad_ref[...] = jnp.sum(gain_sum, axis=0, keepdims=True) / gain_ref[...]
-    for index in range(chips):
+    for index, step in enumerate(bit_reversed(chips)):
         for side, out in ((core, near_out), (1 - core, far_out)):
-            start = meta_ref[slots + index] * group + side * lanes
+            start = meta_ref[2 + step] * group + side * lanes
             out[index] = back[pl.ds(pl.multiple_of(start, lanes), lanes), :].astype(bf16)
-    wait_all(grad_copies)
-    wait_all(wo_copies)
-
-
-def weight_grads(plan, pieces, meta, rows, turned, dq, dkv, gain, near_wo, far_wo, chips):
-    length, width = rows.shape
+
+
+def row_grads(plan, pieces, meta, dq, dkv, chips):
+    length, width = dkv.shape
     half = width // 2
-    group = dq.shape[0]
-    flops = 2 * (4 * length * width * half + 2 * group * width * half)
     return pl.pallas_call(
-        functools.partial(grads_kernel, plan),
-        in_specs=[smem_spec()] + [whole_spec()] * 7 + [any_spec()] * len(pieces),
-        out_specs=[any_spec()] + [whole_spec()] * 3,
-        out_shape=[
-            shaped(bf16, chips, 4, width // chips, half),
-            shaped(bf16, chips, lanes, width),
-            shaped(bf16, chips, lanes, width),
-            shaped(f32, 1, width),
-        ],
+        functools.partial(back_kernel, plan),
+        in_specs=[smem_spec()] + [whole_spec()] * 2 + [any_spec()] * len(pieces),
+        out_specs=[whole_spec()] * 2,
+        out_shape=[shaped(bf16, chips, lanes, width)] * 2,
         scratch_shapes=[
             pltpu.VMEM((3, width, half), bf16),
             pltpu.VMEM((width, width), bf16),
-            pltpu.VMEM((3, width, half), bf16),
             pltpu.VMEM((length, width), f32),
             dma(len(plan)),
-            dma(chips),
-            dma(2 * chips),
-            dma(1),
         ],
         compiler_params=params(),
-        cost_estimate=cost(flops, 20e6),
-        name="weight_grads",
-    )(meta, rows, turned, dq, dkv, gain, near_wo, far_wo, *pieces)
+        cost_estimate=cost(4 * length * width * half, 8e6),
+        name="row_grads",
+    )(meta, dq, dkv, *pieces)
+
+
+def sum_kernel(order_ref, *refs):
+    places = order_ref.shape[0]
+    sources, outs, total_ref = refs[: -1 - places], refs[-1 - places : -1], refs[-1]
+    total_ref[...] = total([source[...] for source in sources])
+    height = total_ref.shape[0] - small_rows
+    rows = height // (8 * places)
+    last = total_ref[height:, :]
+    for turn, out in enumerate(outs):
+        parts = []
+        for block in range(8):
+            start = block * places * rows + order_ref[turn] * rows
+            parts.append(total_ref[pl.ds(pl.multiple_of(start, 8), rows), :])
+        out[...] = jnp.concatenate(parts + [last], axis=0).astype(bf16)
+
+
+def sum_plane(blocks, order):
+    height, half = blocks[0].shape
+    places = order.shape[0]
+    rows = (height - small_rows) // (8 * places)
+    if rows % 8:
+        summed = total(blocks).astype(bf16)
+        split, last = summed[:-small_rows].reshape(8, places, rows, half), summed[-small_rows:]
+        pick = lambda turn: lax.dynamic_index_in_dim(split, order[turn], 1, keepdims=False)
+        return [jnp.concatenate([pick(turn).reshape(-1, half), last], axis=0) for turn in range(places)]
+    return pl.pallas_call(
+        sum_kernel,
+        in_specs=[smem_spec()] + [whole_spec()] * len(blocks),
+        out_specs=[whole_spec()] * places,
+        out_shape=[shaped(bf16, (height - small_rows) // places + small_rows, half)] * places,
+        scratch_shapes=[pltpu.VMEM((height, half), f32)],
+        compiler_params=params(),
+        cost_estimate=cost(1e6, 4e6),
+        name="sum_plane",
+    )(order, *blocks)
 
 
 def core_swap(value):
@@ -762,17 +940,22 @@
     )(order, *blocks)
 
 
-def gather_plane(value):
+def gather_plane(value, later=None):
     chips = lax.axis_size("seq") // 2
     size = value.shape[0]
     if chips != 4:
         pieces = [value] + [plane_swap(value, step) for step in range(1, chips)]
-        return pieces, [(step, 0, 0, size, step) for step in range(chips)]
+        if later is not None:
+            later(pieces)
+        return pieces, [(step, 0, 0, size, step) for step in range(chips)], pieces[-1]
     first, second = plane_swap(value, 1), plane_swap(value, 2)
-    low, high = plane_swap(first[: size // 2], 2), plane_swap(second[size // 2 :], 1)
+    if later is not None:
+        first, second = lax.optimization_barrier((first, second, later((first, second))))[:2]
+    passed = first[: size // 2], second[size // 2 :]
+    low, high = plane_swap(passed[0], 2), plane_swap(passed[1], 1)
     plan = [(0, 0, 0, size, 0), (1, 0, 0, size, 1), (2, 0, 0, size, 2)]
     plan += [(3, 0, 0, size // 2, 3), (4, 0, size // 2, size - size // 2, 3)]
-    return [value, first, second, low, high], plan
+    return [value, first, second, low, high], plan, passed
 
 
 def total(blocks):
@@ -782,27 +965,81 @@
     return summed
 
 
-def scatter_plane(blocks):
-    chips = len(blocks)
-    if chips != 4:
-        return total(blocks[:1] + [plane_swap(blocks[step], step) for step in range(1, chips)])
-    cut = blocks[3].shape[0] // 2
-    low, high = plane_swap(blocks[3][:cut], 1), plane_swap(blocks[3][cut:], 2)
-    add = lambda a, b: total([a, b]).astype(bf16)
-    second = jnp.concatenate([add(blocks[2][:cut], low), blocks[2][cut:]], axis=0)
-    first = jnp.concatenate([blocks[1][:cut], add(blocks[1][cut:], high)], axis=0)
-    return total([blocks[0], plane_swap(first, 1), plane_swap(second, 2)])
-
-
-def scatter_direct(blocks):
-    chips = len(blocks)
-    return total(blocks[:1] + [plane_swap(blocks[step], step) for step in range(1, chips)])
-
-
-def scatter_along(split, dim, place):
+def scatter_first(blocks):
+    if lax.axis_size("seq") != 8:
+        return None
+    return plane_swap(blocks[3], 1), plane_swap(blocks[4], 2)
+
+
+def passing_kernel(first_ref, second_ref, low_ref, high_ref, first_out, second_out, held, sem):
+    at, low_rows = low_ref.shape[0], pl.ds(0, low_ref.shape[0])
+    high_rows = pl.ds(at, high_ref.shape[0])
+    spots = [(second_out.at[low_rows], low_ref, held.at[0, low_rows])]
+    spots.append((first_out.at[high_rows], high_ref, held.at[1, pl.ds(0, high_ref.shape[0])]))
+    loads = run_copies([(place, room) for place, _, room in spots], sem)
+    stores = []
+    for index, (place, moved, room) in enumerate(spots):
+        loads[index].wait()
+        room[...] = (room[...].astype(f32) + moved[...].astype(f32)).astype(bf16)
+        store = pltpu.make_async_copy(room, place, sem.at[index])
+        store.start()
+        stores.append(store)
+    wait_all(stores)
+
+
+def scatter_second(blocks, passing):
+    if passing is None:
+        return blocks[1:]
+    low, high = passing
+    most = max(low.shape[0], high.shape[0])
+    return pl.pallas_call(
+        passing_kernel,
+        in_specs=[any_spec()] * 2 + [whole_spec()] * 2,
+        out_specs=[any_spec()] * 2,
+        out_shape=[shaped(bf16, *blocks[1].shape)] * 2,
+        scratch_shapes=[pltpu.VMEM((2, most) + low.shape[1:], bf16), dma(2)],
+        input_output_aliases={0: 0, 1: 1},
+        compiler_params=params(),
+        cost_estimate=cost(0, 2e6),
+        name="passing",
+    )(blocks[1], blocks[2], low, high)
+
+
+def scatter_sent(parts):
+    return [plane_swap(part, step + 1) for step, part in enumerate(parts)]
+
+
+def bit_reversed(chips):
+    order = [0]
+    while len(order) < chips:
+        order = [2 * step for step in order] + [2 * step + 1 for step in order]
+    return order
+
+
+def halved(blocks, step):
+    count = blocks.shape[0] // 2
+    return blocks[:count], plane_swap(blocks[count:], step)
+
+
+def summed_half(halves):
+    return total(halves).astype(bf16)
+
+
+def finished(halves, step):
+    while halves[0].shape[0] > 1:
+        step *= 2
+        halves = halved(summed_half(halves), step)
+    return total(halves)[0]
+
+
+def spread(values):
+    return [values[0]] + [along(value, step) for step, value in enumerate(values) if step]
+
+
+def spread_along(split, dim, place):
     count = lax.axis_size("batch")
     pick = lambda step: lax.dynamic_index_in_dim(split, (place + step) % count, dim, keepdims=False)
-    return total([pick(0)] + [along(pick(step).astype(bf16), step) for step in range(1, count)])
+    return [pick(0)] + [along(pick(step), step) for step in range(1, count)]
 
 
 def shards(
@@ -845,146 +1082,190 @@
 
     steps = [chip ^ step for step in range(chips)]
     order = jnp.stack([(place + places - step) % places for step in range(places)])
+    onward = jnp.stack([(place + step) % places for step in range(places)])
     flat_tokens, flat_cot = tokens.reshape(tok, width), cotangent.reshape(tok, width)
 
-    attention_low = attention_weight.astype(bf16)
-    sides = [attention_low[..., :half], attention_low[..., half:]]
-    own_side = jnp.where(first_core, sides[0][:3], sides[1][:3])
-    their_side = core_swap(jnp.where(first_core, sides[1][:3], sides[0][:3]))
-    attn_block = jnp.concatenate(
-        [jnp.stack(by_core(own_side, their_side), axis=1), jnp.stack([sides[0][3], sides[1][3]])[None]],
-        axis=0,
-    )
-    ffin_cut = ffin_weight.astype(bf16).reshape(2, rows, chips, 2, grain)
-    sides = [ffin_cut[:, :, :, side].reshape(2, rows, hidden // 2) for side in range(2)]
-    own_side = jnp.where(first_core, sides[0], sides[1])
-    their_side = core_swap(jnp.where(first_core, sides[1], sides[0]))
-    gu_block = jnp.stack(by_core(own_side, their_side), axis=1)
-    down_block = ffout_weight.astype(bf16)
-
-    ids_wide = jnp.broadcast_to(group_ids.reshape(tok, 1), (tok, lanes)).astype(bf16)
-    normed = flat_tokens * rms_scale(flat_tokens) * gains[0]
-    own_rows = jnp.concatenate([normed.astype(bf16), ids_wide], axis=1)
-    chip_rows = jnp.concatenate(by_core(own_rows, core_swap(own_rows)), axis=0)
-    chip_tokens = jnp.concatenate(by_core(flat_tokens, core_swap(flat_tokens)), axis=0)
-    chip_cot = jnp.concatenate(by_core(flat_cot, core_swap(flat_cot)), axis=0)
-
-    row_pieces, row_plan = gather_plane(own_rows)
-    near_rows = jnp.concatenate(row_pieces[1:], axis=0)
+    attn_kept, attn_sent, gu_kept, gu_sent, row_block_own, down_own = make_ready(
+        core,
+        attention_weight,
+        ffin_weight,
+        ffout_weight,
+        flat_tokens,
+        group_ids,
+        gains,
+        chips,
+    )
+    their_tokens, their_cot = core_swap(flat_tokens), core_swap(flat_cot)
+    attn_from, gu_from = core_swap(attn_sent), core_swap(gu_sent)
+    row_block_own, attn_kept = lax.optimization_barrier((row_block_own, attn_kept, their_tokens, their_cot))[:2]
+    attn_block = fill(core, after(attn_kept, gu_from), attn_from)
+    gu_block = fill(core, gu_kept, gu_from)
+
+    attn_blocks = along_all(attn_block)
+    near_rows, step = row_block_own[None], 1
+    while step < chips:
+        arrived = plane_swap(near_rows, step)
+        arrived = after(arrived, attn_block if step * 2 < chips else attn_blocks)
+        near_rows = jnp.concatenate([near_rows, arrived], axis=0)
+        step *= 2
+    own_heads = jnp.where(first_core, bias_table[:, : heads // 2], bias_table[:, heads // 2 :])
+    bias = bias_rows(after(own_heads, attn_block))
+    down_full = lax.all_gather(down_own, ("seq", "batch"), axis=0, tiled=True)
+
+    attn_joined = join(after(attn_blocks, near_rows, bias, gu_block), order).reshape(4, 2 * places * rows, half)
+    gu_joined = join(along_all(after(gu_block, attn_joined)), order)
+    attn_pieces, attn_plan, attn_first = gather_plane(attn_joined, lambda _: gu_joined)
+    near_rows = after(near_rows, attn_first)
     far_rows = core_swap(near_rows)
-    starts = [chip * group]
-    pieces = [chip_rows]
-    for source, side in ((near_rows, core), (far_rows, 1 - core)):
-        offset = 0
-        for _, _, target, size, step in row_plan[1:]:
-            starts.append(steps[step] * group + side * tok + target)
-            pieces.append(source[offset : offset + size])
-            offset += size
-    rows_full, turned, mask = place_rows(pieces, jnp.stack(starts), width)
-    own_heads = jnp.where(first_core, bias_table[:, : heads // 2], bias_table[:, heads // 2 :])
-    bias = bias_rows(own_heads)
-
-    attn_joined = join(along_all(attn_block), order).reshape(4, 2 * places * rows, half)
-    attn_pieces, attn_plan = gather_plane(attn_joined)
-    gu_joined = join(along_all(gu_block), order).reshape(2, 2 * places * rows, hidden // 2)
-    gu_pieces, gu_plan = gather_plane(gu_joined)
-    down_near, down_plan = gather_plane(down_block)
-    if chips == 4:
-        down_near = down_near[:3] + [jnp.concatenate(down_near[3:], axis=0)]
-    down_pieces = along_all(jnp.stack(down_near))
+    gu_joined = after(gu_joined, attn_first).reshape(2, 2 * places * rows, hidden // 2)
+    rows_full, turned, mask = place_rows(jnp.stack(steps + [core]), near_rows, far_rows)
+    attn_pieces, rows_full = lax.optimization_barrier((attn_pieces, rows_full))
+    wo_near = jnp.stack([attn_pieces[i][lead + 3 - target] for i, lead, target, size, _ in attn_plan if target + size == 4])
+    wo_far = core_swap(wo_near)
+    chip_tokens = jnp.concatenate(by_core(flat_tokens, their_tokens), axis=0)
+    chip_cot = jnp.concatenate(by_core(flat_cot, their_cot), axis=0)
 
     step_meta = jnp.stack(steps)
     query, key, value, soft, attended = attend(
         attn_plan, attn_pieces, step_meta, rows_full, mask, bias
     )
-    wo_near = jnp.stack([attn_pieces[i][lead + 3 - target] for i, lead, target, size, _ in attn_plan if target + size == 4])
-    wo_far = core_swap(wo_near)
     wo_meta = jnp.stack([core] + [step * 2 + core for step in steps] + [step * 2 + 1 - core for step in steps])
     part, out_weight = mix(wo_meta, attended, wo_near, wo_far)
-    down_meta = [step * places + order[index] for index in range(places) for step in steps]
-    mixed, out_part, back_part, gu_grads, down_grads = feed(
+    their_part = core_swap(part)
+    gu_pieces, gu_plan, _ = gather_plane(gu_joined, lambda _: attended)
+    down_meta = [2 * step + core for step in range(chips)]
+    down_meta += [step * places + onward[index] for index in range(places) for step in steps]
+    (mixed, out_part, back_part), gu_grads, down_grads = feed(
         gu_plan,
         gu_pieces,
-        down_pieces,
+        down_full,
         jnp.stack(steps + down_meta),
         chip_tokens,
         chip_cot,
         part,
-        core_swap(part),
+        their_part,
         gains[1:2],
         chips,
-    )
+        places,
+    )
+    gu_passing = scatter_first(gu_grads)
+    their_back = core_swap(back_part)
+    add = lambda a, b: total([a, b]).astype(bf16)
+    down_moving = along(down_grads[-1], 1)
     dmixed, attended_grad, second_gain, near_wo, far_wo = settle(
-        core.reshape(1), mixed, chip_cot, back_part, core_swap(back_part), attended, out_weight, gains[1:2], chips
-    )
-    mine = lambda value: lax.dynamic_slice_in_dim(value, core * tok, tok, 0)
-    theirs = lambda value: lax.dynamic_slice_in_dim(value, (1 - core) * tok, tok, 0)
-    layer_output = mine(mixed) + mine(out_part) + core_swap(theirs(out_part))
-
-    dq, dkv, band = retreat(chip.reshape(1), attended_grad, attended, query, key, value, soft)
-    attn_grads, near_back, far_back, first_gain = weight_grads(
+        core.reshape(1), mixed, chip_cot, back_part, their_back, attended, out_weight, gains[1:2], chips
+    )
+    gu_passing, far_wo, attended_grad, down_moving = lax.optimization_barrier(
+        (gu_passing, far_wo, attended_grad, down_moving)
+    )
+    gu_parts = scatter_second(gu_grads, gu_passing)
+    far_wo = core_swap(after(far_wo, gu_passing))
+    gu_parts, attended_grad, _ = lax.optimization_barrier((gu_parts, attended_grad, far_wo))
+    gu_arrived = scatter_sent(gu_parts)
+    down_moving = add(down_moving, down_grads[-2])
+    attended_grad, down_moving = lax.optimization_barrier((attended_grad, down_moving))
+    down_moving = along(down_moving, 1)
+    dq, dkv, bias_part = retreat(chip.reshape(1), attended_grad, attended, query, key, value, soft)
+    pair_meta = jnp.stack([chip, core] + steps)
+    down_moving = after(down_moving, dq)
+    for step in range(places - 3, 0, -1):
+        down_moving = add(down_moving, down_grads[step])
+        if step == places - 3:
+            dq, down_moving = lax.optimization_barrier((dq, down_moving))
+        down_moving = along(down_moving, 1)
+    attn_grads = weight_grads(
         attn_plan,
         attn_pieces,
-        jnp.stack([chip, core] + steps),
+        pair_meta,
         rows_full,
         turned,
         dq,
         dkv,
         gains[:1],
+        second_gain,
+        bias_part,
         near_wo,
-        core_swap(far_wo),
+        far_wo,
         chips,
     )
-    bias_part = bias_sums(band)[:, : bias_table.shape[0]].T
-
-    def own_columns(summed, columns):
-        keep = jnp.where(first_core, summed[:, 0], summed[:, 1])
-        send = jnp.where(first_core, summed[:, 1], summed[:, 0])
-        return columns(by_core(keep, core_swap(send)))
-
-    gu_sum = scatter_plane([gu_grads[step] for step in range(chips)]).astype(bf16)
-    gu_sum = scatter_along(gu_sum.reshape(2, 2, places, rows, hidden // 2), 2, place)
+
+    attn_grads, gu_arrived = lax.optimization_barrier((attn_grads, gu_arrived))
+    attn_passing = scatter_first(attn_grads)
+    gu_sum = total([gu_grads[0]] + list(gu_arrived)).astype(bf16)
+    gu_split = gu_sum.reshape(2, 2, places, rows, hidden // 2)
+    gu_cut = lambda step: lax.dynamic_index_in_dim(gu_split, (place + step) % places, 2, keepdims=False)
+    gu_moving = along(gu_cut(places - 1), 1)
+    down_sum = add(after(down_moving, attn_grads), down_grads[0])
+    down_halves = halved(down_sum, 1)
+    near_back, far_back = row_grads(attn_plan, attn_pieces, pair_meta, after(dq, attn_grads), dkv, chips)
+    if attn_passing is not None:
+        attn_passing = after(attn_passing, near_back, down_halves)
+    attn_parts = scatter_second(attn_grads, attn_passing)
+    attn_arrived = scatter_sent(attn_parts)
+    back_arrived = core_swap(far_back)
+    gu_moving = after(gu_moving, attn_parts)
+    for step in range(places - 2, 0, -1):
+        gu_moving = along(add(gu_moving, gu_cut(step)), 1)
+    gu_sum = total([gu_moving, gu_cut(0)])
+    pick = lambda value, first, dim: jnp.where(
+        first, lax.index_in_dim(value, 0, dim, False), lax.index_in_dim(value, 1, dim, False)
+    )
+    gu_own = pick(gu_sum, first_core, 1)
+    gu_their = core_swap(pick(gu_sum, core == 1, 1))
+    down_sum = summed_half(down_halves)
+    down_halves = halved(after(down_sum, attn_parts), 2)
+    mine = lambda value: lax.dynamic_slice_in_dim(value, core * tok, tok, 0)
+    theirs = lambda value: lax.dynamic_slice_in_dim(value, (1 - core) * tok, tok, 0)
+    their_out = core_swap(after(theirs(out_part), near_back))
+    attn_cuts = sum_plane([attn_grads[0]] + list(attn_arrived), onward)
+    attn_sum = spread(attn_cuts)
+    merged = total([near_back, back_arrived]).astype(bf16)
+    back_halves = halved(after(merged, attn_cuts), 1)
+    own_down = finished(after(down_halves, attn_cuts), 2)
+    back_sum = summed_half(back_halves)
+    back_halves = halved(back_sum, 2)
+
     weave = lambda parts: jnp.stack(
         [part.reshape(2, rows, chips, grain) for part in parts], axis=3
     ).reshape(2, rows, hidden)
-    own_gu = own_columns(gu_sum, weave)
-    down_sum = scatter_along(down_grads.reshape(chips, places, down_rows, width), 1, place).astype(bf16)
-    own_down = scatter_direct([down_sum[step] for step in range(chips)])
-    attn_sum = scatter_direct([attn_grads[step] for step in range(chips)]).astype(bf16)
-    attn_sum = scatter_along(attn_sum.reshape(4, 2, places, rows, half), 2, place)
-    own_qkv = own_columns(attn_sum[:3], lambda parts: jnp.concatenate(parts, axis=-1))
-    own_wo = jnp.concatenate([attn_sum[3, 0], attn_sum[3, 1]], axis=-1)
+    own_gu = weave(by_core(gu_own, gu_their))
+    all_tokens = places * tok * cycle_size
+    inverse_root = 1.0 / math.sqrt(all_tokens)
+    ffin_new = update(ffin_weight, own_gu, ffin_momentum, ffin_average, ffin_rate * inverse_root)
+    ffout_new = update(
+        ffout_weight, own_down, ffout_momentum, ffout_average, ffout_rate * inverse_root
+    )
+    layer_output = mine(mixed) + mine(out_part) + their_out
+    attn_sum, ffin_new, ffout_new, layer_output, _ = lax.optimization_barrier(
+        (attn_sum, ffin_new, ffout_new, layer_output, back_sum)
+    )
+    attn_sum = total(attn_sum)
+    first_grad = finished(back_halves, 2)
+    blocks = attn_sum[:-small_rows].reshape(4, 2, rows, half)
+    small_own = attn_sum[-small_rows:]
+    sent = pick(blocks[:3], core == 1, 1).reshape(3 * rows, half)
+    arrived = core_swap(jnp.concatenate([sent, small_own], axis=0))
+    own_qkv = jnp.concatenate(
+        by_core(pick(blocks[:3], first_core, 1), arrived[: 3 * rows].reshape(3, rows, half)), axis=-1
+    )
+    own_wo = jnp.concatenate([blocks[3, 0], blocks[3, 1]], axis=-1)
     own_attention = jnp.concatenate([own_qkv, own_wo[None]], axis=0)
 
-    arrived = core_swap(far_back)
-    merged = [total([near_back[step], arrived[step]]).astype(bf16) for step in range(chips)]
-    first_grad = scatter_direct(merged)
     scale = rms_scale(flat_tokens)
     gained = first_grad * gains[0]
     inner = jnp.mean(gained * flat_tokens, axis=-1, keepdims=True)
     input_grad = mine(dmixed) + scale * gained - flat_tokens * (scale**3 * inner)
 
-    none = jnp.zeros_like(bias_part)
-    bias_wide = jnp.concatenate(by_core(bias_part, none), axis=1)
-    small = jnp.concatenate([bias_wide.reshape(-1), first_gain[0], second_gain[0]]).reshape(-1, lanes)
-    small = small + core_swap(small)
-    small = scatter_direct([small] * chips)
-    small = total(along_all(small)).reshape(-1)
-    bias_reduced = small[: bias_table.size].reshape(bias_table.shape)
-    gains_reduced = small[bias_table.size :].reshape(gains.shape)
-
-    all_tokens = lax.axis_size("batch") * tok * cycle_size
-    inverse_root = 1.0 / math.sqrt(all_tokens)
+    small_their = arrived[3 * rows :]
+    gains_reduced = (small_own[:4] + small_their[:4]).reshape(gains.shape)
+    pairs = heads // 4
+    heads_of = lambda value: value[4 : 4 + pairs, : 2 * lanes].reshape(heads // 2, lanes)[:, : bias_table.shape[0]]
+    bias_reduced = jnp.concatenate(by_core(heads_of(small_own), heads_of(small_their)), axis=0).T
+
     attention_rate = jnp.array(attention_rates, dtype=f32)[:, None, None] * inverse_root
     gain_rate = jnp.array(gain_rates, dtype=f32)[:, None] * inverse_root
     attn_new = update(
         attention_weight, own_attention, attention_momentum, attention_average, attention_rate
-    )
-    ffin_new = update(
-        ffin_weight, own_gu, ffin_momentum, ffin_average, ffin_rate * inverse_root
-    )
-    ffout_new = update(
-        ffout_weight, own_down, ffout_momentum, ffout_average, ffout_rate * inverse_root
     )
     bias_new = update(bias_table, bias_reduced, bias_momentum, bias_average, bias_rate * inverse_root)
     gain_new = update(gains, gains_reduced, gain_momentum, gain_average, gain_rate)

time: 327 us -> 260 us (0.80)
  starting transfers between devices: 98.8 us -> 49.2 us
  local copies, waits for them, and re-layouts: 34.5 us -> 17.5 us
  waiting for transfers between devices: 79.9 us -> 64.1 us
  Pallas kernels: 73.2 us -> 88.2 us
  between operations: 1.66 us -> 15 us
  other arithmetic: 36.5 us -> 24 us
    ppermute x21 -> x15, starting transfers between devices: 56.3 us -> 21.2 us  [along(): lax.ppermute(value, 'batch', [(i, (i + step) % count) for i in range(coun...]
    ppermute x32 -> x22, starting transfers between devices: 39.3 us -> 26 us  [plane_swap(): return lax.ppermute(value, 'seq', [(i, i ^ 2 * step) for i in range(count)])]
    pallas_call x4 -> x10, Pallas kernels: 32.7 us -> 45.4 us  [the longest x1 13.6 us: feed(): pl.pallas_call(functools.partial(feed_kernel, gu_plan, chips, len(plan),...]
    ppermute x32 -> x22, waiting for transfers between devices: 34.2 us -> 23.5 us  [plane_swap(): return lax.ppermute(value, 'seq', [(i, i ^ 2 * step) for i in range(count)])]
    slice x16, local copies, waits for them, and re-layouts: 12.9 us -> 4 us  [the longest x4 2.6 us: gather_plane(): passed = (first[:size // 2], second[size // 2:])]
    ppermute x21 -> x15, waiting for transfers between devices: 45.2 us -> 37.3 us  [along(): lax.ppermute(value, 'batch', [(i, (i + step) % count) for i in range(coun...]
    squeeze x5 -> x2, local copies, waits for them, and re-layouts: 4.9 us -> 0.71 us  [the longest x1 0.7 us: shards(): lax.dynamic_index_in_dim(gu_split, (place + step) % places, 2, keepdims=F...]
    concatenate x9 -> x5, other arithmetic: 6.83 us -> 2.98 us  [the longest x2 1.07 us: shards(): near_rows = jnp.concatenate([near_rows, arrived], axis=0)]
  transfers between devices with their start and end apart: 68 -> 51, of which waited for: 18 -> 22; matrix products, arithmetic and copies ran while one was open for 20% -> 13% of each run, Pallas kernels for 18% -> 28%
where the time goes in v2:
time: 260 us; the launch traced here: 258 us
  Pallas kernels  88.2 us (34%)
  waiting for transfers between devices  64.1 us (25%)
  starting transfers between devices  49.2 us (19%)
  other arithmetic  24 us (9%)
  local copies, waits for them, and re-layouts  17.5 us (7%)
  between operations  15 us (6%)
    ppermute x15, waiting for transfers between devices, along(): lax.ppermute(value, 'batch', [(i, (i + step) % count) for i in range(coun...  37.3 us
    ppermute x22, starting transfers between devices, plane_swap(): return lax.ppermute(value, 'seq', [(i, i ^ 2 * step) for i in range(count)])  26 us
    ppermute x22, waiting for transfers between devices, plane_swap(): return lax.ppermute(value, 'seq', [(i, i ^ 2 * step) for i in range(count)])  23.5 us
    ppermute x15, starting transfers between devices, along(): lax.ppermute(value, 'batch', [(i, (i + step) % count) for i in range(coun...  21.2 us
    pallas_call x1, Pallas kernels, feed(): pl.pallas_call(functools.partial(feed_kernel, gu_plan, chips, len(plan),...  13.6 us
    pallas_call x1, Pallas kernels, retreat(): pl.pallas_call(retreat_kernel, grid_spec=pltpu.PrefetchScalarGridSpec(num...  13.2 us
    pallas_call x1, Pallas kernels, attend(): pl.pallas_call(functools.partial(attend_kernel, plan), grid_spec=pltpu.Pr...  13 us
    pallas_call x1, Pallas kernels, weight_grads(): pl.pallas_call(functools.partial(grads_kernel, plan, len(cuts)), in_specs...  7.61 us
  transfers between devices with their start and end apart: 51, of which 22 were waited for; matrix products, arithmetic and copies ran while one was open for 13% of the time, Pallas kernels for 28%

profile of v2, /device:TPU:0, one launch (start us, length us, event | category | flops | bytes accessed | tf_op | source)
XLA Modules:
  0.0 258.1 jit_solution(13601345730094671369)
XLA Ops:
  7.8 2.2 make_ready.1
  10.6 1.5 collective-permute-done
  13.4 2.9 %collective-permute-start.7 = (bf16[1,144,768]{2,1,0:T(8,128)(2,1)}, bf16[1,144,768]{2,1,0:T(8,128)(2,1)S(1)}, u32[]{:S(2)}, u32[]{:S(2)}) collective-permute-start(bf16[1,144,768]{2,1,0:T(8,128)(2,1)} %bitcast.166), channel_id=1, source_target_pairs={{0,8},{4,12},{8,0},{12,4},{16,24},{20,28},{24,16},{28,20},{1,9},{5... | collective-permute-start | bytes 663560 | tf_op jit(solution)/shard_map/ppermute | solution.py:908
  18.5 1.6 fill.2.refs_0_
  20.1 2.1 collective-permute-done.7
  23.2 1.8 collective-permute-start.8
  25.2 1.6 collective-permute-start.4
  26.8 2.6 %collective-permute-start.5 = (bf16[4,2,24,384]{3,2,1,0:T(8,128)(2,1)}, bf16[4,2,24,384]{3,2,1,0:T(8,128)(2,1)S(1)}, u32[]{:S(2)}, u32[]{:S(2)}) collective-permute-start(bf16[4,2,24,384]{3,2,1,0:T(8,128)(2,1)} %fill.2.refs_0_), channel_id=1, source_target_pairs={{0,2},{1,3},{2,0},{3,1},{4,6},{5,7},{6,4},{7,5},{8,10},{9,11},{10,... | collective-permute-start | bytes 442376 | tf_op jit(solution)/shard_map/ppermute | solution.py:913
  31.9 1.7 fill.3.refs_0_
  33.6 4.0 %bias_rows.1.bias_ref = f32[6,640,128]{2,1,0:T(8,128)} custom-call(f32[32,6]{1,0:T(8,128)} %broadcast_select_fusion.6.table_ref), custom_call_target="tpu_custom_call" | custom-call | flops 1 | bytes 1 | tf_op jit(solution)/shard_map/bias_rows/pallas_call | solution.py:96
  37.7 2.1 collective-permute-done.5.refs_2_
  40.5 2.3 join.2
  42.8 1.5 collective-permute-start.9
  45.2 3.5 %collective-permute-start.11 = (bf16[2,2,24,1024]{3,2,1,0:T(8,128)(2,1)S(1)}, bf16[2,2,24,1024]{3,2,1,0:T(8,128)(2,1)S(1)}, u32[]{:S(2)}, u32[]{:S(2)}) collective-permute-start(bf16[2,2,24,1024]{3,2,1,0:T(8,128)(2,1)S(1)} %copy-done.22), channel_id=1, source_target_pairs={{0,1},{1,2},{2,3},{3,0},{4,5},{5,6},{6,7},{7,4},{8,9},{9,10},{10,1... | collective-permute-start | bytes 589832 | tf_op jit(solution)/shard_map/ppermute | solution.py:913
  51.1 5.8 %collective-permute-done.11.refs_1_ = bf16[2,2,24,1024]{3,2,1,0:T(8,128)(2,1)S(1)} collective-permute-done((bf16[2,2,24,1024]{3,2,1,0:T(8,128)(2,1)S(1)}, bf16[2,2,24,1024]{3,2,1,0:T(8,128)(2,1)S(1)}, u32[]{:S(2)}, u32[]{:S(2)}) %collective-permute-start.11) | collective-permute-done | bytes 196640 | tf_op jit(solution)/shard_map/ppermute | solution.py:913
  56.9 8.3 %collective-permute-done.12.refs_2_ = bf16[2,2,24,1024]{3,2,1,0:T(8,128)(2,1)S(1)} collective-permute-done((bf16[2,2,24,1024]{3,2,1,0:T(8,128)(2,1)S(1)}, bf16[2,2,24,1024]{3,2,1,0:T(8,128)(2,1)S(1)}, u32[]{:S(2)}, u32[]{:S(2)}) %collective-permute-start.12) | collective-permute-done | bytes 196640 | tf_op jit(solution)/shard_map/ppermute | solution.py:913
  66.6 2.2 join.3
  70.4 1.5 collective-permute-start.14
  74.3 4.1 %place_rows.1 = (bf16[1024,768]{1,0:T(8,128)(2,1)}, bf16[768,1024]{1,0:T(8,128)(2,1)}, f32[1024,256]{1,0:T(8,128)}) custom-call(s32[5]{0:T(128)} %stack.170.meta_ref, bf16[4,144,768]{2,1,0:T(8,128)(2,1)} %copy-done.4, bf16[4,144,768]{2,1,0:T(8,128)(2,1)} %copy-done.15), custom_call_target="tpu_custom_call" | custom-call | flops 1 | bytes 1 | tf_op jit(solution)/shard_map/place_rows/pallas_call | solution.py:235
  78.4 6.3 %collective-permute-done.14.refs_3_ = bf16[2,192,384]{2,1,0:T(8,128)(2,1)S(1)} collective-permute-done((bf16[2,192,384]{2,1,0:T(8,128)(2,1)}, bf16[2,192,384]{2,1,0:T(8,128)(2,1)S(1)}, u32[]{:S(2)}, u32[]{:S(2)}) %collective-permute-start.14) | collective-permute-done | bytes 294944 | tf_op jit(solution)/shard_map/ppermute | solution.py:908
  86.1 1.5 collective-permute-start.19
  90.1 13.0 %attend.1 = (bf16[256,384]{1,0:T(8,128)(2,1)}, bf16[1024,384]{1,0:T(8,128)(2,1)}, bf16[1024,384]{1,0:T(8,128)(2,1)}, f32[6,1024,256]{2,1,0:T(8,128)}, f32[256,384]{1,0:T(8,128)}) custom-call(s32[4]{0:T(128)} %pad_add_fusion.2.meta_ref, bf16[1024,768]{1,0:T(8,128)(2,1)} %get-tuple-element.156.rows_ref, f32[1024,256]{1,0:T(8,128)} %get-tuple-element.158.mask_ref, ...), custom_call_target="tpu_custom_call" | custom-call | flops 1 | bytes 1 | tf_op jit(solution)/shard_map/attend/pallas_call | solution.py:327
  103.1 3.9 %mix.1 = (f32[256,768]{1,0:T(8,128)}, bf16[768,768]{1,0:T(8,128)(2,1)}) custom-call(s32[9]{0:T(128)} %stack.199.meta_ref, f32[256,384]{1,0:T(8,128)} %get-tuple-element.164.attended_ref.o_ref, bf16[4,192,384]{2,1,0:T(8,128)(2,1)} %copy-done.7, bf16[4,192,384]{2,1,0:T(8,128)(2,1)} %collective-permute-done.17.far_ref), custom_call_target="tpu_custom_call" | custom-call | flops 1 | bytes 1 | tf_op jit(solution)/shard_map/mix/pallas_call | solution.py:388
  107.8 1.6 collective-permute-start.21
  113.0 6.3 %collective-permute-done.21.refs_3_ = bf16[1,192,1024]{2,1,0:T(8,128)(2,1)S(1)} collective-permute-done((bf16[1,192,1024]{2,1,0:T(8,128)(2,1)S(1)}, bf16[1,192,1024]{2,1,0:T(8,128)(2,1)S(1)}, u32[]{:S(2)}, u32[]{:S(2)}) %collective-permute-start.21) | collective-permute-done | bytes 393248 | tf_op jit(solution)/shard_map/ppermute | solution.py:908
  119.3 2.4 collective-permute-done.22.refs_4_
  121.8 13.6 %feed.1 = (f32[256,768]{1,0:T(8,128)}, f32[256,768]{1,0:T(8,128)}, f32[256,768]{1,0:T(8,128)}, bf16[2,192,1024]{2,1,0:T(8,128)(2,1)}, bf16[2,192,1024]{2,1,0:T(8...) custom-call(s32[24]{0:T(128)} %stack.190.meta_ref, ...), custom_call_target="tpu_custom_call" | custom-call | flops 1 | bytes 1 | tf_op jit(solution)/shard_map/feed/pallas_call | solution.py:501
  137.4 1.5 collective-permute-start.26
  139.8 4.2 %settle.1 = (f32[256,768]{1,0:T(8,128)}, bf16[256,384]{1,0:T(8,128)(2,1)}, f32[1,768]{1,0:T(1,128)}, bf16[2,96,768]{2,1,0:T(8,128)(2,1)}, bf16[2,96,768]{2,1,0:T(8,128)(2,1)}) custom-call(s32[1]{0:T(128)} %bitcast.5.core_ref.meta_ref, f32[256,768]{1,0:T(8,128)} %get-tuple-element.174.mixed_ref, f32[256,768]{1,0:T(8,128)} %pad_maximum_fusion.2.cot_ref, ...), custom_call_target="tpu_custom_call" | custom-call | flops 1 | bytes 1 | tf_op jit(solution)/shard_map/settle/pallas_call | solution.py:574
  144.0 3.2 %collective-permute-done.23.low_ref = bf16[1,192,1024]{2,1,0:T(8,128)(2,1)S(1)} collective-permute-done((bf16[1,192,1024]{2,1,0:T(8,128)(2,1)}, bf16[1,192,1024]{2,1,0:T(8,128)(2,1)S(1)}, u32[]{:S(2)}, u32[]{:S(2)}) %collective-permute-start.23) | collective-permute-done | bytes 393248 | tf_op jit(solution)/shard_map/ppermute | solution.py:908
  147.5 2.9 %collective-permute-done.26 = bf16[4,64,768]{2,1,0:T(8,128)(2,1)S(1)} collective-permute-done((bf16[4,64,768]{2,1,0:T(8,128)(2,1)}, bf16[4,64,768]{2,1,0:T(8,128)(2,1)S(1)}, u32[]{:S(2)}, u32[]{:S(2)}) %collective-permute-start.26) | collective-permute-done | bytes 393248 | tf_op jit(solution)/shard_map/ppermute | solution.py:913
  150.3 3.1 %passing.2 = (bf16[2,192,1024]{2,1,0:T(8,128)(2,1)}, bf16[2,192,1024]{2,1,0:T(8,128)(2,1)}) custom-call(bf16[2,192,1024]{2,1,0:T(8,128)(2,1)} %get-tuple-element.170.first_ref, bf16[2,192,1024]{2,1,0:T(8,128)(2,1)} %get-tuple-element.171.second_ref, bf16[1,192,1024]{2,1,0:T(8,128)(2,1)} %copy-done.26, ...), custom_call_target="tpu_custom_call", output_to_operand_aliasing={{0}: (0, {}), {1}: (1, {})} | custom-call | flops 1 | bytes 1 | tf_op jit(solution)/shard_map/passing/pallas_call | solution.py:995
  156.5 13.2 %retreat.1 = (bf16[256,384]{1,0:T(8,128)(2,1)}, bf16[1024,768]{1,0:T(8,128)(2,1)}, f32[3,8,128]{2,1,0:T(8,128)}) custom-call(s32[1]{0:T(128)} %bitcast.4.meta_ref, bf16[256,384]{1,0:T(8,128)(2,1)} %get-tuple-element.190.do_ref, f32[256,384]{1,0:T(8,128)} %get-tuple-element.164.attended_ref.o_ref, bf16[256,384]{1,0:T(8,128)(2,1)} %get-tuple-element.191.q_ref, ...), custom_call_target="tpu_custom_call" | custom-call | flops 1 | bytes 1 | tf_op jit(solution)/shard_map/retreat/pallas_call | solution.py:677
  173.7 7.6 %weight_grads.1 = (bf16[784,384]{1,0:T(8,128)(2,1)}, bf16[784,384]{1,0:T(8,128)(2,1)}, bf16[784,384]{1,0:T(8,128)(2,1)}, bf16[384,384]{1,0:T(8,128)(2,1)}, bf16[400,384]{1,0:T(8,128)(2,1)}) custom-call(s32[6]{0:T(128)} %stack.167.meta_ref, bf16[1024,768]{1,0:T(8,128)(2,1)} %get-tuple-element.156.rows_ref, bf16[768,1024]{1,0:T(8,128)(2,1)} %get-tuple-element.157.turned_ref, ...), custom_call_target="tpu_custom_call" | custom-call | flops 1 | bytes 1 | tf_op jit(solution)/shard_map/weight_grads/pallas_call | solution.py:799
  185.6 1.8 add_convert_fusion.1
  188.1 5.9 %row_grads.1 = (bf16[4,128,768]{2,1,0:T(8,128)(2,1)}, bf16[4,128,768]{2,1,0:T(8,128)(2,1)}) custom-call(s32[6]{0:T(128)} %stack.167.meta_ref, bf16[256,384]{1,0:T(8,128)(2,1)} %get-tuple-element.216.dq_ref, bf16[1024,768]{1,0:T(8,128)(2,1)} %get-tuple-element.200.dkv_ref, bf16[4,192,384]{2,1,0:T(8,128)(2,1)} %bitcast.154, bf16[4,192,384]{2,1,0:T(8,128)(2,1)} %copy-done, ...), custom_call_target="tpu_custom_call" | custom-call | flops 1 | bytes 1 | tf_op jit(solution)/shard_map/row_grads/pallas_call | solution.py:848
  194.0 1.5 collective-permute-start.40
  196.1 3.0 %passing.3 = (bf16[784,384]{1,0:T(8,128)(2,1)}, bf16[784,384]{1,0:T(8,128)(2,1)}) custom-call(bf16[784,384]{1,0:T(8,128)(2,1)} %get-tuple-element.212.first_ref, bf16[784,384]{1,0:T(8,128)(2,1)} %get-tuple-element.213.second_ref, bf16[384,384]{1,0:T(8,128)(2,1)} %collective-permute-done.31.low_ref, ...), custom_call_target="tpu_custom_call", output_to_operand_aliasing={{0}: (0, {}), {1}: (1, {})} | custom-call | flops 1 | bytes 1 | tf_op jit(solution)/shard_map/passing/pallas_call | solution.py:995
  204.8 5.5 %collective-permute-done.41 = bf16[2,2,24,1024]{3,2,1,0:T(8,128)(2,1)S(1)} collective-permute-done((bf16[2,2,24,1024]{3,2,1,0:T(8,128)(2,1)S(1)}, bf16[2,2,24,1024]{3,2,1,0:T(8,128)(2,1)S(1)}, u32[]{:S(2)}, u32[]{:S(2)}) %collective-permute-start.41) | collective-permute-done | bytes 196640 | tf_op jit(solution)/shard_map/ppermute | solution.py:913
  211.9 1.8 add_add_fusion
  213.7 5.4 %collective-permute-done.42 = bf16[2,2,24,1024]{3,2,1,0:T(8,128)(2,1)S(1)} collective-permute-done((bf16[2,2,24,1024]{3,2,1,0:T(8,128)(2,1)S(1)}, bf16[2,2,24,1024]{3,2,1,0:T(8,128)(2,1)S(1)}, u32[]{:S(2)}, u32[]{:S(2)}) %collective-permute-start.42) | collective-permute-done | bytes 196640 | tf_op jit(solution)/shard_map/ppermute | solution.py:913
  222.7 2.6 %sum_plane.1 = (bf16[208,384]{1,0:T(8,128)(2,1)}, bf16[208,384]{1,0:T(8,128)(2,1)}, bf16[208,384]{1,0:T(8,128)(2,1)}, bf16[208,384]{1,0:T(8,128)(2,1)}) custom-call(s32[4]{0:T(128)} %pad_add_fusion.order_ref, bf16[784,384]{1,0:T(8,128)(2,1)} %get-tuple-element.211.refs_0_, bf16[784,384]{1,0:T(8,128)(2,1)} %copy-done.24, ...), custom_call_target="tpu_custom_call" | custom-call | flops 1 | bytes 1 | tf_op jit(solution)/shard_map/sum_plane/pallas_call | solution.py:889
  226.4 2.0 add_multiply_fusion
  228.5 3.8 %collective-permute-start.39 = (bf16[208,384]{1,0:T(8,128)(2,1)S(1)}, bf16[208,384]{1,0:T(8,128)(2,1)S(1)}, u32[]{:S(2)}, u32[]{:S(2)}) collective-permute-start(bf16[208,384]{1,0:T(8,128)(2,1)S(1)} %copy-done.62), channel_id=1, source_target_pairs={{0,3},{1,0},{2,1},{3,2},{4,7},{5,4},{6,5},{7,6},{8,11},{9,8},{10,9... | collective-permute-start | bytes 479240 | tf_op jit(solution)/shard_map/ppermute | solution.py:913
  232.4 1.7 add_multiply_fusion.2
  234.1 2.8 %collective-permute-done.47 = bf16[2,128,768]{2,1,0:T(8,128)(2,1)S(1)} collective-permute-done((bf16[2,128,768]{2,1,0:T(8,128)(2,1)S(1)}, bf16[2,128,768]{2,1,0:T(8,128)(2,1)S(1)}, u32[]{:S(2)}, u32[]{:S(2)}) %collective-permute-start.47) | collective-permute-done | bytes 393248 | tf_op jit(solution)/shard_map/ppermute | solution.py:908
  237.3 5.9 %collective-permute-done.38 = bf16[208,384]{1,0:T(8,128)(2,1)S(1)} collective-permute-done((bf16[208,384]{1,0:T(8,128)(2,1)S(1)}, bf16[208,384]{1,0:T(8,128)(2,1)S(1)}, u32[]{:S(2)}, u32[]{:S(2)}) %collective-permute-start.38) | collective-permute-done | bytes 159776 | tf_op jit(solution)/shard_map/ppermute | solution.py:913
  246.5 1.5 fusion.8
  (280 shorter events, 60.1 us)
Async XLA Ops:
  7.2 114.5 %all-gather.2.cloned.1.call-start = ((), (), s32[]{:S(2)}) async-start(), calls=%async_computation | async-start | bytes 3244032 | tf_op jit(solution)/shard_map/all_gather | solution.py:1113
  10.0 2.1 collective-permute-start
  10.5 2.1 collective-permute-start.1
  13.4 8.8 %collective-permute-start.7 = (bf16[1,144,768]{2,1,0:T(8,128)(2,1)}, bf16[1,144,768]{2,1,0:T(8,128)(2,1)S(1)}, u32[]{:S(2)}, u32[]{:S(2)}) collective-permute-start(bf16[1,144,768]{2,1,0:T(8,128)(2,1)} %bitcast.166), channel_id=1, source_target_pairs={{0,8},{4,12},{8,0},{12,4},{16,24},{20,28},{24,16},{28,20},{1,9},{5... | collective-permute-start | bytes 663560 | tf_op jit(solution)/shard_map/ppermute | solution.py:908
  16.3 1.6 collective-permute-start.3
  23.2 16.6 %collective-permute-start.8 = (bf16[2,144,768]{2,1,0:T(8,128)(2,1)S(1)}, bf16[2,144,768]{2,1,0:T(8,128)(2,1)S(1)}, u32[]{:S(2)}, u32[]{:S(2)}) collective-permute-start(bf16[2,144,768]{2,1,0:T(8,128)(2,1)S(1)} %pad_maximum_fusion.4), channel_id=1, source_target_pairs={{0,16},{4,20},{8,24},{12,28},{16,0},{20,4},{24,8},{28,12},{1,17},{... | collective-permute-start | bytes 1327112 | tf_op jit(solution)/shard_map/ppermute | solution.py:908
  25.2 12.4 %collective-permute-start.4 = (bf16[4,2,24,384]{3,2,1,0:T(8,128)(2,1)}, bf16[4,2,24,384]{3,2,1,0:T(8,128)(2,1)S(1)}, u32[]{:S(2)}, u32[]{:S(2)}) collective-permute-start(bf16[4,2,24,384]{3,2,1,0:T(8,128)(2,1)} %fill.2.refs_0_), channel_id=1, source_target_pairs={{0,1},{1,2},{2,3},{3,0},{4,5},{5,6},{6,7},{7,4},{8,9},{9,10},{10,1... | collective-permute-start | bytes 442376 | tf_op jit(solution)/shard_map/ppermute | solution.py:913
  26.8 13.0 %collective-permute-start.5 = (bf16[4,2,24,384]{3,2,1,0:T(8,128)(2,1)}, bf16[4,2,24,384]{3,2,1,0:T(8,128)(2,1)S(1)}, u32[]{:S(2)}, u32[]{:S(2)}) collective-permute-start(bf16[4,2,24,384]{3,2,1,0:T(8,128)(2,1)} %fill.2.refs_0_), channel_id=1, source_target_pairs={{0,2},{1,3},{2,0},{3,1},{4,6},{5,7},{6,4},{7,5},{8,10},{9,11},{10,... | collective-permute-start | bytes 442376 | tf_op jit(solution)/shard_map/ppermute | solution.py:913
  29.4 10.4 %collective-permute-start.6 = (bf16[4,2,24,384]{3,2,1,0:T(8,128)(2,1)}, bf16[4,2,24,384]{3,2,1,0:T(8,128)(2,1)S(1)}, u32[]{:S(2)}, u32[]{:S(2)}) collective-permute-start(bf16[4,2,24,384]{3,2,1,0:T(8,128)(2,1)} %fill.2.refs_0_), channel_id=1, source_target_pairs={{0,3},{1,0},{2,1},{3,2},{4,7},{5,4},{6,5},{7,6},{8,11},{9,8},{10,9... | collective-permute-start | bytes 442376 | tf_op jit(solution)/shard_map/ppermute | solution.py:913
  42.8 26.0 %collective-permute-start.9 = (bf16[4,192,384]{2,1,0:T(8,128)(2,1)}, bf16[4,192,384]{2,1,0:T(8,128)(2,1)S(1)}, u32[]{:S(2)}, u32[]{:S(2)}) collective-permute-start(bf16[4,192,384]{2,1,0:T(8,128)(2,1)} %bitcast.149), channel_id=1, source_target_pairs={{0,8},{4,12},{8,0},{12,4},{16,24},{20,28},{24,16},{28,20},{1,9},{5... | collective-permute-start | bytes 1769480 | tf_op jit(solution)/shard_map/ppermute | solution.py:908
  44.3 24.5 %collective-permute-start.10 = (bf16[4,192,384]{2,1,0:T(8,128)(2,1)}, bf16[4,192,384]{2,1,0:T(8,128)(2,1)S(1)}, u32[]{:S(2)}, u32[]{:S(2)}) collective-permute-start(bf16[4,192,384]{2,1,0:T(8,128)(2,1)} %bitcast.150), channel_id=1, source_target_pairs={{0,16},{4,20},{8,24},{12,28},{16,0},{20,4},{24,8},{28,12},{1,17},{... | collective-permute-start | bytes 1769480 | tf_op jit(solution)/shard_map/ppermute | solution.py:908
  45.2 11.7 %collective-permute-start.11 = (bf16[2,2,24,1024]{3,2,1,0:T(8,128)(2,1)S(1)}, bf16[2,2,24,1024]{3,2,1,0:T(8,128)(2,1)S(1)}, u32[]{:S(2)}, u32[]{:S(2)}) collective-permute-start(bf16[2,2,24,1024]{3,2,1,0:T(8,128)(2,1)S(1)} %copy-done.22), channel_id=1, source_target_pairs={{0,1},{1,2},{2,3},{3,0},{4,5},{5,6},{6,7},{7,4},{8,9},{9,10},{10,1... | collective-permute-start | bytes 589832 | tf_op jit(solution)/shard_map/ppermute | solution.py:913
  48.8 16.5 %collective-permute-start.12 = (bf16[2,2,24,1024]{3,2,1,0:T(8,128)(2,1)S(1)}, bf16[2,2,24,1024]{3,2,1,0:T(8,128)(2,1)S(1)}, u32[]{:S(2)}, u32[]{:S(2)}) collective-permute-start(bf16[2,2,24,1024]{3,2,1,0:T(8,128)(2,1)S(1)} %copy-done.22), channel_id=1, source_target_pairs={{0,2},{1,3},{2,0},{3,1},{4,6},{5,7},{6,4},{7,5},{8,10},{9,11},{10,... | collective-permute-start | bytes 589832 | tf_op jit(solution)/shard_map/ppermute | solution.py:913
  50.2 15.1 %collective-permute-start.13 = (bf16[2,2,24,1024]{3,2,1,0:T(8,128)(2,1)S(1)}, bf16[2,2,24,1024]{3,2,1,0:T(8,128)(2,1)S(1)}, u32[]{:S(2)}, u32[]{:S(2)}) collective-permute-start(bf16[2,2,24,1024]{3,2,1,0:T(8,128)(2,1)S(1)} %copy-done.22), channel_id=1, source_target_pairs={{0,3},{1,0},{2,1},{3,2},{4,7},{5,4},{6,5},{7,6},{8,11},{9,8},{10,9... | collective-permute-start | bytes 589832 | tf_op jit(solution)/shard_map/ppermute | solution.py:913
  70.4 3.0 %collective-permute-start.16 = (bf16[4,144,768]{2,1,0:T(8,128)(2,1)S(1)}, bf16[4,144,768]{2,1,0:T(8,128)(2,1)S(1)}, u32[]{:S(2)}, u32[]{:S(2)}) collective-permute-start(bf16[4,144,768]{2,1,0:T(8,128)(2,1)S(1)} %pad_maximum_fusion.near_ref), channel_id=1, source_target_pairs={{0,4},{4,0},{8,12},{12,8},{16,20},{20,16},{24,28},{28,24},{1,5},{5... | collective-permute-start | bytes 2654216 | tf_op jit(solution)/shard_map/ppermute | solution.py:903
  70.4 14.3 %collective-permute-start.14 = (bf16[2,192,384]{2,1,0:T(8,128)(2,1)}, bf16[2,192,384]{2,1,0:T(8,128)(2,1)S(1)}, u32[]{:S(2)}, u32[]{:S(2)}) collective-permute-start(bf16[2,192,384]{2,1,0:T(8,128)(2,1)} %slice.126), channel_id=1, source_target_pairs={{0,16},{4,20},{8,24},{12,28},{16,0},{20,4},{24,8},{28,12},{1,17},{... | collective-permute-start | bytes 884744 | tf_op jit(solution)/shard_map/ppermute | solution.py:908
  71.9 12.8 %collective-permute-start.15 = (bf16[2,192,384]{2,1,0:T(8,128)(2,1)}, bf16[2,192,384]{2,1,0:T(8,128)(2,1)S(1)}, u32[]{:S(2)}, u32[]{:S(2)}) collective-permute-start(bf16[2,192,384]{2,1,0:T(8,128)(2,1)} %slice.127), channel_id=1, source_target_pairs={{0,8},{4,12},{8,0},{12,4},{16,24},{20,28},{24,16},{28,20},{1,9},{5... | collective-permute-start | bytes 884744 | tf_op jit(solution)/shard_map/ppermute | solution.py:908
  86.0 17.2 %collective-permute-start.17 = (bf16[4,192,384]{2,1,0:T(8,128)(2,1)S(1)}, bf16[4,192,384]{2,1,0:T(8,128)(2,1)}, u32[]{:S(2)}, u32[]{:S(2)}) collective-permute-start(bf16[4,192,384]{2,1,0:T(8,128)(2,1)S(1)} %pad_maximum_fusion.3.near_ref), channel_id=1, source_target_pairs={{0,4},{4,0},{8,12},{12,8},{16,20},{20,16},{24,28},{28,24},{1,5},{5... | collective-permute-start | bytes 1769480 | tf_op jit(solution)/shard_map/ppermute | solution.py:903
  86.1 21.6 %collective-permute-start.19 = (bf16[2,192,1024]{2,1,0:T(8,128)(2,1)S(1)}, bf16[2,192,1024]{2,1,0:T(8,128)(2,1)S(1)}, u32[]{:S(2)}, u32[]{:S(2)}) collective-permute-start(bf16[2,192,1024]{2,1,0:T(8,128)(2,1)S(1)} %bitcast.158), channel_id=1, source_target_pairs={{0,8},{4,12},{8,0},{12,4},{16,24},{20,28},{24,16},{28,20},{1,9},{5... | collective-permute-start | bytes 2359304 | tf_op jit(solution)/shard_map/ppermute | solution.py:908
  87.6 20.1 %collective-permute-start.20 = (bf16[2,192,1024]{2,1,0:T(8,128)(2,1)S(1)}, bf16[2,192,1024]{2,1,0:T(8,128)(2,1)}, u32[]{:S(2)}, u32[]{:S(2)}) collective-permute-start(bf16[2,192,1024]{2,1,0:T(8,128)(2,1)S(1)} %bitcast.159), channel_id=1, source_target_pairs={{0,16},{4,20},{8,24},{12,28},{16,0},{20,4},{24,8},{28,12},{1,17},{... | collective-permute-start | bytes 2359304 | tf_op jit(solution)/shard_map/ppermute | solution.py:908
  107.0 14.7 %collective-permute-start.18 = (f32[256,768]{1,0:T(8,128)}, f32[256,768]{1,0:T(8,128)}, u32[]{:S(2)}, u32[]{:S(2)}) collective-permute-start(f32[256,768]{1,0:T(8,128)} %get-tuple-element.165.part_ref), channel_id=1, source_target_pairs={{0,4},{4,0},{8,12},{12,8},{16,20},{20,16},{24,28},{28,24},{1,5},{5... | collective-permute-start | bytes 2359304 | tf_op jit(solution)/shard_map/ppermute | solution.py:903
  107.8 11.6 %collective-permute-start.21 = (bf16[1,192,1024]{2,1,0:T(8,128)(2,1)S(1)}, bf16[1,192,1024]{2,1,0:T(8,128)(2,1)S(1)}, u32[]{:S(2)}, u32[]{:S(2)}) collective-permute-start(bf16[1,192,1024]{2,1,0:T(8,128)(2,1)S(1)} %slice.133), channel_id=1, source_target_pairs={{0,16},{4,20},{8,24},{12,28},{16,0},{20,4},{24,8},{28,12},{1,17},{... | collective-permute-start | bytes 1179656 | tf_op jit(solution)/shard_map/ppermute | solution.py:908
  110.3 11.4 %collective-permute-start.22 = (bf16[1,192,1024]{2,1,0:T(8,128)(2,1)S(1)}, bf16[1,192,1024]{2,1,0:T(8,128)(2,1)}, u32[]{:S(2)}, u32[]{:S(2)}) collective-permute-start(bf16[1,192,1024]{2,1,0:T(8,128)(2,1)S(1)} %slice.134), channel_id=1, source_target_pairs={{0,8},{4,12},{8,0},{12,4},{16,24},{20,28},{24,16},{28,20},{1,9},{5... | collective-permute-start | bytes 1179656 | tf_op jit(solution)/shard_map/ppermute | solution.py:908
  135.4 3.5 %collective-permute-start.25 = (f32[256,768]{1,0:T(8,128)}, f32[256,768]{1,0:T(8,128)S(1)}, u32[]{:S(2)}, u32[]{:S(2)}) collective-permute-start(f32[256,768]{1,0:T(8,128)} %get-tuple-element.175.back_ref), channel_id=1, source_target_pairs={{0,4},{4,0},{8,12},{12,8},{16,20},{20,16},{24,28},{28,24},{1,5},{5... | collective-permute-start | bytes 2359304 | tf_op jit(solution)/shard_map/ppermute | solution.py:903
  135.5 11.7 %collective-permute-start.23 = (bf16[1,192,1024]{2,1,0:T(8,128)(2,1)}, bf16[1,192,1024]{2,1,0:T(8,128)(2,1)S(1)}, u32[]{:S(2)}, u32[]{:S(2)}) collective-permute-start(bf16[1,192,1024]{2,1,0:T(8,128)(2,1)} %get-tuple-element.172), channel_id=1, source_target_pairs={{0,8},{4,12},{8,0},{12,4},{16,24},{20,28},{24,16},{28,20},{1,9},{5... | collective-permute-start | bytes 1179656 | tf_op jit(solution)/shard_map/ppermute | solution.py:908
  136.1 11.4 %collective-permute-start.24 = (bf16[1,192,1024]{2,1,0:T(8,128)(2,1)}, bf16[1,192,1024]{2,1,0:T(8,128)(2,1)S(1)}, u32[]{:S(2)}, u32[]{:S(2)}) collective-permute-start(bf16[1,192,1024]{2,1,0:T(8,128)(2,1)} %get-tuple-element.173), channel_id=1, source_target_pairs={{0,16},{4,20},{8,24},{12,28},{16,0},{20,4},{24,8},{28,12},{1,17},{... | collective-permute-start | bytes 1179656 | tf_op jit(solution)/shard_map/ppermute | solution.py:908
  137.4 12.9 %collective-permute-start.26 = (bf16[4,64,768]{2,1,0:T(8,128)(2,1)}, bf16[4,64,768]{2,1,0:T(8,128)(2,1)S(1)}, u32[]{:S(2)}, u32[]{:S(2)}) collective-permute-start(bf16[4,64,768]{2,1,0:T(8,128)(2,1)} %get-tuple-element.179), channel_id=1, source_target_pairs={{0,1},{1,2},{2,3},{3,0},{4,5},{5,6},{6,7},{7,4},{8,9},{9,10},{10,1... | collective-permute-start | bytes 1179656 | tf_op jit(solution)/shard_map/ppermute | solution.py:913
  150.3 3.3 %collective-permute-start.27 = (bf16[2,96,768]{2,1,0:T(8,128)(2,1)}, bf16[2,96,768]{2,1,0:T(8,128)(2,1)S(1)}, u32[]{:S(2)}, u32[]{:S(2)}) collective-permute-start(bf16[2,96,768]{2,1,0:T(8,128)(2,1)} %get-tuple-element.186), channel_id=1, source_target_pairs={{0,4},{4,0},{8,12},{12,8},{16,20},{20,16},{24,28},{28,24},{1,5},{5... | collective-permute-start | bytes 884744 | tf_op jit(solution)/shard_map/ppermute | solution.py:903
  154.3 15.4 %collective-permute-start.28 = (bf16[4,64,768]{2,1,0:T(8,128)(2,1)S(1)}, bf16[4,64,768]{2,1,0:T(8,128)(2,1)S(1)}, u32[]{:S(2)}, u32[]{:S(2)}) collective-permute-start(bf16[4,64,768]{2,1,0:T(8,128)(2,1)S(1)} %add_convert_fusion.5), channel_id=1, source_target_pairs={{0,1},{1,2},{2,3},{3,0},{4,5},{5,6},{6,7},{7,4},{8,9},{9,10},{10,1... | collective-permute-start | bytes 1179656 | tf_op jit(solution)/shard_map/ppermute | solution.py:913
  154.3 27.0 %collective-permute-start.29 = (bf16[2,192,1024]{2,1,0:T(8,128)(2,1)}, bf16[2,192,1024]{2,1,0:T(8,128)(2,1)S(1)}, u32[]{:S(2)}, u32[]{:S(2)}) collective-permute-start(bf16[2,192,1024]{2,1,0:T(8,128)(2,1)} %get-tuple-element.209), channel_id=1, source_target_pairs={{0,8},{4,12},{8,0},{12,4},{16,24},{20,28},{24,16},{28,20},{1,9},{5... | collective-permute-start | bytes 2359304 | tf_op jit(solution)/shard_map/ppermute | solution.py:908
  155.2 26.2 %collective-permute-start.30 = (bf16[2,192,1024]{2,1,0:T(8,128)(2,1)}, bf16[2,192,1024]{2,1,0:T(8,128)(2,1)}, u32[]{:S(2)}, u32[]{:S(2)}) collective-permute-start(bf16[2,192,1024]{2,1,0:T(8,128)(2,1)} %get-tuple-element.210), channel_id=1, source_target_pairs={{0,16},{4,20},{8,24},{12,28},{16,0},{20,4},{24,8},{28,12},{1,17},{... | collective-permute-start | bytes 2359304 | tf_op jit(solution)/shard_map/ppermute | solution.py:908
  170.5 13.1 %collective-permute-start.33 = (bf16[4,64,768]{2,1,0:T(8,128)(2,1)}, bf16[4,64,768]{2,1,0:T(8,128)(2,1)}, u32[]{:S(2)}, u32[]{:S(2)}) collective-permute-start(bf16[4,64,768]{2,1,0:T(8,128)(2,1)} %add_convert_fusion.4), channel_id=1, source_target_pairs={{0,1},{1,2},{2,3},{3,0},{4,5},{5,6},{6,7},{7,4},{8,9},{9,10},{10,1... | collective-permute-start | bytes 1179656 | tf_op jit(solution)/shard_map/ppermute | solution.py:913
  181.3 14.8 %collective-permute-start.31 = (bf16[384,384]{1,0:T(8,128)(2,1)}, bf16[384,384]{1,0:T(8,128)(2,1)}, u32[]{:S(2)}, u32[]{:S(2)}) collective-permute-start(bf16[384,384]{1,0:T(8,128)(2,1)} %get-tuple-element.214), channel_id=1, source_target_pairs={{0,8},{4,12},{8,0},{12,4},{16,24},{20,28},{24,16},{28,20},{1,9},{5... | collective-permute-start | bytes 884744 | tf_op jit(solution)/shard_map/ppermute | solution.py:908
  182.3 13.9 %collective-permute-start.32 = (bf16[400,384]{1,0:T(8,128)(2,1)}, bf16[400,384]{1,0:T(8,128)(2,1)}, u32[]{:S(2)}, u32[]{:S(2)}) collective-permute-start(bf16[400,384]{1,0:T(8,128)(2,1)} %get-tuple-element.215), channel_id=1, source_target_pairs={{0,16},{4,20},{8,24},{12,28},{16,0},{20,4},{24,8},{28,12},{1,17},{... | collective-permute-start | bytes 921608 | tf_op jit(solution)/shard_map/ppermute | solution.py:908
  184.7 10.8 %collective-permute-start.34 = (bf16[2,64,768]{2,1,0:T(8,128)(2,1)S(1)}, bf16[2,64,768]{2,1,0:T(8,128)(2,1)S(1)}, u32[]{:S(2)}, u32[]{:S(2)}) collective-permute-start(bf16[2,64,768]{2,1,0:T(8,128)(2,1)S(1)} %slice.162), channel_id=1, source_target_pairs={{0,8},{4,12},{8,0},{12,4},{16,24},{20,28},{24,16},{28,20},{1,9},{5... | collective-permute-start | bytes 589832 | tf_op jit(solution)/shard_map/ppermute | solution.py:908
  194.0 7.8 %collective-permute-start.40 = (bf16[2,2,24,1024]{3,2,1,0:T(8,128)(2,1)}, bf16[2,2,24,1024]{3,2,1,0:T(8,128)(2,1)}, u32[]{:S(2)}, u32[]{:S(2)}) collective-permute-start(bf16[2,2,24,1024]{3,2,1,0:T(8,128)(2,1)} %dynamic-slice_bitcast_fusion), channel_id=1, source_target_pairs={{0,1},{1,2},{2,3},{3,0},{4,5},{5,6},{6,7},{7,4},{8,9},{9,10},{10,1... | collective-permute-start | bytes 589832 | tf_op jit(solution)/shard_map/ppermute | solution.py:913
  195.5 16.0 %collective-permute-start.45 = (f32[128,768]{1,0:T(8,128)}, f32[128,768]{1,0:T(8,128)}, u32[]{:S(2)}, u32[]{:S(2)}) collective-permute-start(f32[128,768]{1,0:T(8,128)} %constant_dynamic-slice_fusion), channel_id=1, source_target_pairs={{0,4},{4,0},{8,12},{12,8},{16,20},{20,16},{24,28},{28,24},{1,5},{5... | collective-permute-start | bytes 1179656 | tf_op jit(solution)/shard_map/ppermute | solution.py:903
  195.6 23.6 %collective-permute-start.46 = (bf16[4,128,768]{2,1,0:T(8,128)(2,1)}, bf16[4,128,768]{2,1,0:T(8,128)(2,1)}, u32[]{:S(2)}, u32[]{:S(2)}) collective-permute-start(bf16[4,128,768]{2,1,0:T(8,128)(2,1)} %get-tuple-element.238), channel_id=1, source_target_pairs={{0,4},{4,0},{8,12},{12,8},{16,20},{20,16},{24,28},{28,24},{1,5},{5... | collective-permute-start | bytes 2359304 | tf_op jit(solution)/shard_map/ppermute | solution.py:903
  199.2 22.7 %collective-permute-start.35 = (bf16[784,384]{1,0:T(8,128)(2,1)}, bf16[784,384]{1,0:T(8,128)(2,1)S(1)}, u32[]{:S(2)}, u32[]{:S(2)}) collective-permute-start(bf16[784,384]{1,0:T(8,128)(2,1)} %get-tuple-element.223), channel_id=1, source_target_pairs={{0,8},{4,12},{8,0},{12,4},{16,24},{20,28},{24,16},{28,20},{1,9},{5... | collective-permute-start | bytes 1806344 | tf_op jit(solution)/shard_map/ppermute | solution.py:908
  200.1 21.7 %collective-permute-start.36 = (bf16[784,384]{1,0:T(8,128)(2,1)}, bf16[784,384]{1,0:T(8,128)(2,1)}, u32[]{:S(2)}, u32[]{:S(2)}) collective-permute-start(bf16[784,384]{1,0:T(8,128)(2,1)} %get-tuple-element.224), channel_id=1, source_target_pairs={{0,16},{4,20},{8,24},{12,28},{16,0},{20,4},{24,8},{28,12},{1,17},{... | collective-permute-start | bytes 1806344 | tf_op jit(solution)/shard_map/ppermute | solution.py:908
  202.8 7.5 %collective-permute-start.41 = (bf16[2,2,24,1024]{3,2,1,0:T(8,128)(2,1)S(1)}, bf16[2,2,24,1024]{3,2,1,0:T(8,128)(2,1)S(1)}, u32[]{:S(2)}, u32[]{:S(2)}) collective-permute-start(bf16[2,2,24,1024]{3,2,1,0:T(8,128)(2,1)S(1)} %fusion.1), channel_id=1, source_target_pairs={{0,1},{1,2},{2,3},{3,0},{4,5},{5,6},{6,7},{7,4},{8,9},{9,10},{10,1... | collective-permute-start | bytes 589832 | tf_op jit(solution)/shard_map/ppermute | solution.py:913
  210.3 22.0 %collective-permute-start.44 = (bf16[1,64,768]{2,1,0:T(8,128)(2,1)}, bf16[1,64,768]{2,1,0:T(8,128)(2,1)}, u32[]{:S(2)}, u32[]{:S(2)}) collective-permute-start(bf16[1,64,768]{2,1,0:T(8,128)(2,1)} %get-tuple-element.279), channel_id=1, source_target_pairs={{0,16},{4,20},{8,24},{12,28},{16,0},{20,4},{24,8},{28,12},{1,17},{... | collective-permute-start | bytes 294920 | tf_op jit(solution)/shard_map/ppermute | solution.py:908
  211.5 7.5 %collective-permute-start.42 = (bf16[2,2,24,1024]{3,2,1,0:T(8,128)(2,1)S(1)}, bf16[2,2,24,1024]{3,2,1,0:T(8,128)(2,1)S(1)}, u32[]{:S(2)}, u32[]{:S(2)}) collective-permute-start(bf16[2,2,24,1024]{3,2,1,0:T(8,128)(2,1)S(1)} %fusion), channel_id=1, source_target_pairs={{0,1},{1,2},{2,3},{3,0},{4,5},{5,6},{6,7},{7,4},{8,9},{9,10},{10,1... | collective-permute-start | bytes 589832 | tf_op jit(solution)/shard_map/ppermute | solution.py:913
  225.4 11.5 %collective-permute-start.47 = (bf16[2,128,768]{2,1,0:T(8,128)(2,1)S(1)}, bf16[2,128,768]{2,1,0:T(8,128)(2,1)S(1)}, u32[]{:S(2)}, u32[]{:S(2)}) collective-permute-start(bf16[2,128,768]{2,1,0:T(8,128)(2,1)S(1)} %slice.143), channel_id=1, source_target_pairs={{0,8},{4,12},{8,0},{12,4},{16,24},{20,28},{24,16},{28,20},{1,9},{5... | collective-permute-start | bytes 1179656 | tf_op jit(solution)/shard_map/ppermute | solution.py:908
  228.4 8.9 %collective-permute-start.37 = (bf16[208,384]{1,0:T(8,128)(2,1)S(1)}, bf16[208,384]{1,0:T(8,128)(2,1)S(1)}, u32[]{:S(2)}, u32[]{:S(2)}) collective-permute-start(bf16[208,384]{1,0:T(8,128)(2,1)S(1)} %copy-done.64), channel_id=1, source_target_pairs={{0,1},{1,2},{2,3},{3,0},{4,5},{5,6},{6,7},{7,4},{8,9},{9,10},{10,1... | collective-permute-start | bytes 479240 | tf_op jit(solution)/shard_map/ppermute | solution.py:913
  228.5 14.8 %collective-permute-start.38 = (bf16[208,384]{1,0:T(8,128)(2,1)S(1)}, bf16[208,384]{1,0:T(8,128)(2,1)S(1)}, u32[]{:S(2)}, u32[]{:S(2)}) collective-permute-start(bf16[208,384]{1,0:T(8,128)(2,1)S(1)} %copy-done.63), channel_id=1, source_target_pairs={{0,2},{1,3},{2,0},{3,1},{4,6},{5,7},{6,4},{7,5},{8,10},{9,11},{10,... | collective-permute-start | bytes 479240 | tf_op jit(solution)/shard_map/ppermute | solution.py:913
  228.5 14.7 %collective-permute-start.39 = (bf16[208,384]{1,0:T(8,128)(2,1)S(1)}, bf16[208,384]{1,0:T(8,128)(2,1)S(1)}, u32[]{:S(2)}, u32[]{:S(2)}) collective-permute-start(bf16[208,384]{1,0:T(8,128)(2,1)S(1)} %copy-done.62), channel_id=1, source_target_pairs={{0,3},{1,0},{2,1},{3,2},{4,7},{5,4},{6,5},{7,6},{8,11},{9,8},{10,9... | collective-permute-start | bytes 479240 | tf_op jit(solution)/shard_map/ppermute | solution.py:913
  243.4 6.7 %collective-permute-start.48 = (bf16[1,128,768]{2,1,0:T(8,128)(2,1)S(1)}, bf16[1,128,768]{2,1,0:T(8,128)(2,1)S(1)}, u32[]{:S(2)}, u32[]{:S(2)}) collective-permute-start(bf16[1,128,768]{2,1,0:T(8,128)(2,1)S(1)} %slice.166), channel_id=1, source_target_pairs={{0,16},{4,20},{8,24},{12,28},{16,0},{20,4},{24,8},{28,12},{1,17},{... | collective-permute-start | bytes 589832 | tf_op jit(solution)/shard_map/ppermute | solution.py:908
  (68 other events, 426.0 us)
Sparse Core Ops, SparseCore 0:
  11.5 78.2 all-gather.1

commit v3 on v2

--- a/solution.py
+++ b/solution.py
@@ -106,8 +106,7 @@
 
 
 def ready_kernel(meta_ref, attn_ref, ffin_ref, ffout_ref, tokens_ref, ids_ref, gain_ref, *outs):
-    attn_out, attn_send, gu_out, gu_send, row_out, down_out = outs
-    down_out[...] = ffout_ref[...].astype(bf16)
+    attn_out, attn_send, gu_out, gu_send, row_out = outs
     core = meta_ref[0]
     first = core == 0
     width = tokens_ref.shape[1]
@@ -131,7 +130,8 @@
     row_out[:tok, :] = (tokens * rms_scale(tokens) * gain_ref[0:1, :]).astype(bf16)
     ids = jnp.broadcast_to(ids_ref[...].astype(f32), (16, tok))
     ids = jnp.concatenate([ids, jnp.zeros((16, width - tok), f32)], axis=1)
-    row_out[tok:, :] = ids.astype(bf16)
+    row_out[tok : tok + 16, :] = ids.astype(bf16)
+    row_out[tok + 16 :, :] = ffout_ref[...].astype(bf16)
 
 
 def make_ready(core, attention_weight, ffin_weight, ffout_weight, tokens, ids, gain, chips):
@@ -140,14 +140,13 @@
     return pl.pallas_call(
         ready_kernel,
         in_specs=[smem_spec()] + [whole_spec()] * 6,
-        out_specs=[whole_spec()] * 6,
+        out_specs=[whole_spec()] * 5,
         out_shape=[
             shaped(bf16, 4, 2, rows, half),
             shaped(bf16, 3, rows, half),
             shaped(bf16, 2, 2, rows, hidden // 2),
             shaped(bf16, 2, rows, hidden // 2),
-            shaped(bf16, tok + 16, width),
-            shaped(bf16, *ffout_weight.shape),
+            shaped(bf16, tok + 16 + ffout_weight.shape[0], width),
         ],
         compiler_params=params(),
         cost_estimate=cost(1e6, 2e6),
@@ -257,11 +256,10 @@
     return pl.ds(pl.multiple_of(kind * lanes, lanes), lanes)
 
 
-def attend_kernel(plan, meta_ref, rows_ref, mask_ref, bias_ref, *refs):
-    count = plan[-1][0] + 1
+def attend_kernel(count, meta_ref, rows_ref, mask_ref, bias_ref, *refs):
     pieces = refs[:count]
-    q_ref, k_ref, v_ref, p_ref, o_ref = refs[count : count + 5]
-    weight, score, soft, sem = refs[count + 5 :]
+    q_ref, k_ref, v_ref, p_ref, o_ref, low_ref = refs[count : count + 6]
+    weight, score, soft, sem = refs[count + 6 :]
     pair = pl.program_id(0)
     chip = meta_ref[0]
     length = rows_ref.shape[0]
@@ -270,14 +268,7 @@
 
     @pl.when(pair == 0)
     def _():
-        pairs = []
-        for index, lead, target, size, slot in plan:
-            size = min(size, 3 - target)
-            place = row_block(meta_ref, slot, pieces[index].shape[1])
-            pairs.append(
-                (pieces[index].at[lead : lead + size], weight.at[target : target + size, place, :])
-            )
-        wait_all(run_copies(pairs, sem))
+        wait_all(run_copies(load_pairs(pieces, meta_ref, 0, weight), sem))
 
     cols = pl.ds(pl.multiple_of(pair * lanes, lanes), lanes)
     own = rows_ref[pl.ds(pl.multiple_of(chip * group, group), group), :]
@@ -313,10 +304,12 @@
             soft[rows, :] = now.astype(bf16)
         features = lanes // 2
         turned.append(mm_tn(value, soft[...])[half * features : (half + 1) * features])
-    o_ref[...] = jnp.concatenate(turned, axis=0).T
-
-
-def attend(plan, pieces, meta, rows, mask, bias):
+    attended = jnp.concatenate(turned, axis=0).T
+    o_ref[...] = attended
+    low_ref[...] = attended.astype(bf16)
+
+
+def attend(pieces, meta, rows, mask, bias):
     length, width = rows.shape
     half = width // 2
     group = 2 * lanes
@@ -325,7 +318,7 @@
     fixed = lambda i, *_: (0, 0)
     flops = 2 * (group * width * half + 2 * length * width * half + 4 * group * length * half)
     return pl.pallas_call(
-        functools.partial(attend_kernel, plan),
+        functools.partial(attend_kernel, len(pieces)),
         grid_spec=pltpu.PrefetchScalarGridSpec(
             num_scalar_prefetch=1,
             grid=(pairs,),
@@ -341,12 +334,13 @@
                 pl.BlockSpec((length, lanes), col),
                 pl.BlockSpec((2, length, group), lambda i, *_: (i, 0, 0)),
                 pl.BlockSpec((group, lanes), col),
+                pl.BlockSpec((group, lanes), col),
             ],
             scratch_shapes=[
                 pltpu.VMEM((3, width, half), bf16),
                 pltpu.VMEM((length, group), f32),
                 pltpu.VMEM((length, group), bf16),
-                dma(len(plan)),
+                dma(len(pieces)),
             ],
         ),
         out_shape=[
@@ -355,6 +349,7 @@
             shaped(bf16, length, half),
             shaped(f32, 2 * pairs, length, group),
             shaped(f32, group, half),
+            shaped(bf16, group, half),
         ],
         compiler_params=params(),
         cost_estimate=cost(flops, 30e6, 2 * group * length * pairs),
@@ -362,7 +357,9 @@
     )(meta, rows, mask, bias, *pieces)
 
 
-def mix_kernel(meta_ref, attended_ref, near_ref, far_ref, part_ref, weight_ref, sem):
+def mix_kernel(
+    meta_ref, tokens_ref, own_ref, their_ref, gain_ref, near_ref, far_ref, mixed_ref, normed_ref, joined_ref, weight_ref, sem
+):
     chips, rows, half = near_ref.shape
     rows = rows // 2
     pairs = []
@@ -376,76 +373,99 @@
                         weight_ref.at[place, side * half : (side + 1) * half],
                     )
                 )
-    wait_all(run_copies(pairs, sem))
-    core = meta_ref[0]
-    mine = weight_ref[pl.ds(pl.multiple_of(core * half, half), half), :]
-    part_ref[...] = mm(attended_ref[...].astype(bf16), mine)
-
-
-def mix(meta, attended, near, far):
-    group, half = attended.shape
+    copies = run_copies(pairs, sem)
+    first = meta_ref[0] == 0
+    joined_ref[:, :half] = jnp.where(first, own_ref[...], their_ref[...])
+    joined_ref[:, half:] = jnp.where(first, their_ref[...], own_ref[...])
+    wait_all(copies)
+    mixed = tokens_ref[...] + mm(joined_ref[...], weight_ref[...])
+    mixed_ref[...] = mixed
+    normed_ref[...] = (mixed * rms_scale(mixed) * gain_ref[...]).astype(bf16)
+
+
+def mix(meta, tokens, own, their, gain, near, far):
+    group, half = own.shape
     width = 2 * half
     return pl.pallas_call(
         mix_kernel,
-        in_specs=[smem_spec(), whole_spec(), any_spec(), any_spec()],
-        out_specs=[whole_spec()] * 2,
-        out_shape=[shaped(f32, group, width), shaped(bf16, width, width)],
+        in_specs=[smem_spec()] + [whole_spec()] * 4 + [any_spec()] * 2,
+        out_specs=[whole_spec()] * 4,
+        out_shape=[
+            shaped(f32, group, width),
+            shaped(bf16, group, width),
+            shaped(bf16, group, width),
+            shaped(bf16, width, width),
+        ],
         scratch_shapes=[dma(4 * near.shape[0])],
         compiler_params=params(),
-        cost_estimate=cost(2 * group * width * half, 4e6),
+        cost_estimate=cost(4 * group * width * half, 4e6),
         name="mix",
-    )(meta, attended, near, far)
+    )(meta, tokens, own, their, gain, near, far)
 
 
 def feed_kernel(
-    gu_plan,
     chips,
+    places,
     gu_count,
-    places,
     meta_ref,
-    tokens_ref,
+    normed_low,
     cot_ref,
-    part_ref,
-    arrived_ref,
-    gain_ref,
     *refs,
 ):
     refs = list(refs)
     take = lambda n: [refs.pop(0) for _ in range(n)]
-    gu_pieces = take(gu_plan[-1][0] + 1)
-    (down_full,) = take(1)
-    mixed_ref, out_ref, back_ref = take(3)
-    gu_outs, down_outs = take(gu_count), take(places)
-    gu, down, grad_gu, grad_down, cot_low, normed_low = take(6)
+    gu_pieces = take(gu_count)
+    down_pieces = take(places)
+    out_ref, back_ref = take(2)
+    gu_outs, down_outs = take(chips), take(2)
+    gu, down, grad_gu, grad_down, cot_low = take(5)
     gu_sem, down_sem, gu_out_sem, down_out_sem = take(4)
     step = pl.program_id(0)
     steps = pl.num_programs(0)
     block = 256
 
+    count = gu.shape[2] // block
+
+    def gu_loads(turn):
+        columns = pl.ds(pl.multiple_of(turn * block, block), block)
+        pairs = []
+        for index, piece in enumerate(gu_pieces):
+            place = row_block(meta_ref, min(index, chips - 1), piece.shape[1])
+            lead = slice(0, 2) if piece.shape[0] == 2 else slice(index - 3, index - 2)
+            pairs.append((piece.at[:, :, columns], gu.at[lead, place, columns]))
+        return [
+            pltpu.make_async_copy(a, b, gu_sem.at[turn, index]) for index, (a, b) in enumerate(pairs)
+        ]
+
+    def gu_stores(turn):
+        columns = pl.ds(pl.multiple_of(turn * block, block), block)
+        copies = []
+        for chip, out in enumerate(gu_outs):
+            source = grad_gu.at[:, row_block(meta_ref, chip, out.shape[1]), columns]
+            copies.append(pltpu.make_async_copy(source, out.at[:, :, columns], gu_out_sem.at[turn, chip]))
+        return copies
+
     @pl.when(step == 0)
     def _():
+        for copy in gu_loads(0):
+            copy.start()
         pairs = []
-        for index, lead, target, size, slot in gu_plan:
-            place = row_block(meta_ref, slot, gu_pieces[index].shape[1])
-            pairs.append(
-                (gu_pieces[index].at[lead : lead + size], gu.at[target : target + size, place, :])
-            )
-        gu_copies = run_copies(pairs, gu_sem)
-        pairs = []
-        grain = down.shape[0] // chips
-        for index in range(chips):
-            source = down_full.at[row_block(meta_ref, chips + index, grain), :]
-            pairs.append((source, down.at[index * grain : (index + 1) * grain, :]))
+        slot = chips
+        for piece in down_pieces:
+            for chip in range(chips):
+                pairs.append((piece.at[chip], down.at[row_block(meta_ref, slot, piece.shape[1]), :]))
+                slot += 1
         down_copies = run_copies(pairs, down_sem)
-        mixed = tokens_ref[...] + part_ref[...] + arrived_ref[...]
-        mixed_ref[...] = mixed
-        normed_low[...] = (mixed * rms_scale(mixed) * gain_ref[...]).astype(bf16)
+        for turn in range(1, count):
+            for copy in gu_loads(turn):
+                copy.start()
         cot_low[...] = cot_ref[...].astype(bf16)
         out_ref[...] = jnp.zeros_like(out_ref)
         back_ref[...] = jnp.zeros_like(back_ref)
-        wait_all(gu_copies)
         wait_all(down_copies)
 
+    for copy in gu_loads(step):
+        copy.wait()
     cols = pl.ds(pl.multiple_of(step * block, block), block)
     normed = normed_low[...]
     cot = cot_low[...]
@@ -466,68 +486,59 @@
     grad_gu[0, :, cols] = mm_tn(normed, dgate).astype(bf16)
     grad_gu[1, :, cols] = mm_tn(normed, dup).astype(bf16)
 
+    for copy in gu_stores(step):
+        copy.start()
+
     @pl.when(step == steps - 1)
     def _():
         pairs = []
-        for out, (lead, step) in zip(gu_outs, cut_plan(chips, 2)):
-            place = row_block(meta_ref, step, out.shape[1])
-            pairs.append((grad_gu.at[lead : lead + out.shape[0], place, :], out))
-        gu_copies = run_copies(pairs, gu_out_sem)
-        pairs = []
         for turn, out in enumerate(down_outs):
-            for spot, step in enumerate(bit_reversed(chips)):
-                place = row_block(meta_ref, 2 * chips + turn * chips + step, out.shape[1])
-                pairs.append((grad_down.at[place, :], out.at[spot]))
+            for spot in range(places // 2):
+                for chip in range(chips):
+                    slot = chips * (1 + places + turn * (places // 2) + spot) + chip
+                    place = row_block(meta_ref, slot, out.shape[2])
+                    pairs.append((grad_down.at[place, :], out.at[spot, chip]))
         down_copies = run_copies(pairs, down_out_sem)
-        wait_all(gu_copies)
+        for turn in range(count):
+            wait_all(gu_stores(turn))
         wait_all(down_copies)
 
 
-def cut_plan(chips, size):
-    if chips != 4:
-        return [(0, step) for step in range(chips)]
-    return [(0, 0), (0, 1), (0, 2), (0, 3), (size // 2, 3)]
-
-
-def feed(gu_plan, gu_pieces, down_full, meta, tokens, cot, part, arrived, gain, chips, places):
-    group, width = tokens.shape
+def feed(gu_pieces, down_pieces, meta, normed, cot, chips, places):
+    group, width = normed.shape
     hidden = gu_pieces[0].shape[2]
     block = 256
     fixed = lambda i, *_: (0, 0)
     full = lambda *shape: pl.BlockSpec(shape, fixed)
     flops = 2 * 9 * group * width * hidden
-    plan = cut_plan(chips, 2)
-    size = [1 if chips == 4 and step == 3 else 2 for _, step in plan]
     results = pl.pallas_call(
-        functools.partial(feed_kernel, gu_plan, chips, len(plan), places),
+        functools.partial(feed_kernel, chips, places, len(gu_pieces)),
         grid_spec=pltpu.PrefetchScalarGridSpec(
             num_scalar_prefetch=1,
             grid=(hidden // block,),
-            in_specs=[full(group, width)] * 4
-            + [full(1, width)]
-            + [any_spec()] * (len(gu_pieces) + 1),
-            out_specs=[full(group, width)] * 3 + [any_spec()] * (len(plan) + places),
+            in_specs=[full(group, width)] * 2
+            + [any_spec()] * (len(gu_pieces) + places),
+            out_specs=[full(group, width)] * 2 + [any_spec()] * (chips + 2),
             scratch_shapes=[
                 pltpu.VMEM((2, width, hidden), bf16),
                 pltpu.VMEM((hidden, width), bf16),
                 pltpu.VMEM((2, width, hidden), bf16),
                 pltpu.VMEM((hidden, width), bf16),
                 pltpu.VMEM((group, width), bf16),
-                pltpu.VMEM((group, width), bf16),
-                dma(len(gu_plan)),
-                dma(chips),
-                dma(len(plan)),
+                pltpu.SemaphoreType.DMA((hidden // block, len(gu_pieces))),
+                dma(chips * places),
+                pltpu.SemaphoreType.DMA((hidden // block, chips)),
                 dma(chips * places),
             ],
         ),
-        out_shape=[shaped(f32, group, width)] * 3
-        + [shaped(bf16, lead, width // chips, hidden) for lead in size]
-        + [shaped(bf16, chips, hidden // (chips * places), width)] * places,
+        out_shape=[shaped(f32, group, width)] * 2
+        + [shaped(bf16, 2, width // chips, hidden)] * chips
+        + [shaped(bf16, places // 2, chips, hidden // (chips * places), width)] * 2,
         compiler_params=params(),
         cost_estimate=cost(flops, 25e6, group * hidden),
         name="feed",
-    )(meta, tokens, cot, part, arrived, gain, *gu_pieces, down_full)
-    return results[:3], results[3 : 3 + len(plan)], results[3 + len(plan) :]
+    )(meta, normed, cot, *gu_pieces, *down_pieces)
+    return results[:2], results[2 : 2 + chips], results[2 + chips :]
 
 
 def settle_kernel(
@@ -536,17 +547,15 @@
     cot_ref,
     back_ref,
     arrived_ref,
-    attended_ref,
     weight_ref,
     gain_ref,
     dmixed_ref,
     do_ref,
     gain_grad_ref,
-    near_ref,
-    far_ref,
+    branch_ref,
 ):
     core = meta_ref[0]
-    half = attended_ref.shape[1]
+    half = do_ref.shape[1]
     mixed = mixed_ref[...]
     scale = rms_scale(mixed)
     dn2 = back_ref[...] + arrived_ref[...]
@@ -556,36 +565,28 @@
     dmixed_ref[...] = dmixed
     gain_grad_ref[...] = 0.5 * jnp.sum(dn2 * mixed * scale, axis=0, keepdims=True)
     branch = dmixed.astype(bf16)
+    branch_ref[...] = branch
     mine = weight_ref[pl.ds(pl.multiple_of(core * half, half), half), :]
     do_ref[...] = mm_nt(branch, mine).astype(bf16)
-    grad = mm_tn(attended_ref[...].astype(bf16), branch).astype(bf16)
-    count, rows = near_ref.shape[0], near_ref.shape[1]
-    blocks = [grad[i * rows : (i + 1) * rows] for i in range(2 * count)]
-    for index in range(count):
-        even, odd = blocks[2 * index], blocks[2 * index + 1]
-        near_ref[index] = jnp.where(core == 0, even, odd)
-        far_ref[index] = jnp.where(core == 0, odd, even)
-
-
-def settle(meta, mixed, cot, back, arrived, attended, weight, gain, chips):
+
+
+def settle(meta, mixed, cot, back, arrived, weight, gain):
     group, width = mixed.shape
     half = width // 2
-    rows = half // chips
     return pl.pallas_call(
         settle_kernel,
-        in_specs=[smem_spec()] + [whole_spec()] * 7,
-        out_specs=[whole_spec()] * 5,
+        in_specs=[smem_spec()] + [whole_spec()] * 6,
+        out_specs=[whole_spec()] * 4,
         out_shape=[
             shaped(f32, group, width),
             shaped(bf16, group, half),
             shaped(f32, 1, width),
-            shaped(bf16, chips // 2, rows, width),
-            shaped(bf16, chips // 2, rows, width),
+            shaped(bf16, group, width),
         ],
         compiler_params=params(),
-        cost_estimate=cost(4 * group * width * half, 6e6),
+        cost_estimate=cost(2 * group * width * half, 6e6),
         name="settle",
-    )(meta, mixed, cot, back, arrived, attended, weight, gain)
+    )(meta, mixed, cot, back, arrived, weight, gain)
 
 
 def band_rows(band_ref):
@@ -713,32 +714,32 @@
 small_rows = 16
 
 
-def load_plan(plan, pieces, meta_ref, first, weight):
+def load_pairs(pieces, meta_ref, first, weight):
     pairs = []
-    for index, lead, target, size, slot in plan:
-        size = min(size, 3 - target)
-        place = row_block(meta_ref, first + slot, pieces[index].shape[1])
-        pairs.append((pieces[index].at[lead : lead + size], weight.at[target : target + size, place, :]))
+    for step, piece in enumerate(pieces):
+        place = row_block(meta_ref, first + step, piece.shape[1])
+        pairs.append((piece.at[0:3], weight.at[:, place, :]))
     return pairs
 
 
 def grads_kernel(
-    plan, count, meta_ref, rows_ref, turned_ref, dq_ref, dkv_ref, gains_ref, second_ref, bias_ref, near_wo, far_wo, *refs
+    chips, meta_ref, rows_ref, turned_ref, dq_ref, dkv_ref, gains_ref, second_ref, bias_ref, joined_ref, branch_ref, *refs
 ):
     refs = list(refs)
     take = lambda n: [refs.pop(0) for _ in range(n)]
-    pieces = take(plan[-1][0] + 1)
-    outs = take(count)
+    pieces, outs = take(chips), take(chips)
     weight, grad, wo, small, sem, out_sem = take(6)
     chip, core = meta_ref[0], meta_ref[1]
     width = rows_ref.shape[1]
     half = width // 2
     group = dq_ref.shape[0]
-    chips = wo.shape[0]
-    loads = run_copies(load_plan(plan, pieces, meta_ref, 2, weight), sem)
-    for index in range(chips // 2):
-        wo[core * (chips // 2) + index] = near_wo[index]
-        wo[(1 - core) * (chips // 2) + index] = far_wo[index]
+    loads = run_copies(load_pairs(pieces, meta_ref, 2, weight), sem)
+    out_grad = mm_tn(joined_ref[...], branch_ref[...]).astype(bf16)
+    wo_rows = wo.shape[1]
+    for index in range(chips):
+        even = out_grad[2 * index * wo_rows : (2 * index + 1) * wo_rows]
+        odd = out_grad[(2 * index + 1) * wo_rows : (2 * index + 2) * wo_rows]
+        wo[index] = jnp.where(core == 0, even, odd)
     own_rows = pl.ds(pl.multiple_of(chip * group, group), group)
     query_grad = mm_tn(rows_ref[own_rows, :], dq_ref[...])
     grad[0] = query_grad.astype(bf16)
@@ -766,67 +767,56 @@
     rows = width // chips
     side_rows = rows // 2
     pairs = []
-    for out, (matrix, step) in zip(outs, cut_plan(chips, 4)):
+    for step, out in enumerate(outs):
         place = row_block(meta_ref, 2 + step, rows)
-        last = 2 if chips == 4 and step == 3 and matrix == 0 else 4
         at = 0
-        for index in range(matrix, min(last, 3)):
-            pairs.append((grad.at[index, place, :], out.at[at : at + rows, :]))
+        for matrix in range(3):
+            pairs.append((grad.at[matrix, place, :], out.at[at : at + rows, :]))
             at += rows
-        if last == 4:
-            target = meta_ref[2 + step]
-            for side in range(2):
-                pairs.append(
-                    (wo.at[target, :, side * half : (side + 1) * half], out.at[at : at + side_rows, :])
-                )
-                at += side_rows
-            pairs.append((small, out.at[at : at + small_rows, :]))
+        for side in range(2):
+            source = wo.at[meta_ref[2 + step], :, side * half : (side + 1) * half]
+            pairs.append((source, out.at[at : at + side_rows, :]))
+            at += side_rows
+        pairs.append((small, out.at[at : at + small_rows, :]))
     wait_all(run_copies(pairs, out_sem))
 
 
-def weight_grads(plan, pieces, meta, rows, turned, dq, dkv, gain, second, bias, near_wo, far_wo, chips):
+def weight_grads(pieces, meta, rows, turned, dq, dkv, gain, second, bias, joined, branch, chips):
     length, width = rows.shape
     half = width // 2
     group = dq.shape[0]
     flops = 2 * (2 * length * width * half + group * width * half)
     block = width // chips
-    cuts = cut_plan(chips, 4)
-    sizes = []
-    for matrix, step in cuts:
-        whole = 4 * block + small_rows
-        parted = chips == 4 and step == 3
-        sizes.append(whole if not parted else 2 * block if matrix == 0 else whole - 2 * block)
     return pl.pallas_call(
-        functools.partial(grads_kernel, plan, len(cuts)),
+        functools.partial(grads_kernel, chips),
         in_specs=[smem_spec()] + [whole_spec()] * 9 + [any_spec()] * len(pieces),
-        out_specs=[any_spec()] * len(cuts),
-        out_shape=[shaped(bf16, size, half) for size in sizes],
+        out_specs=[any_spec()] * chips,
+        out_shape=[shaped(bf16, 4 * block + small_rows, half)] * chips,
         scratch_shapes=[
             pltpu.VMEM((3, width, half), bf16),
             pltpu.VMEM((3, width, half), bf16),
             pltpu.VMEM((chips, block // 2, width), bf16),
             pltpu.VMEM((small_rows, half), bf16),
-            dma(len(plan)),
-            dma(6 * chips + 1),
+            dma(chips),
+            dma(6 * chips),
         ],
         compiler_params=params(),
         cost_estimate=cost(flops, 12e6),
         name="weight_grads",
-    )(meta, rows, turned, dq, dkv, gain, second, bias, near_wo, far_wo, *pieces)
-
-
-def back_kernel(plan, meta_ref, dq_ref, dkv_ref, *refs):
+    )(meta, rows, turned, dq, dkv, gain, second, bias, joined, branch, *pieces)
+
+
+def back_kernel(chips, meta_ref, dq_ref, dkv_ref, *refs):
     refs = list(refs)
     take = lambda n: [refs.pop(0) for _ in range(n)]
-    pieces = take(plan[-1][0] + 1)
+    pieces = take(chips)
     near_out, far_out = take(2)
     weight, both, back, sem = take(4)
     chip, core = meta_ref[0], meta_ref[1]
     length = dkv_ref.shape[0]
     half = dq_ref.shape[1]
     group = dq_ref.shape[0]
-    chips = near_out.shape[0]
-    wait_all(run_copies(load_plan(plan, pieces, meta_ref, 2, weight), sem))
+    wait_all(run_copies(load_pairs(pieces, meta_ref, 2, weight), sem))
     for pair in range(half // lanes):
         wide = pair * 2 * lanes
         cols = slice(pair * lanes, (pair + 1) * lanes)
@@ -842,11 +832,11 @@
             out[index] = back[pl.ds(pl.multiple_of(start, lanes), lanes), :].astype(bf16)
 
 
-def row_grads(plan, pieces, meta, dq, dkv, chips):
+def row_grads(pieces, meta, dq, dkv, chips):
     length, width = dkv.shape
     half = width // 2
     return pl.pallas_call(
-        functools.partial(back_kernel, plan),
+        functools.partial(back_kernel, chips),
         in_specs=[smem_spec()] + [whole_spec()] * 2 + [any_spec()] * len(pieces),
         out_specs=[whole_spec()] * 2,
         out_shape=[shaped(bf16, chips, lanes, width)] * 2,
@@ -854,7 +844,7 @@
             pltpu.VMEM((3, width, half), bf16),
             pltpu.VMEM((width, width), bf16),
             pltpu.VMEM((length, width), f32),
-            dma(len(plan)),
+            dma(chips),
         ],
         compiler_params=params(),
         cost_estimate=cost(4 * length * width * half, 8e6),
@@ -898,6 +888,66 @@
     )(order, *blocks)
 
 
+def last_kernel(core_ref, *refs):
+    sources, (sum_ref, sent_ref) = refs[:-2], refs[-2:]
+    summed = total([source[...] for source in sources])
+    sum_ref[...] = summed
+    rows = (summed.shape[0] - small_rows) // 8
+    first = core_ref[0] == 0
+    block = lambda index: summed[index * rows : (index + 1) * rows]
+    parts = [jnp.where(first, block(2 * matrix + 1), block(2 * matrix)) for matrix in range(3)]
+    sent_ref[...] = jnp.concatenate(parts + [summed[8 * rows :]], axis=0)
+
+
+def last_sum(core, arrived):
+    height, half = arrived[0].shape
+    rows = (height - small_rows) // 8
+    return pl.pallas_call(
+        last_kernel,
+        in_specs=[smem_spec()] + [whole_spec()] * len(arrived),
+        out_specs=[whole_spec()] * 2,
+        out_shape=[shaped(f32, height, half), shaped(f32, 3 * rows + small_rows, half)],
+        compiler_params=params(),
+        cost_estimate=cost(1e6, 1e6),
+        name="last_sum",
+    )(core.reshape(1), *arrived)
+
+
+def attention_kernel(
+    rates, core_ref, sum_ref, arrived_ref, weight_ref, momentum_ref, average_ref, *outs
+):
+    new_weight, new_momentum, new_average, copy = outs
+    rows, width = weight_ref.shape[1:]
+    half = width // 2
+    first = core_ref[0] == 0
+    block = lambda index: sum_ref[index * rows : (index + 1) * rows, :]
+    for matrix in range(4):
+        left, right = block(2 * matrix), block(2 * matrix + 1)
+        if matrix < 3:
+            mine = jnp.where(first, left, right)
+            theirs = arrived_ref[matrix * rows : (matrix + 1) * rows, :]
+            left, right = jnp.where(first, mine, theirs), jnp.where(first, theirs, mine)
+        for side, grad in enumerate((left, right)):
+            at = (matrix, slice(None), slice(side * half, (side + 1) * half))
+            values = update(
+                weight_ref[at], grad, momentum_ref[at], average_ref[at], rates[matrix]
+            )
+            new_weight[at], new_momentum[at], new_average[at] = values
+            copy[at] = values[0].astype(bf16)
+
+
+def attention_update(core, summed, arrived, weight, momentum, average, rates):
+    return pl.pallas_call(
+        functools.partial(attention_kernel, rates),
+        in_specs=[smem_spec()] + [whole_spec()] * 5,
+        out_specs=[whole_spec()] * 4,
+        out_shape=[shaped(f32, *weight.shape)] * 3 + [shaped(bf16, *weight.shape)],
+        compiler_params=params(),
+        cost_estimate=cost(1e6, 2e6),
+        name="attention_update",
+    )(core.reshape(1), summed, arrived, weight, momentum, average)
+
+
 def core_swap(value):
     count = lax.axis_size("seq")
     return lax.ppermute(value, "seq", [(i, i ^ 1) for i in range(count)])
@@ -940,22 +990,8 @@
     )(order, *blocks)
 
 
-def gather_plane(value, later=None):
-    chips = lax.axis_size("seq") // 2
-    size = value.shape[0]
-    if chips != 4:
-        pieces = [value] + [plane_swap(value, step) for step in range(1, chips)]
-        if later is not None:
-            later(pieces)
-        return pieces, [(step, 0, 0, size, step) for step in range(chips)], pieces[-1]
-    first, second = plane_swap(value, 1), plane_swap(value, 2)
-    if later is not None:
-        first, second = lax.optimization_barrier((first, second, later((first, second))))[:2]
-    passed = first[: size // 2], second[size // 2 :]
-    low, high = plane_swap(passed[0], 2), plane_swap(passed[1], 1)
-    plan = [(0, 0, 0, size, 0), (1, 0, 0, size, 1), (2, 0, 0, size, 2)]
-    plan += [(3, 0, 0, size // 2, 3), (4, 0, size // 2, size - size // 2, 3)]
-    return [value, first, second, low, high], plan, passed
+def gather_plane(value):
+    return [value] + [plane_swap(value, step) for step in range(1, lax.axis_size("seq") // 2)]
 
 
 def total(blocks):
@@ -965,48 +1001,8 @@
     return summed
 
 
-def scatter_first(blocks):
-    if lax.axis_size("seq") != 8:
-        return None
-    return plane_swap(blocks[3], 1), plane_swap(blocks[4], 2)
-
-
-def passing_kernel(first_ref, second_ref, low_ref, high_ref, first_out, second_out, held, sem):
-    at, low_rows = low_ref.shape[0], pl.ds(0, low_ref.shape[0])
-    high_rows = pl.ds(at, high_ref.shape[0])
-    spots = [(second_out.at[low_rows], low_ref, held.at[0, low_rows])]
-    spots.append((first_out.at[high_rows], high_ref, held.at[1, pl.ds(0, high_ref.shape[0])]))
-    loads = run_copies([(place, room) for place, _, room in spots], sem)
-    stores = []
-    for index, (place, moved, room) in enumerate(spots):
-        loads[index].wait()
-        room[...] = (room[...].astype(f32) + moved[...].astype(f32)).astype(bf16)
-        store = pltpu.make_async_copy(room, place, sem.at[index])
-        store.start()
-        stores.append(store)
-    wait_all(stores)
-
-
-def scatter_second(blocks, passing):
-    if passing is None:
-        return blocks[1:]
-    low, high = passing
-    most = max(low.shape[0], high.shape[0])
-    return pl.pallas_call(
-        passing_kernel,
-        in_specs=[any_spec()] * 2 + [whole_spec()] * 2,
-        out_specs=[any_spec()] * 2,
-        out_shape=[shaped(bf16, *blocks[1].shape)] * 2,
-        scratch_shapes=[pltpu.VMEM((2, most) + low.shape[1:], bf16), dma(2)],
-        input_output_aliases={0: 0, 1: 1},
-        compiler_params=params(),
-        cost_estimate=cost(0, 2e6),
-        name="passing",
-    )(blocks[1], blocks[2], low, high)
-
-
-def scatter_sent(parts):
-    return [plane_swap(part, step + 1) for step, part in enumerate(parts)]
+def scatter_plane(blocks):
+    return [blocks[0]] + [plane_swap(part, step) for step, part in enumerate(blocks) if step]
 
 
 def bit_reversed(chips):
@@ -1016,6 +1012,19 @@
     return order
 
 
+def halves_along(value, dim, place):
+    count = value.shape[dim] // 2
+    split = value.reshape(value.shape[:dim] + (2, count) + value.shape[dim + 1 :])
+    side = (place // count) % 2
+    pick = lambda index: lax.dynamic_index_in_dim(split, index, dim, keepdims=False)
+    return pick(side), pick(1 - side)
+
+
+def across(value, step):
+    count = lax.axis_size("batch")
+    return lax.ppermute(value, "batch", [(i, i ^ step) for i in range(count)])
+
+
 def halved(blocks, step):
     count = blocks.shape[0] // 2
     return blocks[:count], plane_swap(blocks[count:], step)
@@ -1025,9 +1034,8 @@
     return total(halves).astype(bf16)
 
 
-def finished(halves, step):
-    while halves[0].shape[0] > 1:
-        step *= 2
+def finished(halves, steps):
+    for step in steps:
         halves = halved(summed_half(halves), step)
     return total(halves)[0]
 
@@ -1085,7 +1093,7 @@
     onward = jnp.stack([(place + step) % places for step in range(places)])
     flat_tokens, flat_cot = tokens.reshape(tok, width), cotangent.reshape(tok, width)
 
-    attn_kept, attn_sent, gu_kept, gu_sent, row_block_own, down_own = make_ready(
+    attn_kept, attn_sent, gu_kept, gu_sent, row_block_own = make_ready(
         core,
         attention_weight,
         ffin_weight,
@@ -1102,79 +1110,73 @@
     gu_block = fill(core, gu_kept, gu_from)
 
     attn_blocks = along_all(attn_block)
-    near_rows, step = row_block_own[None], 1
+    row_blocks, step = row_block_own[None], 1
     while step < chips:
-        arrived = plane_swap(near_rows, step)
+        arrived = plane_swap(row_blocks, step)
         arrived = after(arrived, attn_block if step * 2 < chips else attn_blocks)
-        near_rows = jnp.concatenate([near_rows, arrived], axis=0)
+        row_blocks = jnp.concatenate([row_blocks, arrived], axis=0)
         step *= 2
+    near_rows, down_block = row_blocks[:, : tok + 16], row_blocks[:, tok + 16 :]
     own_heads = jnp.where(first_core, bias_table[:, : heads // 2], bias_table[:, heads // 2 :])
     bias = bias_rows(after(own_heads, attn_block))
-    down_full = lax.all_gather(down_own, ("seq", "batch"), axis=0, tiled=True)
 
     attn_joined = join(after(attn_blocks, near_rows, bias, gu_block), order).reshape(4, 2 * places * rows, half)
-    gu_joined = join(along_all(after(gu_block, attn_joined)), order)
-    attn_pieces, attn_plan, attn_first = gather_plane(attn_joined, lambda _: gu_joined)
-    near_rows = after(near_rows, attn_first)
-    far_rows = core_swap(near_rows)
-    gu_joined = after(gu_joined, attn_first).reshape(2, 2 * places * rows, hidden // 2)
+    far_rows = core_swap(after(near_rows, attn_joined))
     rows_full, turned, mask = place_rows(jnp.stack(steps + [core]), near_rows, far_rows)
-    attn_pieces, rows_full = lax.optimization_barrier((attn_pieces, rows_full))
-    wo_near = jnp.stack([attn_pieces[i][lead + 3 - target] for i, lead, target, size, _ in attn_plan if target + size == 4])
+    attn_pieces = gather_plane(attn_joined)
+    gu_blocks = [after(gu_block, attn_joined)]
+    for step in range(1, places):
+        if step == 2:
+            gu_blocks[-1], down_block = lax.optimization_barrier((gu_blocks[-1], down_block, rows_full))[:2]
+        gu_blocks.append(along(gu_blocks[-1], 1))
+    down_pieces = [down_block, along(down_block, 1)]
+    gu_joined = join(gu_blocks, order)
+    attn_pieces, rows_full, gu_joined, down_pieces = lax.optimization_barrier(
+        (attn_pieces, rows_full, gu_joined, down_pieces)
+    )
+    wo_near = jnp.stack([piece[3] for piece in attn_pieces])
     wo_far = core_swap(wo_near)
+    gu_joined, down_pieces, mask = lax.optimization_barrier((gu_joined, down_pieces, mask, wo_far))[:3]
+    down_pieces.append(along(down_pieces[-1], 1))
+    gu_own = gu_joined.reshape(2, 2 * places * rows, hidden // 2)
+    gu_pieces = [gu_own] + [plane_swap(gu_own, step) for step in range(1, 3 if chips == 4 else chips)]
     chip_tokens = jnp.concatenate(by_core(flat_tokens, their_tokens), axis=0)
     chip_cot = jnp.concatenate(by_core(flat_cot, their_cot), axis=0)
 
     step_meta = jnp.stack(steps)
-    query, key, value, soft, attended = attend(
-        attn_plan, attn_pieces, step_meta, rows_full, mask, bias
+    query, key, value, soft, attended, attended_low = attend(
+        attn_pieces, step_meta, rows_full, mask, bias
     )
     wo_meta = jnp.stack([core] + [step * 2 + core for step in steps] + [step * 2 + 1 - core for step in steps])
-    part, out_weight = mix(wo_meta, attended, wo_near, wo_far)
-    their_part = core_swap(part)
-    gu_pieces, gu_plan, _ = gather_plane(gu_joined, lambda _: attended)
-    down_meta = [2 * step + core for step in range(chips)]
-    down_meta += [step * places + onward[index] for index in range(places) for step in steps]
-    (mixed, out_part, back_part), gu_grads, down_grads = feed(
-        gu_plan,
-        gu_pieces,
-        down_full,
-        jnp.stack(steps + down_meta),
-        chip_tokens,
-        chip_cot,
-        part,
-        their_part,
-        gains[1:2],
-        chips,
-        places,
-    )
-    gu_passing = scatter_first(gu_grads)
+    their_attended = core_swap(attended_low)
+    their_attended, gu_pieces, down_pieces = lax.optimization_barrier((their_attended, gu_pieces, down_pieces))
+    if chips == 4:
+        passed = [gu_pieces[1][:1], gu_pieces[2][1:]]
+        their_attended, passed = lax.optimization_barrier((their_attended, passed))
+        gu_pieces += [plane_swap(passed[0], 2), plane_swap(passed[1], 1)]
+    for _ in range(3, places):
+        down_pieces.append(along(down_pieces[-1], 1))
+    mixed, second_low, joined, out_weight = mix(
+        wo_meta, chip_tokens, attended_low, their_attended, gains[1:2], wo_near, wo_far
+    )
+    down_meta = [step * places + order[index] for index in range(places) for step in steps]
+    high = place // (places // 2)
+    for side in (high, 1 - high):
+        for spot in range(places // 2):
+            down_meta += [step * places + side * (places // 2) + spot for step in steps]
+    (out_part, back_part), gu_grads, down_grads = feed(
+        gu_pieces, down_pieces, jnp.stack(steps + down_meta), second_low, chip_cot, chips, places
+    )
+    add = lambda a, b: total([a, b]).astype(bf16)
+    gu_arrived = scatter_plane(gu_grads)
+    down_moving = across(down_grads[1], places // 2)
     their_back = core_swap(back_part)
-    add = lambda a, b: total([a, b]).astype(bf16)
-    down_moving = along(down_grads[-1], 1)
-    dmixed, attended_grad, second_gain, near_wo, far_wo = settle(
-        core.reshape(1), mixed, chip_cot, back_part, their_back, attended, out_weight, gains[1:2], chips
-    )
-    gu_passing, far_wo, attended_grad, down_moving = lax.optimization_barrier(
-        (gu_passing, far_wo, attended_grad, down_moving)
-    )
-    gu_parts = scatter_second(gu_grads, gu_passing)
-    far_wo = core_swap(after(far_wo, gu_passing))
-    gu_parts, attended_grad, _ = lax.optimization_barrier((gu_parts, attended_grad, far_wo))
-    gu_arrived = scatter_sent(gu_parts)
-    down_moving = add(down_moving, down_grads[-2])
-    attended_grad, down_moving = lax.optimization_barrier((attended_grad, down_moving))
-    down_moving = along(down_moving, 1)
+    dmixed, attended_grad, second_gain, branch = settle(
+        core.reshape(1), mixed, chip_cot, back_part, their_back, out_weight, gains[1:2]
+    )
     dq, dkv, bias_part = retreat(chip.reshape(1), attended_grad, attended, query, key, value, soft)
     pair_meta = jnp.stack([chip, core] + steps)
-    down_moving = after(down_moving, dq)
-    for step in range(places - 3, 0, -1):
-        down_moving = add(down_moving, down_grads[step])
-        if step == places - 3:
-            dq, down_moving = lax.optimization_barrier((dq, down_moving))
-        down_moving = along(down_moving, 1)
     attn_grads = weight_grads(
-        attn_plan,
         attn_pieces,
         pair_meta,
         rows_full,
@@ -1184,45 +1186,56 @@
         gains[:1],
         second_gain,
         bias_part,
-        near_wo,
-        far_wo,
+        joined,
+        branch,
         chips,
     )
 
-    attn_grads, gu_arrived = lax.optimization_barrier((attn_grads, gu_arrived))
-    attn_passing = scatter_first(attn_grads)
-    gu_sum = total([gu_grads[0]] + list(gu_arrived)).astype(bf16)
-    gu_split = gu_sum.reshape(2, 2, places, rows, hidden // 2)
-    gu_cut = lambda step: lax.dynamic_index_in_dim(gu_split, (place + step) % places, 2, keepdims=False)
-    gu_moving = along(gu_cut(places - 1), 1)
-    down_sum = add(after(down_moving, attn_grads), down_grads[0])
-    down_halves = halved(down_sum, 1)
-    near_back, far_back = row_grads(attn_plan, attn_pieces, pair_meta, after(dq, attn_grads), dkv, chips)
-    if attn_passing is not None:
-        attn_passing = after(attn_passing, near_back, down_halves)
-    attn_parts = scatter_second(attn_grads, attn_passing)
-    attn_arrived = scatter_sent(attn_parts)
+    near_back, far_back = row_grads(attn_pieces, pair_meta, after(dq, attn_grads), dkv, chips)
+    mine = lambda value: lax.dynamic_slice_in_dim(value, core * tok, tok, 0)
+    theirs = lambda value: lax.dynamic_slice_in_dim(value, (1 - core) * tok, tok, 0)
     back_arrived = core_swap(far_back)
-    gu_moving = after(gu_moving, attn_parts)
-    for step in range(places - 2, 0, -1):
-        gu_moving = along(add(gu_moving, gu_cut(step)), 1)
-    gu_sum = total([gu_moving, gu_cut(0)])
+    attn_grads, gu_arrived, down_moving = lax.optimization_barrier(
+        (attn_grads, gu_arrived, down_moving, back_arrived)
+    )[:3]
+    attn_arrived = [attn_grads[0]] + [plane_swap(attn_grads[step], step) for step in range(1, min(chips, 3))]
+    gu_sum = total(gu_arrived).astype(bf16).reshape(2, 2, places, rows, hidden // 2)
+    down_sum = add(down_moving, down_grads[0])
+    reach = places // 2
+    gu_kept, gu_sent = halves_along(gu_sum, 2, place)
+    gu_moving = across(gu_sent, reach)
+    down_kept, down_sent = halves_along(down_sum, 0, place)
+    down_moving = across(down_sent, reach // 2)
+    attn_arrived, gu_moving, down_moving, out_part = lax.optimization_barrier(
+        (attn_arrived, gu_moving, down_moving, out_part)
+    )
+    their_out = core_swap(theirs(out_part))
+    last_attn = [plane_swap(attn_grads[step], step) for step in range(3, chips)]
+    while reach > 1:
+        gu_kept, gu_sent = halves_along(add(gu_kept, gu_moving), 2, place)
+        reach //= 2
+        gu_moving = across(gu_sent, reach)
+        if reach > 1:
+            down_kept, down_sent = halves_along(add(down_kept, down_moving), 0, place)
+            down_moving = across(down_sent, reach // 2)
+    gu_sum = total([gu_kept, gu_moving])[:, :, 0]
+    down_halves = halved(add(down_kept, down_moving)[0], chips // 2)
+    layer_output = mine(mixed) + mine(out_part) + their_out
+    attn_arrived, gu_sum, down_halves, layer_output = lax.optimization_barrier(
+        (attn_arrived + last_attn, gu_sum, down_halves, layer_output)
+    )
     pick = lambda value, first, dim: jnp.where(
         first, lax.index_in_dim(value, 0, dim, False), lax.index_in_dim(value, 1, dim, False)
     )
     gu_own = pick(gu_sum, first_core, 1)
     gu_their = core_swap(pick(gu_sum, core == 1, 1))
-    down_sum = summed_half(down_halves)
-    down_halves = halved(after(down_sum, attn_parts), 2)
-    mine = lambda value: lax.dynamic_slice_in_dim(value, core * tok, tok, 0)
-    theirs = lambda value: lax.dynamic_slice_in_dim(value, (1 - core) * tok, tok, 0)
-    their_out = core_swap(after(theirs(out_part), near_back))
-    attn_cuts = sum_plane([attn_grads[0]] + list(attn_arrived), onward)
+    attn_cuts = sum_plane(attn_arrived, onward)
     attn_sum = spread(attn_cuts)
     merged = total([near_back, back_arrived]).astype(bf16)
-    back_halves = halved(after(merged, attn_cuts), 1)
-    own_down = finished(after(down_halves, attn_cuts), 2)
-    back_sum = summed_half(back_halves)
+    later_steps = [chips // 2 >> turn for turn in range(1, chips.bit_length() - 1)]
+    down_sum = after(summed_half(down_halves), attn_cuts)
+    own_down = finished(halved(down_sum, later_steps[0]), later_steps[1:])
+    back_sum = summed_half(halved(after(merged, attn_cuts), 1))
     back_halves = halved(back_sum, 2)
 
     weave = lambda parts: jnp.stack(
@@ -1235,38 +1248,31 @@
     ffout_new = update(
         ffout_weight, own_down, ffout_momentum, ffout_average, ffout_rate * inverse_root
     )
-    layer_output = mine(mixed) + mine(out_part) + their_out
-    attn_sum, ffin_new, ffout_new, layer_output, _ = lax.optimization_barrier(
-        (attn_sum, ffin_new, ffout_new, layer_output, back_sum)
-    )
-    attn_sum = total(attn_sum)
-    first_grad = finished(back_halves, 2)
-    blocks = attn_sum[:-small_rows].reshape(4, 2, rows, half)
-    small_own = attn_sum[-small_rows:]
-    sent = pick(blocks[:3], core == 1, 1).reshape(3 * rows, half)
-    arrived = core_swap(jnp.concatenate([sent, small_own], axis=0))
-    own_qkv = jnp.concatenate(
-        by_core(pick(blocks[:3], first_core, 1), arrived[: 3 * rows].reshape(3, rows, half)), axis=-1
-    )
-    own_wo = jnp.concatenate([blocks[3, 0], blocks[3, 1]], axis=-1)
-    own_attention = jnp.concatenate([own_qkv, own_wo[None]], axis=0)
-
+    attn_sum, ffin_new, ffout_new, _ = lax.optimization_barrier((attn_sum, ffin_new, ffout_new, back_sum))
+    first_grad = finished(back_halves, [2 << turn for turn in range(1, chips.bit_length() - 2)])
+    summed, sent = last_sum(core, attn_sum)
+    arrived = core_swap(sent)
     scale = rms_scale(flat_tokens)
     gained = first_grad * gains[0]
     inner = jnp.mean(gained * flat_tokens, axis=-1, keepdims=True)
     input_grad = mine(dmixed) + scale * gained - flat_tokens * (scale**3 * inner)
 
-    small_their = arrived[3 * rows :]
+    attn_new = attention_update(
+        core,
+        summed,
+        arrived,
+        attention_weight,
+        attention_momentum,
+        attention_average,
+        [rate * inverse_root for rate in attention_rates],
+    )
+    small_own, small_their = summed[-small_rows:], arrived[-small_rows:]
     gains_reduced = (small_own[:4] + small_their[:4]).reshape(gains.shape)
     pairs = heads // 4
     heads_of = lambda value: value[4 : 4 + pairs, : 2 * lanes].reshape(heads // 2, lanes)[:, : bias_table.shape[0]]
     bias_reduced = jnp.concatenate(by_core(heads_of(small_own), heads_of(small_their)), axis=0).T
 
-    attention_rate = jnp.array(attention_rates, dtype=f32)[:, None, None] * inverse_root
     gain_rate = jnp.array(gain_rates, dtype=f32)[:, None] * inverse_root
-    attn_new = update(
-        attention_weight, own_attention, attention_momentum, attention_average, attention_rate
-    )
     bias_new = update(bias_table, bias_reduced, bias_momentum, bias_average, bias_rate * inverse_root)
     gain_new = update(gains, gains_reduced, gain_momentum, gain_average, gain_rate)
     return (
@@ -1287,7 +1293,7 @@
         ffout_new[2],
         bias_new[2],
         gain_new[2],
-        attn_new[0].astype(bf16),
+        attn_new[3],
         ffin_new[0].astype(bf16),
         ffout_new[0].astype(bf16),
     )

time: 260 us -> 238 us (0.915)
  between operations: 15 us -> 1.56 us
  waiting for transfers between devices: 64.1 us -> 74.4 us
  starting transfers between devices: 49.2 us -> 41.8 us
  other arithmetic: 24 us -> 18.5 us
  local copies, waits for them, and re-layouts: 17.5 us -> 14.3 us
    ppermute x0 -> x4, waiting for transfers between devices: none -> 20.7 us  [across(): return lax.ppermute(value, 'batch', [(i, i ^ step) for i in range(count)])]
    ppermute x15 -> x12, waiting for transfers between devices: 37.3 us -> 25.1 us  [along(): lax.ppermute(value, 'batch', [(i, (i + step) % count) for i in range(coun...]
    ppermute x15 -> x12, starting transfers between devices: 21.2 us -> 14.2 us  [along(): lax.ppermute(value, 'batch', [(i, (i + step) % count) for i in range(coun...]
    ppermute x0 -> x4, starting transfers between devices: none -> 3.49 us  [across(): return lax.ppermute(value, 'batch', [(i, i ^ step) for i in range(count)])]
    ppermute x22 -> x19, starting transfers between devices: 26 us -> 22.6 us  [plane_swap(): return lax.ppermute(value, 'seq', [(i, i ^ 2 * step) for i in range(count)])]
    pallas_call x8, Pallas kernels: 54.3 us -> 51.6 us  [the longest x1 13 us: attend(): pl.pallas_call(functools.partial(attend_kernel, len(pieces)), grid_spec=p...]
    convert_element_type x5 -> x3, other arithmetic: 3.05 us -> 0.43 us  [shards(): add = lambda a, b: total([a, b]).astype(bf16)]
    unnamed x132 -> x118, local copies, waits for them, and re-layouts: 7.08 us -> 5.4 us
  transfers between devices with their start and end apart: 51 -> 47, of which waited for: 22 -> 22; matrix products, arithmetic and copies ran while one was open for 13% -> 9% of each run, Pallas kernels for 28% -> 28%
where the time goes in v3:
time: 238 us; the launch traced here: 237 us
  Pallas kernels  86 us (36%)
  waiting for transfers between devices  74.4 us (31%)
  starting transfers between devices  41.8 us (18%)
  other arithmetic  18.5 us (8%)
  local copies, waits for them, and re-layouts  14.3 us (6%)
    ppermute x12, waiting for transfers between devices, along(): lax.ppermute(value, 'batch', [(i, (i + step) % count) for i in range(coun...  25.1 us
    ppermute x19, waiting for transfers between devices, plane_swap(): return lax.ppermute(value, 'seq', [(i, i ^ 2 * step) for i in range(count)])  24.5 us
    ppermute x19, starting transfers between devices, plane_swap(): return lax.ppermute(value, 'seq', [(i, i ^ 2 * step) for i in range(count)])  22.6 us
    ppermute x4, waiting for transfers between devices, across(): return lax.ppermute(value, 'batch', [(i, i ^ step) for i in range(count)])  20.7 us
    ppermute x12, starting transfers between devices, along(): lax.ppermute(value, 'batch', [(i, (i + step) % count) for i in range(coun...  14.2 us
    pallas_call x1, Pallas kernels, retreat(): pl.pallas_call(retreat_kernel, grid_spec=pltpu.PrefetchScalarGridSpec(num...  13.1 us
    pallas_call x1, Pallas kernels, attend(): pl.pallas_call(functools.partial(attend_kernel, len(pieces)), grid_spec=p...  13 us
    pallas_call x1, Pallas kernels, feed(): pl.pallas_call(functools.partial(feed_kernel, chips, places, len(gu_piece...  12 us
  transfers between devices with their start and end apart: 47, of which 22 were waited for; matrix products, arithmetic and copies ran while one was open for 9% of the time, Pallas kernels for 28%

profile of v3, /device:TPU:0, one launch (start us, length us, event | category | flops | bytes accessed | tf_op | source)
XLA Modules:
  0.0 236.6 jit_solution(9920573838880388276)
XLA Ops:
  1.8 2.2 make_ready.1
  4.0 3.0 %collective-permute-start.7 = (bf16[1,208,768]{2,1,0:T(8,128)(2,1)}, bf16[1,208,768]{2,1,0:T(8,128)(2,1)S(1)}, u32[]{:S(2)}, u32[]{:S(2)}) collective-permute-start(bf16[1,208,768]{2,1,0:T(8,128)(2,1)} %bitcast.129), channel_id=1, source_target_pairs={{0,8},{4,12},{8,0},{12,4},{16,24},{20,28},{24,16},{28,20},{1,9},{5... | collective-permute-start | bytes 958472 | tf_op jit(solution)/shard_map/ppermute | solution.py:958
  9.2 1.6 fill.2.refs_0_
  10.8 4.2 %collective-permute-done.7 = bf16[1,208,768]{2,1,0:T(8,128)(2,1)S(1)} collective-permute-done((bf16[1,208,768]{2,1,0:T(8,128)(2,1)}, bf16[1,208,768]{2,1,0:T(8,128)(2,1)S(1)}, u32[]{:S(2)}, u32[]{:S(2)}) %collective-permute-start.7) | collective-permute-done | bytes 319520 | tf_op jit(solution)/shard_map/ppermute | solution.py:958
  16.1 1.8 collective-permute-start.8
  18.1 3.6 %collective-permute-start.6 = (bf16[4,2,24,384]{3,2,1,0:T(8,128)(2,1)}, bf16[4,2,24,384]{3,2,1,0:T(8,128)(2,1)S(1)}, u32[]{:S(2)}, u32[]{:S(2)}) collective-permute-start(bf16[4,2,24,384]{3,2,1,0:T(8,128)(2,1)} %fill.2.refs_0_), channel_id=1, source_target_pairs={{0,3},{1,0},{2,1},{3,2},{4,7},{5,4},{6,5},{7,6},{8,11},{9,8},{10,9... | collective-permute-start | bytes 442376 | tf_op jit(solution)/shard_map/ppermute | solution.py:963
  24.0 1.7 fill.3.refs_0_
  25.6 4.1 %bias_rows.1.bias_ref = f32[6,640,128]{2,1,0:T(8,128)} custom-call(f32[32,6]{1,0:T(8,128)} %broadcast_select_fusion.4.table_ref), custom_call_target="tpu_custom_call" | custom-call | flops 1 | bytes 1 | tf_op jit(solution)/shard_map/bias_rows/pallas_call | solution.py:96
  29.7 4.2 %collective-permute-done.5.refs_2_ = bf16[4,2,24,384]{3,2,1,0:T(8,128)(2,1)S(1)} collective-permute-done((bf16[4,2,24,384]{3,2,1,0:T(8,128)(2,1)}, bf16[4,2,24,384]{3,2,1,0:T(8,128)(2,1)S(1)}, u32[]{:S(2)}, u32[]{:S(2)}) %collective-permute-start.5) | collective-permute-done | bytes 147488 | tf_op jit(solution)/shard_map/ppermute | solution.py:963
  34.9 2.4 %join.2 = bf16[4,2,4,24,384]{4,3,2,1,0:T(8,128)(2,1)} custom-call(s32[4]{0:T(128)} %get-tuple-element.293.order_ref, bf16[4,2,24,384]{3,2,1,0:T(8,128)(2,1)} %fill.2.refs_0_, bf16[4,2,24,384]{3,2,1,0:T(8,128)(2,1)} %copy-done.44, bf16[4,2,24,384]{3,2,1,0:T(8,128)(2,1)} %copy-done.43, bf16[4,2,24,384]{3,2,1,0:T(8,128)(2,1)} %copy-done.42), custom_call_target="tpu_custom_call" | custom-call | flops 1 | bytes 1 | tf_op jit(solution)/shard_map/join/pallas_call | solution.py:982
  37.7 1.4 collective-permute-start.11
  39.2 1.5 collective-permute-start.10
  42.8 4.2 %place_rows.1 = (bf16[1024,768]{1,0:T(8,128)(2,1)}, bf16[768,1024]{1,0:T(8,128)(2,1)}, f32[1024,256]{1,0:T(8,128)}) custom-call(s32[5]{0:T(128)} %stack.206.meta_ref, bf16[4,144,768]{2,1,0:T(8,128)(2,1)} %copy-done.4, bf16[4,144,768]{2,1,0:T(8,128)(2,1)} %collective-permute-done.12.far_ref), custom_call_target="tpu_custom_call" | custom-call | flops 1 | bytes 1 | tf_op jit(solution)/shard_map/place_rows/pallas_call | solution.py:234
  47.1 2.4 %collective-permute-start.14 = (bf16[2,2,24,1024]{3,2,1,0:T(8,128)(2,1)}, bf16[2,2,24,1024]{3,2,1,0:T(8,128)(2,1)S(1)}, u32[]{:S(2)}, u32[]{:S(2)}) collective-permute-start(bf16[2,2,24,1024]{3,2,1,0:T(8,128)(2,1)} %collective-permute-done.13.refs_1_), channel_id=1, source_target_pairs={{0,1},{1,2},{2,3},{3,0},{4,5},{5,6},{6,7},{7,4},{8,9},{9,10},{10,1... | collective-permute-start | bytes 589832 | tf_op jit(solution)/shard_map/ppermute | solution.py:963
  49.5 7.4 %collective-permute-done.14.refs_2_ = bf16[2,2,24,1024]{3,2,1,0:T(8,128)(2,1)S(1)} collective-permute-done((bf16[2,2,24,1024]{3,2,1,0:T(8,128)(2,1)}, bf16[2,2,24,1024]{3,2,1,0:T(8,128)(2,1)S(1)}, u32[]{:S(2)}, u32[]{:S(2)}) %collective-permute-start.14) | collective-permute-done | bytes 196640 | tf_op jit(solution)/shard_map/ppermute | solution.py:963
  57.5 10.4 %collective-permute-done.15.refs_3_ = bf16[2,2,24,1024]{3,2,1,0:T(8,128)(2,1)S(1)} collective-permute-done((bf16[2,2,24,1024]{3,2,1,0:T(8,128)(2,1)S(1)}, bf16[2,2,24,1024]{3,2,1,0:T(8,128)(2,1)S(1)}, u32[]{:S(2)}, u32[]{:S(2)}) %collective-permute-start.15) | collective-permute-done | bytes 196640 | tf_op jit(solution)/shard_map/ppermute | solution.py:963
  68.5 2.2 join.3
  70.8 1.4 slice.104
  72.5 2.0 collective-permute-done.17.far_ref
  75.0 1.5 collective-permute-start.19
  78.4 13.0 %attend.1 = (bf16[256,384]{1,0:T(8,128)(2,1)}, bf16[1024,384]{1,0:T(8,128)(2,1)}, bf16[1024,384]{1,0:T(8,128)(2,1)}, f32[6,1024,256]{2,1,0:T(8,128)}, f32[256,384]{1,0:T(8,128)}, /*index=5*/bf16[256,384]{1,0:T(8,128)(2,1)}) custom-call(s32[4]{0:T(128)} %get-tuple-element.294.meta_ref, bf16[1024,768]{1,0:T(8,128)(2,1)} %get-tuple-element.161.rows_ref, ...), custom_call_target="tpu_custom_call" | custom-call | flops 1 | bytes 1 | tf_op jit(solution)/shard_map/attend/pallas_call | solution.py:320
  96.4 1.6 collective-permute-start.22
  98.0 1.5 collective-permute-start.23
  102.1 4.8 %mix.1 = (f32[256,768]{1,0:T(8,128)}, bf16[256,768]{1,0:T(8,128)(2,1)}, bf16[256,768]{1,0:T(8,128)(2,1)}, bf16[768,768]{1,0:T(8,128)(2,1)}) custom-call(s32[9]{0:T(128)} %stack.215.meta_ref, f32[256,768]{1,0:T(8,128)} %pad_maximum_fusion.1.tokens_ref, bf16[256,384]{1,0:T(8,128)(2,1)} %get-tuple-element.172.own_ref, bf16[256,384]{1,0:T(8,128)(2,1)} %copy-done.39, ...), custom_call_target="tpu_custom_call" | custom-call | flops 1 | bytes 1 | tf_op jit(solution)/shard_map/mix/pallas_call | solution.py:389
  107.8 3.1 %collective-permute-done.24.refs_8_ = bf16[4,64,768]{2,1,0:T(8,128)(2,1)S(1)} collective-permute-done((bf16[4,64,768]{2,1,0:T(8,128)(2,1)}, bf16[4,64,768]{2,1,0:T(8,128)(2,1)S(1)}, u32[]{:S(2)}, u32[]{:S(2)}) %collective-permute-start.24) | collective-permute-done | bytes 393248 | tf_op jit(solution)/shard_map/ppermute | solution.py:963
  111.7 12.0 %feed.1 = (f32[256,768]{1,0:T(8,128)}, f32[256,768]{1,0:T(8,128)}, bf16[2,192,1024]{2,1,0:T(8,128)(2,1)}, bf16[2,192,1024]{2,1,0:T(8,128)(2,1)}, bf16[2,192,1024...) custom-call(s32[36]{0:T(128)} %stack.250.meta_ref, ...), custom_call_target="tpu_custom_call" | custom-call | flops 1 | bytes 1 | tf_op jit(solution)/shard_map/feed/pallas_call | solution.py:514
  125.5 2.3 collective-permute-start.28
  128.8 3.7 %settle.1 = (f32[256,768]{1,0:T(8,128)}, bf16[256,384]{1,0:T(8,128)(2,1)}, f32[1,768]{1,0:T(1,128)}, bf16[256,768]{1,0:T(8,128)(2,1)}) custom-call(s32[1]{0:T(128)} %bitcast.1.core_ref.meta_ref, f32[256,768]{1,0:T(8,128)} %get-tuple-element.180.mixed_ref, f32[256,768]{1,0:T(8,128)} %pad_maximum_fusion.2.cot_ref, f32[256,768]{1,0:T(8,128)} %get-tuple-element.188.back_ref, ...), custom_call_target="tpu_custom_call" | custom-call | flops 1 | bytes 1 | tf_op jit(solution)/shard_map/settle/pallas_call | solution.py:576
  132.6 13.1 %retreat.1 = (bf16[256,384]{1,0:T(8,128)(2,1)}, bf16[1024,768]{1,0:T(8,128)(2,1)}, f32[3,8,128]{2,1,0:T(8,128)}) custom-call(s32[1]{0:T(128)} %bitcast.meta_ref, bf16[256,384]{1,0:T(8,128)(2,1)} %get-tuple-element.190.do_ref, f32[256,384]{1,0:T(8,128)} %get-tuple-element.191.o_ref, bf16[256,384]{1,0:T(8,128)(2,1)} %get-tuple-element.192.q_ref, ...), custom_call_target="tpu_custom_call" | custom-call | flops 1 | bytes 1 | tf_op jit(solution)/shard_map/retreat/pallas_call | solution.py:678
  145.7 7.8 %weight_grads.1 = (bf16[784,384]{1,0:T(8,128)(2,1)}, bf16[784,384]{1,0:T(8,128)(2,1)}, bf16[784,384]{1,0:T(8,128)(2,1)}, bf16[784,384]{1,0:T(8,128)(2,1)}) custom-call(s32[6]{0:T(128)} %stack.200.meta_ref, bf16[1024,768]{1,0:T(8,128)(2,1)} %get-tuple-element.161.rows_ref, bf16[768,1024]{1,0:T(8,128)(2,1)} %get-tuple-element.162.turned_ref, ...), custom_call_target="tpu_custom_call" | custom-call | flops 1 | bytes 1 | tf_op jit(solution)/shard_map/weight_grads/pallas_call | solution.py:790
  153.5 6.0 %row_grads.1 = (bf16[4,128,768]{2,1,0:T(8,128)(2,1)}, bf16[4,128,768]{2,1,0:T(8,128)(2,1)}) custom-call(s32[6]{0:T(128)} %stack.200.meta_ref, bf16[256,384]{1,0:T(8,128)(2,1)} %get-tuple-element.211.dq_ref, bf16[1024,768]{1,0:T(8,128)(2,1)} %get-tuple-element.197.dkv_ref, bf16[4,192,384]{2,1,0:T(8,128)(2,1)} %bitcast.121, bf16[4,192,384]{2,1,0:T(8,128)(2,1)} %copy-done.3, ...), custom_call_target="tpu_custom_call" | custom-call | flops 1 | bytes 1 | tf_op jit(solution)/shard_map/row_grads/pallas_call | solution.py:838
  159.6 2.2 collective-permute-done.27
  165.9 2.0 add_convert_fusion.2
  167.9 2.3 collective-permute-start.33
  170.9 1.7 collective-permute-start.35
  172.8 6.7 %collective-permute-done.34 = bf16[1,4,64,768]{3,2,1,0:T(8,128)(2,1)S(1)} collective-permute-done((bf16[1,4,64,768]{3,2,1,0:T(8,128)(2,1)S(1)}, bf16[1,4,64,768]{3,2,1,0:T(8,128)(2,1)S(1)}, u32[]{:S(2)}, u32[]{:S(2)}) %collective-permute-start.34) | collective-permute-done | bytes 393248 | tf_op jit(solution)/shard_map/ppermute | solution.py:1025
  179.5 8.4 %collective-permute-done.33 = bf16[2,2,2,24,1024]{4,3,2,1,0:T(8,128)(2,1)S(1)} collective-permute-done((bf16[2,2,2,24,1024]{4,3,2,1,0:T(8,128)(2,1)S(1)}, bf16[2,2,2,24,1024]{4,3,2,1,0:T(8,128)(2,1)S(1)}, u32[]{:S(2)}, u32[]{:S(2)}) %collective-permute-start.33) | collective-permute-done | bytes 393248 | tf_op jit(solution)/shard_map/ppermute | solution.py:1025
  187.9 5.7 %collective-permute-done.32.refs_2_ = bf16[784,384]{1,0:T(8,128)(2,1)S(1)} collective-permute-done((bf16[784,384]{1,0:T(8,128)(2,1)S(1)}, bf16[784,384]{1,0:T(8,128)(2,1)S(1)}, u32[]{:S(2)}, u32[]{:S(2)}) %collective-permute-start.32) | collective-permute-done | bytes 602144 | tf_op jit(solution)/shard_map/ppermute | solution.py:958
  195.2 4.3 %collective-permute-done.36 = bf16[2,2,1,24,1024]{4,3,2,1,0:T(8,128)(2,1)S(1)} collective-permute-done((bf16[2,2,1,24,1024]{4,3,2,1,0:T(8,128)(2,1)S(1)}, bf16[2,2,1,24,1024]{4,3,2,1,0:T(8,128)(2,1)S(1)}, u32[]{:S(2)}, u32[]{:S(2)}) %collective-permute-start.36) | collective-permute-done | bytes 196640 | tf_op jit(solution)/shard_map/ppermute | solution.py:1025
  200.3 2.1 collective-permute-done.37
  202.5 2.9 %sum_plane.1 = (bf16[208,384]{1,0:T(8,128)(2,1)}, bf16[208,384]{1,0:T(8,128)(2,1)}, bf16[208,384]{1,0:T(8,128)(2,1)}, bf16[208,384]{1,0:T(8,128)(2,1)}) custom-call(s32[4]{0:T(128)} %pad_add_fusion.2.order_ref, bf16[784,384]{1,0:T(8,128)(2,1)} %get-tuple-element.233.refs_0_, bf16[784,384]{1,0:T(8,128)(2,1)} %copy-done.21, bf16[784,384]{1,0:T(8,128)(2,1)} %copy-done.22, ...), custom_call_target="tpu_custom_call" | custom-call | flops 1 | bytes 1 | tf_op jit(solution)/shard_map/sum_plane/pallas_call | solution.py:879
  206.4 1.9 collective-permute-start.42
  208.4 1.9 collective-permute-start.43
  211.4 3.7 %collective-permute-done.45 = bf16[1,64,768]{2,1,0:T(8,128)(2,1)S(1)} collective-permute-done((bf16[1,64,768]{2,1,0:T(8,128)(2,1)S(1)}, bf16[1,64,768]{2,1,0:T(8,128)(2,1)S(1)}, u32[]{:S(2)}, u32[]{:S(2)}) %collective-permute-start.45) | collective-permute-done | bytes 98336 | tf_op jit(solution)/shard_map/ppermute | solution.py:958
  217.9 2.1 add_multiply_fusion
  220.0 4.3 %collective-permute-done.39 = bf16[2,128,768]{2,1,0:T(8,128)(2,1)} collective-permute-done((bf16[2,128,768]{2,1,0:T(8,128)(2,1)S(1)}, bf16[2,128,768]{2,1,0:T(8,128)(2,1)}, u32[]{:S(2)}, u32[]{:S(2)}) %collective-permute-start.39) | collective-permute-done | bytes 393248 | tf_op jit(solution)/shard_map/ppermute | solution.py:958
  226.0 2.0 last_sum.1
  232.2 2.3 attention_update.1
  (244 shorter events, 46.5 us)
Async XLA Ops:
  0.7 3.3 %collective-permute-start.1 = (f32[128,768]{1,0:T(8,128)}, f32[128,768]{1,0:T(8,128)S(1)}, u32[]{:S(2)}, u32[]{:S(2)}) collective-permute-start(f32[128,768]{1,0:T(8,128)} %bitcast.134), channel_id=1, source_target_pairs={{0,4},{4,0},{8,12},{12,8},{16,20},{20,16},{24,28},{28,24},{1,5},{5... | collective-permute-start | bytes 1179656 | tf_op jit(solution)/shard_map/ppermute | solution.py:953
  1.2 2.8 %collective-permute-start = (f32[128,768]{1,0:T(8,128)}, f32[128,768]{1,0:T(8,128)S(1)}, u32[]{:S(2)}, u32[]{:S(2)}) collective-permute-start(f32[128,768]{1,0:T(8,128)} %bitcast.122), channel_id=1, source_target_pairs={{0,4},{4,0},{8,12},{12,8},{16,20},{20,16},{24,28},{28,24},{1,5},{5... | collective-permute-start | bytes 1179656 | tf_op jit(solution)/shard_map/ppermute | solution.py:953
  4.0 11.0 %collective-permute-start.7 = (bf16[1,208,768]{2,1,0:T(8,128)(2,1)}, bf16[1,208,768]{2,1,0:T(8,128)(2,1)S(1)}, u32[]{:S(2)}, u32[]{:S(2)}) collective-permute-start(bf16[1,208,768]{2,1,0:T(8,128)(2,1)} %bitcast.129), channel_id=1, source_target_pairs={{0,8},{4,12},{8,0},{12,4},{16,24},{20,28},{24,16},{28,20},{1,9},{5... | collective-permute-start | bytes 958472 | tf_op jit(solution)/shard_map/ppermute | solution.py:958
  7.0 1.5 collective-permute-start.2
  7.0 1.6 collective-permute-start.3
  16.1 17.9 %collective-permute-start.8 = (bf16[2,208,768]{2,1,0:T(8,128)(2,1)S(1)}, bf16[2,208,768]{2,1,0:T(8,128)(2,1)S(1)}, u32[]{:S(2)}, u32[]{:S(2)}) collective-permute-start(bf16[2,208,768]{2,1,0:T(8,128)(2,1)S(1)} %pad_maximum_fusion.3), channel_id=1, source_target_pairs={{0,16},{4,20},{8,24},{12,28},{16,0},{20,4},{24,8},{28,12},{1,17},{... | collective-permute-start | bytes 1916936 | tf_op jit(solution)/shard_map/ppermute | solution.py:958
  18.1 11.7 %collective-permute-start.6 = (bf16[4,2,24,384]{3,2,1,0:T(8,128)(2,1)}, bf16[4,2,24,384]{3,2,1,0:T(8,128)(2,1)S(1)}, u32[]{:S(2)}, u32[]{:S(2)}) collective-permute-start(bf16[4,2,24,384]{3,2,1,0:T(8,128)(2,1)} %fill.2.refs_0_), channel_id=1, source_target_pairs={{0,3},{1,0},{2,1},{3,2},{4,7},{5,4},{6,5},{7,6},{8,11},{9,8},{10,9... | collective-permute-start | bytes 442376 | tf_op jit(solution)/shard_map/ppermute | solution.py:963
  21.7 12.2 %collective-permute-start.5 = (bf16[4,2,24,384]{3,2,1,0:T(8,128)(2,1)}, bf16[4,2,24,384]{3,2,1,0:T(8,128)(2,1)S(1)}, u32[]{:S(2)}, u32[]{:S(2)}) collective-permute-start(bf16[4,2,24,384]{3,2,1,0:T(8,128)(2,1)} %fill.2.refs_0_), channel_id=1, source_target_pairs={{0,2},{1,3},{2,0},{3,1},{4,6},{5,7},{6,4},{7,5},{8,10},{9,11},{10,... | collective-permute-start | bytes 442376 | tf_op jit(solution)/shard_map/ppermute | solution.py:963
  21.7 12.2 %collective-permute-start.4 = (bf16[4,2,24,384]{3,2,1,0:T(8,128)(2,1)}, bf16[4,2,24,384]{3,2,1,0:T(8,128)(2,1)S(1)}, u32[]{:S(2)}, u32[]{:S(2)}) collective-permute-start(bf16[4,2,24,384]{3,2,1,0:T(8,128)(2,1)} %fill.2.refs_0_), channel_id=1, source_target_pairs={{0,1},{1,2},{2,3},{3,0},{4,5},{5,6},{6,7},{7,4},{8,9},{9,10},{10,1... | collective-permute-start | bytes 442376 | tf_op jit(solution)/shard_map/ppermute | solution.py:963
  37.2 5.6 %collective-permute-start.12 = (bf16[4,144,768]{2,1,0:T(8,128)(2,1)S(1)}, bf16[4,144,768]{2,1,0:T(8,128)(2,1)}, u32[]{:S(2)}, u32[]{:S(2)}) collective-permute-start(bf16[4,144,768]{2,1,0:T(8,128)(2,1)S(1)} %slice.130.near_ref), channel_id=1, source_target_pairs={{0,4},{4,0},{8,12},{12,8},{16,20},{20,16},{24,28},{28,24},{1,5},{5... | collective-permute-start | bytes 2654216 | tf_op jit(solution)/shard_map/ppermute | solution.py:953
  37.2 9.8 %collective-permute-start.13 = (bf16[2,2,24,1024]{3,2,1,0:T(8,128)(2,1)S(1)}, bf16[2,2,24,1024]{3,2,1,0:T(8,128)(2,1)}, u32[]{:S(2)}, u32[]{:S(2)}) collective-permute-start(bf16[2,2,24,1024]{3,2,1,0:T(8,128)(2,1)S(1)} %copy-done.18), channel_id=1, source_target_pairs={{0,1},{1,2},{2,3},{3,0},{4,5},{5,6},{6,7},{7,4},{8,9},{9,10},{10,1... | collective-permute-start | bytes 589832 | tf_op jit(solution)/shard_map/ppermute | solution.py:963
  37.7 33.0 %collective-permute-start.11 = (bf16[4,192,384]{2,1,0:T(8,128)(2,1)}, bf16[4,192,384]{2,1,0:T(8,128)(2,1)S(1)}, u32[]{:S(2)}, u32[]{:S(2)}) collective-permute-start(bf16[4,192,384]{2,1,0:T(8,128)(2,1)} %bitcast.115), channel_id=1, source_target_pairs={{0,24},{4,28},{8,16},{12,20},{16,8},{20,12},{24,0},{28,4},{1,25},{... | collective-permute-start | bytes 1769480 | tf_op jit(solution)/shard_map/ppermute | solution.py:958
  39.2 31.6 %collective-permute-start.10 = (bf16[4,192,384]{2,1,0:T(8,128)(2,1)}, bf16[4,192,384]{2,1,0:T(8,128)(2,1)S(1)}, u32[]{:S(2)}, u32[]{:S(2)}) collective-permute-start(bf16[4,192,384]{2,1,0:T(8,128)(2,1)} %bitcast.116), channel_id=1, source_target_pairs={{0,16},{4,20},{8,24},{12,28},{16,0},{20,4},{24,8},{28,12},{1,17},{... | collective-permute-start | bytes 1769480 | tf_op jit(solution)/shard_map/ppermute | solution.py:958
  40.7 30.1 %collective-permute-start.9 = (bf16[4,192,384]{2,1,0:T(8,128)(2,1)}, bf16[4,192,384]{2,1,0:T(8,128)(2,1)S(1)}, u32[]{:S(2)}, u32[]{:S(2)}) collective-permute-start(bf16[4,192,384]{2,1,0:T(8,128)(2,1)} %bitcast.117), channel_id=1, source_target_pairs={{0,8},{4,12},{8,0},{12,4},{16,24},{20,28},{24,16},{28,20},{1,9},{5... | collective-permute-start | bytes 1769480 | tf_op jit(solution)/shard_map/ppermute | solution.py:958
  42.8 27.9 %copy-start.10 = (bf16[4,64,768]{2,1,0:T(8,128)(2,1)}, bf16[4,64,768]{2,1,0:T(8,128)(2,1)S(1)}, u32[]{:S(2)}) copy-start(bf16[4,64,768]{2,1,0:T(8,128)(2,1)S(1)} %pad_maximum_fusion.5.refs_5_) | copy-start | bytes 1179652
  47.1 9.9 %collective-permute-start.14 = (bf16[2,2,24,1024]{3,2,1,0:T(8,128)(2,1)}, bf16[2,2,24,1024]{3,2,1,0:T(8,128)(2,1)S(1)}, u32[]{:S(2)}, u32[]{:S(2)}) collective-permute-start(bf16[2,2,24,1024]{3,2,1,0:T(8,128)(2,1)} %collective-permute-done.13.refs_1_), channel_id=1, source_target_pairs={{0,1},{1,2},{2,3},{3,0},{4,5},{5,6},{6,7},{7,4},{8,9},{9,10},{10,1... | collective-permute-start | bytes 589832 | tf_op jit(solution)/shard_map/ppermute | solution.py:963
  49.4 21.4 %collective-permute-start.16 = (bf16[4,64,768]{2,1,0:T(8,128)(2,1)S(1)}, bf16[4,64,768]{2,1,0:T(8,128)(2,1)S(1)}, u32[]{:S(2)}, u32[]{:S(2)}) collective-permute-start(bf16[4,64,768]{2,1,0:T(8,128)(2,1)S(1)} %pad_maximum_fusion.5.refs_5_), channel_id=1, source_target_pairs={{0,1},{1,2},{2,3},{3,0},{4,5},{5,6},{6,7},{7,4},{8,9},{9,10},{10,1... | collective-permute-start | bytes 1179656 | tf_op jit(solution)/shard_map/ppermute | solution.py:963
  56.9 10.9 %collective-permute-start.15 = (bf16[2,2,24,1024]{3,2,1,0:T(8,128)(2,1)S(1)}, bf16[2,2,24,1024]{3,2,1,0:T(8,128)(2,1)S(1)}, u32[]{:S(2)}, u32[]{:S(2)}) collective-permute-start(bf16[2,2,24,1024]{3,2,1,0:T(8,128)(2,1)S(1)} %collective-permute-done.14.refs_2_), channel_id=1, source_target_pairs={{0,1},{1,2},{2,3},{3,0},{4,5},{5,6},{6,7},{7,4},{8,9},{9,10},{10,1... | collective-permute-start | bytes 589832 | tf_op jit(solution)/shard_map/ppermute | solution.py:963
  72.4 2.1 collective-permute-start.17
  74.5 19.7 %collective-permute-start.20 = (bf16[2,192,1024]{2,1,0:T(8,128)(2,1)S(1)}, bf16[2,192,1024]{2,1,0:T(8,128)(2,1)}, u32[]{:S(2)}, u32[]{:S(2)}) collective-permute-start(bf16[2,192,1024]{2,1,0:T(8,128)(2,1)S(1)} %bitcast.125), channel_id=1, source_target_pairs={{0,16},{4,20},{8,24},{12,28},{16,0},{20,4},{24,8},{28,12},{1,17},{... | collective-permute-start | bytes 2359304 | tf_op jit(solution)/shard_map/ppermute | solution.py:958
  75.0 19.4 %collective-permute-start.19 = (bf16[2,192,1024]{2,1,0:T(8,128)(2,1)S(1)}, bf16[2,192,1024]{2,1,0:T(8,128)(2,1)}, u32[]{:S(2)}, u32[]{:S(2)}) collective-permute-start(bf16[2,192,1024]{2,1,0:T(8,128)(2,1)S(1)} %bitcast.126), channel_id=1, source_target_pairs={{0,8},{4,12},{8,0},{12,4},{16,24},{20,28},{24,16},{28,20},{1,9},{5... | collective-permute-start | bytes 2359304 | tf_op jit(solution)/shard_map/ppermute | solution.py:958
  76.5 16.7 %collective-permute-start.21 = (bf16[4,64,768]{2,1,0:T(8,128)(2,1)S(1)}, bf16[4,64,768]{2,1,0:T(8,128)(2,1)}, u32[]{:S(2)}, u32[]{:S(2)}) collective-permute-start(bf16[4,64,768]{2,1,0:T(8,128)(2,1)S(1)} %collective-permute-done.16.refs_6_), channel_id=1, source_target_pairs={{0,1},{1,2},{2,3},{3,0},{4,5},{5,6},{6,7},{7,4},{8,9},{9,10},{10,1... | collective-permute-start | bytes 1179656 | tf_op jit(solution)/shard_map/ppermute | solution.py:963
  91.5 1.7 collective-permute-start.18
  96.4 10.5 %collective-permute-start.22 = (bf16[1,192,1024]{2,1,0:T(8,128)(2,1)S(1)}, bf16[1,192,1024]{2,1,0:T(8,128)(2,1)S(1)}, u32[]{:S(2)}, u32[]{:S(2)}) collective-permute-start(bf16[1,192,1024]{2,1,0:T(8,128)(2,1)S(1)} %slice.108), channel_id=1, source_target_pairs={{0,16},{4,20},{8,24},{12,28},{16,0},{20,4},{24,8},{28,12},{1,17},{... | collective-permute-start | bytes 1179656 | tf_op jit(solution)/shard_map/ppermute | solution.py:958
  98.0 9.8 %collective-permute-start.23 = (bf16[1,192,1024]{2,1,0:T(8,128)(2,1)S(1)}, bf16[1,192,1024]{2,1,0:T(8,128)(2,1)S(1)}, u32[]{:S(2)}, u32[]{:S(2)}) collective-permute-start(bf16[1,192,1024]{2,1,0:T(8,128)(2,1)S(1)} %slice.109), channel_id=1, source_target_pairs={{0,8},{4,12},{8,0},{12,4},{16,24},{20,28},{24,16},{28,20},{1,9},{5... | collective-permute-start | bytes 1179656 | tf_op jit(solution)/shard_map/ppermute | solution.py:958
  99.5 11.5 %collective-permute-start.24 = (bf16[4,64,768]{2,1,0:T(8,128)(2,1)}, bf16[4,64,768]{2,1,0:T(8,128)(2,1)S(1)}, u32[]{:S(2)}, u32[]{:S(2)}) collective-permute-start(bf16[4,64,768]{2,1,0:T(8,128)(2,1)} %collective-permute-done.21.refs_7_), channel_id=1, source_target_pairs={{0,1},{1,2},{2,3},{3,0},{4,5},{5,6},{6,7},{7,4},{8,9},{9,10},{10,1... | collective-permute-start | bytes 1179656 | tf_op jit(solution)/shard_map/ppermute | solution.py:963
  123.7 4.2 %collective-permute-start.25 = (f32[256,768]{1,0:T(8,128)}, f32[256,768]{1,0:T(8,128)S(1)}, u32[]{:S(2)}, u32[]{:S(2)}) collective-permute-start(f32[256,768]{1,0:T(8,128)} %get-tuple-element.188.back_ref), channel_id=1, source_target_pairs={{0,4},{4,0},{8,12},{12,8},{16,20},{20,16},{24,28},{28,24},{1,5},{5... | collective-permute-start | bytes 2359304 | tf_op jit(solution)/shard_map/ppermute | solution.py:953
  124.4 35.2 %collective-permute-start.26 = (bf16[2,192,1024]{2,1,0:T(8,128)(2,1)}, bf16[2,192,1024]{2,1,0:T(8,128)(2,1)S(1)}, u32[]{:S(2)}, u32[]{:S(2)}) collective-permute-start(bf16[2,192,1024]{2,1,0:T(8,128)(2,1)} %get-tuple-element.207), channel_id=1, source_target_pairs={{0,8},{4,12},{8,0},{12,4},{16,24},{20,28},{24,16},{28,20},{1,9},{5... | collective-permute-start | bytes 2359304 | tf_op jit(solution)/shard_map/ppermute | solution.py:958
  125.0 36.8 %collective-permute-start.27 = (bf16[2,192,1024]{2,1,0:T(8,128)(2,1)}, bf16[2,192,1024]{2,1,0:T(8,128)(2,1)}, u32[]{:S(2)}, u32[]{:S(2)}) collective-permute-start(bf16[2,192,1024]{2,1,0:T(8,128)(2,1)} %get-tuple-element.208), channel_id=1, source_target_pairs={{0,16},{4,20},{8,24},{12,28},{16,0},{20,4},{24,8},{28,12},{1,17},{... | collective-permute-start | bytes 2359304 | tf_op jit(solution)/shard_map/ppermute | solution.py:958
  125.5 36.3 %collective-permute-start.28 = (bf16[2,192,1024]{2,1,0:T(8,128)(2,1)}, bf16[2,192,1024]{2,1,0:T(8,128)(2,1)}, u32[]{:S(2)}, u32[]{:S(2)}) collective-permute-start(bf16[2,192,1024]{2,1,0:T(8,128)(2,1)} %get-tuple-element.209), channel_id=1, source_target_pairs={{0,24},{4,28},{8,16},{12,20},{16,8},{20,12},{24,0},{28,4},{1,25},{... | collective-permute-start | bytes 2359304 | tf_op jit(solution)/shard_map/ppermute | solution.py:958
  127.9 35.3 %collective-permute-start.29 = (bf16[2,4,64,768]{3,2,1,0:T(8,128)(2,1)}, bf16[2,4,64,768]{3,2,1,0:T(8,128)(2,1)S(1)}, u32[]{:S(2)}, u32[]{:S(2)}) collective-permute-start(bf16[2,4,64,768]{3,2,1,0:T(8,128)(2,1)} %get-tuple-element.210), channel_id=1, source_target_pairs={{0,2},{1,3},{2,0},{3,1},{4,6},{5,7},{6,4},{7,5},{8,10},{9,11},{10,... | collective-permute-start | bytes 2359304 | tf_op jit(solution)/shard_map/ppermute | solution.py:1025
  159.4 3.7 %collective-permute-start.30 = (bf16[4,128,768]{2,1,0:T(8,128)(2,1)}, bf16[4,128,768]{2,1,0:T(8,128)(2,1)S(1)}, u32[]{:S(2)}, u32[]{:S(2)}) collective-permute-start(bf16[4,128,768]{2,1,0:T(8,128)(2,1)} %get-tuple-element.212), channel_id=1, source_target_pairs={{0,4},{4,0},{8,12},{12,8},{16,20},{20,16},{24,28},{28,24},{1,5},{5... | collective-permute-start | bytes 2359304 | tf_op jit(solution)/shard_map/ppermute | solution.py:953
  163.4 16.0 %collective-permute-start.34 = (bf16[1,4,64,768]{3,2,1,0:T(8,128)(2,1)S(1)}, bf16[1,4,64,768]{3,2,1,0:T(8,128)(2,1)S(1)}, u32[]{:S(2)}, u32[]{:S(2)}) collective-permute-start(bf16[1,4,64,768]{3,2,1,0:T(8,128)(2,1)S(1)} %constant_dynamic-slice_fusion.2), channel_id=1, source_target_pairs={{0,1},{1,0},{2,3},{3,2},{4,5},{5,4},{6,7},{7,6},{8,9},{9,8},{10,11... | collective-permute-start | bytes 1179656 | tf_op jit(solution)/shard_map/ppermute | solution.py:1025
  164.2 23.7 %collective-permute-start.31 = (bf16[784,384]{1,0:T(8,128)(2,1)S(1)}, bf16[784,384]{1,0:T(8,128)(2,1)S(1)}, u32[]{:S(2)}, u32[]{:S(2)}) collective-permute-start(bf16[784,384]{1,0:T(8,128)(2,1)S(1)} %copy-done.57), channel_id=1, source_target_pairs={{0,8},{4,12},{8,0},{12,4},{16,24},{20,28},{24,16},{28,20},{1,9},{5... | collective-permute-start | bytes 1806344 | tf_op jit(solution)/shard_map/ppermute | solution.py:958
  165.4 28.1 %collective-permute-start.32 = (bf16[784,384]{1,0:T(8,128)(2,1)S(1)}, bf16[784,384]{1,0:T(8,128)(2,1)S(1)}, u32[]{:S(2)}, u32[]{:S(2)}) collective-permute-start(bf16[784,384]{1,0:T(8,128)(2,1)S(1)} %copy-done.56), channel_id=1, source_target_pairs={{0,16},{4,20},{8,24},{12,28},{16,0},{20,4},{24,8},{28,12},{1,17},{... | collective-permute-start | bytes 1806344 | tf_op jit(solution)/shard_map/ppermute | solution.py:958
  167.9 19.9 %collective-permute-start.33 = (bf16[2,2,2,24,1024]{4,3,2,1,0:T(8,128)(2,1)S(1)}, bf16[2,2,2,24,1024]{4,3,2,1,0:T(8,128)(2,1)S(1)}, u32[]{:S(2)}, u32[]{:S(2)}) collective-permute-start(bf16[2,2,2,24,1024]{4,3,2,1,0:T(8,128)(2,1)S(1)} %dynamic-slice_bitcast_fusion), channel_id=1, source_target_pairs={{0,2},{1,3},{2,0},{3,1},{4,6},{5,7},{6,4},{7,5},{8,10},{9,11},{10,... | collective-permute-start | bytes 1179656 | tf_op jit(solution)/shard_map/ppermute | solution.py:1025
  170.9 29.5 %collective-permute-start.35 = (bf16[784,384]{1,0:T(8,128)(2,1)S(1)}, bf16[784,384]{1,0:T(8,128)(2,1)S(1)}, u32[]{:S(2)}, u32[]{:S(2)}) collective-permute-start(bf16[784,384]{1,0:T(8,128)(2,1)S(1)} %copy-done.55), channel_id=1, source_target_pairs={{0,24},{4,28},{8,16},{12,20},{16,8},{20,12},{24,0},{28,4},{1,25},{... | collective-permute-start | bytes 1806344 | tf_op jit(solution)/shard_map/ppermute | solution.py:958
  193.7 5.7 %collective-permute-start.36 = (bf16[2,2,1,24,1024]{4,3,2,1,0:T(8,128)(2,1)S(1)}, bf16[2,2,1,24,1024]{4,3,2,1,0:T(8,128)(2,1)S(1)}, u32[]{:S(2)}, u32[]{:S(2)}) collective-permute-start(bf16[2,2,1,24,1024]{4,3,2,1,0:T(8,128)(2,1)S(1)} %constant_dynamic-slice_fusion.1), channel_id=1, source_target_pairs={{0,1},{1,0},{2,3},{3,2},{4,5},{5,4},{6,7},{7,6},{8,9},{9,8},{10,11... | collective-permute-start | bytes 589832 | tf_op jit(solution)/shard_map/ppermute | solution.py:1025
  194.8 4.7 %collective-permute-start.38 = (f32[128,768]{1,0:T(8,128)S(1)}, f32[128,768]{1,0:T(8,128)S(1)}, u32[]{:S(2)}, u32[]{:S(2)}) collective-permute-start(f32[128,768]{1,0:T(8,128)S(1)} %constant_dynamic-slice_fusion), channel_id=1, source_target_pairs={{0,4},{4,0},{8,12},{12,8},{16,20},{20,16},{24,28},{28,24},{1,5},{5... | collective-permute-start | bytes 1179656 | tf_op jit(solution)/shard_map/ppermute | solution.py:953
  195.1 7.4 %collective-permute-start.37 = (bf16[2,64,768]{2,1,0:T(8,128)(2,1)S(1)}, bf16[2,64,768]{2,1,0:T(8,128)(2,1)S(1)}, u32[]{:S(2)}, u32[]{:S(2)}) collective-permute-start(bf16[2,64,768]{2,1,0:T(8,128)(2,1)S(1)} %get-tuple-element.282), channel_id=1, source_target_pairs={{0,16},{4,20},{8,24},{12,28},{16,0},{20,4},{24,8},{28,12},{1,17},{... | collective-permute-start | bytes 589832 | tf_op jit(solution)/shard_map/ppermute | solution.py:958
  205.4 20.0 %collective-permute-start.41 = (bf16[208,384]{1,0:T(8,128)(2,1)}, bf16[208,384]{1,0:T(8,128)(2,1)S(1)}, u32[]{:S(2)}, u32[]{:S(2)}) collective-permute-start(bf16[208,384]{1,0:T(8,128)(2,1)} %get-tuple-element.238), channel_id=1, source_target_pairs={{0,1},{1,2},{2,3},{3,0},{4,5},{5,6},{6,7},{7,4},{8,9},{9,10},{10,1... | collective-permute-start | bytes 479240 | tf_op jit(solution)/shard_map/ppermute | solution.py:963
  206.4 18.9 %collective-permute-start.42 = (bf16[208,384]{1,0:T(8,128)(2,1)}, bf16[208,384]{1,0:T(8,128)(2,1)}, u32[]{:S(2)}, u32[]{:S(2)}) collective-permute-start(bf16[208,384]{1,0:T(8,128)(2,1)} %get-tuple-element.239), channel_id=1, source_target_pairs={{0,2},{1,3},{2,0},{3,1},{4,6},{5,7},{6,4},{7,5},{8,10},{9,11},{10,... | collective-permute-start | bytes 479240 | tf_op jit(solution)/shard_map/ppermute | solution.py:963
  208.4 17.0 %collective-permute-start.43 = (bf16[208,384]{1,0:T(8,128)(2,1)}, bf16[208,384]{1,0:T(8,128)(2,1)}, u32[]{:S(2)}, u32[]{:S(2)}) collective-permute-start(bf16[208,384]{1,0:T(8,128)(2,1)} %get-tuple-element.240), channel_id=1, source_target_pairs={{0,3},{1,0},{2,1},{3,2},{4,7},{5,4},{6,5},{7,6},{8,11},{9,8},{10,9... | collective-permute-start | bytes 479240 | tf_op jit(solution)/shard_map/ppermute | solution.py:963
  210.4 4.7 %collective-permute-start.45 = (bf16[1,64,768]{2,1,0:T(8,128)(2,1)S(1)}, bf16[1,64,768]{2,1,0:T(8,128)(2,1)S(1)}, u32[]{:S(2)}, u32[]{:S(2)}) collective-permute-start(bf16[1,64,768]{2,1,0:T(8,128)(2,1)S(1)} %slice.123), channel_id=1, source_target_pairs={{0,8},{4,12},{8,0},{12,4},{16,24},{20,28},{24,16},{28,20},{1,9},{5... | collective-permute-start | bytes 294920 | tf_op jit(solution)/shard_map/ppermute | solution.py:958
  211.3 5.4 %collective-permute-start.44 = (f32[2,24,1024]{2,1,0:T(8,128)S(1)}, f32[2,24,1024]{2,1,0:T(8,128)S(1)}, u32[]{:S(2)}, u32[]{:S(2)}) collective-permute-start(f32[2,24,1024]{2,1,0:T(8,128)S(1)} %fusion.3), channel_id=1, source_target_pairs={{0,4},{4,0},{8,12},{12,8},{16,20},{20,16},{24,28},{28,24},{1,5},{5... | collective-permute-start | bytes 589832 | tf_op jit(solution)/shard_map/ppermute | solution.py:953
  215.0 9.2 %collective-permute-start.39 = (bf16[2,128,768]{2,1,0:T(8,128)(2,1)S(1)}, bf16[2,128,768]{2,1,0:T(8,128)(2,1)}, u32[]{:S(2)}, u32[]{:S(2)}) collective-permute-start(bf16[2,128,768]{2,1,0:T(8,128)(2,1)S(1)} %slice.117), channel_id=1, source_target_pairs={{0,8},{4,12},{8,0},{12,4},{16,24},{20,28},{24,16},{28,20},{1,9},{5... | collective-permute-start | bytes 1179656 | tf_op jit(solution)/shard_map/ppermute | solution.py:958
  228.1 2.6 %collective-permute-start.46 = (f32[88,384]{1,0:T(8,128)}, f32[88,384]{1,0:T(8,128)S(1)}, u32[]{:S(2)}, u32[]{:S(2)}) collective-permute-start(f32[88,384]{1,0:T(8,128)} %get-tuple-element.251), channel_id=1, source_target_pairs={{0,4},{4,0},{8,12},{12,8},{16,20},{20,16},{24,28},{28,24},{1,5},{5... | collective-permute-start | bytes 405512 | tf_op jit(solution)/shard_map/ppermute | solution.py:953
  228.1 7.4 %collective-permute-start.40 = (bf16[1,128,768]{2,1,0:T(8,128)(2,1)S(1)}, bf16[1,128,768]{2,1,0:T(8,128)(2,1)S(1)}, u32[]{:S(2)}, u32[]{:S(2)}) collective-permute-start(bf16[1,128,768]{2,1,0:T(8,128)(2,1)S(1)} %slice.134), channel_id=1, source_target_pairs={{0,16},{4,20},{8,24},{12,28},{16,0},{20,4},{24,8},{28,12},{1,17},{... | collective-permute-start | bytes 589832 | tf_op jit(solution)/shard_map/ppermute | solution.py:958
  (57 other events, 425.6 us)

commit v4 on v3

--- a/solution.py
+++ b/solution.py
@@ -258,17 +258,20 @@
 
 def attend_kernel(count, meta_ref, rows_ref, mask_ref, bias_ref, *refs):
     pieces = refs[:count]
-    q_ref, k_ref, v_ref, p_ref, o_ref, low_ref = refs[count : count + 6]
-    weight, score, soft, sem = refs[count + 6 :]
+    q_ref, k_ref, v_ref, p_ref, o_ref, low_ref, out_rows = refs[count : count + 7]
+    weight, score, soft, sem, out_sem = refs[count + 7 :]
     pair = pl.program_id(0)
     chip = meta_ref[0]
     length = rows_ref.shape[0]
     blocks = length // lanes
     group = 2 * lanes
+    stacked = [(piece.at[3], out_rows.at[step]) for step, piece in enumerate(pieces)]
 
     @pl.when(pair == 0)
     def _():
-        wait_all(run_copies(load_pairs(pieces, meta_ref, 0, weight), sem))
+        loads = run_copies(load_pairs(pieces, meta_ref, 0, weight), sem)
+        run_copies(stacked, out_sem)
+        wait_all(loads)
 
     cols = pl.ds(pl.multiple_of(pair * lanes, lanes), lanes)
     own = rows_ref[pl.ds(pl.multiple_of(chip * group, group), group), :]
@@ -279,34 +282,39 @@
     q_ref[...] = query
     k_ref[...] = key
     v_ref[...] = value
-    turned = []
+    score[...] = mm_nt(key, jnp.concatenate([one_head(query, half) for half in range(2)], axis=0))
     for half in range(2):
-        score[...] = mm_nt(key, one_head(query, half))
+        lane = slice(half * group, (half + 1) * group)
         best = jnp.full((8, group), masked_score, f32)
         for block in range(blocks):
             rows = slice(block * lanes, (block + 1) * lanes)
             bias = [bias_ref[half, band_place(block, chip, part), :] for part in range(2)]
-            now = score[rows, :] + jnp.concatenate(bias, axis=1) + mask_ref[rows, :]
-            score[rows, :] = now
+            now = score[rows, lane] + jnp.concatenate(bias, axis=1) + mask_ref[rows, :]
+            score[rows, lane] = now
             best = jnp.maximum(best, jnp.max(now.reshape(lanes // 8, 8, group), axis=0))
         top = jnp.max(best, axis=0, keepdims=True)
         total = jnp.zeros((8, group), f32)
         for block in range(blocks):
             rows = slice(block * lanes, (block + 1) * lanes)
-            now = jnp.exp(score[rows, :] - top)
-            score[rows, :] = now
+            now = jnp.exp(score[rows, lane] - top)
+            score[rows, lane] = now
             total = total + jnp.sum(now.reshape(lanes // 8, 8, group), axis=0)
         inverse = 1.0 / jnp.sum(total, axis=0, keepdims=True)
         for block in range(blocks):
             rows = slice(block * lanes, (block + 1) * lanes)
-            now = score[rows, :] * inverse
+            now = score[rows, lane] * inverse
             p_ref[half, rows, :] = now
-            soft[rows, :] = now.astype(bf16)
-        features = lanes // 2
-        turned.append(mm_tn(value, soft[...])[half * features : (half + 1) * features])
+            soft[rows, lane] = now.astype(bf16)
+    features = lanes // 2
+    both_turned = mm_tn(value, soft[...])
+    turned = [both_turned[:features, :group], both_turned[features:, group:]]
     attended = jnp.concatenate(turned, axis=0).T
     o_ref[...] = attended
     low_ref[...] = attended.astype(bf16)
+
+    @pl.when(pair == pl.num_programs(0) - 1)
+    def _():
+        wait_all([pltpu.make_async_copy(a, b, out_sem.at[i]) for i, (a, b) in enumerate(stacked)])
 
 
 def attend(pieces, meta, rows, mask, bias):
@@ -335,11 +343,13 @@
                 pl.BlockSpec((2, length, group), lambda i, *_: (i, 0, 0)),
                 pl.BlockSpec((group, lanes), col),
                 pl.BlockSpec((group, lanes), col),
+                pl.BlockSpec((len(pieces),) + pieces[0].shape[1:], lambda i, *_: (0, 0, 0)),
             ],
             scratch_shapes=[
                 pltpu.VMEM((3, width, half), bf16),
-                pltpu.VMEM((length, group), f32),
-                pltpu.VMEM((length, group), bf16),
+                pltpu.VMEM((length, 2 * group), f32),
+                pltpu.VMEM((length, 2 * group), bf16),
+                dma(len(pieces)),
                 dma(len(pieces)),
             ],
         ),
@@ -350,6 +360,7 @@
             shaped(f32, 2 * pairs, length, group),
             shaped(f32, group, half),
             shaped(bf16, group, half),
+            shaped(bf16, len(pieces), *pieces[0].shape[1:]),
         ],
         compiler_params=params(),
         cost_estimate=cost(flops, 30e6, 2 * group * length * pairs),
@@ -358,7 +369,7 @@
 
 
 def mix_kernel(
-    meta_ref, tokens_ref, own_ref, their_ref, gain_ref, near_ref, far_ref, mixed_ref, normed_ref, joined_ref, weight_ref, sem
+    meta_ref, tokens_ref, own_ref, their_ref, gain_ref, near_ref, far_ref, mixed_ref, normed_ref, turned_ref, joined_ref, weight_ref, held, sem
 ):
     chips, rows, half = near_ref.shape
     rows = rows // 2
@@ -375,12 +386,15 @@
                 )
     copies = run_copies(pairs, sem)
     first = meta_ref[0] == 0
-    joined_ref[:, :half] = jnp.where(first, own_ref[...], their_ref[...])
-    joined_ref[:, half:] = jnp.where(first, their_ref[...], own_ref[...])
+    held[:, :half] = jnp.where(first, own_ref[...], their_ref[...])
+    held[:, half:] = jnp.where(first, their_ref[...], own_ref[...])
+    joined_ref[...] = held[...].T
     wait_all(copies)
-    mixed = tokens_ref[...] + mm(joined_ref[...], weight_ref[...])
+    mixed = tokens_ref[...] + mm(held[...], weight_ref[...])
     mixed_ref[...] = mixed
-    normed_ref[...] = (mixed * rms_scale(mixed) * gain_ref[...]).astype(bf16)
+    normed = (mixed * rms_scale(mixed) * gain_ref[...]).astype(bf16)
+    normed_ref[...] = normed
+    turned_ref[...] = normed.T
 
 
 def mix(meta, tokens, own, their, gain, near, far):
@@ -389,14 +403,15 @@
     return pl.pallas_call(
         mix_kernel,
         in_specs=[smem_spec()] + [whole_spec()] * 4 + [any_spec()] * 2,
-        out_specs=[whole_spec()] * 4,
+        out_specs=[whole_spec()] * 5,
         out_shape=[
             shaped(f32, group, width),
             shaped(bf16, group, width),
-            shaped(bf16, group, width),
+            shaped(bf16, width, group),
+            shaped(bf16, width, group),
             shaped(bf16, width, width),
         ],
-        scratch_shapes=[dma(4 * near.shape[0])],
+        scratch_shapes=[pltpu.VMEM((group, width), bf16), dma(4 * near.shape[0])],
         compiler_params=params(),
         cost_estimate=cost(4 * group * width * half, 4e6),
         name="mix",
@@ -409,6 +424,7 @@
     gu_count,
     meta_ref,
     normed_low,
+    turned_low,
     cot_ref,
     *refs,
 ):
@@ -422,7 +438,7 @@
     gu_sem, down_sem, gu_out_sem, down_out_sem = take(4)
     step = pl.program_id(0)
     steps = pl.num_programs(0)
-    block = 256
+    block = 512
 
     count = gu.shape[2] // block
 
@@ -483,8 +499,9 @@
     out_ref[...] += mm(hidden, down_w)
     back_ref[...] += mm_nt(dgate, gate_w) + mm_nt(dup, up_w)
     grad_down[cols, :] = mm_tn(hidden, cot).astype(bf16)
-    grad_gu[0, :, cols] = mm_tn(normed, dgate).astype(bf16)
-    grad_gu[1, :, cols] = mm_tn(normed, dup).astype(bf16)
+    both = mm(turned_low[...], jnp.concatenate([dgate, dup], axis=1)).astype(bf16)
+    grad_gu[0, :, cols] = both[:, :block]
+    grad_gu[1, :, cols] = both[:, block:]
 
     for copy in gu_stores(step):
         copy.start()
@@ -504,10 +521,10 @@
         wait_all(down_copies)
 
 
-def feed(gu_pieces, down_pieces, meta, normed, cot, chips, places):
+def feed(gu_pieces, down_pieces, meta, normed, turned, cot, chips, places):
     group, width = normed.shape
     hidden = gu_pieces[0].shape[2]
-    block = 256
+    block = 512
     fixed = lambda i, *_: (0, 0)
     full = lambda *shape: pl.BlockSpec(shape, fixed)
     flops = 2 * 9 * group * width * hidden
@@ -516,7 +533,7 @@
         grid_spec=pltpu.PrefetchScalarGridSpec(
             num_scalar_prefetch=1,
             grid=(hidden // block,),
-            in_specs=[full(group, width)] * 2
+            in_specs=[full(group, width), full(width, group), full(group, width)]
             + [any_spec()] * (len(gu_pieces) + places),
             out_specs=[full(group, width)] * 2 + [any_spec()] * (chips + 2),
             scratch_shapes=[
@@ -537,7 +554,7 @@
         compiler_params=params(),
         cost_estimate=cost(flops, 25e6, group * hidden),
         name="feed",
-    )(meta, normed, cot, *gu_pieces, *down_pieces)
+    )(meta, normed, turned, cot, *gu_pieces, *down_pieces)
     return results[:2], results[2 : 2 + chips], results[2 + chips :]
 
 
@@ -607,7 +624,7 @@
     return jnp.concatenate(found, axis=1)
 
 
-def retreat_kernel(meta_ref, do_ref, o_ref, q_ref, k_ref, v_ref, p_ref, dq_ref, dkv_ref, bias_ref, low, sums, band_ref, onehot):
+def retreat_kernel(meta_ref, do_ref, o_ref, q_ref, k_ref, v_ref, p_ref, dq_ref, dkv_ref, bias_ref, low, soft_low, spread_of, band_ref, onehot):
     chip = meta_ref[0]
     blocks = k_ref.shape[0] // lanes
     group = 2 * lanes
@@ -625,37 +642,34 @@
         offset = lanes * (spot // (2 * lanes)) - 1 - spot % (2 * lanes)
         onehot[...] = (bucket_of(offset) == bucket).astype(f32)
 
-    turned = []
+    do_two = jnp.concatenate([one_head(do, half) for half in range(2)], axis=0)
+    query_two = jnp.concatenate([one_head(q_ref[...], half) for half in range(2)], axis=0)
+    spread_of[...] = mm_nt(v_ref[...], do_two)
     for half in range(2):
-        do_half, query_half = one_head(do, half), one_head(q_ref[...], half)
+        lane = slice(half * group, (half + 1) * group)
         delta = jnp.sum(spread[half * features : (half + 1) * features], axis=0, keepdims=True)
         for block in range(blocks):
             rows = slice(block * lanes, (block + 1) * lanes)
             soft = p_ref[half, rows, :]
-            ds = soft * (mm_nt(v_ref[rows, :], do_half) - delta)
+            ds = soft * (spread_of[rows, lane] - delta)
             for part in range(2):
                 place = band_place(block, chip, part)
                 band_ref[place, :] += ds[:, part * lanes : (part + 1) * lanes]
-            ds_low = ds.astype(bf16)
-            low[rows, :] = ds_low
-            dk = mm(ds_low, query_half)
-            dv = mm(soft.astype(bf16), do_half)
-            if half == 0:
-                sums[rows, :lanes] = dk
-                sums[rows, lanes:] = dv
-            else:
-                dkv_ref[rows, :lanes] = (sums[rows, :lanes] + dk).astype(bf16)
-                dkv_ref[rows, lanes:] = (sums[rows, lanes:] + dv).astype(bf16)
-        turned.append(mm_tn(k_ref[...], low[...])[half * features : (half + 1) * features])
+            low[rows, lane] = ds.astype(bf16)
+            soft_low[rows, lane] = soft.astype(bf16)
         rows_of.append(band_rows(band_ref))
         low_sum = jnp.sum(band_ref[0:lanes, :])
         high_sum = jnp.sum(band_ref[4 * lanes : 5 * lanes, :])
-        lane = lax.broadcasted_iota(jnp.int32, (8, lanes), 1)
+        lane_id = lax.broadcasted_iota(jnp.int32, (8, lanes), 1)
         line = lax.broadcasted_iota(jnp.int32, (8, lanes), 0)
-        far = far + jnp.where((lane == 15) & (line == half), low_sum, 0.0)
-        far = far + jnp.where((lane == 31) & (line == half), high_sum, 0.0)
+        far = far + jnp.where((lane_id == 15) & (line == half), low_sum, 0.0)
+        far = far + jnp.where((lane_id == 31) & (line == half), high_sum, 0.0)
         if half == 0:
             band_ref[...] = jnp.zeros_like(band_ref)
+    dkv_ref[:, :lanes] = mm(low[...], query_two).astype(bf16)
+    dkv_ref[:, lanes:] = mm(soft_low[...], do_two).astype(bf16)
+    both_turned = mm_tn(k_ref[...], low[...])
+    turned = [both_turned[:features, :group], both_turned[features:, group:]]
     dq_ref[...] = jnp.concatenate(turned, axis=0).T.astype(bf16)
     rows_of.append(jnp.zeros((6, rows_of[0].shape[1]), f32))
     near = lax.dot_general(
@@ -694,8 +708,9 @@
                 pl.BlockSpec((1, 8, lanes), deep),
             ],
             scratch_shapes=[
-                pltpu.VMEM((length, group), bf16),
-                pltpu.VMEM((length, 2 * lanes), f32),
+                pltpu.VMEM((length, 2 * group), bf16),
+                pltpu.VMEM((length, 2 * group), bf16),
+                pltpu.VMEM((length, 2 * group), f32),
                 pltpu.VMEM((5 * lanes, lanes), f32),
                 pltpu.VMEM((6 * lanes, lanes), f32),
             ],
@@ -723,25 +738,28 @@
 
 
 def grads_kernel(
-    chips, meta_ref, rows_ref, turned_ref, dq_ref, dkv_ref, gains_ref, second_ref, bias_ref, joined_ref, branch_ref, *refs
+    chips, meta_ref, turned_ref, dq_ref, dkv_ref, gains_ref, second_ref, bias_ref, joined_ref, branch_ref, *refs
 ):
     refs = list(refs)
     take = lambda n: [refs.pop(0) for _ in range(n)]
     pieces, outs = take(chips), take(chips)
     weight, grad, wo, small, sem, out_sem = take(6)
     chip, core = meta_ref[0], meta_ref[1]
-    width = rows_ref.shape[1]
+    width = turned_ref.shape[0]
     half = width // 2
     group = dq_ref.shape[0]
     loads = run_copies(load_pairs(pieces, meta_ref, 2, weight), sem)
-    out_grad = mm_tn(joined_ref[...], branch_ref[...]).astype(bf16)
     wo_rows = wo.shape[1]
+    mine = []
     for index in range(chips):
-        even = out_grad[2 * index * wo_rows : (2 * index + 1) * wo_rows]
-        odd = out_grad[(2 * index + 1) * wo_rows : (2 * index + 2) * wo_rows]
-        wo[index] = jnp.where(core == 0, even, odd)
+        even = joined_ref[2 * index * wo_rows : (2 * index + 1) * wo_rows, :]
+        odd = joined_ref[(2 * index + 1) * wo_rows : (2 * index + 2) * wo_rows, :]
+        mine.append(jnp.where(core == 0, even, odd))
+    out_grad = mm(jnp.concatenate(mine, axis=0), branch_ref[...]).astype(bf16)
+    for index in range(chips):
+        wo[index] = out_grad[index * wo_rows : (index + 1) * wo_rows]
     own_rows = pl.ds(pl.multiple_of(chip * group, group), group)
-    query_grad = mm_tn(rows_ref[own_rows, :], dq_ref[...])
+    query_grad = mm(turned_ref[:, own_rows], dq_ref[...])
     grad[0] = query_grad.astype(bf16)
     wait_all(loads)
     along_row = [query_grad[:, at : at + lanes] * weight[0, :, at : at + lanes].astype(f32) for at in range(0, half, lanes)]
@@ -781,15 +799,15 @@
     wait_all(run_copies(pairs, out_sem))
 
 
-def weight_grads(pieces, meta, rows, turned, dq, dkv, gain, second, bias, joined, branch, chips):
-    length, width = rows.shape
+def weight_grads(pieces, meta, turned, dq, dkv, gain, second, bias, joined, branch, chips):
+    width, length = turned.shape
     half = width // 2
     group = dq.shape[0]
     flops = 2 * (2 * length * width * half + group * width * half)
     block = width // chips
     return pl.pallas_call(
         functools.partial(grads_kernel, chips),
-        in_specs=[smem_spec()] + [whole_spec()] * 9 + [any_spec()] * len(pieces),
+        in_specs=[smem_spec()] + [whole_spec()] * 8 + [any_spec()] * len(pieces),
         out_specs=[any_spec()] * chips,
         out_shape=[shaped(bf16, 4 * block + small_rows, half)] * chips,
         scratch_shapes=[
@@ -803,7 +821,7 @@
         compiler_params=params(),
         cost_estimate=cost(flops, 12e6),
         name="weight_grads",
-    )(meta, rows, turned, dq, dkv, gain, second, bias, joined, branch, *pieces)
+    )(meta, turned, dq, dkv, gain, second, bias, joined, branch, *pieces)
 
 
 def back_kernel(chips, meta_ref, dq_ref, dkv_ref, *refs):
@@ -850,6 +868,31 @@
         cost_estimate=cost(4 * length * width * half, 8e6),
         name="row_grads",
     )(meta, dq, dkv, *pieces)
+
+
+def cut_kernel(side_ref, *refs):
+    sources, (kept_ref, sent_ref) = refs[:-2], refs[-2:]
+    count = kept_ref.shape[2]
+    for index, out in ((side_ref[0], kept_ref), (1 - side_ref[0], sent_ref)):
+        for part in range(2):
+            start = pl.multiple_of((2 * part + index) * count, count)
+            out[0, part] = total([source[0, pl.ds(start, count), :] for source in sources]).astype(bf16)
+
+
+def cut_plane(blocks, side):
+    lead, height, width = blocks[0].shape
+    shape = (lead, 2, height // 4, width)
+    row = lambda *shape: pl.BlockSpec((1,) + shape, lambda i: (i,) + (0,) * len(shape))
+    return pl.pallas_call(
+        cut_kernel,
+        grid=(lead,),
+        in_specs=[smem_spec()] + [row(height, width)] * len(blocks),
+        out_specs=[row(*shape[1:])] * 2,
+        out_shape=[shaped(bf16, *shape)] * 2,
+        compiler_params=params(),
+        cost_estimate=cost(1e6, 6e6),
+        name="cut_plane",
+    )(side.reshape(1), *blocks)
 
 
 def sum_kernel(order_ref, *refs):
@@ -1121,6 +1164,8 @@
     bias = bias_rows(after(own_heads, attn_block))
 
     attn_joined = join(after(attn_blocks, near_rows, bias, gu_block), order).reshape(4, 2 * places * rows, half)
+    chip_tokens = jnp.concatenate(by_core(flat_tokens, their_tokens), axis=0)
+    chip_cot = jnp.concatenate(by_core(flat_cot, their_cot), axis=0)
     far_rows = core_swap(after(near_rows, attn_joined))
     rows_full, turned, mask = place_rows(jnp.stack(steps + [core]), near_rows, far_rows)
     attn_pieces = gather_plane(attn_joined)
@@ -1134,29 +1179,28 @@
     attn_pieces, rows_full, gu_joined, down_pieces = lax.optimization_barrier(
         (attn_pieces, rows_full, gu_joined, down_pieces)
     )
-    wo_near = jnp.stack([piece[3] for piece in attn_pieces])
-    wo_far = core_swap(wo_near)
-    gu_joined, down_pieces, mask = lax.optimization_barrier((gu_joined, down_pieces, mask, wo_far))[:3]
+    chip_tokens, chip_cot, mask = lax.optimization_barrier((chip_tokens, chip_cot, mask))
+    gu_joined, down_pieces, mask = lax.optimization_barrier((gu_joined, down_pieces, mask))
     down_pieces.append(along(down_pieces[-1], 1))
     gu_own = gu_joined.reshape(2, 2 * places * rows, hidden // 2)
     gu_pieces = [gu_own] + [plane_swap(gu_own, step) for step in range(1, 3 if chips == 4 else chips)]
-    chip_tokens = jnp.concatenate(by_core(flat_tokens, their_tokens), axis=0)
-    chip_cot = jnp.concatenate(by_core(flat_cot, their_cot), axis=0)
-
     step_meta = jnp.stack(steps)
-    query, key, value, soft, attended, attended_low = attend(
+    query, key, value, soft, attended, attended_low, wo_near = attend(
         attn_pieces, step_meta, rows_full, mask, bias
     )
     wo_meta = jnp.stack([core] + [step * 2 + core for step in steps] + [step * 2 + 1 - core for step in steps])
     their_attended = core_swap(attended_low)
-    their_attended, gu_pieces, down_pieces = lax.optimization_barrier((their_attended, gu_pieces, down_pieces))
+    their_attended, gu_pieces, down_pieces, wo_near = lax.optimization_barrier(
+        (their_attended, gu_pieces, down_pieces, wo_near)
+    )
     if chips == 4:
         passed = [gu_pieces[1][:1], gu_pieces[2][1:]]
-        their_attended, passed = lax.optimization_barrier((their_attended, passed))
+        their_attended, passed, wo_near = lax.optimization_barrier((their_attended, passed, wo_near))
         gu_pieces += [plane_swap(passed[0], 2), plane_swap(passed[1], 1)]
     for _ in range(3, places):
         down_pieces.append(along(down_pieces[-1], 1))
-    mixed, second_low, joined, out_weight = mix(
+    wo_far = core_swap(wo_near)
+    mixed, second_low, second_turned, joined, out_weight = mix(
         wo_meta, chip_tokens, attended_low, their_attended, gains[1:2], wo_near, wo_far
     )
     down_meta = [step * places + order[index] for index in range(places) for step in steps]
@@ -1165,7 +1209,7 @@
         for spot in range(places // 2):
             down_meta += [step * places + side * (places // 2) + spot for step in steps]
     (out_part, back_part), gu_grads, down_grads = feed(
-        gu_pieces, down_pieces, jnp.stack(steps + down_meta), second_low, chip_cot, chips, places
+        gu_pieces, down_pieces, jnp.stack(steps + down_meta), second_low, second_turned, chip_cot, chips, places
     )
     add = lambda a, b: total([a, b]).astype(bf16)
     gu_arrived = scatter_plane(gu_grads)
@@ -1179,7 +1223,6 @@
     attn_grads = weight_grads(
         attn_pieces,
         pair_meta,
-        rows_full,
         turned,
         dq,
         dkv,
@@ -1199,10 +1242,14 @@
         (attn_grads, gu_arrived, down_moving, back_arrived)
     )[:3]
     attn_arrived = [attn_grads[0]] + [plane_swap(attn_grads[step], step) for step in range(1, min(chips, 3))]
-    gu_sum = total(gu_arrived).astype(bf16).reshape(2, 2, places, rows, hidden // 2)
     down_sum = add(down_moving, down_grads[0])
     reach = places // 2
-    gu_kept, gu_sent = halves_along(gu_sum, 2, place)
+    if rows * reach % 16 == 0:
+        halves = cut_plane(gu_arrived, place // reach)
+        gu_kept, gu_sent = [part.reshape(2, 2, reach, rows, hidden // 2) for part in halves]
+    else:
+        gu_sum = total(gu_arrived).astype(bf16).reshape(2, 2, places, rows, hidden // 2)
+        gu_kept, gu_sent = halves_along(gu_sum, 2, place)
     gu_moving = across(gu_sent, reach)
     down_kept, down_sent = halves_along(down_sum, 0, place)
     down_moving = across(down_sent, reach // 2)
@@ -1233,10 +1280,10 @@
     attn_sum = spread(attn_cuts)
     merged = total([near_back, back_arrived]).astype(bf16)
     later_steps = [chips // 2 >> turn for turn in range(1, chips.bit_length() - 1)]
-    down_sum = after(summed_half(down_halves), attn_cuts)
-    own_down = finished(halved(down_sum, later_steps[0]), later_steps[1:])
     back_sum = summed_half(halved(after(merged, attn_cuts), 1))
     back_halves = halved(back_sum, 2)
+    down_sum = after(summed_half(down_halves), back_sum)
+    own_down = finished(halved(down_sum, later_steps[0]), later_steps[1:])
 
     weave = lambda parts: jnp.stack(
         [part.reshape(2, rows, chips, grain) for part in parts], axis=3
@@ -1248,7 +1295,9 @@
     ffout_new = update(
         ffout_weight, own_down, ffout_momentum, ffout_average, ffout_rate * inverse_root
     )
-    attn_sum, ffin_new, ffout_new, _ = lax.optimization_barrier((attn_sum, ffin_new, ffout_new, back_sum))
+    ffin_new += (ffin_new[0].astype(bf16),)
+    ffout_new += (ffout_new[0].astype(bf16),)
+    attn_sum, ffin_new, _ = lax.optimization_barrier((attn_sum, ffin_new, back_sum))
     first_grad = finished(back_halves, [2 << turn for turn in range(1, chips.bit_length() - 2)])
     summed, sent = last_sum(core, attn_sum)
     arrived = core_swap(sent)
@@ -1294,8 +1343,8 @@
         bias_new[2],
         gain_new[2],
         attn_new[3],
-        ffin_new[0].astype(bf16),
-        ffout_new[0].astype(bf16),
+        ffin_new[3],
+        ffout_new[3],
     )
 
 

time: 238 us -> 233 us (0.979)
  Pallas kernels: 86 us -> 82.4 us
  starting transfers between devices: 41.8 us -> 39.4 us
    pallas_call x1, Pallas kernels: 13.1 us -> 7.88 us  [retreat(): pl.pallas_call(retreat_kernel, grid_spec=pltpu.PrefetchScalarGridSpec(num...]
    ppermute x19, waiting for transfers between devices: 24.5 us -> 29 us  [plane_swap(): return lax.ppermute(value, 'seq', [(i, i ^ 2 * step) for i in range(count)])]
    pallas_call x0 -> x1, Pallas kernels: none -> 2.78 us  [cut_plane(): pl.pallas_call(cut_kernel, grid=(lead,), in_specs=[smem_spec()] + [row(he...]
    ppermute x12, starting transfers between devices: 14.2 us -> 11.6 us  [along(): lax.ppermute(value, 'batch', [(i, (i + step) % count) for i in range(coun...]
    unnamed x118 -> x100, local copies, waits for them, and re-layouts: 5.4 us -> 7.82 us
  transfers between devices with their start and end apart: 47 -> 47, of which waited for: 22 -> 22; matrix products, arithmetic and copies ran while one was open for 9% -> 9% of each run, Pallas kernels for 28% -> 29%
where the time goes in v4:
time: 233 us; the launch traced here: 232 us
  Pallas kernels  82.4 us (35%)
  waiting for transfers between devices  75.6 us (32%)
  starting transfers between devices  39.4 us (17%)
  other arithmetic  17.7 us (8%)
  local copies, waits for them, and re-layouts  15.5 us (7%)
    ppermute x19, waiting for transfers between devices, plane_swap(): return lax.ppermute(value, 'seq', [(i, i ^ 2 * step) for i in range(count)])  29 us
    ppermute x19, starting transfers between devices, plane_swap(): return lax.ppermute(value, 'seq', [(i, i ^ 2 * step) for i in range(count)])  23.8 us
    ppermute x12, waiting for transfers between devices, along(): lax.ppermute(value, 'batch', [(i, (i + step) % count) for i in range(coun...  22.8 us
    ppermute x4, waiting for transfers between devices, across(): return lax.ppermute(value, 'batch', [(i, i ^ step) for i in range(count)])  21.1 us
    pallas_call x1, Pallas kernels, attend(): pl.pallas_call(functools.partial(attend_kernel, len(pieces)), grid_spec=p...  12.7 us
    pallas_call x1, Pallas kernels, feed(): pl.pallas_call(functools.partial(feed_kernel, chips, places, len(gu_piece...  11.7 us
    ppermute x12, starting transfers between devices, along(): lax.ppermute(value, 'batch', [(i, (i + step) % count) for i in range(coun...  11.6 us
    pallas_call x1, Pallas kernels, retreat(): pl.pallas_call(retreat_kernel, grid_spec=pltpu.PrefetchScalarGridSpec(num...  7.88 us
  transfers between devices with their start and end apart: 47, of which 22 were waited for; matrix products, arithmetic and copies ran while one was open for 9% of the time, Pallas kernels for 29%

profile of v4, /device:TPU:0, one launch (start us, length us, event | category | flops | bytes accessed | tf_op | source)
XLA Modules:
  0.0 232.0 jit_solution(1488375072698153677)
XLA Ops:
  1.8 2.2 make_ready.1
  4.8 2.9 %collective-permute-start.2 = (bf16[1,208,768]{2,1,0:T(8,128)(2,1)}, bf16[1,208,768]{2,1,0:T(8,128)(2,1)S(1)}, u32[]{:S(2)}, u32[]{:S(2)}) collective-permute-start(bf16[1,208,768]{2,1,0:T(8,128)(2,1)} %bitcast.124), channel_id=1, source_target_pairs={{0,8},{4,12},{8,0},{12,4},{16,24},{20,28},{24,16},{28,20},{1,9},{5... | collective-permute-start | bytes 958472 | tf_op jit(solution)/shard_map/ppermute | solution.py:1001
  9.9 1.6 fill.2.refs_0_
  11.5 4.2 %collective-permute-done.2 = bf16[1,208,768]{2,1,0:T(8,128)(2,1)S(1)} collective-permute-done((bf16[1,208,768]{2,1,0:T(8,128)(2,1)}, bf16[1,208,768]{2,1,0:T(8,128)(2,1)S(1)}, u32[]{:S(2)}, u32[]{:S(2)}) %collective-permute-start.2) | collective-permute-done | bytes 319520 | tf_op jit(solution)/shard_map/ppermute | solution.py:1001
  16.8 1.8 collective-permute-start.5
  18.8 3.6 %collective-permute-start.8 = (bf16[4,2,24,384]{3,2,1,0:T(8,128)(2,1)}, bf16[4,2,24,384]{3,2,1,0:T(8,128)(2,1)S(1)}, u32[]{:S(2)}, u32[]{:S(2)}) collective-permute-start(bf16[4,2,24,384]{3,2,1,0:T(8,128)(2,1)} %fill.2.refs_0_), channel_id=1, source_target_pairs={{0,3},{1,0},{2,1},{3,2},{4,7},{5,4},{6,5},{7,6},{8,11},{9,8},{10,9... | collective-permute-start | bytes 442376 | tf_op jit(solution)/shard_map/ppermute | solution.py:1006
  24.7 1.7 fill.3.refs_0_
  26.3 4.0 %bias_rows.1.bias_ref = f32[6,640,128]{2,1,0:T(8,128)} custom-call(f32[32,6]{1,0:T(8,128)} %broadcast_select_fusion.4.table_ref), custom_call_target="tpu_custom_call" | custom-call | flops 1 | bytes 1 | tf_op jit(solution)/shard_map/bias_rows/pallas_call | solution.py:96
  30.4 4.3 %collective-permute-done.7.refs_2_ = bf16[4,2,24,384]{3,2,1,0:T(8,128)(2,1)S(1)} collective-permute-done((bf16[4,2,24,384]{3,2,1,0:T(8,128)(2,1)}, bf16[4,2,24,384]{3,2,1,0:T(8,128)(2,1)S(1)}, u32[]{:S(2)}, u32[]{:S(2)}) %collective-permute-start.7) | collective-permute-done | bytes 147488 | tf_op jit(solution)/shard_map/ppermute | solution.py:1006
  37.1 2.3 %join.2 = bf16[4,2,4,24,384]{4,3,2,1,0:T(8,128)(2,1)} custom-call(s32[4]{0:T(128)} %get-tuple-element.307.order_ref, bf16[4,2,24,384]{3,2,1,0:T(8,128)(2,1)} %fill.2.refs_0_, bf16[4,2,24,384]{3,2,1,0:T(8,128)(2,1)} %copy-done.38, bf16[4,2,24,384]{3,2,1,0:T(8,128)(2,1)} %copy-done.37, bf16[4,2,24,384]{3,2,1,0:T(8,128)(2,1)} %copy-done.36), custom_call_target="tpu_custom_call" | custom-call | flops 1 | bytes 1 | tf_op jit(solution)/shard_map/join/pallas_call | solution.py:1025
  40.0 1.4 collective-permute-start.12
  41.5 1.5 collective-permute-start.11
  44.6 4.2 %place_rows.1 = (bf16[1024,768]{1,0:T(8,128)(2,1)}, bf16[768,1024]{1,0:T(8,128)(2,1)}, f32[1024,256]{1,0:T(8,128)}) custom-call(s32[5]{0:T(128)} %stack.198.meta_ref, bf16[4,144,768]{2,1,0:T(8,128)(2,1)} %copy-done.4, bf16[4,144,768]{2,1,0:T(8,128)(2,1)} %collective-permute-done.9.far_ref), custom_call_target="tpu_custom_call" | custom-call | flops 1 | bytes 1 | tf_op jit(solution)/shard_map/place_rows/pallas_call | solution.py:234
  48.9 2.1 collective-permute-start.14
  52.4 6.2 %collective-permute-done.14.refs_2_ = bf16[2,2,24,1024]{3,2,1,0:T(8,128)(2,1)S(1)} collective-permute-done((bf16[2,2,24,1024]{3,2,1,0:T(8,128)(2,1)}, bf16[2,2,24,1024]{3,2,1,0:T(8,128)(2,1)S(1)}, u32[]{:S(2)}, u32[]{:S(2)}) %collective-permute-start.14) | collective-permute-done | bytes 196640 | tf_op jit(solution)/shard_map/ppermute | solution.py:1006
  60.9 9.1 %collective-permute-done.15.refs_3_ = bf16[2,2,24,1024]{3,2,1,0:T(8,128)(2,1)S(1)} collective-permute-done((bf16[2,2,24,1024]{3,2,1,0:T(8,128)(2,1)S(1)}, bf16[2,2,24,1024]{3,2,1,0:T(8,128)(2,1)S(1)}, u32[]{:S(2)}, u32[]{:S(2)}) %collective-permute-start.15) | collective-permute-done | bytes 196640 | tf_op jit(solution)/shard_map/ppermute | solution.py:1006
  70.7 2.2 join.3
  73.5 1.5 collective-permute-start.18
  75.0 12.7 %attend.1 = (bf16[256,384]{1,0:T(8,128)(2,1)}, bf16[1024,384]{1,0:T(8,128)(2,1)}, bf16[1024,384]{1,0:T(8,128)(2,1)}, f32[6,1024,256]{2,1,0:T(8,128)}, f32[256,38...) custom-call(s32[4]{0:T(128)} %get-tuple-element.308.meta_ref, ...), custom_call_target="tpu_custom_call" | custom-call | flops 1 | bytes 1 | tf_op jit(solution)/shard_map/attend/pallas_call | solution.py:328
  87.8 1.6 collective-permute-done.17.their_ref
  89.5 2.0 collective-permute-done.19.refs_2_
  94.2 1.5 collective-permute-start.22
  95.7 1.5 collective-permute-start.23
  100.0 4.9 %mix.1 = (f32[256,768]{1,0:T(8,128)}, bf16[256,768]{1,0:T(8,128)(2,1)}, bf16[768,256]{1,0:T(8,128)(2,1)}, bf16[768,256]{1,0:T(8,128)(2,1)}, bf16[768,768]{1,0:T(8,128)(2,1)}) custom-call(s32[9]{0:T(128)} %stack.212.meta_ref, f32[256,768]{1,0:T(8,128)} %pad_maximum_fusion.1.tokens_ref, bf16[256,384]{1,0:T(8,128)(2,1)} %get-tuple-element.181.own_ref, ...), custom_call_target="tpu_custom_call" | custom-call | flops 1 | bytes 1 | tf_op jit(solution)/shard_map/mix/pallas_call | solution.py:403
  107.3 3.0 %collective-permute-done.24.refs_8_ = bf16[4,64,768]{2,1,0:T(8,128)(2,1)} collective-permute-done((bf16[4,64,768]{2,1,0:T(8,128)(2,1)}, bf16[4,64,768]{2,1,0:T(8,128)(2,1)}, u32[]{:S(2)}, u32[]{:S(2)}) %collective-permute-start.24) | collective-permute-done | bytes 393248 | tf_op jit(solution)/shard_map/ppermute | solution.py:1006
  110.3 11.7 %feed.1 = (f32[256,768]{1,0:T(8,128)}, f32[256,768]{1,0:T(8,128)}, bf16[2,192,1024]{2,1,0:T(8,128)(2,1)}, bf16[2,192,1024]{2,1,0:T(8,128)(2,1)}, bf16[2,192,1024...) custom-call(s32[36]{0:T(128)} %stack.246.meta_ref, ...), custom_call_target="tpu_custom_call" | custom-call | flops 1 | bytes 1 | tf_op jit(solution)/shard_map/feed/pallas_call | solution.py:531
  123.7 2.4 %collective-permute-start.28 = (bf16[2,192,1024]{2,1,0:T(8,128)(2,1)}, bf16[2,192,1024]{2,1,0:T(8,128)(2,1)}, u32[]{:S(2)}, u32[]{:S(2)}) collective-permute-start(bf16[2,192,1024]{2,1,0:T(8,128)(2,1)} %get-tuple-element.223), channel_id=1, source_target_pairs={{0,24},{4,28},{8,16},{12,20},{16,8},{20,12},{24,0},{28,4},{1,25},{... | collective-permute-start | bytes 2359304 | tf_op jit(solution)/shard_map/ppermute | solution.py:1001
  127.1 3.7 %settle.1 = (f32[256,768]{1,0:T(8,128)}, bf16[256,384]{1,0:T(8,128)(2,1)}, f32[1,768]{1,0:T(1,128)}, bf16[256,768]{1,0:T(8,128)(2,1)}) custom-call(s32[1]{0:T(128)} %bitcast.1.core_ref.meta_ref, f32[256,768]{1,0:T(8,128)} %get-tuple-element.192.mixed_ref, f32[256,768]{1,0:T(8,128)} %pad_maximum_fusion.2.cot_ref, f32[256,768]{1,0:T(8,128)} %get-tuple-element.202.back_ref, ...), custom_call_target="tpu_custom_call" | custom-call | flops 1 | bytes 1 | tf_op jit(solution)/shard_map/settle/pallas_call | solution.py:593
  130.9 7.9 %retreat.1 = (bf16[256,384]{1,0:T(8,128)(2,1)}, bf16[1024,768]{1,0:T(8,128)(2,1)}, f32[3,8,128]{2,1,0:T(8,128)}) custom-call(s32[1]{0:T(128)} %bitcast.meta_ref, bf16[256,384]{1,0:T(8,128)(2,1)} %get-tuple-element.204.do_ref, f32[256,384]{1,0:T(8,128)} %get-tuple-element.205.o_ref, bf16[256,384]{1,0:T(8,128)(2,1)} %get-tuple-element.206.q_ref, ...), custom_call_target="tpu_custom_call" | custom-call | flops 1 | bytes 1 | tf_op jit(solution)/shard_map/retreat/pallas_call | solution.py:692
  138.7 7.3 %weight_grads.1 = (bf16[784,384]{1,0:T(8,128)(2,1)}, bf16[784,384]{1,0:T(8,128)(2,1)}, bf16[784,384]{1,0:T(8,128)(2,1)}, bf16[784,384]{1,0:T(8,128)(2,1)}) custom-call(s32[6]{0:T(128)} %stack.197.meta_ref, bf16[768,1024]{1,0:T(8,128)(2,1)} %get-tuple-element.164.turned_ref, bf16[256,384]{1,0:T(8,128)(2,1)} %get-tuple-element.225.dq_ref, ...), custom_call_target="tpu_custom_call" | custom-call | flops 1 | bytes 1 | tf_op jit(solution)/shard_map/weight_grads/pallas_call | solution.py:808
  146.0 5.9 %row_grads.1 = (bf16[4,128,768]{2,1,0:T(8,128)(2,1)}, bf16[4,128,768]{2,1,0:T(8,128)(2,1)}) custom-call(s32[6]{0:T(128)} %stack.197.meta_ref, bf16[256,384]{1,0:T(8,128)(2,1)} %get-tuple-element.225.dq_ref, bf16[1024,768]{1,0:T(8,128)(2,1)} %get-tuple-element.211.dkv_ref, bf16[4,192,384]{2,1,0:T(8,128)(2,1)} %bitcast.118, bf16[4,192,384]{2,1,0:T(8,128)(2,1)} %copy-done.3, ...), custom_call_target="tpu_custom_call" | custom-call | flops 1 | bytes 1 | tf_op jit(solution)/shard_map/row_grads/pallas_call | solution.py:856
  152.1 7.9 %collective-permute-done.27.refs_2_ = bf16[2,192,1024]{2,1,0:T(8,128)(2,1)} collective-permute-done((bf16[2,192,1024]{2,1,0:T(8,128)(2,1)}, bf16[2,192,1024]{2,1,0:T(8,128)(2,1)}, u32[]{:S(2)}, u32[]{:S(2)}) %collective-permute-start.27) | collective-permute-done | bytes 786464 | tf_op jit(solution)/shard_map/ppermute | solution.py:1001
  163.2 2.8 %cut_plane.1 = (bf16[2,2,48,1024]{3,2,1,0:T(8,128)(2,1)}, bf16[2,2,48,1024]{3,2,1,0:T(8,128)(2,1)}) custom-call(s32[1]{0:T(128)} %bitcast.54.side_ref, bf16[2,192,1024]{2,1,0:T(8,128)(2,1)} %get-tuple-element.230.refs_0_, bf16[2,192,1024]{2,1,0:T(8,128)(2,1)} %copy-done.19, bf16[2,192,1024]{2,1,0:T(8,128)(2,1)} %collective-permute-done.27.refs_2_, ...), custom_call_target="tpu_custom_call" | custom-call | flops 1 | bytes 1 | tf_op jit(solution)/shard_map/cut_plane/pallas_call | solution.py:886
  166.0 2.5 %collective-permute-start.33 = (bf16[2,2,2,24,1024]{4,3,2,1,0:T(8,128)(2,1)}, bf16[2,2,2,24,1024]{4,3,2,1,0:T(8,128)(2,1)S(1)}, u32[]{:S(2)}, u32[]{:S(2)}) collective-permute-start(bf16[2,2,2,24,1024]{4,3,2,1,0:T(8,128)(2,1)} %bitcast.131), channel_id=1, source_target_pairs={{0,2},{1,3},{2,0},{3,1},{4,6},{5,7},{6,4},{7,5},{8,10},{9,11},{10,... | collective-permute-start | bytes 1179656 | tf_op jit(solution)/shard_map/ppermute | solution.py:1068
  169.1 2.1 collective-permute-start.35
  171.4 6.3 %collective-permute-done.34 = bf16[1,4,64,768]{3,2,1,0:T(8,128)(2,1)S(1)} collective-permute-done((bf16[1,4,64,768]{3,2,1,0:T(8,128)(2,1)}, bf16[1,4,64,768]{3,2,1,0:T(8,128)(2,1)S(1)}, u32[]{:S(2)}, u32[]{:S(2)}) %collective-permute-start.34) | collective-permute-done | bytes 393248 | tf_op jit(solution)/shard_map/ppermute | solution.py:1068
  177.7 8.3 %collective-permute-done.33 = bf16[2,2,2,24,1024]{4,3,2,1,0:T(8,128)(2,1)S(1)} collective-permute-done((bf16[2,2,2,24,1024]{4,3,2,1,0:T(8,128)(2,1)}, bf16[2,2,2,24,1024]{4,3,2,1,0:T(8,128)(2,1)S(1)}, u32[]{:S(2)}, u32[]{:S(2)}) %collective-permute-start.33) | collective-permute-done | bytes 393248 | tf_op jit(solution)/shard_map/ppermute | solution.py:1068
  186.0 4.1 %collective-permute-done.32.refs_2_ = bf16[784,384]{1,0:T(8,128)(2,1)} collective-permute-done((bf16[784,384]{1,0:T(8,128)(2,1)}, bf16[784,384]{1,0:T(8,128)(2,1)}, u32[]{:S(2)}, u32[]{:S(2)}) %collective-permute-start.32) | collective-permute-done | bytes 602144 | tf_op jit(solution)/shard_map/ppermute | solution.py:1001
  190.8 5.3 %collective-permute-done.36 = bf16[2,2,1,24,1024]{4,3,2,1,0:T(8,128)(2,1)S(1)} collective-permute-done((bf16[2,2,1,24,1024]{4,3,2,1,0:T(8,128)(2,1)S(1)}, bf16[2,2,1,24,1024]{4,3,2,1,0:T(8,128)(2,1)S(1)}, u32[]{:S(2)}, u32[]{:S(2)}) %collective-permute-start.36) | collective-permute-done | bytes 196640 | tf_op jit(solution)/shard_map/ppermute | solution.py:1068
  198.2 2.9 %sum_plane.1 = (bf16[208,384]{1,0:T(8,128)(2,1)}, bf16[208,384]{1,0:T(8,128)(2,1)}, bf16[208,384]{1,0:T(8,128)(2,1)}, bf16[208,384]{1,0:T(8,128)(2,1)}) custom-call(s32[4]{0:T(128)} %pad_add_fusion.2.order_ref, bf16[784,384]{1,0:T(8,128)(2,1)} %get-tuple-element.249.refs_0_, bf16[784,384]{1,0:T(8,128)(2,1)} %collective-permute-done.31.refs_1_, ...), custom_call_target="tpu_custom_call" | custom-call | flops 1 | bytes 1 | tf_op jit(solution)/shard_map/sum_plane/pallas_call | solution.py:922
  201.1 2.0 collective-permute-start.41
  203.1 2.4 %collective-permute-start.43 = (bf16[208,384]{1,0:T(8,128)(2,1)}, bf16[208,384]{1,0:T(8,128)(2,1)}, u32[]{:S(2)}, u32[]{:S(2)}) collective-permute-start(bf16[208,384]{1,0:T(8,128)(2,1)} %get-tuple-element.256), channel_id=1, source_target_pairs={{0,3},{1,0},{2,1},{3,2},{4,7},{5,4},{6,5},{7,6},{8,11},{9,8},{10,9... | collective-permute-start | bytes 479240 | tf_op jit(solution)/shard_map/ppermute | solution.py:1006
  205.5 1.6 collective-permute-start.39
  208.4 1.9 fusion.7
  210.3 6.3 %collective-permute-done.39 = bf16[2,128,768]{2,1,0:T(8,128)(2,1)} collective-permute-done((bf16[2,128,768]{2,1,0:T(8,128)(2,1)S(1)}, bf16[2,128,768]{2,1,0:T(8,128)(2,1)}, u32[]{:S(2)}, u32[]{:S(2)}) %collective-permute-start.39) | collective-permute-done | bytes 393248 | tf_op jit(solution)/shard_map/ppermute | solution.py:1001
  217.7 1.6 collective-permute-start.46
  220.8 2.0 last_sum.1
  227.1 2.3 attention_update.1
  (220 shorter events, 45.0 us)
Async XLA Ops:
  0.7 3.3 %collective-permute-start.1 = (f32[128,768]{1,0:T(8,128)}, f32[128,768]{1,0:T(8,128)S(1)}, u32[]{:S(2)}, u32[]{:S(2)}) collective-permute-start(f32[128,768]{1,0:T(8,128)} %bitcast.130), channel_id=1, source_target_pairs={{0,4},{4,0},{8,12},{12,8},{16,20},{20,16},{24,28},{28,24},{1,5},{5... | collective-permute-start | bytes 1179656 | tf_op jit(solution)/shard_map/ppermute | solution.py:996
  1.2 2.8 %collective-permute-start = (f32[128,768]{1,0:T(8,128)}, f32[128,768]{1,0:T(8,128)S(1)}, u32[]{:S(2)}, u32[]{:S(2)}) collective-permute-start(f32[128,768]{1,0:T(8,128)} %bitcast.119), channel_id=1, source_target_pairs={{0,4},{4,0},{8,12},{12,8},{16,20},{20,16},{24,28},{28,24},{1,5},{5... | collective-permute-start | bytes 1179656 | tf_op jit(solution)/shard_map/ppermute | solution.py:996
  4.8 10.9 %collective-permute-start.2 = (bf16[1,208,768]{2,1,0:T(8,128)(2,1)}, bf16[1,208,768]{2,1,0:T(8,128)(2,1)S(1)}, u32[]{:S(2)}, u32[]{:S(2)}) collective-permute-start(bf16[1,208,768]{2,1,0:T(8,128)(2,1)} %bitcast.124), channel_id=1, source_target_pairs={{0,8},{4,12},{8,0},{12,4},{16,24},{20,28},{24,16},{28,20},{1,9},{5... | collective-permute-start | bytes 958472 | tf_op jit(solution)/shard_map/ppermute | solution.py:1001
  7.7 1.5 collective-permute-start.3
  7.7 1.6 collective-permute-start.4
  16.8 19.2 %collective-permute-start.5 = (bf16[2,208,768]{2,1,0:T(8,128)(2,1)S(1)}, bf16[2,208,768]{2,1,0:T(8,128)(2,1)S(1)}, u32[]{:S(2)}, u32[]{:S(2)}) collective-permute-start(bf16[2,208,768]{2,1,0:T(8,128)(2,1)S(1)} %pad_maximum_fusion.3), channel_id=1, source_target_pairs={{0,16},{4,20},{8,24},{12,28},{16,0},{20,4},{24,8},{28,12},{1,17},{... | collective-permute-start | bytes 1916936 | tf_op jit(solution)/shard_map/ppermute | solution.py:1001
  18.8 11.6 %collective-permute-start.8 = (bf16[4,2,24,384]{3,2,1,0:T(8,128)(2,1)}, bf16[4,2,24,384]{3,2,1,0:T(8,128)(2,1)S(1)}, u32[]{:S(2)}, u32[]{:S(2)}) collective-permute-start(bf16[4,2,24,384]{3,2,1,0:T(8,128)(2,1)} %fill.2.refs_0_), channel_id=1, source_target_pairs={{0,3},{1,0},{2,1},{3,2},{4,7},{5,4},{6,5},{7,6},{8,11},{9,8},{10,9... | collective-permute-start | bytes 442376 | tf_op jit(solution)/shard_map/ppermute | solution.py:1006
  22.4 12.2 %collective-permute-start.7 = (bf16[4,2,24,384]{3,2,1,0:T(8,128)(2,1)}, bf16[4,2,24,384]{3,2,1,0:T(8,128)(2,1)S(1)}, u32[]{:S(2)}, u32[]{:S(2)}) collective-permute-start(bf16[4,2,24,384]{3,2,1,0:T(8,128)(2,1)} %fill.2.refs_0_), channel_id=1, source_target_pairs={{0,2},{1,3},{2,0},{3,1},{4,6},{5,7},{6,4},{7,5},{8,10},{9,11},{10,... | collective-permute-start | bytes 442376 | tf_op jit(solution)/shard_map/ppermute | solution.py:1006
  22.4 12.2 %collective-permute-start.6 = (bf16[4,2,24,384]{3,2,1,0:T(8,128)(2,1)}, bf16[4,2,24,384]{3,2,1,0:T(8,128)(2,1)S(1)}, u32[]{:S(2)}, u32[]{:S(2)}) collective-permute-start(bf16[4,2,24,384]{3,2,1,0:T(8,128)(2,1)} %fill.2.refs_0_), channel_id=1, source_target_pairs={{0,1},{1,2},{2,3},{3,0},{4,5},{5,6},{6,7},{7,4},{8,9},{9,10},{10,1... | collective-permute-start | bytes 442376 | tf_op jit(solution)/shard_map/ppermute | solution.py:1006
  39.4 5.1 %collective-permute-start.9 = (bf16[4,144,768]{2,1,0:T(8,128)(2,1)S(1)}, bf16[4,144,768]{2,1,0:T(8,128)(2,1)}, u32[]{:S(2)}, u32[]{:S(2)}) collective-permute-start(bf16[4,144,768]{2,1,0:T(8,128)(2,1)S(1)} %slice.114.near_ref), channel_id=1, source_target_pairs={{0,4},{4,0},{8,12},{12,8},{16,20},{20,16},{24,28},{28,24},{1,5},{5... | collective-permute-start | bytes 2654216 | tf_op jit(solution)/shard_map/ppermute | solution.py:996
  39.4 9.4 %collective-permute-start.13 = (bf16[2,2,24,1024]{3,2,1,0:T(8,128)(2,1)}, bf16[2,2,24,1024]{3,2,1,0:T(8,128)(2,1)}, u32[]{:S(2)}, u32[]{:S(2)}) collective-permute-start(bf16[2,2,24,1024]{3,2,1,0:T(8,128)(2,1)} %fill.3.refs_0_), channel_id=1, source_target_pairs={{0,1},{1,2},{2,3},{3,0},{4,5},{5,6},{6,7},{7,4},{8,9},{9,10},{10,1... | collective-permute-start | bytes 589832 | tf_op jit(solution)/shard_map/ppermute | solution.py:1006
  40.0 32.9 %collective-permute-start.12 = (bf16[4,192,384]{2,1,0:T(8,128)(2,1)}, bf16[4,192,384]{2,1,0:T(8,128)(2,1)S(1)}, u32[]{:S(2)}, u32[]{:S(2)}) collective-permute-start(bf16[4,192,384]{2,1,0:T(8,128)(2,1)} %bitcast.113), channel_id=1, source_target_pairs={{0,24},{4,28},{8,16},{12,20},{16,8},{20,12},{24,0},{28,4},{1,25},{... | collective-permute-start | bytes 1769480 | tf_op jit(solution)/shard_map/ppermute | solution.py:1001
  41.5 31.4 %collective-permute-start.11 = (bf16[4,192,384]{2,1,0:T(8,128)(2,1)}, bf16[4,192,384]{2,1,0:T(8,128)(2,1)S(1)}, u32[]{:S(2)}, u32[]{:S(2)}) collective-permute-start(bf16[4,192,384]{2,1,0:T(8,128)(2,1)} %bitcast.114), channel_id=1, source_target_pairs={{0,16},{4,20},{8,24},{12,28},{16,0},{20,4},{24,8},{28,12},{1,17},{... | collective-permute-start | bytes 1769480 | tf_op jit(solution)/shard_map/ppermute | solution.py:1001
  43.0 29.9 %collective-permute-start.10 = (bf16[4,192,384]{2,1,0:T(8,128)(2,1)}, bf16[4,192,384]{2,1,0:T(8,128)(2,1)S(1)}, u32[]{:S(2)}, u32[]{:S(2)}) collective-permute-start(bf16[4,192,384]{2,1,0:T(8,128)(2,1)} %bitcast.115), channel_id=1, source_target_pairs={{0,8},{4,12},{8,0},{12,4},{16,24},{20,28},{24,16},{28,20},{1,9},{5... | collective-permute-start | bytes 1769480 | tf_op jit(solution)/shard_map/ppermute | solution.py:1001
  48.9 9.8 %collective-permute-start.14 = (bf16[2,2,24,1024]{3,2,1,0:T(8,128)(2,1)}, bf16[2,2,24,1024]{3,2,1,0:T(8,128)(2,1)S(1)}, u32[]{:S(2)}, u32[]{:S(2)}) collective-permute-start(bf16[2,2,24,1024]{3,2,1,0:T(8,128)(2,1)} %collective-permute-done.13.refs_1_), channel_id=1, source_target_pairs={{0,1},{1,2},{2,3},{3,0},{4,5},{5,6},{6,7},{7,4},{8,9},{9,10},{10,1... | collective-permute-start | bytes 589832 | tf_op jit(solution)/shard_map/ppermute | solution.py:1006
  51.0 21.9 %collective-permute-start.16 = (bf16[4,64,768]{2,1,0:T(8,128)(2,1)S(1)}, bf16[4,64,768]{2,1,0:T(8,128)(2,1)}, u32[]{:S(2)}, u32[]{:S(2)}) collective-permute-start(bf16[4,64,768]{2,1,0:T(8,128)(2,1)S(1)} %pad_maximum_fusion.4.refs_5_), channel_id=1, source_target_pairs={{0,1},{1,2},{2,3},{3,0},{4,5},{5,6},{6,7},{7,4},{8,9},{9,10},{10,1... | collective-permute-start | bytes 1179656 | tf_op jit(solution)/shard_map/ppermute | solution.py:1006
  58.7 11.4 %collective-permute-start.15 = (bf16[2,2,24,1024]{3,2,1,0:T(8,128)(2,1)S(1)}, bf16[2,2,24,1024]{3,2,1,0:T(8,128)(2,1)S(1)}, u32[]{:S(2)}, u32[]{:S(2)}) collective-permute-start(bf16[2,2,24,1024]{3,2,1,0:T(8,128)(2,1)S(1)} %collective-permute-done.14.refs_2_), channel_id=1, source_target_pairs={{0,1},{1,2},{2,3},{3,0},{4,5},{5,6},{6,7},{7,4},{8,9},{9,10},{10,1... | collective-permute-start | bytes 589832 | tf_op jit(solution)/shard_map/ppermute | solution.py:1006
  72.9 18.6 %collective-permute-start.19 = (bf16[2,192,1024]{2,1,0:T(8,128)(2,1)}, bf16[2,192,1024]{2,1,0:T(8,128)(2,1)S(1)}, u32[]{:S(2)}, u32[]{:S(2)}) collective-permute-start(bf16[2,192,1024]{2,1,0:T(8,128)(2,1)} %bitcast.121), channel_id=1, source_target_pairs={{0,16},{4,20},{8,24},{12,28},{16,0},{20,4},{24,8},{28,12},{1,17},{... | collective-permute-start | bytes 2359304 | tf_op jit(solution)/shard_map/ppermute | solution.py:1001
  73.5 18.2 %collective-permute-start.18 = (bf16[2,192,1024]{2,1,0:T(8,128)(2,1)}, bf16[2,192,1024]{2,1,0:T(8,128)(2,1)S(1)}, u32[]{:S(2)}, u32[]{:S(2)}) collective-permute-start(bf16[2,192,1024]{2,1,0:T(8,128)(2,1)} %bitcast.122), channel_id=1, source_target_pairs={{0,8},{4,12},{8,0},{12,4},{16,24},{20,28},{24,16},{28,20},{1,9},{5... | collective-permute-start | bytes 2359304 | tf_op jit(solution)/shard_map/ppermute | solution.py:1001
  75.0 14.5 %collective-permute-start.20 = (bf16[4,64,768]{2,1,0:T(8,128)(2,1)}, bf16[4,64,768]{2,1,0:T(8,128)(2,1)}, u32[]{:S(2)}, u32[]{:S(2)}) collective-permute-start(bf16[4,64,768]{2,1,0:T(8,128)(2,1)} %collective-permute-done.16.refs_6_), channel_id=1, source_target_pairs={{0,1},{1,2},{2,3},{3,0},{4,5},{5,6},{6,7},{7,4},{8,9},{9,10},{10,1... | collective-permute-start | bytes 1179656 | tf_op jit(solution)/shard_map/ppermute | solution.py:1006
  87.8 1.7 collective-permute-start.17
  94.2 4.9 %collective-permute-start.21 = (bf16[4,192,384]{2,1,0:T(8,128)(2,1)S(1)}, bf16[4,192,384]{2,1,0:T(8,128)(2,1)S(1)}, u32[]{:S(2)}, u32[]{:S(2)}) collective-permute-start(bf16[4,192,384]{2,1,0:T(8,128)(2,1)S(1)} %copy-done.21), channel_id=1, source_target_pairs={{0,4},{4,0},{8,12},{12,8},{16,20},{20,16},{24,28},{28,24},{1,5},{5... | collective-permute-start | bytes 1769480 | tf_op jit(solution)/shard_map/ppermute | solution.py:996
  94.2 11.7 %collective-permute-start.22 = (bf16[1,192,1024]{2,1,0:T(8,128)(2,1)}, bf16[1,192,1024]{2,1,0:T(8,128)(2,1)S(1)}, u32[]{:S(2)}, u32[]{:S(2)}) collective-permute-start(bf16[1,192,1024]{2,1,0:T(8,128)(2,1)} %slice.92), channel_id=1, source_target_pairs={{0,16},{4,20},{8,24},{12,28},{16,0},{20,4},{24,8},{28,12},{1,17},{... | collective-permute-start | bytes 1179656 | tf_op jit(solution)/shard_map/ppermute | solution.py:1001
  95.7 11.6 %collective-permute-start.23 = (bf16[1,192,1024]{2,1,0:T(8,128)(2,1)}, bf16[1,192,1024]{2,1,0:T(8,128)(2,1)}, u32[]{:S(2)}, u32[]{:S(2)}) collective-permute-start(bf16[1,192,1024]{2,1,0:T(8,128)(2,1)} %slice.93), channel_id=1, source_target_pairs={{0,8},{4,12},{8,0},{12,4},{16,24},{20,28},{24,16},{28,20},{1,9},{5... | collective-permute-start | bytes 1179656 | tf_op jit(solution)/shard_map/ppermute | solution.py:1001
  97.2 13.1 %collective-permute-start.24 = (bf16[4,64,768]{2,1,0:T(8,128)(2,1)}, bf16[4,64,768]{2,1,0:T(8,128)(2,1)}, u32[]{:S(2)}, u32[]{:S(2)}) collective-permute-start(bf16[4,64,768]{2,1,0:T(8,128)(2,1)} %collective-permute-done.20.refs_7_), channel_id=1, source_target_pairs={{0,1},{1,2},{2,3},{3,0},{4,5},{5,6},{6,7},{7,4},{8,9},{9,10},{10,1... | collective-permute-start | bytes 1179656 | tf_op jit(solution)/shard_map/ppermute | solution.py:1006
  122.0 4.2 %collective-permute-start.25 = (f32[256,768]{1,0:T(8,128)}, f32[256,768]{1,0:T(8,128)S(1)}, u32[]{:S(2)}, u32[]{:S(2)}) collective-permute-start(f32[256,768]{1,0:T(8,128)} %get-tuple-element.202.back_ref), channel_id=1, source_target_pairs={{0,4},{4,0},{8,12},{12,8},{16,20},{20,16},{24,28},{28,24},{1,5},{5... | collective-permute-start | bytes 2359304 | tf_op jit(solution)/shard_map/ppermute | solution.py:996
  122.7 29.4 %collective-permute-start.26 = (bf16[2,192,1024]{2,1,0:T(8,128)(2,1)}, bf16[2,192,1024]{2,1,0:T(8,128)(2,1)S(1)}, u32[]{:S(2)}, u32[]{:S(2)}) collective-permute-start(bf16[2,192,1024]{2,1,0:T(8,128)(2,1)} %get-tuple-element.221), channel_id=1, source_target_pairs={{0,8},{4,12},{8,0},{12,4},{16,24},{20,28},{24,16},{28,20},{1,9},{5... | collective-permute-start | bytes 2359304 | tf_op jit(solution)/shard_map/ppermute | solution.py:1001
  123.2 36.8 %collective-permute-start.27 = (bf16[2,192,1024]{2,1,0:T(8,128)(2,1)}, bf16[2,192,1024]{2,1,0:T(8,128)(2,1)}, u32[]{:S(2)}, u32[]{:S(2)}) collective-permute-start(bf16[2,192,1024]{2,1,0:T(8,128)(2,1)} %get-tuple-element.222), channel_id=1, source_target_pairs={{0,16},{4,20},{8,24},{12,28},{16,0},{20,4},{24,8},{28,12},{1,17},{... | collective-permute-start | bytes 2359304 | tf_op jit(solution)/shard_map/ppermute | solution.py:1001
  123.7 36.3 %collective-permute-start.28 = (bf16[2,192,1024]{2,1,0:T(8,128)(2,1)}, bf16[2,192,1024]{2,1,0:T(8,128)(2,1)}, u32[]{:S(2)}, u32[]{:S(2)}) collective-permute-start(bf16[2,192,1024]{2,1,0:T(8,128)(2,1)} %get-tuple-element.223), channel_id=1, source_target_pairs={{0,24},{4,28},{8,16},{12,20},{16,8},{20,12},{24,0},{28,4},{1,25},{... | collective-permute-start | bytes 2359304 | tf_op jit(solution)/shard_map/ppermute | solution.py:1001
  126.2 35.0 %collective-permute-start.29 = (bf16[2,4,64,768]{3,2,1,0:T(8,128)(2,1)}, bf16[2,4,64,768]{3,2,1,0:T(8,128)(2,1)S(1)}, u32[]{:S(2)}, u32[]{:S(2)}) collective-permute-start(bf16[2,4,64,768]{3,2,1,0:T(8,128)(2,1)} %get-tuple-element.224), channel_id=1, source_target_pairs={{0,2},{1,3},{2,0},{3,1},{4,6},{5,7},{6,4},{7,5},{8,10},{9,11},{10,... | collective-permute-start | bytes 2359304 | tf_op jit(solution)/shard_map/ppermute | solution.py:1068
  152.0 9.2 %collective-permute-start.30 = (bf16[4,128,768]{2,1,0:T(8,128)(2,1)}, bf16[4,128,768]{2,1,0:T(8,128)(2,1)S(1)}, u32[]{:S(2)}, u32[]{:S(2)}) collective-permute-start(bf16[4,128,768]{2,1,0:T(8,128)(2,1)} %get-tuple-element.226), channel_id=1, source_target_pairs={{0,4},{4,0},{8,12},{12,8},{16,20},{20,16},{24,28},{28,24},{1,5},{5... | collective-permute-start | bytes 2359304 | tf_op jit(solution)/shard_map/ppermute | solution.py:996
  161.2 24.9 %collective-permute-start.31 = (bf16[784,384]{1,0:T(8,128)(2,1)}, bf16[784,384]{1,0:T(8,128)(2,1)}, u32[]{:S(2)}, u32[]{:S(2)}) collective-permute-start(bf16[784,384]{1,0:T(8,128)(2,1)} %get-tuple-element.228), channel_id=1, source_target_pairs={{0,8},{4,12},{8,0},{12,4},{16,24},{20,28},{24,16},{28,20},{1,9},{5... | collective-permute-start | bytes 1806344 | tf_op jit(solution)/shard_map/ppermute | solution.py:1001
  161.7 28.5 %collective-permute-start.32 = (bf16[784,384]{1,0:T(8,128)(2,1)}, bf16[784,384]{1,0:T(8,128)(2,1)}, u32[]{:S(2)}, u32[]{:S(2)}) collective-permute-start(bf16[784,384]{1,0:T(8,128)(2,1)} %get-tuple-element.229), channel_id=1, source_target_pairs={{0,16},{4,20},{8,24},{12,28},{16,0},{20,4},{24,8},{28,12},{1,17},{... | collective-permute-start | bytes 1806344 | tf_op jit(solution)/shard_map/ppermute | solution.py:1001
  163.2 14.6 %collective-permute-start.34 = (bf16[1,4,64,768]{3,2,1,0:T(8,128)(2,1)}, bf16[1,4,64,768]{3,2,1,0:T(8,128)(2,1)S(1)}, u32[]{:S(2)}, u32[]{:S(2)}) collective-permute-start(bf16[1,4,64,768]{3,2,1,0:T(8,128)(2,1)} %constant_dynamic-slice_fusion.2), channel_id=1, source_target_pairs={{0,1},{1,0},{2,3},{3,2},{4,5},{5,4},{6,7},{7,6},{8,9},{9,8},{10,11... | collective-permute-start | bytes 1179656 | tf_op jit(solution)/shard_map/ppermute | solution.py:1068
  166.0 24.2 %copy-start.25 = (bf16[2,2,48,1024]{3,2,1,0:T(8,128)(2,1)S(1)}, bf16[2,2,48,1024]{3,2,1,0:T(8,128)(2,1)}, u32[]{:S(2)}) copy-start(bf16[2,2,48,1024]{3,2,1,0:T(8,128)(2,1)} %get-tuple-element.242) | copy-start | bytes 1179652
  166.0 20.1 %collective-permute-start.33 = (bf16[2,2,2,24,1024]{4,3,2,1,0:T(8,128)(2,1)}, bf16[2,2,2,24,1024]{4,3,2,1,0:T(8,128)(2,1)S(1)}, u32[]{:S(2)}, u32[]{:S(2)}) collective-permute-start(bf16[2,2,2,24,1024]{4,3,2,1,0:T(8,128)(2,1)} %bitcast.131), channel_id=1, source_target_pairs={{0,2},{1,3},{2,0},{3,1},{4,6},{5,7},{6,4},{7,5},{8,10},{9,11},{10,... | collective-permute-start | bytes 1179656 | tf_op jit(solution)/shard_map/ppermute | solution.py:1068
  169.1 27.9 %collective-permute-start.35 = (bf16[784,384]{1,0:T(8,128)(2,1)}, bf16[784,384]{1,0:T(8,128)(2,1)}, u32[]{:S(2)}, u32[]{:S(2)}) collective-permute-start(bf16[784,384]{1,0:T(8,128)(2,1)} %get-tuple-element.241), channel_id=1, source_target_pairs={{0,24},{4,28},{8,16},{12,20},{16,8},{20,12},{24,0},{28,4},{1,25},{... | collective-permute-start | bytes 1806344 | tf_op jit(solution)/shard_map/ppermute | solution.py:1001
  190.3 5.7 %collective-permute-start.36 = (bf16[2,2,1,24,1024]{4,3,2,1,0:T(8,128)(2,1)S(1)}, bf16[2,2,1,24,1024]{4,3,2,1,0:T(8,128)(2,1)S(1)}, u32[]{:S(2)}, u32[]{:S(2)}) collective-permute-start(bf16[2,2,1,24,1024]{4,3,2,1,0:T(8,128)(2,1)S(1)} %constant_dynamic-slice_fusion.1), channel_id=1, source_target_pairs={{0,1},{1,0},{2,3},{3,2},{4,5},{5,4},{6,7},{7,6},{8,9},{9,8},{10,11... | collective-permute-start | bytes 589832 | tf_op jit(solution)/shard_map/ppermute | solution.py:1068
  190.5 5.6 %collective-permute-start.38 = (f32[128,768]{1,0:T(8,128)S(1)}, f32[128,768]{1,0:T(8,128)S(1)}, u32[]{:S(2)}, u32[]{:S(2)}) collective-permute-start(f32[128,768]{1,0:T(8,128)S(1)} %constant_dynamic-slice_fusion), channel_id=1, source_target_pairs={{0,4},{4,0},{8,12},{12,8},{16,20},{20,16},{24,28},{28,24},{1,5},{5... | collective-permute-start | bytes 1179656 | tf_op jit(solution)/shard_map/ppermute | solution.py:996
  190.7 7.4 %collective-permute-start.37 = (bf16[2,64,768]{2,1,0:T(8,128)(2,1)S(1)}, bf16[2,64,768]{2,1,0:T(8,128)(2,1)S(1)}, u32[]{:S(2)}, u32[]{:S(2)}) collective-permute-start(bf16[2,64,768]{2,1,0:T(8,128)(2,1)S(1)} %get-tuple-element.296), channel_id=1, source_target_pairs={{0,16},{4,20},{8,24},{12,28},{16,0},{20,4},{24,8},{28,12},{1,17},{... | collective-permute-start | bytes 589832 | tf_op jit(solution)/shard_map/ppermute | solution.py:1001
  198.1 9.1 %collective-permute-start.44 = (f32[2,24,1024]{2,1,0:T(8,128)S(1)}, f32[2,24,1024]{2,1,0:T(8,128)S(1)}, u32[]{:S(2)}, u32[]{:S(2)}) collective-permute-start(f32[2,24,1024]{2,1,0:T(8,128)S(1)} %fusion.3), channel_id=1, source_target_pairs={{0,4},{4,0},{8,12},{12,8},{16,20},{20,16},{24,28},{28,24},{1,5},{5... | collective-permute-start | bytes 589832 | tf_op jit(solution)/shard_map/ppermute | solution.py:996
  201.1 19.0 %collective-permute-start.41 = (bf16[208,384]{1,0:T(8,128)(2,1)}, bf16[208,384]{1,0:T(8,128)(2,1)S(1)}, u32[]{:S(2)}, u32[]{:S(2)}) collective-permute-start(bf16[208,384]{1,0:T(8,128)(2,1)} %get-tuple-element.254), channel_id=1, source_target_pairs={{0,1},{1,2},{2,3},{3,0},{4,5},{5,6},{6,7},{7,4},{8,9},{9,10},{10,1... | collective-permute-start | bytes 479240 | tf_op jit(solution)/shard_map/ppermute | solution.py:1006
  203.1 17.1 %collective-permute-start.42 = (bf16[208,384]{1,0:T(8,128)(2,1)}, bf16[208,384]{1,0:T(8,128)(2,1)}, u32[]{:S(2)}, u32[]{:S(2)}) collective-permute-start(bf16[208,384]{1,0:T(8,128)(2,1)} %get-tuple-element.255), channel_id=1, source_target_pairs={{0,2},{1,3},{2,0},{3,1},{4,6},{5,7},{6,4},{7,5},{8,10},{9,11},{10,... | collective-permute-start | bytes 479240 | tf_op jit(solution)/shard_map/ppermute | solution.py:1006
  203.1 17.1 %collective-permute-start.43 = (bf16[208,384]{1,0:T(8,128)(2,1)}, bf16[208,384]{1,0:T(8,128)(2,1)}, u32[]{:S(2)}, u32[]{:S(2)}) collective-permute-start(bf16[208,384]{1,0:T(8,128)(2,1)} %get-tuple-element.256), channel_id=1, source_target_pairs={{0,3},{1,0},{2,1},{3,2},{4,7},{5,4},{6,5},{7,6},{8,11},{9,8},{10,9... | collective-permute-start | bytes 479240 | tf_op jit(solution)/shard_map/ppermute | solution.py:1006
  205.5 11.1 %collective-permute-start.39 = (bf16[2,128,768]{2,1,0:T(8,128)(2,1)S(1)}, bf16[2,128,768]{2,1,0:T(8,128)(2,1)}, u32[]{:S(2)}, u32[]{:S(2)}) collective-permute-start(bf16[2,128,768]{2,1,0:T(8,128)(2,1)S(1)} %slice.101), channel_id=1, source_target_pairs={{0,8},{4,12},{8,0},{12,4},{16,24},{20,28},{24,16},{28,20},{1,9},{5... | collective-permute-start | bytes 1179656 | tf_op jit(solution)/shard_map/ppermute | solution.py:1001
  217.7 6.4 %collective-permute-start.46 = (bf16[1,64,768]{2,1,0:T(8,128)(2,1)S(1)}, bf16[1,64,768]{2,1,0:T(8,128)(2,1)S(1)}, u32[]{:S(2)}, u32[]{:S(2)}) collective-permute-start(bf16[1,64,768]{2,1,0:T(8,128)(2,1)S(1)} %slice.107), channel_id=1, source_target_pairs={{0,8},{4,12},{8,0},{12,4},{16,24},{20,28},{24,16},{28,20},{1,9},{5... | collective-permute-start | bytes 294920 | tf_op jit(solution)/shard_map/ppermute | solution.py:1001
  223.5 2.1 collective-permute-start.45
  223.6 7.3 %collective-permute-start.40 = (bf16[1,128,768]{2,1,0:T(8,128)(2,1)S(1)}, bf16[1,128,768]{2,1,0:T(8,128)(2,1)S(1)}, u32[]{:S(2)}, u32[]{:S(2)}) collective-permute-start(bf16[1,128,768]{2,1,0:T(8,128)(2,1)S(1)} %slice.118), channel_id=1, source_target_pairs={{0,16},{4,20},{8,24},{12,28},{16,0},{20,4},{24,8},{28,12},{1,17},{... | collective-permute-start | bytes 589832 | tf_op jit(solution)/shard_map/ppermute | solution.py:1001
  (48 other events, 343.7 us)

commit v5 on v4

--- a/solution.py
+++ b/solution.py
@@ -1253,24 +1253,24 @@
     gu_moving = across(gu_sent, reach)
     down_kept, down_sent = halves_along(down_sum, 0, place)
     down_moving = across(down_sent, reach // 2)
+    attn_arrived += [plane_swap(attn_grads[step], step) for step in range(3, chips)]
     attn_arrived, gu_moving, down_moving, out_part = lax.optimization_barrier(
         (attn_arrived, gu_moving, down_moving, out_part)
     )
     their_out = core_swap(theirs(out_part))
-    last_attn = [plane_swap(attn_grads[step], step) for step in range(3, chips)]
-    while reach > 1:
+    while reach > 2:
         gu_kept, gu_sent = halves_along(add(gu_kept, gu_moving), 2, place)
         reach //= 2
         gu_moving = across(gu_sent, reach)
-        if reach > 1:
-            down_kept, down_sent = halves_along(add(down_kept, down_moving), 0, place)
-            down_moving = across(down_sent, reach // 2)
+        down_kept, down_sent = halves_along(add(down_kept, down_moving), 0, place)
+        down_moving = across(down_sent, reach // 2)
+    down_last = add(down_kept, down_moving)[0]
+    gu_kept, gu_sent = halves_along(add(gu_kept, gu_moving), 2, place)
+    attn_arrived, gu_sent, down_last = lax.optimization_barrier((attn_arrived, gu_sent, down_last))
+    down_halves = halved(down_last, chips // 2)
+    gu_moving = across(gu_sent, 1)
     gu_sum = total([gu_kept, gu_moving])[:, :, 0]
-    down_halves = halved(add(down_kept, down_moving)[0], chips // 2)
     layer_output = mine(mixed) + mine(out_part) + their_out
-    attn_arrived, gu_sum, down_halves, layer_output = lax.optimization_barrier(
-        (attn_arrived + last_attn, gu_sum, down_halves, layer_output)
-    )
     pick = lambda value, first, dim: jnp.where(
         first, lax.index_in_dim(value, 0, dim, False), lax.index_in_dim(value, 1, dim, False)
     )
@@ -1280,7 +1280,7 @@
     attn_sum = spread(attn_cuts)
     merged = total([near_back, back_arrived]).astype(bf16)
     later_steps = [chips // 2 >> turn for turn in range(1, chips.bit_length() - 1)]
-    back_sum = summed_half(halved(after(merged, attn_cuts), 1))
+    back_sum = summed_half(halved(after(merged, attn_cuts, gu_sum), 1))
     back_halves = halved(back_sum, 2)
     down_sum = after(summed_half(down_halves), back_sum)
     own_down = finished(halved(down_sum, later_steps[0]), later_steps[1:])
@@ -1297,15 +1297,10 @@
     )
     ffin_new += (ffin_new[0].astype(bf16),)
     ffout_new += (ffout_new[0].astype(bf16),)
-    attn_sum, ffin_new, _ = lax.optimization_barrier((attn_sum, ffin_new, back_sum))
-    first_grad = finished(back_halves, [2 << turn for turn in range(1, chips.bit_length() - 2)])
+    attn_sum, ffin_new = lax.optimization_barrier((attn_sum, ffin_new))
     summed, sent = last_sum(core, attn_sum)
     arrived = core_swap(sent)
-    scale = rms_scale(flat_tokens)
-    gained = first_grad * gains[0]
-    inner = jnp.mean(gained * flat_tokens, axis=-1, keepdims=True)
-    input_grad = mine(dmixed) + scale * gained - flat_tokens * (scale**3 * inner)
-
+    arrived = lax.optimization_barrier((arrived, back_sum))[0]
     attn_new = attention_update(
         core,
         summed,
@@ -1315,6 +1310,13 @@
         attention_average,
         [rate * inverse_root for rate in attention_rates],
     )
+    back_halves = after(back_halves, attn_new[0])
+    first_grad = finished(back_halves, [2 << turn for turn in range(1, chips.bit_length() - 2)])
+    scale = rms_scale(flat_tokens)
+    gained = first_grad * gains[0]
+    inner = jnp.mean(gained * flat_tokens, axis=-1, keepdims=True)
+    input_grad = mine(dmixed) + scale * gained - flat_tokens * (scale**3 * inner)
+
     small_own, small_their = summed[-small_rows:], arrived[-small_rows:]
     gains_reduced = (small_own[:4] + small_their[:4]).reshape(gains.shape)
     pairs = heads // 4

time: 233 us -> 231 us (level)
  waiting for transfers between devices: 75.6 us -> 67.1 us
  other arithmetic: 17.7 us -> 21.8 us
    ppermute x19, waiting for transfers between devices: 29 us -> 21.9 us  [plane_swap(): return lax.ppermute(value, 'seq', [(i, i ^ 2 * step) for i in range(count)])]
    ppermute x4, waiting for transfers between devices: 21.1 us -> 18.2 us  [across(): return lax.ppermute(value, 'batch', [(i, i ^ step) for i in range(count)])]
    unnamed x100 -> x98, local copies, waits for them, and re-layouts: 7.82 us -> 7.86 us
  transfers between devices with their start and end apart: 47 -> 47, of which waited for: 22 -> 21; matrix products, arithmetic and copies ran while one was open for 9% -> 11% of each run, Pallas kernels for 29% -> 30%
where the time goes in v5:
time: 231 us; the launch traced here: 230 us
  Pallas kernels  82.6 us (36%)
  waiting for transfers between devices  67.1 us (29%)
  starting transfers between devices  39.5 us (17%)
  other arithmetic  21.8 us (9%)
  local copies, waits for them, and re-layouts  17.7 us (8%)
    ppermute x19, starting transfers between devices, plane_swap(): return lax.ppermute(value, 'seq', [(i, i ^ 2 * step) for i in range(count)])  23.9 us
    ppermute x12, waiting for transfers between devices, along(): lax.ppermute(value, 'batch', [(i, (i + step) % count) for i in range(coun...  22.8 us
    ppermute x19, waiting for transfers between devices, plane_swap(): return lax.ppermute(value, 'seq', [(i, i ^ 2 * step) for i in range(count)])  21.9 us
    ppermute x4, waiting for transfers between devices, across(): return lax.ppermute(value, 'batch', [(i, i ^ step) for i in range(count)])  18.2 us
    pallas_call x1, Pallas kernels, attend(): pl.pallas_call(functools.partial(attend_kernel, len(pieces)), grid_spec=p...  12.7 us
    ppermute x12, starting transfers between devices, along(): lax.ppermute(value, 'batch', [(i, (i + step) % count) for i in range(coun...  11.9 us
    pallas_call x1, Pallas kernels, feed(): pl.pallas_call(functools.partial(feed_kernel, chips, places, len(gu_piece...  11.9 us
    pallas_call x1, Pallas kernels, retreat(): pl.pallas_call(retreat_kernel, grid_spec=pltpu.PrefetchScalarGridSpec(num...  7.88 us
  transfers between devices with their start and end apart: 47, of which 21 were waited for; matrix products, arithmetic and copies ran while one was open for 11% of the time, Pallas kernels for 30%

profile of v5, /device:TPU:0, one launch (start us, length us, event | category | flops | bytes accessed | tf_op | source)
XLA Modules:
  0.0 229.9 jit_solution(10889599897262078308)
XLA Ops:
  1.8 2.2 make_ready.1
  4.8 2.9 %collective-permute-start.2 = (bf16[1,208,768]{2,1,0:T(8,128)(2,1)}, bf16[1,208,768]{2,1,0:T(8,128)(2,1)S(1)}, u32[]{:S(2)}, u32[]{:S(2)}) collective-permute-start(bf16[1,208,768]{2,1,0:T(8,128)(2,1)} %bitcast.132), channel_id=1, source_target_pairs={{0,8},{4,12},{8,0},{12,4},{16,24},{20,28},{24,16},{28,20},{1,9},{5... | collective-permute-start | bytes 958472 | tf_op jit(solution)/shard_map/ppermute | solution.py:1001
  9.9 1.6 fill.2.refs_0_
  11.5 4.2 %collective-permute-done.2 = bf16[1,208,768]{2,1,0:T(8,128)(2,1)S(1)} collective-permute-done((bf16[1,208,768]{2,1,0:T(8,128)(2,1)}, bf16[1,208,768]{2,1,0:T(8,128)(2,1)S(1)}, u32[]{:S(2)}, u32[]{:S(2)}) %collective-permute-start.2) | collective-permute-done | bytes 319520 | tf_op jit(solution)/shard_map/ppermute | solution.py:1001
  16.8 1.8 collective-permute-start.5
  18.8 3.6 %collective-permute-start.8 = (bf16[4,2,24,384]{3,2,1,0:T(8,128)(2,1)}, bf16[4,2,24,384]{3,2,1,0:T(8,128)(2,1)S(1)}, u32[]{:S(2)}, u32[]{:S(2)}) collective-permute-start(bf16[4,2,24,384]{3,2,1,0:T(8,128)(2,1)} %fill.2.refs_0_), channel_id=1, source_target_pairs={{0,3},{1,0},{2,1},{3,2},{4,7},{5,4},{6,5},{7,6},{8,11},{9,8},{10,9... | collective-permute-start | bytes 442376 | tf_op jit(solution)/shard_map/ppermute | solution.py:1006
  24.7 1.7 fill.3.refs_0_
  26.3 4.1 %bias_rows.1.bias_ref = f32[6,640,128]{2,1,0:T(8,128)} custom-call(f32[32,6]{1,0:T(8,128)} %broadcast_select_fusion.6.table_ref), custom_call_target="tpu_custom_call" | custom-call | flops 1 | bytes 1 | tf_op jit(solution)/shard_map/bias_rows/pallas_call | solution.py:96
  30.4 4.3 %collective-permute-done.7.refs_2_ = bf16[4,2,24,384]{3,2,1,0:T(8,128)(2,1)S(1)} collective-permute-done((bf16[4,2,24,384]{3,2,1,0:T(8,128)(2,1)}, bf16[4,2,24,384]{3,2,1,0:T(8,128)(2,1)S(1)}, u32[]{:S(2)}, u32[]{:S(2)}) %collective-permute-start.7) | collective-permute-done | bytes 147488 | tf_op jit(solution)/shard_map/ppermute | solution.py:1006
  37.1 2.4 %join.2 = bf16[4,2,4,24,384]{4,3,2,1,0:T(8,128)(2,1)} custom-call(s32[4]{0:T(128)} %get-tuple-element.311.order_ref, bf16[4,2,24,384]{3,2,1,0:T(8,128)(2,1)} %fill.2.refs_0_, bf16[4,2,24,384]{3,2,1,0:T(8,128)(2,1)} %copy-done.38, bf16[4,2,24,384]{3,2,1,0:T(8,128)(2,1)} %copy-done.37, bf16[4,2,24,384]{3,2,1,0:T(8,128)(2,1)} %copy-done.36), custom_call_target="tpu_custom_call" | custom-call | flops 1 | bytes 1 | tf_op jit(solution)/shard_map/join/pallas_call | solution.py:1025
  40.0 1.4 collective-permute-start.12
  41.5 1.5 collective-permute-start.11
  44.6 4.2 %place_rows.1 = (bf16[1024,768]{1,0:T(8,128)(2,1)}, bf16[768,1024]{1,0:T(8,128)(2,1)}, f32[1024,256]{1,0:T(8,128)}) custom-call(s32[5]{0:T(128)} %stack.206.meta_ref, bf16[4,144,768]{2,1,0:T(8,128)(2,1)} %copy-done.4, bf16[4,144,768]{2,1,0:T(8,128)(2,1)} %collective-permute-done.9.far_ref), custom_call_target="tpu_custom_call" | custom-call | flops 1 | bytes 1 | tf_op jit(solution)/shard_map/place_rows/pallas_call | solution.py:234
  48.9 2.1 collective-permute-start.14
  51.0 1.4 broadcast_select_fusion.1
  52.4 6.3 %collective-permute-done.14.refs_2_ = bf16[2,2,24,1024]{3,2,1,0:T(8,128)(2,1)S(1)} collective-permute-done((bf16[2,2,24,1024]{3,2,1,0:T(8,128)(2,1)}, bf16[2,2,24,1024]{3,2,1,0:T(8,128)(2,1)S(1)}, u32[]{:S(2)}, u32[]{:S(2)}) %collective-permute-start.14) | collective-permute-done | bytes 196640 | tf_op jit(solution)/shard_map/ppermute | solution.py:1006
  60.9 9.1 %collective-permute-done.15.refs_3_ = bf16[2,2,24,1024]{3,2,1,0:T(8,128)(2,1)S(1)} collective-permute-done((bf16[2,2,24,1024]{3,2,1,0:T(8,128)(2,1)S(1)}, bf16[2,2,24,1024]{3,2,1,0:T(8,128)(2,1)S(1)}, u32[]{:S(2)}, u32[]{:S(2)}) %collective-permute-start.15) | collective-permute-done | bytes 196640 | tf_op jit(solution)/shard_map/ppermute | solution.py:1006
  70.7 2.2 join.3
  73.5 1.5 collective-permute-start.18
  75.0 12.7 %attend.1 = (bf16[256,384]{1,0:T(8,128)(2,1)}, bf16[1024,384]{1,0:T(8,128)(2,1)}, bf16[1024,384]{1,0:T(8,128)(2,1)}, f32[6,1024,256]{2,1,0:T(8,128)}, f32[256,38...) custom-call(s32[4]{0:T(128)} %get-tuple-element.312.meta_ref, ...), custom_call_target="tpu_custom_call" | custom-call | flops 1 | bytes 1 | tf_op jit(solution)/shard_map/attend/pallas_call | solution.py:328
  87.9 1.6 collective-permute-done.17.their_ref
  89.5 2.0 collective-permute-done.19.refs_2_
  94.2 1.4 collective-permute-start.22
  95.7 1.5 collective-permute-start.23
  100.0 4.9 %mix.1 = (f32[256,768]{1,0:T(8,128)}, bf16[256,768]{1,0:T(8,128)(2,1)}, bf16[768,256]{1,0:T(8,128)(2,1)}, bf16[768,256]{1,0:T(8,128)(2,1)}, bf16[768,768]{1,0:T(8,128)(2,1)}) custom-call(s32[9]{0:T(128)} %stack.201.meta_ref, f32[256,768]{1,0:T(8,128)} %pad_maximum_fusion.1.tokens_ref, bf16[256,384]{1,0:T(8,128)(2,1)} %get-tuple-element.182.own_ref, ...), custom_call_target="tpu_custom_call" | custom-call | flops 1 | bytes 1 | tf_op jit(solution)/shard_map/mix/pallas_call | solution.py:403
  107.3 3.0 %collective-permute-done.24.refs_8_ = bf16[4,64,768]{2,1,0:T(8,128)(2,1)} collective-permute-done((bf16[4,64,768]{2,1,0:T(8,128)(2,1)}, bf16[4,64,768]{2,1,0:T(8,128)(2,1)}, u32[]{:S(2)}, u32[]{:S(2)}) %collective-permute-start.24) | collective-permute-done | bytes 393248 | tf_op jit(solution)/shard_map/ppermute | solution.py:1006
  110.3 11.9 %feed.1 = (f32[256,768]{1,0:T(8,128)}, f32[256,768]{1,0:T(8,128)}, bf16[2,192,1024]{2,1,0:T(8,128)(2,1)}, bf16[2,192,1024]{2,1,0:T(8,128)(2,1)}, bf16[2,192,1024...) custom-call(s32[36]{0:T(128)} %stack.246.meta_ref, ...), custom_call_target="tpu_custom_call" | custom-call | flops 1 | bytes 1 | tf_op jit(solution)/shard_map/feed/pallas_call | solution.py:531
  123.9 2.4 %collective-permute-start.28 = (bf16[2,192,1024]{2,1,0:T(8,128)(2,1)}, bf16[2,192,1024]{2,1,0:T(8,128)(2,1)}, u32[]{:S(2)}, u32[]{:S(2)}) collective-permute-start(bf16[2,192,1024]{2,1,0:T(8,128)(2,1)} %get-tuple-element.225), channel_id=1, source_target_pairs={{0,24},{4,28},{8,16},{12,20},{16,8},{20,12},{24,0},{28,4},{1,25},{... | collective-permute-start | bytes 2359304 | tf_op jit(solution)/shard_map/ppermute | solution.py:1001
  127.2 3.7 %settle.1 = (f32[256,768]{1,0:T(8,128)}, bf16[256,384]{1,0:T(8,128)(2,1)}, f32[1,768]{1,0:T(1,128)}, bf16[256,768]{1,0:T(8,128)(2,1)}) custom-call(s32[1]{0:T(128)} %bitcast.core_ref.meta_ref, f32[256,768]{1,0:T(8,128)} %get-tuple-element.193.mixed_ref, f32[256,768]{1,0:T(8,128)} %pad_maximum_fusion.2.cot_ref, f32[256,768]{1,0:T(8,128)} %get-tuple-element.204.back_ref, ...), custom_call_target="tpu_custom_call" | custom-call | flops 1 | bytes 1 | tf_op jit(solution)/shard_map/settle/pallas_call | solution.py:593
  130.9 7.9 %retreat.1 = (bf16[256,384]{1,0:T(8,128)(2,1)}, bf16[1024,768]{1,0:T(8,128)(2,1)}, f32[3,8,128]{2,1,0:T(8,128)}) custom-call(s32[1]{0:T(128)} %bitcast.11.meta_ref, bf16[256,384]{1,0:T(8,128)(2,1)} %get-tuple-element.206.do_ref, f32[256,384]{1,0:T(8,128)} %get-tuple-element.207.o_ref, bf16[256,384]{1,0:T(8,128)(2,1)} %get-tuple-element.208.q_ref, ...), custom_call_target="tpu_custom_call" | custom-call | flops 1 | bytes 1 | tf_op jit(solution)/shard_map/retreat/pallas_call | solution.py:692
  138.8 7.2 %weight_grads.1 = (bf16[784,384]{1,0:T(8,128)(2,1)}, bf16[784,384]{1,0:T(8,128)(2,1)}, bf16[784,384]{1,0:T(8,128)(2,1)}, bf16[784,384]{1,0:T(8,128)(2,1)}) custom-call(s32[6]{0:T(128)} %stack.213.meta_ref, bf16[768,1024]{1,0:T(8,128)(2,1)} %get-tuple-element.194.turned_ref, bf16[256,384]{1,0:T(8,128)(2,1)} %get-tuple-element.227.dq_ref, ...), custom_call_target="tpu_custom_call" | custom-call | flops 1 | bytes 1 | tf_op jit(solution)/shard_map/weight_grads/pallas_call | solution.py:808
  146.1 5.9 %row_grads.1 = (bf16[4,128,768]{2,1,0:T(8,128)(2,1)}, bf16[4,128,768]{2,1,0:T(8,128)(2,1)}) custom-call(s32[6]{0:T(128)} %stack.213.meta_ref, bf16[256,384]{1,0:T(8,128)(2,1)} %get-tuple-element.227.dq_ref, bf16[1024,768]{1,0:T(8,128)(2,1)} %get-tuple-element.213.dkv_ref, bf16[4,192,384]{2,1,0:T(8,128)(2,1)} %bitcast.126, bf16[4,192,384]{2,1,0:T(8,128)(2,1)} %copy-done.3, ...), custom_call_target="tpu_custom_call" | custom-call | flops 1 | bytes 1 | tf_op jit(solution)/shard_map/row_grads/pallas_call | solution.py:856
  152.1 8.0 %collective-permute-done.27.refs_2_ = bf16[2,192,1024]{2,1,0:T(8,128)(2,1)} collective-permute-done((bf16[2,192,1024]{2,1,0:T(8,128)(2,1)}, bf16[2,192,1024]{2,1,0:T(8,128)(2,1)}, u32[]{:S(2)}, u32[]{:S(2)}) %collective-permute-start.27) | collective-permute-done | bytes 786464 | tf_op jit(solution)/shard_map/ppermute | solution.py:1001
  162.5 2.4 %collective-permute-start.33 = (bf16[784,384]{1,0:T(8,128)(2,1)}, bf16[784,384]{1,0:T(8,128)(2,1)}, u32[]{:S(2)}, u32[]{:S(2)}) collective-permute-start(bf16[784,384]{1,0:T(8,128)(2,1)} %get-tuple-element.232), channel_id=1, source_target_pairs={{0,24},{4,28},{8,16},{12,20},{16,8},{20,12},{24,0},{28,4},{1,25},{... | collective-permute-start | bytes 1806344 | tf_op jit(solution)/shard_map/ppermute | solution.py:1001
  167.0 2.7 %cut_plane.1 = (bf16[2,2,48,1024]{3,2,1,0:T(8,128)(2,1)}, bf16[2,2,48,1024]{3,2,1,0:T(8,128)(2,1)}) custom-call(s32[1]{0:T(128)} %bitcast.54.side_ref, bf16[2,192,1024]{2,1,0:T(8,128)(2,1)} %get-tuple-element.233.refs_0_, bf16[2,192,1024]{2,1,0:T(8,128)(2,1)} %collective-permute-done.26.refs_1_, bf16[2,192,1024]{2,1,0:T(8,128)(2,1)} %collective-permute-done.27.refs_2_, ...), custom_call_target="tpu_custom_call" | custom-call | flops 1 | bytes 1 | tf_op jit(solution)/shard_map/cut_plane/pallas_call | solution.py:886
  169.7 2.2 collective-permute-start.34
  172.5 8.7 %collective-permute-done.35 = bf16[1,4,64,768]{3,2,1,0:T(8,128)(2,1)S(1)} collective-permute-done((bf16[1,4,64,768]{3,2,1,0:T(8,128)(2,1)}, bf16[1,4,64,768]{3,2,1,0:T(8,128)(2,1)S(1)}, u32[]{:S(2)}, u32[]{:S(2)}) %collective-permute-start.35) | collective-permute-done | bytes 393248 | tf_op jit(solution)/shard_map/ppermute | solution.py:1068
  181.2 8.3 %collective-permute-done.34 = bf16[2,2,2,24,1024]{4,3,2,1,0:T(8,128)(2,1)S(1)} collective-permute-done((bf16[2,2,2,24,1024]{4,3,2,1,0:T(8,128)(2,1)}, bf16[2,2,2,24,1024]{4,3,2,1,0:T(8,128)(2,1)S(1)}, u32[]{:S(2)}, u32[]{:S(2)}) %collective-permute-start.34) | collective-permute-done | bytes 393248 | tf_op jit(solution)/shard_map/ppermute | solution.py:1068
  192.7 3.0 %sum_plane.1 = (bf16[208,384]{1,0:T(8,128)(2,1)}, bf16[208,384]{1,0:T(8,128)(2,1)}, bf16[208,384]{1,0:T(8,128)(2,1)}, bf16[208,384]{1,0:T(8,128)(2,1)}) custom-call(s32[4]{0:T(128)} %pad_add_fusion.2.order_ref, bf16[784,384]{1,0:T(8,128)(2,1)} %get-tuple-element.251.refs_0_, bf16[784,384]{1,0:T(8,128)(2,1)} %collective-permute-done.31.refs_1_, ...), custom_call_target="tpu_custom_call" | custom-call | flops 1 | bytes 1 | tf_op jit(solution)/shard_map/sum_plane/pallas_call | solution.py:922
  195.7 2.0 collective-permute-start.40
  197.7 2.8 %collective-permute-start.42 = (bf16[208,384]{1,0:T(8,128)(2,1)}, bf16[208,384]{1,0:T(8,128)(2,1)}, u32[]{:S(2)}, u32[]{:S(2)}) collective-permute-start(bf16[208,384]{1,0:T(8,128)(2,1)} %get-tuple-element.258), channel_id=1, source_target_pairs={{0,3},{1,0},{2,1},{3,2},{4,7},{5,4},{6,5},{7,6},{8,11},{9,8},{10,9... | collective-permute-start | bytes 479240 | tf_op jit(solution)/shard_map/ppermute | solution.py:1006
  203.0 3.2 %collective-permute-done.45 = bf16[2,64,768]{2,1,0:T(8,128)(2,1)S(1)} collective-permute-done((bf16[2,64,768]{2,1,0:T(8,128)(2,1)S(1)}, bf16[2,64,768]{2,1,0:T(8,128)(2,1)S(1)}, u32[]{:S(2)}, u32[]{:S(2)}) %collective-permute-start.45) | collective-permute-done | bytes 196640 | tf_op jit(solution)/shard_map/ppermute | solution.py:1001
  206.3 1.4 collective-permute-done.43
  210.0 2.0 fusion.8
  213.5 2.0 last_sum.1
  216.3 1.8 add_bitcast_fusion.1
  223.6 1.4 add_multiply_fusion.3
  224.9 2.3 %attention_update.1 = (f32[4,24,768]{2,1,0:T(8,128)}, f32[4,24,768]{2,1,0:T(8,128)}, f32[4,24,768]{2,1,0:T(8,128)}, bf16[4,24,768]{2,1,0:T(8,128)(2,1)}) custom-call(s32[1]{0:T(128)} %bitcast.core_ref.meta_ref, f32[208,384]{1,0:T(8,128)} %get-tuple-element.265.sum_ref, f32[88,384]{1,0:T(8,128)} %copy-done.35, f32[4,24,768]{2,1,0:T(8,128)} %weight_ref.1, ...), custom_call_target="tpu_custom_call" | custom-call | flops 1 | bytes 1 | tf_op jit(solution)/shard_map/attention_update/pallas_call | solution.py:983
  (218 shorter events, 49.9 us)
Async XLA Ops:
  0.7 3.3 %collective-permute-start.1 = (f32[128,768]{1,0:T(8,128)}, f32[128,768]{1,0:T(8,128)S(1)}, u32[]{:S(2)}, u32[]{:S(2)}) collective-permute-start(f32[128,768]{1,0:T(8,128)} %bitcast.137), channel_id=1, source_target_pairs={{0,4},{4,0},{8,12},{12,8},{16,20},{20,16},{24,28},{28,24},{1,5},{5... | collective-permute-start | bytes 1179656 | tf_op jit(solution)/shard_map/ppermute | solution.py:996
  1.2 2.8 %collective-permute-start = (f32[128,768]{1,0:T(8,128)}, f32[128,768]{1,0:T(8,128)S(1)}, u32[]{:S(2)}, u32[]{:S(2)}) collective-permute-start(f32[128,768]{1,0:T(8,128)} %bitcast.127), channel_id=1, source_target_pairs={{0,4},{4,0},{8,12},{12,8},{16,20},{20,16},{24,28},{28,24},{1,5},{5... | collective-permute-start | bytes 1179656 | tf_op jit(solution)/shard_map/ppermute | solution.py:996
  4.8 10.9 %collective-permute-start.2 = (bf16[1,208,768]{2,1,0:T(8,128)(2,1)}, bf16[1,208,768]{2,1,0:T(8,128)(2,1)S(1)}, u32[]{:S(2)}, u32[]{:S(2)}) collective-permute-start(bf16[1,208,768]{2,1,0:T(8,128)(2,1)} %bitcast.132), channel_id=1, source_target_pairs={{0,8},{4,12},{8,0},{12,4},{16,24},{20,28},{24,16},{28,20},{1,9},{5... | collective-permute-start | bytes 958472 | tf_op jit(solution)/shard_map/ppermute | solution.py:1001
  7.7 1.5 collective-permute-start.3
  7.7 1.6 collective-permute-start.4
  16.8 19.2 %collective-permute-start.5 = (bf16[2,208,768]{2,1,0:T(8,128)(2,1)S(1)}, bf16[2,208,768]{2,1,0:T(8,128)(2,1)S(1)}, u32[]{:S(2)}, u32[]{:S(2)}) collective-permute-start(bf16[2,208,768]{2,1,0:T(8,128)(2,1)S(1)} %pad_maximum_fusion.3), channel_id=1, source_target_pairs={{0,16},{4,20},{8,24},{12,28},{16,0},{20,4},{24,8},{28,12},{1,17},{... | collective-permute-start | bytes 1916936 | tf_op jit(solution)/shard_map/ppermute | solution.py:1001
  18.8 11.6 %collective-permute-start.8 = (bf16[4,2,24,384]{3,2,1,0:T(8,128)(2,1)}, bf16[4,2,24,384]{3,2,1,0:T(8,128)(2,1)S(1)}, u32[]{:S(2)}, u32[]{:S(2)}) collective-permute-start(bf16[4,2,24,384]{3,2,1,0:T(8,128)(2,1)} %fill.2.refs_0_), channel_id=1, source_target_pairs={{0,3},{1,0},{2,1},{3,2},{4,7},{5,4},{6,5},{7,6},{8,11},{9,8},{10,9... | collective-permute-start | bytes 442376 | tf_op jit(solution)/shard_map/ppermute | solution.py:1006
  22.4 12.2 %collective-permute-start.7 = (bf16[4,2,24,384]{3,2,1,0:T(8,128)(2,1)}, bf16[4,2,24,384]{3,2,1,0:T(8,128)(2,1)S(1)}, u32[]{:S(2)}, u32[]{:S(2)}) collective-permute-start(bf16[4,2,24,384]{3,2,1,0:T(8,128)(2,1)} %fill.2.refs_0_), channel_id=1, source_target_pairs={{0,2},{1,3},{2,0},{3,1},{4,6},{5,7},{6,4},{7,5},{8,10},{9,11},{10,... | collective-permute-start | bytes 442376 | tf_op jit(solution)/shard_map/ppermute | solution.py:1006
  22.4 12.2 %collective-permute-start.6 = (bf16[4,2,24,384]{3,2,1,0:T(8,128)(2,1)}, bf16[4,2,24,384]{3,2,1,0:T(8,128)(2,1)S(1)}, u32[]{:S(2)}, u32[]{:S(2)}) collective-permute-start(bf16[4,2,24,384]{3,2,1,0:T(8,128)(2,1)} %fill.2.refs_0_), channel_id=1, source_target_pairs={{0,1},{1,2},{2,3},{3,0},{4,5},{5,6},{6,7},{7,4},{8,9},{9,10},{10,1... | collective-permute-start | bytes 442376 | tf_op jit(solution)/shard_map/ppermute | solution.py:1006
  39.4 5.1 %collective-permute-start.9 = (bf16[4,144,768]{2,1,0:T(8,128)(2,1)S(1)}, bf16[4,144,768]{2,1,0:T(8,128)(2,1)}, u32[]{:S(2)}, u32[]{:S(2)}) collective-permute-start(bf16[4,144,768]{2,1,0:T(8,128)(2,1)S(1)} %slice.106.near_ref), channel_id=1, source_target_pairs={{0,4},{4,0},{8,12},{12,8},{16,20},{20,16},{24,28},{28,24},{1,5},{5... | collective-permute-start | bytes 2654216 | tf_op jit(solution)/shard_map/ppermute | solution.py:996
  39.4 9.4 %collective-permute-start.13 = (bf16[2,2,24,1024]{3,2,1,0:T(8,128)(2,1)}, bf16[2,2,24,1024]{3,2,1,0:T(8,128)(2,1)}, u32[]{:S(2)}, u32[]{:S(2)}) collective-permute-start(bf16[2,2,24,1024]{3,2,1,0:T(8,128)(2,1)} %fill.3.refs_0_), channel_id=1, source_target_pairs={{0,1},{1,2},{2,3},{3,0},{4,5},{5,6},{6,7},{7,4},{8,9},{9,10},{10,1... | collective-permute-start | bytes 589832 | tf_op jit(solution)/shard_map/ppermute | solution.py:1006
  40.0 32.9 %collective-permute-start.12 = (bf16[4,192,384]{2,1,0:T(8,128)(2,1)}, bf16[4,192,384]{2,1,0:T(8,128)(2,1)S(1)}, u32[]{:S(2)}, u32[]{:S(2)}) collective-permute-start(bf16[4,192,384]{2,1,0:T(8,128)(2,1)} %bitcast.121), channel_id=1, source_target_pairs={{0,24},{4,28},{8,16},{12,20},{16,8},{20,12},{24,0},{28,4},{1,25},{... | collective-permute-start | bytes 1769480 | tf_op jit(solution)/shard_map/ppermute | solution.py:1001
  41.5 31.4 %collective-permute-start.11 = (bf16[4,192,384]{2,1,0:T(8,128)(2,1)}, bf16[4,192,384]{2,1,0:T(8,128)(2,1)S(1)}, u32[]{:S(2)}, u32[]{:S(2)}) collective-permute-start(bf16[4,192,384]{2,1,0:T(8,128)(2,1)} %bitcast.122), channel_id=1, source_target_pairs={{0,16},{4,20},{8,24},{12,28},{16,0},{20,4},{24,8},{28,12},{1,17},{... | collective-permute-start | bytes 1769480 | tf_op jit(solution)/shard_map/ppermute | solution.py:1001
  43.0 29.9 %collective-permute-start.10 = (bf16[4,192,384]{2,1,0:T(8,128)(2,1)}, bf16[4,192,384]{2,1,0:T(8,128)(2,1)S(1)}, u32[]{:S(2)}, u32[]{:S(2)}) collective-permute-start(bf16[4,192,384]{2,1,0:T(8,128)(2,1)} %bitcast.123), channel_id=1, source_target_pairs={{0,8},{4,12},{8,0},{12,4},{16,24},{20,28},{24,16},{28,20},{1,9},{5... | collective-permute-start | bytes 1769480 | tf_op jit(solution)/shard_map/ppermute | solution.py:1001
  48.9 9.8 %collective-permute-start.14 = (bf16[2,2,24,1024]{3,2,1,0:T(8,128)(2,1)}, bf16[2,2,24,1024]{3,2,1,0:T(8,128)(2,1)S(1)}, u32[]{:S(2)}, u32[]{:S(2)}) collective-permute-start(bf16[2,2,24,1024]{3,2,1,0:T(8,128)(2,1)} %collective-permute-done.13.refs_1_), channel_id=1, source_target_pairs={{0,1},{1,2},{2,3},{3,0},{4,5},{5,6},{6,7},{7,4},{8,9},{9,10},{10,1... | collective-permute-start | bytes 589832 | tf_op jit(solution)/shard_map/ppermute | solution.py:1006
  51.0 22.0 %collective-permute-start.16 = (bf16[4,64,768]{2,1,0:T(8,128)(2,1)S(1)}, bf16[4,64,768]{2,1,0:T(8,128)(2,1)}, u32[]{:S(2)}, u32[]{:S(2)}) collective-permute-start(bf16[4,64,768]{2,1,0:T(8,128)(2,1)S(1)} %pad_maximum_fusion.4.refs_5_), channel_id=1, source_target_pairs={{0,1},{1,2},{2,3},{3,0},{4,5},{5,6},{6,7},{7,4},{8,9},{9,10},{10,1... | collective-permute-start | bytes 1179656 | tf_op jit(solution)/shard_map/ppermute | solution.py:1006
  58.7 11.4 %collective-permute-start.15 = (bf16[2,2,24,1024]{3,2,1,0:T(8,128)(2,1)S(1)}, bf16[2,2,24,1024]{3,2,1,0:T(8,128)(2,1)S(1)}, u32[]{:S(2)}, u32[]{:S(2)}) collective-permute-start(bf16[2,2,24,1024]{3,2,1,0:T(8,128)(2,1)S(1)} %collective-permute-done.14.refs_2_), channel_id=1, source_target_pairs={{0,1},{1,2},{2,3},{3,0},{4,5},{5,6},{6,7},{7,4},{8,9},{9,10},{10,1... | collective-permute-start | bytes 589832 | tf_op jit(solution)/shard_map/ppermute | solution.py:1006
  73.0 18.6 %collective-permute-start.19 = (bf16[2,192,1024]{2,1,0:T(8,128)(2,1)}, bf16[2,192,1024]{2,1,0:T(8,128)(2,1)S(1)}, u32[]{:S(2)}, u32[]{:S(2)}) collective-permute-start(bf16[2,192,1024]{2,1,0:T(8,128)(2,1)} %bitcast.129), channel_id=1, source_target_pairs={{0,16},{4,20},{8,24},{12,28},{16,0},{20,4},{24,8},{28,12},{1,17},{... | collective-permute-start | bytes 2359304 | tf_op jit(solution)/shard_map/ppermute | solution.py:1001
  73.5 18.2 %collective-permute-start.18 = (bf16[2,192,1024]{2,1,0:T(8,128)(2,1)}, bf16[2,192,1024]{2,1,0:T(8,128)(2,1)S(1)}, u32[]{:S(2)}, u32[]{:S(2)}) collective-permute-start(bf16[2,192,1024]{2,1,0:T(8,128)(2,1)} %bitcast.130), channel_id=1, source_target_pairs={{0,8},{4,12},{8,0},{12,4},{16,24},{20,28},{24,16},{28,20},{1,9},{5... | collective-permute-start | bytes 2359304 | tf_op jit(solution)/shard_map/ppermute | solution.py:1001
  75.0 14.5 %collective-permute-start.20 = (bf16[4,64,768]{2,1,0:T(8,128)(2,1)}, bf16[4,64,768]{2,1,0:T(8,128)(2,1)}, u32[]{:S(2)}, u32[]{:S(2)}) collective-permute-start(bf16[4,64,768]{2,1,0:T(8,128)(2,1)} %collective-permute-done.16.refs_6_), channel_id=1, source_target_pairs={{0,1},{1,2},{2,3},{3,0},{4,5},{5,6},{6,7},{7,4},{8,9},{9,10},{10,1... | collective-permute-start | bytes 1179656 | tf_op jit(solution)/shard_map/ppermute | solution.py:1006
  87.8 1.7 collective-permute-start.17
  94.2 4.9 %collective-permute-start.21 = (bf16[4,192,384]{2,1,0:T(8,128)(2,1)S(1)}, bf16[4,192,384]{2,1,0:T(8,128)(2,1)S(1)}, u32[]{:S(2)}, u32[]{:S(2)}) collective-permute-start(bf16[4,192,384]{2,1,0:T(8,128)(2,1)S(1)} %copy-done.21), channel_id=1, source_target_pairs={{0,4},{4,0},{8,12},{12,8},{16,20},{20,16},{24,28},{28,24},{1,5},{5... | collective-permute-start | bytes 1769480 | tf_op jit(solution)/shard_map/ppermute | solution.py:996
  94.2 11.7 %collective-permute-start.22 = (bf16[1,192,1024]{2,1,0:T(8,128)(2,1)}, bf16[1,192,1024]{2,1,0:T(8,128)(2,1)S(1)}, u32[]{:S(2)}, u32[]{:S(2)}) collective-permute-start(bf16[1,192,1024]{2,1,0:T(8,128)(2,1)} %slice.86), channel_id=1, source_target_pairs={{0,16},{4,20},{8,24},{12,28},{16,0},{20,4},{24,8},{28,12},{1,17},{... | collective-permute-start | bytes 1179656 | tf_op jit(solution)/shard_map/ppermute | solution.py:1001
  95.7 11.6 %collective-permute-start.23 = (bf16[1,192,1024]{2,1,0:T(8,128)(2,1)}, bf16[1,192,1024]{2,1,0:T(8,128)(2,1)}, u32[]{:S(2)}, u32[]{:S(2)}) collective-permute-start(bf16[1,192,1024]{2,1,0:T(8,128)(2,1)} %slice.87), channel_id=1, source_target_pairs={{0,8},{4,12},{8,0},{12,4},{16,24},{20,28},{24,16},{28,20},{1,9},{5... | collective-permute-start | bytes 1179656 | tf_op jit(solution)/shard_map/ppermute | solution.py:1001
  97.2 13.1 %collective-permute-start.24 = (bf16[4,64,768]{2,1,0:T(8,128)(2,1)}, bf16[4,64,768]{2,1,0:T(8,128)(2,1)}, u32[]{:S(2)}, u32[]{:S(2)}) collective-permute-start(bf16[4,64,768]{2,1,0:T(8,128)(2,1)} %collective-permute-done.20.refs_7_), channel_id=1, source_target_pairs={{0,1},{1,2},{2,3},{3,0},{4,5},{5,6},{6,7},{7,4},{8,9},{9,10},{10,1... | collective-permute-start | bytes 1179656 | tf_op jit(solution)/shard_map/ppermute | solution.py:1006
  122.1 4.2 %collective-permute-start.25 = (f32[256,768]{1,0:T(8,128)}, f32[256,768]{1,0:T(8,128)S(1)}, u32[]{:S(2)}, u32[]{:S(2)}) collective-permute-start(f32[256,768]{1,0:T(8,128)} %get-tuple-element.204.back_ref), channel_id=1, source_target_pairs={{0,4},{4,0},{8,12},{12,8},{16,20},{20,16},{24,28},{28,24},{1,5},{5... | collective-permute-start | bytes 2359304 | tf_op jit(solution)/shard_map/ppermute | solution.py:996
  122.8 29.3 %collective-permute-start.26 = (bf16[2,192,1024]{2,1,0:T(8,128)(2,1)}, bf16[2,192,1024]{2,1,0:T(8,128)(2,1)}, u32[]{:S(2)}, u32[]{:S(2)}) collective-permute-start(bf16[2,192,1024]{2,1,0:T(8,128)(2,1)} %get-tuple-element.223), channel_id=1, source_target_pairs={{0,8},{4,12},{8,0},{12,4},{16,24},{20,28},{24,16},{28,20},{1,9},{5... | collective-permute-start | bytes 2359304 | tf_op jit(solution)/shard_map/ppermute | solution.py:1001
  123.3 36.8 %collective-permute-start.27 = (bf16[2,192,1024]{2,1,0:T(8,128)(2,1)}, bf16[2,192,1024]{2,1,0:T(8,128)(2,1)}, u32[]{:S(2)}, u32[]{:S(2)}) collective-permute-start(bf16[2,192,1024]{2,1,0:T(8,128)(2,1)} %get-tuple-element.224), channel_id=1, source_target_pairs={{0,16},{4,20},{8,24},{12,28},{16,0},{20,4},{24,8},{28,12},{1,17},{... | collective-permute-start | bytes 2359304 | tf_op jit(solution)/shard_map/ppermute | solution.py:1001
  123.9 36.2 %collective-permute-start.28 = (bf16[2,192,1024]{2,1,0:T(8,128)(2,1)}, bf16[2,192,1024]{2,1,0:T(8,128)(2,1)}, u32[]{:S(2)}, u32[]{:S(2)}) collective-permute-start(bf16[2,192,1024]{2,1,0:T(8,128)(2,1)} %get-tuple-element.225), channel_id=1, source_target_pairs={{0,24},{4,28},{8,16},{12,20},{16,8},{20,12},{24,0},{28,4},{1,25},{... | collective-permute-start | bytes 2359304 | tf_op jit(solution)/shard_map/ppermute | solution.py:1001
  126.3 35.1 %collective-permute-start.29 = (bf16[2,4,64,768]{3,2,1,0:T(8,128)(2,1)}, bf16[2,4,64,768]{3,2,1,0:T(8,128)(2,1)}, u32[]{:S(2)}, u32[]{:S(2)}) collective-permute-start(bf16[2,4,64,768]{3,2,1,0:T(8,128)(2,1)} %get-tuple-element.226), channel_id=1, source_target_pairs={{0,2},{1,3},{2,0},{3,1},{4,6},{5,7},{6,4},{7,5},{8,10},{9,11},{10,... | collective-permute-start | bytes 2359304 | tf_op jit(solution)/shard_map/ppermute | solution.py:1068
  152.0 9.4 %collective-permute-start.30 = (bf16[4,128,768]{2,1,0:T(8,128)(2,1)}, bf16[4,128,768]{2,1,0:T(8,128)(2,1)S(1)}, u32[]{:S(2)}, u32[]{:S(2)}) collective-permute-start(bf16[4,128,768]{2,1,0:T(8,128)(2,1)} %get-tuple-element.228), channel_id=1, source_target_pairs={{0,4},{4,0},{8,12},{12,8},{16,20},{20,16},{24,28},{28,24},{1,5},{5... | collective-permute-start | bytes 2359304 | tf_op jit(solution)/shard_map/ppermute | solution.py:996
  161.4 28.1 %collective-permute-start.31 = (bf16[784,384]{1,0:T(8,128)(2,1)}, bf16[784,384]{1,0:T(8,128)(2,1)}, u32[]{:S(2)}, u32[]{:S(2)}) collective-permute-start(bf16[784,384]{1,0:T(8,128)(2,1)} %get-tuple-element.230), channel_id=1, source_target_pairs={{0,8},{4,12},{8,0},{12,4},{16,24},{20,28},{24,16},{28,20},{1,9},{5... | collective-permute-start | bytes 1806344 | tf_op jit(solution)/shard_map/ppermute | solution.py:1001
  161.9 28.5 %collective-permute-start.32 = (bf16[784,384]{1,0:T(8,128)(2,1)}, bf16[784,384]{1,0:T(8,128)(2,1)}, u32[]{:S(2)}, u32[]{:S(2)}) collective-permute-start(bf16[784,384]{1,0:T(8,128)(2,1)} %get-tuple-element.231), channel_id=1, source_target_pairs={{0,16},{4,20},{8,24},{12,28},{16,0},{20,4},{24,8},{28,12},{1,17},{... | collective-permute-start | bytes 1806344 | tf_op jit(solution)/shard_map/ppermute | solution.py:1001
  162.5 27.9 %collective-permute-start.33 = (bf16[784,384]{1,0:T(8,128)(2,1)}, bf16[784,384]{1,0:T(8,128)(2,1)}, u32[]{:S(2)}, u32[]{:S(2)}) collective-permute-start(bf16[784,384]{1,0:T(8,128)(2,1)} %get-tuple-element.232), channel_id=1, source_target_pairs={{0,24},{4,28},{8,16},{12,20},{16,8},{20,12},{24,0},{28,4},{1,25},{... | collective-permute-start | bytes 1806344 | tf_op jit(solution)/shard_map/ppermute | solution.py:1001
  167.0 14.2 %collective-permute-start.35 = (bf16[1,4,64,768]{3,2,1,0:T(8,128)(2,1)}, bf16[1,4,64,768]{3,2,1,0:T(8,128)(2,1)S(1)}, u32[]{:S(2)}, u32[]{:S(2)}) collective-permute-start(bf16[1,4,64,768]{3,2,1,0:T(8,128)(2,1)} %constant_dynamic-slice_fusion.2), channel_id=1, source_target_pairs={{0,1},{1,0},{2,3},{3,2},{4,5},{5,4},{6,7},{7,6},{8,9},{9,8},{10,11... | collective-permute-start | bytes 1179656 | tf_op jit(solution)/shard_map/ppermute | solution.py:1068
  169.7 22.8 %copy-start.17 = (bf16[4,128,768]{2,1,0:T(8,128)(2,1)S(1)}, bf16[4,128,768]{2,1,0:T(8,128)(2,1)}, u32[]{:S(2)}) copy-start(bf16[4,128,768]{2,1,0:T(8,128)(2,1)} %get-tuple-element.243) | copy-start | bytes 2359300
  169.7 19.8 %collective-permute-start.34 = (bf16[2,2,2,24,1024]{4,3,2,1,0:T(8,128)(2,1)}, bf16[2,2,2,24,1024]{4,3,2,1,0:T(8,128)(2,1)S(1)}, u32[]{:S(2)}, u32[]{:S(2)}) collective-permute-start(bf16[2,2,2,24,1024]{4,3,2,1,0:T(8,128)(2,1)} %bitcast.138), channel_id=1, source_target_pairs={{0,2},{1,3},{2,0},{3,1},{4,6},{5,7},{6,4},{7,5},{8,10},{9,11},{10,... | collective-permute-start | bytes 1179656 | tf_op jit(solution)/shard_map/ppermute | solution.py:1068
  192.4 9.7 %collective-permute-start.37 = (bf16[2,2,1,24,1024]{4,3,2,1,0:T(8,128)(2,1)}, bf16[2,2,1,24,1024]{4,3,2,1,0:T(8,128)(2,1)S(1)}, u32[]{:S(2)}, u32[]{:S(2)}) collective-permute-start(bf16[2,2,1,24,1024]{4,3,2,1,0:T(8,128)(2,1)} %constant_dynamic-slice_fusion), channel_id=1, source_target_pairs={{0,1},{1,0},{2,3},{3,2},{4,5},{5,4},{6,7},{7,6},{8,9},{9,8},{10,11... | collective-permute-start | bytes 589832 | tf_op jit(solution)/shard_map/ppermute | solution.py:1068
  195.7 17.1 %collective-permute-start.40 = (bf16[208,384]{1,0:T(8,128)(2,1)}, bf16[208,384]{1,0:T(8,128)(2,1)S(1)}, u32[]{:S(2)}, u32[]{:S(2)}) collective-permute-start(bf16[208,384]{1,0:T(8,128)(2,1)} %get-tuple-element.256), channel_id=1, source_target_pairs={{0,1},{1,2},{2,3},{3,0},{4,5},{5,6},{6,7},{7,4},{8,9},{9,10},{10,1... | collective-permute-start | bytes 479240 | tf_op jit(solution)/shard_map/ppermute | solution.py:1006
  197.7 15.1 %collective-permute-start.41 = (bf16[208,384]{1,0:T(8,128)(2,1)}, bf16[208,384]{1,0:T(8,128)(2,1)}, u32[]{:S(2)}, u32[]{:S(2)}) collective-permute-start(bf16[208,384]{1,0:T(8,128)(2,1)} %get-tuple-element.257), channel_id=1, source_target_pairs={{0,2},{1,3},{2,0},{3,1},{4,6},{5,7},{6,4},{7,5},{8,10},{9,11},{10,... | collective-permute-start | bytes 479240 | tf_op jit(solution)/shard_map/ppermute | solution.py:1006
  197.7 15.1 %collective-permute-start.42 = (bf16[208,384]{1,0:T(8,128)(2,1)}, bf16[208,384]{1,0:T(8,128)(2,1)}, u32[]{:S(2)}, u32[]{:S(2)}) collective-permute-start(bf16[208,384]{1,0:T(8,128)(2,1)} %get-tuple-element.258), channel_id=1, source_target_pairs={{0,3},{1,0},{2,1},{3,2},{4,7},{5,4},{6,5},{7,6},{8,11},{9,8},{10,9... | collective-permute-start | bytes 479240 | tf_op jit(solution)/shard_map/ppermute | solution.py:1006
  200.5 5.7 %collective-permute-start.45 = (bf16[2,64,768]{2,1,0:T(8,128)(2,1)S(1)}, bf16[2,64,768]{2,1,0:T(8,128)(2,1)S(1)}, u32[]{:S(2)}, u32[]{:S(2)}) collective-permute-start(bf16[2,64,768]{2,1,0:T(8,128)(2,1)S(1)} %slice.97), channel_id=1, source_target_pairs={{0,16},{4,20},{8,24},{12,28},{16,0},{20,4},{24,8},{28,12},{1,17},{... | collective-permute-start | bytes 589832 | tf_op jit(solution)/shard_map/ppermute | solution.py:1001
  202.2 14.1 %collective-permute-start.36 = (f32[128,768]{1,0:T(8,128)}, f32[128,768]{1,0:T(8,128)}, u32[]{:S(2)}, u32[]{:S(2)}) collective-permute-start(f32[128,768]{1,0:T(8,128)} %constant_dynamic-slice_fusion.1), channel_id=1, source_target_pairs={{0,4},{4,0},{8,12},{12,8},{16,20},{20,16},{24,28},{28,24},{1,5},{5... | collective-permute-start | bytes 1179656 | tf_op jit(solution)/shard_map/ppermute | solution.py:996
  206.3 1.4 collective-permute-start.43
  207.7 11.5 %collective-permute-start.38 = (bf16[2,128,768]{2,1,0:T(8,128)(2,1)}, bf16[2,128,768]{2,1,0:T(8,128)(2,1)}, u32[]{:S(2)}, u32[]{:S(2)}) collective-permute-start(bf16[2,128,768]{2,1,0:T(8,128)(2,1)} %slice.91), channel_id=1, source_target_pairs={{0,8},{4,12},{8,0},{12,4},{16,24},{20,28},{24,16},{28,20},{1,9},{5... | collective-permute-start | bytes 1179656 | tf_op jit(solution)/shard_map/ppermute | solution.py:1001
  216.2 4.1 %collective-permute-start.44 = (f32[88,384]{1,0:T(8,128)}, f32[88,384]{1,0:T(8,128)S(1)}, u32[]{:S(2)}, u32[]{:S(2)}) collective-permute-start(f32[88,384]{1,0:T(8,128)} %get-tuple-element.266), channel_id=1, source_target_pairs={{0,4},{4,0},{8,12},{12,8},{16,20},{20,16},{24,28},{28,24},{1,5},{5... | collective-permute-start | bytes 405512 | tf_op jit(solution)/shard_map/ppermute | solution.py:996
  221.2 6.1 %collective-permute-start.46 = (bf16[1,64,768]{2,1,0:T(8,128)(2,1)S(1)}, bf16[1,64,768]{2,1,0:T(8,128)(2,1)S(1)}, u32[]{:S(2)}, u32[]{:S(2)}) collective-permute-start(bf16[1,64,768]{2,1,0:T(8,128)(2,1)S(1)} %slice.99), channel_id=1, source_target_pairs={{0,8},{4,12},{8,0},{12,4},{16,24},{20,28},{24,16},{28,20},{1,9},{5... | collective-permute-start | bytes 294920 | tf_op jit(solution)/shard_map/ppermute | solution.py:1001
  222.3 6.5 %collective-permute-start.39 = (bf16[1,128,768]{2,1,0:T(8,128)(2,1)S(1)}, bf16[1,128,768]{2,1,0:T(8,128)(2,1)S(1)}, u32[]{:S(2)}, u32[]{:S(2)}) collective-permute-start(bf16[1,128,768]{2,1,0:T(8,128)(2,1)S(1)} %get-tuple-element.300), channel_id=1, source_target_pairs={{0,16},{4,20},{8,24},{12,28},{16,0},{20,4},{24,8},{28,12},{1,17},{... | collective-permute-start | bytes 589832 | tf_op jit(solution)/shard_map/ppermute | solution.py:1001
  (47 other events, 295.0 us)

commit v6 on v5

--- a/solution.py
+++ b/solution.py
@@ -1242,7 +1242,6 @@
         (attn_grads, gu_arrived, down_moving, back_arrived)
     )[:3]
     attn_arrived = [attn_grads[0]] + [plane_swap(attn_grads[step], step) for step in range(1, min(chips, 3))]
-    down_sum = add(down_moving, down_grads[0])
     reach = places // 2
     if rows * reach % 16 == 0:
         halves = cut_plane(gu_arrived, place // reach)
@@ -1251,6 +1250,7 @@
         gu_sum = total(gu_arrived).astype(bf16).reshape(2, 2, places, rows, hidden // 2)
         gu_kept, gu_sent = halves_along(gu_sum, 2, place)
     gu_moving = across(gu_sent, reach)
+    down_sum = add(after(down_moving, gu_sent), down_grads[0])
     down_kept, down_sent = halves_along(down_sum, 0, place)
     down_moving = across(down_sent, reach // 2)
     attn_arrived += [plane_swap(attn_grads[step], step) for step in range(3, chips)]

time: 231 us -> 230 us (level)
    unnamed x98 -> x102, local copies, waits for them, and re-layouts: 7.86 us -> 7.18 us
where the time goes in v6:
time: 230 us; the launch traced here: 229 us
  Pallas kernels  82.4 us (36%)
  waiting for transfers between devices  67 us (29%)
  starting transfers between devices  40.2 us (17%)
  other arithmetic  21.7 us (9%)
  local copies, waits for them, and re-layouts  16.4 us (7%)
    ppermute x19, starting transfers between devices, plane_swap(): return lax.ppermute(value, 'seq', [(i, i ^ 2 * step) for i in range(count)])  25.1 us
    ppermute x12, waiting for transfers between devices, along(): lax.ppermute(value, 'batch', [(i, (i + step) % count) for i in range(coun...  22.9 us
    ppermute x19, waiting for transfers between devices, plane_swap(): return lax.ppermute(value, 'seq', [(i, i ^ 2 * step) for i in range(count)])  21.7 us
    ppermute x4, waiting for transfers between devices, across(): return lax.ppermute(value, 'batch', [(i, i ^ step) for i in range(count)])  18.3 us
    pallas_call x1, Pallas kernels, attend(): pl.pallas_call(functools.partial(attend_kernel, len(pieces)), grid_spec=p...  12.7 us
    pallas_call x1, Pallas kernels, feed(): pl.pallas_call(functools.partial(feed_kernel, chips, places, len(gu_piece...  11.8 us
    ppermute x12, starting transfers between devices, along(): lax.ppermute(value, 'batch', [(i, (i + step) % count) for i in range(coun...  11.5 us
    pallas_call x1, Pallas kernels, retreat(): pl.pallas_call(retreat_kernel, grid_spec=pltpu.PrefetchScalarGridSpec(num...  7.87 us
  transfers between devices with their start and end apart: 47, of which 21 were waited for; matrix products, arithmetic and copies ran while one was open for 11% of the time, Pallas kernels for 30%

profile of v6, /device:TPU:0, one launch (start us, length us, event | category | flops | bytes accessed | tf_op | source)
XLA Modules:
  0.0 229.1 jit_solution(6228202652590806619)
XLA Ops:
  1.8 2.2 make_ready.1
  4.8 2.9 %collective-permute-start.2 = (bf16[1,208,768]{2,1,0:T(8,128)(2,1)}, bf16[1,208,768]{2,1,0:T(8,128)(2,1)S(1)}, u32[]{:S(2)}, u32[]{:S(2)}) collective-permute-start(bf16[1,208,768]{2,1,0:T(8,128)(2,1)} %bitcast.132), channel_id=1, source_target_pairs={{0,8},{4,12},{8,0},{12,4},{16,24},{20,28},{24,16},{28,20},{1,9},{5... | collective-permute-start | bytes 958472 | tf_op jit(solution)/shard_map/ppermute | solution.py:1001
  9.9 1.6 fill.2.refs_0_
  11.5 4.2 %collective-permute-done.2 = bf16[1,208,768]{2,1,0:T(8,128)(2,1)S(1)} collective-permute-done((bf16[1,208,768]{2,1,0:T(8,128)(2,1)}, bf16[1,208,768]{2,1,0:T(8,128)(2,1)S(1)}, u32[]{:S(2)}, u32[]{:S(2)}) %collective-permute-start.2) | collective-permute-done | bytes 319520 | tf_op jit(solution)/shard_map/ppermute | solution.py:1001
  16.8 1.8 collective-permute-start.5
  18.8 3.6 %collective-permute-start.8 = (bf16[4,2,24,384]{3,2,1,0:T(8,128)(2,1)}, bf16[4,2,24,384]{3,2,1,0:T(8,128)(2,1)S(1)}, u32[]{:S(2)}, u32[]{:S(2)}) collective-permute-start(bf16[4,2,24,384]{3,2,1,0:T(8,128)(2,1)} %fill.2.refs_0_), channel_id=1, source_target_pairs={{0,3},{1,0},{2,1},{3,2},{4,7},{5,4},{6,5},{7,6},{8,11},{9,8},{10,9... | collective-permute-start | bytes 442376 | tf_op jit(solution)/shard_map/ppermute | solution.py:1006
  24.7 1.7 fill.3.refs_0_
  26.3 4.0 %bias_rows.1.bias_ref = f32[6,640,128]{2,1,0:T(8,128)} custom-call(f32[32,6]{1,0:T(8,128)} %broadcast_select_fusion.6.table_ref), custom_call_target="tpu_custom_call" | custom-call | flops 1 | bytes 1 | tf_op jit(solution)/shard_map/bias_rows/pallas_call | solution.py:96
  30.4 4.3 %collective-permute-done.7.refs_2_ = bf16[4,2,24,384]{3,2,1,0:T(8,128)(2,1)S(1)} collective-permute-done((bf16[4,2,24,384]{3,2,1,0:T(8,128)(2,1)}, bf16[4,2,24,384]{3,2,1,0:T(8,128)(2,1)S(1)}, u32[]{:S(2)}, u32[]{:S(2)}) %collective-permute-start.7) | collective-permute-done | bytes 147488 | tf_op jit(solution)/shard_map/ppermute | solution.py:1006
  37.1 2.3 %join.2 = bf16[4,2,4,24,384]{4,3,2,1,0:T(8,128)(2,1)} custom-call(s32[4]{0:T(128)} %get-tuple-element.313.order_ref, bf16[4,2,24,384]{3,2,1,0:T(8,128)(2,1)} %fill.2.refs_0_, bf16[4,2,24,384]{3,2,1,0:T(8,128)(2,1)} %copy-done.40, bf16[4,2,24,384]{3,2,1,0:T(8,128)(2,1)} %copy-done.39, bf16[4,2,24,384]{3,2,1,0:T(8,128)(2,1)} %copy-done.38), custom_call_target="tpu_custom_call" | custom-call | flops 1 | bytes 1 | tf_op jit(solution)/shard_map/join/pallas_call | solution.py:1025
  40.0 1.4 collective-permute-start.12
  41.5 1.5 collective-permute-start.11
  44.6 4.1 %place_rows.1 = (bf16[1024,768]{1,0:T(8,128)(2,1)}, bf16[768,1024]{1,0:T(8,128)(2,1)}, f32[1024,256]{1,0:T(8,128)}) custom-call(s32[5]{0:T(128)} %stack.206.meta_ref, bf16[4,144,768]{2,1,0:T(8,128)(2,1)} %copy-done.4, bf16[4,144,768]{2,1,0:T(8,128)(2,1)} %collective-permute-done.9.far_ref), custom_call_target="tpu_custom_call" | custom-call | flops 1 | bytes 1 | tf_op jit(solution)/shard_map/place_rows/pallas_call | solution.py:234
  48.8 2.1 collective-permute-start.14
  52.4 6.3 %collective-permute-done.14.refs_2_ = bf16[2,2,24,1024]{3,2,1,0:T(8,128)(2,1)S(1)} collective-permute-done((bf16[2,2,24,1024]{3,2,1,0:T(8,128)(2,1)}, bf16[2,2,24,1024]{3,2,1,0:T(8,128)(2,1)S(1)}, u32[]{:S(2)}, u32[]{:S(2)}) %collective-permute-start.14) | collective-permute-done | bytes 196640 | tf_op jit(solution)/shard_map/ppermute | solution.py:1006
  60.8 9.2 %collective-permute-done.15.refs_3_ = bf16[2,2,24,1024]{3,2,1,0:T(8,128)(2,1)S(1)} collective-permute-done((bf16[2,2,24,1024]{3,2,1,0:T(8,128)(2,1)S(1)}, bf16[2,2,24,1024]{3,2,1,0:T(8,128)(2,1)S(1)}, u32[]{:S(2)}, u32[]{:S(2)}) %collective-permute-start.15) | collective-permute-done | bytes 196640 | tf_op jit(solution)/shard_map/ppermute | solution.py:1006
  70.7 2.2 join.3
  73.5 1.5 collective-permute-start.18
  75.0 12.7 %attend.1 = (bf16[256,384]{1,0:T(8,128)(2,1)}, bf16[1024,384]{1,0:T(8,128)(2,1)}, bf16[1024,384]{1,0:T(8,128)(2,1)}, f32[6,1024,256]{2,1,0:T(8,128)}, f32[256,38...) custom-call(s32[4]{0:T(128)} %get-tuple-element.314.meta_ref, ...), custom_call_target="tpu_custom_call" | custom-call | flops 1 | bytes 1 | tf_op jit(solution)/shard_map/attend/pallas_call | solution.py:328
  87.8 1.6 collective-permute-done.17.their_ref
  89.5 2.0 collective-permute-done.19.refs_2_
  94.2 1.5 collective-permute-start.22
  95.7 1.5 collective-permute-start.23
  100.0 4.9 %mix.1 = (f32[256,768]{1,0:T(8,128)}, bf16[256,768]{1,0:T(8,128)(2,1)}, bf16[768,256]{1,0:T(8,128)(2,1)}, bf16[768,256]{1,0:T(8,128)(2,1)}, bf16[768,768]{1,0:T(8,128)(2,1)}) custom-call(s32[9]{0:T(128)} %stack.201.meta_ref, f32[256,768]{1,0:T(8,128)} %pad_maximum_fusion.1.tokens_ref, bf16[256,384]{1,0:T(8,128)(2,1)} %get-tuple-element.183.own_ref, ...), custom_call_target="tpu_custom_call" | custom-call | flops 1 | bytes 1 | tf_op jit(solution)/shard_map/mix/pallas_call | solution.py:403
  107.3 3.0 %collective-permute-done.24.refs_8_ = bf16[4,64,768]{2,1,0:T(8,128)(2,1)} collective-permute-done((bf16[4,64,768]{2,1,0:T(8,128)(2,1)}, bf16[4,64,768]{2,1,0:T(8,128)(2,1)}, u32[]{:S(2)}, u32[]{:S(2)}) %collective-permute-start.24) | collective-permute-done | bytes 393248 | tf_op jit(solution)/shard_map/ppermute | solution.py:1006
  110.3 11.8 %feed.1 = (f32[256,768]{1,0:T(8,128)}, f32[256,768]{1,0:T(8,128)}, bf16[2,192,1024]{2,1,0:T(8,128)(2,1)}, bf16[2,192,1024]{2,1,0:T(8,128)(2,1)}, bf16[2,192,1024...) custom-call(s32[36]{0:T(128)} %stack.246.meta_ref, ...), custom_call_target="tpu_custom_call" | custom-call | flops 1 | bytes 1 | tf_op jit(solution)/shard_map/feed/pallas_call | solution.py:531
  123.8 2.4 %collective-permute-start.28 = (bf16[2,192,1024]{2,1,0:T(8,128)(2,1)}, bf16[2,192,1024]{2,1,0:T(8,128)(2,1)}, u32[]{:S(2)}, u32[]{:S(2)}) collective-permute-start(bf16[2,192,1024]{2,1,0:T(8,128)(2,1)} %get-tuple-element.226), channel_id=1, source_target_pairs={{0,24},{4,28},{8,16},{12,20},{16,8},{20,12},{24,0},{28,4},{1,25},{... | collective-permute-start | bytes 2359304 | tf_op jit(solution)/shard_map/ppermute | solution.py:1001
  127.1 3.7 %settle.1 = (f32[256,768]{1,0:T(8,128)}, bf16[256,384]{1,0:T(8,128)(2,1)}, f32[1,768]{1,0:T(1,128)}, bf16[256,768]{1,0:T(8,128)(2,1)}) custom-call(s32[1]{0:T(128)} %bitcast.core_ref.meta_ref, f32[256,768]{1,0:T(8,128)} %get-tuple-element.194.mixed_ref, f32[256,768]{1,0:T(8,128)} %pad_maximum_fusion.2.cot_ref, f32[256,768]{1,0:T(8,128)} %get-tuple-element.205.back_ref, ...), custom_call_target="tpu_custom_call" | custom-call | flops 1 | bytes 1 | tf_op jit(solution)/shard_map/settle/pallas_call | solution.py:593
  130.9 7.9 %retreat.1 = (bf16[256,384]{1,0:T(8,128)(2,1)}, bf16[1024,768]{1,0:T(8,128)(2,1)}, f32[3,8,128]{2,1,0:T(8,128)}) custom-call(s32[1]{0:T(128)} %bitcast.11.meta_ref, bf16[256,384]{1,0:T(8,128)(2,1)} %get-tuple-element.207.do_ref, f32[256,384]{1,0:T(8,128)} %get-tuple-element.208.o_ref, bf16[256,384]{1,0:T(8,128)(2,1)} %get-tuple-element.209.q_ref, ...), custom_call_target="tpu_custom_call" | custom-call | flops 1 | bytes 1 | tf_op jit(solution)/shard_map/retreat/pallas_call | solution.py:692
  138.8 7.3 %weight_grads.1 = (bf16[784,384]{1,0:T(8,128)(2,1)}, bf16[784,384]{1,0:T(8,128)(2,1)}, bf16[784,384]{1,0:T(8,128)(2,1)}, bf16[784,384]{1,0:T(8,128)(2,1)}) custom-call(s32[6]{0:T(128)} %stack.213.meta_ref, bf16[768,1024]{1,0:T(8,128)(2,1)} %get-tuple-element.195.turned_ref, bf16[256,384]{1,0:T(8,128)(2,1)} %get-tuple-element.228.dq_ref, ...), custom_call_target="tpu_custom_call" | custom-call | flops 1 | bytes 1 | tf_op jit(solution)/shard_map/weight_grads/pallas_call | solution.py:808
  146.0 5.9 %row_grads.1 = (bf16[4,128,768]{2,1,0:T(8,128)(2,1)}, bf16[4,128,768]{2,1,0:T(8,128)(2,1)}) custom-call(s32[6]{0:T(128)} %stack.213.meta_ref, bf16[256,384]{1,0:T(8,128)(2,1)} %get-tuple-element.228.dq_ref, bf16[1024,768]{1,0:T(8,128)(2,1)} %get-tuple-element.214.dkv_ref, bf16[4,192,384]{2,1,0:T(8,128)(2,1)} %bitcast.126, bf16[4,192,384]{2,1,0:T(8,128)(2,1)} %copy-done.3, ...), custom_call_target="tpu_custom_call" | custom-call | flops 1 | bytes 1 | tf_op jit(solution)/shard_map/row_grads/pallas_call | solution.py:856
  152.0 8.1 %collective-permute-done.27.refs_2_ = bf16[2,192,1024]{2,1,0:T(8,128)(2,1)} collective-permute-done((bf16[2,192,1024]{2,1,0:T(8,128)(2,1)}, bf16[2,192,1024]{2,1,0:T(8,128)(2,1)}, u32[]{:S(2)}, u32[]{:S(2)}) %collective-permute-start.27) | collective-permute-done | bytes 786464 | tf_op jit(solution)/shard_map/ppermute | solution.py:1001
  162.4 2.4 %collective-permute-start.33 = (bf16[784,384]{1,0:T(8,128)(2,1)}, bf16[784,384]{1,0:T(8,128)(2,1)}, u32[]{:S(2)}, u32[]{:S(2)}) collective-permute-start(bf16[784,384]{1,0:T(8,128)(2,1)} %get-tuple-element.233), channel_id=1, source_target_pairs={{0,24},{4,28},{8,16},{12,20},{16,8},{20,12},{24,0},{28,4},{1,25},{... | collective-permute-start | bytes 1806344 | tf_op jit(solution)/shard_map/ppermute | solution.py:1001
  164.8 2.8 %cut_plane.1 = (bf16[2,2,48,1024]{3,2,1,0:T(8,128)(2,1)}, bf16[2,2,48,1024]{3,2,1,0:T(8,128)(2,1)}) custom-call(s32[1]{0:T(128)} %bitcast.54.side_ref, bf16[2,192,1024]{2,1,0:T(8,128)(2,1)} %get-tuple-element.234.refs_0_, bf16[2,192,1024]{2,1,0:T(8,128)(2,1)} %copy-done.20, bf16[2,192,1024]{2,1,0:T(8,128)(2,1)} %collective-permute-done.27.refs_2_, ...), custom_call_target="tpu_custom_call" | custom-call | flops 1 | bytes 1 | tf_op jit(solution)/shard_map/cut_plane/pallas_call | solution.py:886
  169.8 2.2 collective-permute-start.34
  172.5 14.2 %collective-permute-done.35 = bf16[1,4,64,768]{3,2,1,0:T(8,128)(2,1)S(1)} collective-permute-done((bf16[1,4,64,768]{3,2,1,0:T(8,128)(2,1)}, bf16[1,4,64,768]{3,2,1,0:T(8,128)(2,1)S(1)}, u32[]{:S(2)}, u32[]{:S(2)}) %collective-permute-start.35) | collective-permute-done | bytes 393248 | tf_op jit(solution)/shard_map/ppermute | solution.py:1068
  186.7 2.9 %collective-permute-done.34 = bf16[2,2,2,24,1024]{4,3,2,1,0:T(8,128)(2,1)} collective-permute-done((bf16[2,2,2,24,1024]{4,3,2,1,0:T(8,128)(2,1)}, bf16[2,2,2,24,1024]{4,3,2,1,0:T(8,128)(2,1)}, u32[]{:S(2)}, u32[]{:S(2)}) %collective-permute-start.34) | collective-permute-done | bytes 393248 | tf_op jit(solution)/shard_map/ppermute | solution.py:1068
  192.0 3.0 %sum_plane.1 = (bf16[208,384]{1,0:T(8,128)(2,1)}, bf16[208,384]{1,0:T(8,128)(2,1)}, bf16[208,384]{1,0:T(8,128)(2,1)}, bf16[208,384]{1,0:T(8,128)(2,1)}) custom-call(s32[4]{0:T(128)} %pad_add_fusion.2.order_ref, bf16[784,384]{1,0:T(8,128)(2,1)} %get-tuple-element.253.refs_0_, bf16[784,384]{1,0:T(8,128)(2,1)} %collective-permute-done.31.refs_1_, ...), custom_call_target="tpu_custom_call" | custom-call | flops 1 | bytes 1 | tf_op jit(solution)/shard_map/sum_plane/pallas_call | solution.py:922
  195.0 2.0 collective-permute-start.40
  197.0 2.4 %collective-permute-start.42 = (bf16[208,384]{1,0:T(8,128)(2,1)}, bf16[208,384]{1,0:T(8,128)(2,1)}, u32[]{:S(2)}, u32[]{:S(2)}) collective-permute-start(bf16[208,384]{1,0:T(8,128)(2,1)} %get-tuple-element.260), channel_id=1, source_target_pairs={{0,3},{1,0},{2,1},{3,2},{4,7},{5,4},{6,5},{7,6},{8,11},{9,8},{10,9... | collective-permute-start | bytes 479240 | tf_op jit(solution)/shard_map/ppermute | solution.py:1006
  202.3 2.8 %collective-permute-done.45 = bf16[2,64,768]{2,1,0:T(8,128)(2,1)S(1)} collective-permute-done((bf16[2,64,768]{2,1,0:T(8,128)(2,1)S(1)}, bf16[2,64,768]{2,1,0:T(8,128)(2,1)S(1)}, u32[]{:S(2)}, u32[]{:S(2)}) %collective-permute-start.45) | collective-permute-done | bytes 196640 | tf_op jit(solution)/shard_map/ppermute | solution.py:1001
  205.2 1.4 collective-permute-done.43
  206.6 1.5 collective-permute-start.38
  209.3 2.0 fusion.8
  212.1 2.0 last_sum.1
  214.9 1.8 add_bitcast_fusion.1
  220.0 1.5 collective-permute-start.46
  224.1 2.3 %attention_update.1 = (f32[4,24,768]{2,1,0:T(8,128)}, f32[4,24,768]{2,1,0:T(8,128)}, f32[4,24,768]{2,1,0:T(8,128)}, bf16[4,24,768]{2,1,0:T(8,128)(2,1)}) custom-call(s32[1]{0:T(128)} %bitcast.core_ref.meta_ref, f32[208,384]{1,0:T(8,128)} %get-tuple-element.267.sum_ref, f32[88,384]{1,0:T(8,128)} %copy-done.37, f32[4,24,768]{2,1,0:T(8,128)} %weight_ref.1, ...), custom_call_target="tpu_custom_call" | custom-call | flops 1 | bytes 1 | tf_op jit(solution)/shard_map/attention_update/pallas_call | solution.py:983
  (222 shorter events, 49.2 us)
Async XLA Ops:
  0.7 3.3 %collective-permute-start.1 = (f32[128,768]{1,0:T(8,128)}, f32[128,768]{1,0:T(8,128)S(1)}, u32[]{:S(2)}, u32[]{:S(2)}) collective-permute-start(f32[128,768]{1,0:T(8,128)} %bitcast.137), channel_id=1, source_target_pairs={{0,4},{4,0},{8,12},{12,8},{16,20},{20,16},{24,28},{28,24},{1,5},{5... | collective-permute-start | bytes 1179656 | tf_op jit(solution)/shard_map/ppermute | solution.py:996
  1.2 2.8 %collective-permute-start = (f32[128,768]{1,0:T(8,128)}, f32[128,768]{1,0:T(8,128)S(1)}, u32[]{:S(2)}, u32[]{:S(2)}) collective-permute-start(f32[128,768]{1,0:T(8,128)} %bitcast.127), channel_id=1, source_target_pairs={{0,4},{4,0},{8,12},{12,8},{16,20},{20,16},{24,28},{28,24},{1,5},{5... | collective-permute-start | bytes 1179656 | tf_op jit(solution)/shard_map/ppermute | solution.py:996
  4.8 10.9 %collective-permute-start.2 = (bf16[1,208,768]{2,1,0:T(8,128)(2,1)}, bf16[1,208,768]{2,1,0:T(8,128)(2,1)S(1)}, u32[]{:S(2)}, u32[]{:S(2)}) collective-permute-start(bf16[1,208,768]{2,1,0:T(8,128)(2,1)} %bitcast.132), channel_id=1, source_target_pairs={{0,8},{4,12},{8,0},{12,4},{16,24},{20,28},{24,16},{28,20},{1,9},{5... | collective-permute-start | bytes 958472 | tf_op jit(solution)/shard_map/ppermute | solution.py:1001
  7.7 1.5 collective-permute-start.3
  7.7 1.6 collective-permute-start.4
  16.8 19.2 %collective-permute-start.5 = (bf16[2,208,768]{2,1,0:T(8,128)(2,1)S(1)}, bf16[2,208,768]{2,1,0:T(8,128)(2,1)S(1)}, u32[]{:S(2)}, u32[]{:S(2)}) collective-permute-start(bf16[2,208,768]{2,1,0:T(8,128)(2,1)S(1)} %pad_maximum_fusion.3), channel_id=1, source_target_pairs={{0,16},{4,20},{8,24},{12,28},{16,0},{20,4},{24,8},{28,12},{1,17},{... | collective-permute-start | bytes 1916936 | tf_op jit(solution)/shard_map/ppermute | solution.py:1001
  18.8 11.6 %collective-permute-start.8 = (bf16[4,2,24,384]{3,2,1,0:T(8,128)(2,1)}, bf16[4,2,24,384]{3,2,1,0:T(8,128)(2,1)S(1)}, u32[]{:S(2)}, u32[]{:S(2)}) collective-permute-start(bf16[4,2,24,384]{3,2,1,0:T(8,128)(2,1)} %fill.2.refs_0_), channel_id=1, source_target_pairs={{0,3},{1,0},{2,1},{3,2},{4,7},{5,4},{6,5},{7,6},{8,11},{9,8},{10,9... | collective-permute-start | bytes 442376 | tf_op jit(solution)/shard_map/ppermute | solution.py:1006
  22.4 12.2 %collective-permute-start.7 = (bf16[4,2,24,384]{3,2,1,0:T(8,128)(2,1)}, bf16[4,2,24,384]{3,2,1,0:T(8,128)(2,1)S(1)}, u32[]{:S(2)}, u32[]{:S(2)}) collective-permute-start(bf16[4,2,24,384]{3,2,1,0:T(8,128)(2,1)} %fill.2.refs_0_), channel_id=1, source_target_pairs={{0,2},{1,3},{2,0},{3,1},{4,6},{5,7},{6,4},{7,5},{8,10},{9,11},{10,... | collective-permute-start | bytes 442376 | tf_op jit(solution)/shard_map/ppermute | solution.py:1006
  22.4 12.2 %collective-permute-start.6 = (bf16[4,2,24,384]{3,2,1,0:T(8,128)(2,1)}, bf16[4,2,24,384]{3,2,1,0:T(8,128)(2,1)S(1)}, u32[]{:S(2)}, u32[]{:S(2)}) collective-permute-start(bf16[4,2,24,384]{3,2,1,0:T(8,128)(2,1)} %fill.2.refs_0_), channel_id=1, source_target_pairs={{0,1},{1,2},{2,3},{3,0},{4,5},{5,6},{6,7},{7,4},{8,9},{9,10},{10,1... | collective-permute-start | bytes 442376 | tf_op jit(solution)/shard_map/ppermute | solution.py:1006
  39.4 5.1 %collective-permute-start.9 = (bf16[4,144,768]{2,1,0:T(8,128)(2,1)S(1)}, bf16[4,144,768]{2,1,0:T(8,128)(2,1)}, u32[]{:S(2)}, u32[]{:S(2)}) collective-permute-start(bf16[4,144,768]{2,1,0:T(8,128)(2,1)S(1)} %slice.106.near_ref), channel_id=1, source_target_pairs={{0,4},{4,0},{8,12},{12,8},{16,20},{20,16},{24,28},{28,24},{1,5},{5... | collective-permute-start | bytes 2654216 | tf_op jit(solution)/shard_map/ppermute | solution.py:996
  39.4 9.4 %collective-permute-start.13 = (bf16[2,2,24,1024]{3,2,1,0:T(8,128)(2,1)}, bf16[2,2,24,1024]{3,2,1,0:T(8,128)(2,1)}, u32[]{:S(2)}, u32[]{:S(2)}) collective-permute-start(bf16[2,2,24,1024]{3,2,1,0:T(8,128)(2,1)} %fill.3.refs_0_), channel_id=1, source_target_pairs={{0,1},{1,2},{2,3},{3,0},{4,5},{5,6},{6,7},{7,4},{8,9},{9,10},{10,1... | collective-permute-start | bytes 589832 | tf_op jit(solution)/shard_map/ppermute | solution.py:1006
  40.0 32.9 %collective-permute-start.12 = (bf16[4,192,384]{2,1,0:T(8,128)(2,1)}, bf16[4,192,384]{2,1,0:T(8,128)(2,1)S(1)}, u32[]{:S(2)}, u32[]{:S(2)}) collective-permute-start(bf16[4,192,384]{2,1,0:T(8,128)(2,1)} %bitcast.121), channel_id=1, source_target_pairs={{0,24},{4,28},{8,16},{12,20},{16,8},{20,12},{24,0},{28,4},{1,25},{... | collective-permute-start | bytes 1769480 | tf_op jit(solution)/shard_map/ppermute | solution.py:1001
  41.5 31.4 %collective-permute-start.11 = (bf16[4,192,384]{2,1,0:T(8,128)(2,1)}, bf16[4,192,384]{2,1,0:T(8,128)(2,1)S(1)}, u32[]{:S(2)}, u32[]{:S(2)}) collective-permute-start(bf16[4,192,384]{2,1,0:T(8,128)(2,1)} %bitcast.122), channel_id=1, source_target_pairs={{0,16},{4,20},{8,24},{12,28},{16,0},{20,4},{24,8},{28,12},{1,17},{... | collective-permute-start | bytes 1769480 | tf_op jit(solution)/shard_map/ppermute | solution.py:1001
  43.0 29.9 %collective-permute-start.10 = (bf16[4,192,384]{2,1,0:T(8,128)(2,1)}, bf16[4,192,384]{2,1,0:T(8,128)(2,1)S(1)}, u32[]{:S(2)}, u32[]{:S(2)}) collective-permute-start(bf16[4,192,384]{2,1,0:T(8,128)(2,1)} %bitcast.123), channel_id=1, source_target_pairs={{0,8},{4,12},{8,0},{12,4},{16,24},{20,28},{24,16},{28,20},{1,9},{5... | collective-permute-start | bytes 1769480 | tf_op jit(solution)/shard_map/ppermute | solution.py:1001
  48.8 9.8 %collective-permute-start.14 = (bf16[2,2,24,1024]{3,2,1,0:T(8,128)(2,1)}, bf16[2,2,24,1024]{3,2,1,0:T(8,128)(2,1)S(1)}, u32[]{:S(2)}, u32[]{:S(2)}) collective-permute-start(bf16[2,2,24,1024]{3,2,1,0:T(8,128)(2,1)} %collective-permute-done.13.refs_1_), channel_id=1, source_target_pairs={{0,1},{1,2},{2,3},{3,0},{4,5},{5,6},{6,7},{7,4},{8,9},{9,10},{10,1... | collective-permute-start | bytes 589832 | tf_op jit(solution)/shard_map/ppermute | solution.py:1006
  50.9 22.0 %collective-permute-start.16 = (bf16[4,64,768]{2,1,0:T(8,128)(2,1)S(1)}, bf16[4,64,768]{2,1,0:T(8,128)(2,1)}, u32[]{:S(2)}, u32[]{:S(2)}) collective-permute-start(bf16[4,64,768]{2,1,0:T(8,128)(2,1)S(1)} %pad_maximum_fusion.4.refs_5_), channel_id=1, source_target_pairs={{0,1},{1,2},{2,3},{3,0},{4,5},{5,6},{6,7},{7,4},{8,9},{9,10},{10,1... | collective-permute-start | bytes 1179656 | tf_op jit(solution)/shard_map/ppermute | solution.py:1006
  58.6 11.4 %collective-permute-start.15 = (bf16[2,2,24,1024]{3,2,1,0:T(8,128)(2,1)S(1)}, bf16[2,2,24,1024]{3,2,1,0:T(8,128)(2,1)S(1)}, u32[]{:S(2)}, u32[]{:S(2)}) collective-permute-start(bf16[2,2,24,1024]{3,2,1,0:T(8,128)(2,1)S(1)} %collective-permute-done.14.refs_2_), channel_id=1, source_target_pairs={{0,1},{1,2},{2,3},{3,0},{4,5},{5,6},{6,7},{7,4},{8,9},{9,10},{10,1... | collective-permute-start | bytes 589832 | tf_op jit(solution)/shard_map/ppermute | solution.py:1006
  72.9 18.6 %collective-permute-start.19 = (bf16[2,192,1024]{2,1,0:T(8,128)(2,1)}, bf16[2,192,1024]{2,1,0:T(8,128)(2,1)S(1)}, u32[]{:S(2)}, u32[]{:S(2)}) collective-permute-start(bf16[2,192,1024]{2,1,0:T(8,128)(2,1)} %bitcast.129), channel_id=1, source_target_pairs={{0,16},{4,20},{8,24},{12,28},{16,0},{20,4},{24,8},{28,12},{1,17},{... | collective-permute-start | bytes 2359304 | tf_op jit(solution)/shard_map/ppermute | solution.py:1001
  73.5 18.2 %collective-permute-start.18 = (bf16[2,192,1024]{2,1,0:T(8,128)(2,1)}, bf16[2,192,1024]{2,1,0:T(8,128)(2,1)S(1)}, u32[]{:S(2)}, u32[]{:S(2)}) collective-permute-start(bf16[2,192,1024]{2,1,0:T(8,128)(2,1)} %bitcast.130), channel_id=1, source_target_pairs={{0,8},{4,12},{8,0},{12,4},{16,24},{20,28},{24,16},{28,20},{1,9},{5... | collective-permute-start | bytes 2359304 | tf_op jit(solution)/shard_map/ppermute | solution.py:1001
  75.0 14.5 %collective-permute-start.20 = (bf16[4,64,768]{2,1,0:T(8,128)(2,1)}, bf16[4,64,768]{2,1,0:T(8,128)(2,1)}, u32[]{:S(2)}, u32[]{:S(2)}) collective-permute-start(bf16[4,64,768]{2,1,0:T(8,128)(2,1)} %collective-permute-done.16.refs_6_), channel_id=1, source_target_pairs={{0,1},{1,2},{2,3},{3,0},{4,5},{5,6},{6,7},{7,4},{8,9},{9,10},{10,1... | collective-permute-start | bytes 1179656 | tf_op jit(solution)/shard_map/ppermute | solution.py:1006
  87.7 1.7 collective-permute-start.17
  94.2 5.0 %collective-permute-start.21 = (bf16[4,192,384]{2,1,0:T(8,128)(2,1)S(1)}, bf16[4,192,384]{2,1,0:T(8,128)(2,1)S(1)}, u32[]{:S(2)}, u32[]{:S(2)}) collective-permute-start(bf16[4,192,384]{2,1,0:T(8,128)(2,1)S(1)} %copy-done.22), channel_id=1, source_target_pairs={{0,4},{4,0},{8,12},{12,8},{16,20},{20,16},{24,28},{28,24},{1,5},{5... | collective-permute-start | bytes 1769480 | tf_op jit(solution)/shard_map/ppermute | solution.py:996
  94.2 11.7 %collective-permute-start.22 = (bf16[1,192,1024]{2,1,0:T(8,128)(2,1)}, bf16[1,192,1024]{2,1,0:T(8,128)(2,1)S(1)}, u32[]{:S(2)}, u32[]{:S(2)}) collective-permute-start(bf16[1,192,1024]{2,1,0:T(8,128)(2,1)} %slice.86), channel_id=1, source_target_pairs={{0,16},{4,20},{8,24},{12,28},{16,0},{20,4},{24,8},{28,12},{1,17},{... | collective-permute-start | bytes 1179656 | tf_op jit(solution)/shard_map/ppermute | solution.py:1001
  95.7 11.6 %collective-permute-start.23 = (bf16[1,192,1024]{2,1,0:T(8,128)(2,1)}, bf16[1,192,1024]{2,1,0:T(8,128)(2,1)}, u32[]{:S(2)}, u32[]{:S(2)}) collective-permute-start(bf16[1,192,1024]{2,1,0:T(8,128)(2,1)} %slice.87), channel_id=1, source_target_pairs={{0,8},{4,12},{8,0},{12,4},{16,24},{20,28},{24,16},{28,20},{1,9},{5... | collective-permute-start | bytes 1179656 | tf_op jit(solution)/shard_map/ppermute | solution.py:1001
  97.2 13.1 %collective-permute-start.24 = (bf16[4,64,768]{2,1,0:T(8,128)(2,1)}, bf16[4,64,768]{2,1,0:T(8,128)(2,1)}, u32[]{:S(2)}, u32[]{:S(2)}) collective-permute-start(bf16[4,64,768]{2,1,0:T(8,128)(2,1)} %collective-permute-done.20.refs_7_), channel_id=1, source_target_pairs={{0,1},{1,2},{2,3},{3,0},{4,5},{5,6},{6,7},{7,4},{8,9},{9,10},{10,1... | collective-permute-start | bytes 1179656 | tf_op jit(solution)/shard_map/ppermute | solution.py:1006
  122.1 4.2 %collective-permute-start.25 = (f32[256,768]{1,0:T(8,128)}, f32[256,768]{1,0:T(8,128)S(1)}, u32[]{:S(2)}, u32[]{:S(2)}) collective-permute-start(f32[256,768]{1,0:T(8,128)} %get-tuple-element.205.back_ref), channel_id=1, source_target_pairs={{0,4},{4,0},{8,12},{12,8},{16,20},{20,16},{24,28},{28,24},{1,5},{5... | collective-permute-start | bytes 2359304 | tf_op jit(solution)/shard_map/ppermute | solution.py:996
  122.7 29.3 %collective-permute-start.26 = (bf16[2,192,1024]{2,1,0:T(8,128)(2,1)}, bf16[2,192,1024]{2,1,0:T(8,128)(2,1)S(1)}, u32[]{:S(2)}, u32[]{:S(2)}) collective-permute-start(bf16[2,192,1024]{2,1,0:T(8,128)(2,1)} %get-tuple-element.224), channel_id=1, source_target_pairs={{0,8},{4,12},{8,0},{12,4},{16,24},{20,28},{24,16},{28,20},{1,9},{5... | collective-permute-start | bytes 2359304 | tf_op jit(solution)/shard_map/ppermute | solution.py:1001
  123.3 36.8 %collective-permute-start.27 = (bf16[2,192,1024]{2,1,0:T(8,128)(2,1)}, bf16[2,192,1024]{2,1,0:T(8,128)(2,1)}, u32[]{:S(2)}, u32[]{:S(2)}) collective-permute-start(bf16[2,192,1024]{2,1,0:T(8,128)(2,1)} %get-tuple-element.225), channel_id=1, source_target_pairs={{0,16},{4,20},{8,24},{12,28},{16,0},{20,4},{24,8},{28,12},{1,17},{... | collective-permute-start | bytes 2359304 | tf_op jit(solution)/shard_map/ppermute | solution.py:1001
  123.8 36.3 %collective-permute-start.28 = (bf16[2,192,1024]{2,1,0:T(8,128)(2,1)}, bf16[2,192,1024]{2,1,0:T(8,128)(2,1)}, u32[]{:S(2)}, u32[]{:S(2)}) collective-permute-start(bf16[2,192,1024]{2,1,0:T(8,128)(2,1)} %get-tuple-element.226), channel_id=1, source_target_pairs={{0,24},{4,28},{8,16},{12,20},{16,8},{20,12},{24,0},{28,4},{1,25},{... | collective-permute-start | bytes 2359304 | tf_op jit(solution)/shard_map/ppermute | solution.py:1001
  126.2 35.1 %collective-permute-start.29 = (bf16[2,4,64,768]{3,2,1,0:T(8,128)(2,1)}, bf16[2,4,64,768]{3,2,1,0:T(8,128)(2,1)}, u32[]{:S(2)}, u32[]{:S(2)}) collective-permute-start(bf16[2,4,64,768]{3,2,1,0:T(8,128)(2,1)} %get-tuple-element.227), channel_id=1, source_target_pairs={{0,2},{1,3},{2,0},{3,1},{4,6},{5,7},{6,4},{7,5},{8,10},{9,11},{10,... | collective-permute-start | bytes 2359304 | tf_op jit(solution)/shard_map/ppermute | solution.py:1068
  151.9 9.4 %collective-permute-start.30 = (bf16[4,128,768]{2,1,0:T(8,128)(2,1)}, bf16[4,128,768]{2,1,0:T(8,128)(2,1)S(1)}, u32[]{:S(2)}, u32[]{:S(2)}) collective-permute-start(bf16[4,128,768]{2,1,0:T(8,128)(2,1)} %get-tuple-element.229), channel_id=1, source_target_pairs={{0,4},{4,0},{8,12},{12,8},{16,20},{20,16},{24,28},{28,24},{1,5},{5... | collective-permute-start | bytes 2359304 | tf_op jit(solution)/shard_map/ppermute | solution.py:996
  161.3 28.3 %collective-permute-start.31 = (bf16[784,384]{1,0:T(8,128)(2,1)}, bf16[784,384]{1,0:T(8,128)(2,1)}, u32[]{:S(2)}, u32[]{:S(2)}) collective-permute-start(bf16[784,384]{1,0:T(8,128)(2,1)} %get-tuple-element.231), channel_id=1, source_target_pairs={{0,8},{4,12},{8,0},{12,4},{16,24},{20,28},{24,16},{28,20},{1,9},{5... | collective-permute-start | bytes 1806344 | tf_op jit(solution)/shard_map/ppermute | solution.py:1001
  161.9 28.5 %collective-permute-start.32 = (bf16[784,384]{1,0:T(8,128)(2,1)}, bf16[784,384]{1,0:T(8,128)(2,1)}, u32[]{:S(2)}, u32[]{:S(2)}) collective-permute-start(bf16[784,384]{1,0:T(8,128)(2,1)} %get-tuple-element.232), channel_id=1, source_target_pairs={{0,16},{4,20},{8,24},{12,28},{16,0},{20,4},{24,8},{28,12},{1,17},{... | collective-permute-start | bytes 1806344 | tf_op jit(solution)/shard_map/ppermute | solution.py:1001
  162.4 27.9 %collective-permute-start.33 = (bf16[784,384]{1,0:T(8,128)(2,1)}, bf16[784,384]{1,0:T(8,128)(2,1)}, u32[]{:S(2)}, u32[]{:S(2)}) collective-permute-start(bf16[784,384]{1,0:T(8,128)(2,1)} %get-tuple-element.233), channel_id=1, source_target_pairs={{0,24},{4,28},{8,16},{12,20},{16,8},{20,12},{24,0},{28,4},{1,25},{... | collective-permute-start | bytes 1806344 | tf_op jit(solution)/shard_map/ppermute | solution.py:1001
  167.6 22.7 %copy-start.26 = (bf16[2,2,48,1024]{3,2,1,0:T(8,128)(2,1)S(1)}, bf16[2,2,48,1024]{3,2,1,0:T(8,128)(2,1)}, u32[]{:S(2)}) copy-start(bf16[2,2,48,1024]{3,2,1,0:T(8,128)(2,1)} %get-tuple-element.250) | copy-start | bytes 1179652
  169.8 17.0 %collective-permute-start.35 = (bf16[1,4,64,768]{3,2,1,0:T(8,128)(2,1)}, bf16[1,4,64,768]{3,2,1,0:T(8,128)(2,1)S(1)}, u32[]{:S(2)}, u32[]{:S(2)}) collective-permute-start(bf16[1,4,64,768]{3,2,1,0:T(8,128)(2,1)} %constant_dynamic-slice_fusion.2), channel_id=1, source_target_pairs={{0,1},{1,0},{2,3},{3,2},{4,5},{5,4},{6,7},{7,6},{8,9},{9,8},{10,11... | collective-permute-start | bytes 1179656 | tf_op jit(solution)/shard_map/ppermute | solution.py:1068
  169.8 19.9 %collective-permute-start.34 = (bf16[2,2,2,24,1024]{4,3,2,1,0:T(8,128)(2,1)}, bf16[2,2,2,24,1024]{4,3,2,1,0:T(8,128)(2,1)}, u32[]{:S(2)}, u32[]{:S(2)}) collective-permute-start(bf16[2,2,2,24,1024]{4,3,2,1,0:T(8,128)(2,1)} %bitcast.55), channel_id=1, source_target_pairs={{0,2},{1,3},{2,0},{3,1},{4,6},{5,7},{6,4},{7,5},{8,10},{9,11},{10,... | collective-permute-start | bytes 1179656 | tf_op jit(solution)/shard_map/ppermute | solution.py:1068
  191.7 9.7 %collective-permute-start.37 = (bf16[2,2,1,24,1024]{4,3,2,1,0:T(8,128)(2,1)S(1)}, bf16[2,2,1,24,1024]{4,3,2,1,0:T(8,128)(2,1)S(1)}, u32[]{:S(2)}, u32[]{:S(2)}) collective-permute-start(bf16[2,2,1,24,1024]{4,3,2,1,0:T(8,128)(2,1)S(1)} %constant_dynamic-slice_fusion), channel_id=1, source_target_pairs={{0,1},{1,0},{2,3},{3,2},{4,5},{5,4},{6,7},{7,6},{8,9},{9,8},{10,11... | collective-permute-start | bytes 589832 | tf_op jit(solution)/shard_map/ppermute | solution.py:1068
  195.0 17.1 %collective-permute-start.40 = (bf16[208,384]{1,0:T(8,128)(2,1)}, bf16[208,384]{1,0:T(8,128)(2,1)}, u32[]{:S(2)}, u32[]{:S(2)}) collective-permute-start(bf16[208,384]{1,0:T(8,128)(2,1)} %get-tuple-element.258), channel_id=1, source_target_pairs={{0,1},{1,2},{2,3},{3,0},{4,5},{5,6},{6,7},{7,4},{8,9},{9,10},{10,1... | collective-permute-start | bytes 479240 | tf_op jit(solution)/shard_map/ppermute | solution.py:1006
  197.0 15.1 %collective-permute-start.41 = (bf16[208,384]{1,0:T(8,128)(2,1)}, bf16[208,384]{1,0:T(8,128)(2,1)}, u32[]{:S(2)}, u32[]{:S(2)}) collective-permute-start(bf16[208,384]{1,0:T(8,128)(2,1)} %get-tuple-element.259), channel_id=1, source_target_pairs={{0,2},{1,3},{2,0},{3,1},{4,6},{5,7},{6,4},{7,5},{8,10},{9,11},{10,... | collective-permute-start | bytes 479240 | tf_op jit(solution)/shard_map/ppermute | solution.py:1006
  197.0 15.1 %collective-permute-start.42 = (bf16[208,384]{1,0:T(8,128)(2,1)}, bf16[208,384]{1,0:T(8,128)(2,1)}, u32[]{:S(2)}, u32[]{:S(2)}) collective-permute-start(bf16[208,384]{1,0:T(8,128)(2,1)} %get-tuple-element.260), channel_id=1, source_target_pairs={{0,3},{1,0},{2,1},{3,2},{4,7},{5,4},{6,5},{7,6},{8,11},{9,8},{10,9... | collective-permute-start | bytes 479240 | tf_op jit(solution)/shard_map/ppermute | solution.py:1006
  199.4 5.7 %collective-permute-start.45 = (bf16[2,64,768]{2,1,0:T(8,128)(2,1)S(1)}, bf16[2,64,768]{2,1,0:T(8,128)(2,1)S(1)}, u32[]{:S(2)}, u32[]{:S(2)}) collective-permute-start(bf16[2,64,768]{2,1,0:T(8,128)(2,1)S(1)} %slice.97), channel_id=1, source_target_pairs={{0,16},{4,20},{8,24},{12,28},{16,0},{20,4},{24,8},{28,12},{1,17},{... | collective-permute-start | bytes 589832 | tf_op jit(solution)/shard_map/ppermute | solution.py:1001
  201.4 13.5 %collective-permute-start.36 = (f32[128,768]{1,0:T(8,128)}, f32[128,768]{1,0:T(8,128)}, u32[]{:S(2)}, u32[]{:S(2)}) collective-permute-start(f32[128,768]{1,0:T(8,128)} %constant_dynamic-slice_fusion.1), channel_id=1, source_target_pairs={{0,4},{4,0},{8,12},{12,8},{16,20},{20,16},{24,28},{28,24},{1,5},{5... | collective-permute-start | bytes 1179656 | tf_op jit(solution)/shard_map/ppermute | solution.py:996
  205.1 1.4 collective-permute-start.43
  206.6 11.5 %collective-permute-start.38 = (bf16[2,128,768]{2,1,0:T(8,128)(2,1)}, bf16[2,128,768]{2,1,0:T(8,128)(2,1)}, u32[]{:S(2)}, u32[]{:S(2)}) collective-permute-start(bf16[2,128,768]{2,1,0:T(8,128)(2,1)} %slice.91), channel_id=1, source_target_pairs={{0,8},{4,12},{8,0},{12,4},{16,24},{20,28},{24,16},{28,20},{1,9},{5... | collective-permute-start | bytes 1179656 | tf_op jit(solution)/shard_map/ppermute | solution.py:1001
  214.8 4.4 %collective-permute-start.44 = (f32[88,384]{1,0:T(8,128)}, f32[88,384]{1,0:T(8,128)S(1)}, u32[]{:S(2)}, u32[]{:S(2)}) collective-permute-start(f32[88,384]{1,0:T(8,128)} %get-tuple-element.268), channel_id=1, source_target_pairs={{0,4},{4,0},{8,12},{12,8},{16,20},{20,16},{24,28},{28,24},{1,5},{5... | collective-permute-start | bytes 405512 | tf_op jit(solution)/shard_map/ppermute | solution.py:996
  220.0 6.4 %collective-permute-start.46 = (bf16[1,64,768]{2,1,0:T(8,128)(2,1)S(1)}, bf16[1,64,768]{2,1,0:T(8,128)(2,1)S(1)}, u32[]{:S(2)}, u32[]{:S(2)}) collective-permute-start(bf16[1,64,768]{2,1,0:T(8,128)(2,1)S(1)} %slice.99), channel_id=1, source_target_pairs={{0,8},{4,12},{8,0},{12,4},{16,24},{20,28},{24,16},{28,20},{1,9},{5... | collective-permute-start | bytes 294920 | tf_op jit(solution)/shard_map/ppermute | solution.py:1001
  221.6 6.4 %collective-permute-start.39 = (bf16[1,128,768]{2,1,0:T(8,128)(2,1)S(1)}, bf16[1,128,768]{2,1,0:T(8,128)(2,1)S(1)}, u32[]{:S(2)}, u32[]{:S(2)}) collective-permute-start(bf16[1,128,768]{2,1,0:T(8,128)(2,1)S(1)} %get-tuple-element.302), channel_id=1, source_target_pairs={{0,16},{4,20},{8,24},{12,28},{16,0},{20,4},{24,8},{28,12},{1,17},{... | collective-permute-start | bytes 589832 | tf_op jit(solution)/shard_map/ppermute | solution.py:1001
  (49 other events, 320.3 us)

commit v7 on v6

--- a/solution.py
+++ b/solution.py
@@ -1172,7 +1172,9 @@
     gu_blocks = [after(gu_block, attn_joined)]
     for step in range(1, places):
         if step == 2:
-            gu_blocks[-1], down_block = lax.optimization_barrier((gu_blocks[-1], down_block, rows_full))[:2]
+            gu_blocks[-1], down_block = lax.optimization_barrier((gu_blocks[-1], down_block, far_rows))[:2]
+        if step == 3:
+            gu_blocks[-1] = after(gu_blocks[-1], rows_full)
         gu_blocks.append(along(gu_blocks[-1], 1))
     down_pieces = [down_block, along(down_block, 1)]
     gu_joined = join(gu_blocks, order)

time: 230 us -> 230 us (level)
  transfers between devices with their start and end apart: 47 -> 47, of which waited for: 21 -> 21; matrix products, arithmetic and copies ran while one was open for 11% -> 12% of each run, Pallas kernels for 30% -> 30%
where the time goes in v7:
time: 230 us; the launch traced here: 229 us
  Pallas kernels  82.3 us (36%)
  waiting for transfers between devices  67 us (29%)
  starting transfers between devices  38.2 us (17%)
  other arithmetic  23.8 us (10%)
  local copies, waits for them, and re-layouts  16.4 us (7%)
    ppermute x19, starting transfers between devices, plane_swap(): return lax.ppermute(value, 'seq', [(i, i ^ 2 * step) for i in range(count)])  25.1 us
    ppermute x12, waiting for transfers between devices, along(): lax.ppermute(value, 'batch', [(i, (i + step) % count) for i in range(coun...  23 us
    ppermute x19, waiting for transfers between devices, plane_swap(): return lax.ppermute(value, 'seq', [(i, i ^ 2 * step) for i in range(count)])  21.7 us
    ppermute x4, waiting for transfers between devices, across(): return lax.ppermute(value, 'batch', [(i, i ^ step) for i in range(count)])  18.2 us
    pallas_call x1, Pallas kernels, attend(): pl.pallas_call(functools.partial(attend_kernel, len(pieces)), grid_spec=p...  12.7 us
    pallas_call x1, Pallas kernels, feed(): pl.pallas_call(functools.partial(feed_kernel, chips, places, len(gu_piece...  11.7 us
    ppermute x12, starting transfers between devices, along(): lax.ppermute(value, 'batch', [(i, (i + step) % count) for i in range(coun...  9.43 us
    pallas_call x1, Pallas kernels, retreat(): pl.pallas_call(retreat_kernel, grid_spec=pltpu.PrefetchScalarGridSpec(num...  7.88 us
  transfers between devices with their start and end apart: 47, of which 21 were waited for; matrix products, arithmetic and copies ran while one was open for 12% of the time, Pallas kernels for 30%

profile of v7, /device:TPU:0, one launch (start us, length us, event | category | flops | bytes accessed | tf_op | source)
XLA Modules:
  0.0 228.9 jit_solution(3006896714726869239)
XLA Ops:
  1.8 2.2 make_ready.1
  4.8 2.9 %collective-permute-start.2 = (bf16[1,208,768]{2,1,0:T(8,128)(2,1)}, bf16[1,208,768]{2,1,0:T(8,128)(2,1)S(1)}, u32[]{:S(2)}, u32[]{:S(2)}) collective-permute-start(bf16[1,208,768]{2,1,0:T(8,128)(2,1)} %bitcast.132), channel_id=1, source_target_pairs={{0,8},{4,12},{8,0},{12,4},{16,24},{20,28},{24,16},{28,20},{1,9},{5... | collective-permute-start | bytes 958472 | tf_op jit(solution)/shard_map/ppermute | solution.py:1001
  9.9 1.6 fill.2.refs_0_
  11.5 4.2 %collective-permute-done.2 = bf16[1,208,768]{2,1,0:T(8,128)(2,1)S(1)} collective-permute-done((bf16[1,208,768]{2,1,0:T(8,128)(2,1)}, bf16[1,208,768]{2,1,0:T(8,128)(2,1)S(1)}, u32[]{:S(2)}, u32[]{:S(2)}) %collective-permute-start.2) | collective-permute-done | bytes 319520 | tf_op jit(solution)/shard_map/ppermute | solution.py:1001
  16.8 1.8 collective-permute-start.5
  18.8 3.6 %collective-permute-start.8 = (bf16[4,2,24,384]{3,2,1,0:T(8,128)(2,1)}, bf16[4,2,24,384]{3,2,1,0:T(8,128)(2,1)S(1)}, u32[]{:S(2)}, u32[]{:S(2)}) collective-permute-start(bf16[4,2,24,384]{3,2,1,0:T(8,128)(2,1)} %fill.2.refs_0_), channel_id=1, source_target_pairs={{0,3},{1,0},{2,1},{3,2},{4,7},{5,4},{6,5},{7,6},{8,11},{9,8},{10,9... | collective-permute-start | bytes 442376 | tf_op jit(solution)/shard_map/ppermute | solution.py:1006
  24.7 1.7 fill.3.refs_0_
  26.3 4.0 %bias_rows.1.bias_ref = f32[6,640,128]{2,1,0:T(8,128)} custom-call(f32[32,6]{1,0:T(8,128)} %broadcast_select_fusion.6.table_ref), custom_call_target="tpu_custom_call" | custom-call | flops 1 | bytes 1 | tf_op jit(solution)/shard_map/bias_rows/pallas_call | solution.py:96
  30.4 4.3 %collective-permute-done.7.refs_2_ = bf16[4,2,24,384]{3,2,1,0:T(8,128)(2,1)S(1)} collective-permute-done((bf16[4,2,24,384]{3,2,1,0:T(8,128)(2,1)}, bf16[4,2,24,384]{3,2,1,0:T(8,128)(2,1)S(1)}, u32[]{:S(2)}, u32[]{:S(2)}) %collective-permute-start.7) | collective-permute-done | bytes 147488 | tf_op jit(solution)/shard_map/ppermute | solution.py:1006
  37.1 2.3 %join.2 = bf16[4,2,4,24,384]{4,3,2,1,0:T(8,128)(2,1)} custom-call(s32[4]{0:T(128)} %get-tuple-element.315.order_ref, bf16[4,2,24,384]{3,2,1,0:T(8,128)(2,1)} %fill.2.refs_0_, bf16[4,2,24,384]{3,2,1,0:T(8,128)(2,1)} %copy-done.40, bf16[4,2,24,384]{3,2,1,0:T(8,128)(2,1)} %copy-done.39, bf16[4,2,24,384]{3,2,1,0:T(8,128)(2,1)} %copy-done.38), custom_call_target="tpu_custom_call" | custom-call | flops 1 | bytes 1 | tf_op jit(solution)/shard_map/join/pallas_call | solution.py:1025
  41.5 1.5 collective-permute-start.11
  44.6 4.3 %collective-permute-done.13.refs_1_ = bf16[2,2,24,1024]{3,2,1,0:T(8,128)(2,1)} collective-permute-done((bf16[2,2,24,1024]{3,2,1,0:T(8,128)(2,1)}, bf16[2,2,24,1024]{3,2,1,0:T(8,128)(2,1)}, u32[]{:S(2)}, u32[]{:S(2)}) %collective-permute-start.13) | collective-permute-done | bytes 196640 | tf_op jit(solution)/shard_map/ppermute | solution.py:1006
  49.3 2.3 %broadcast_select_fusion.1 = (f32[128,768]{1,0:T(8,128)}, f32[128,768]{1,0:T(8,128)}, f32[128,768]{1,0:T(8,128)S(1)}, f32[128,768]{1,0:T(8,128)}) fusion(f32[128,768]{1,0:T(8,128)} %copy-done.30, pred[]{:T(512)S(6)} %eq.18, f32[1,128,768]{2,1,0:T(8,128)} %param.20, f32[128,768]{1,0:T(8,128)} %copy-done.31, f32[1,128,768]{2,1,0:T(8,128)S(1)} %copy-done), kind=kLoop, calls=%fused_computation.33 | loop fusion | flops 393216 | bytes 3145729 | tf_op jit(solution)/shard_map/jit(_where)/select_n | solution.py:1132
  51.6 4.0 %place_rows.1 = (bf16[1024,768]{1,0:T(8,128)(2,1)}, bf16[768,1024]{1,0:T(8,128)(2,1)}, f32[1024,256]{1,0:T(8,128)}) custom-call(s32[5]{0:T(128)} %stack.206.meta_ref, bf16[4,144,768]{2,1,0:T(8,128)(2,1)} %copy-done.4, bf16[4,144,768]{2,1,0:T(8,128)(2,1)} %collective-permute-done.9.far_ref), custom_call_target="tpu_custom_call" | custom-call | flops 1 | bytes 1 | tf_op jit(solution)/shard_map/place_rows/pallas_call | solution.py:234
  55.6 3.2 %collective-permute-done.14.refs_2_ = bf16[2,2,24,1024]{3,2,1,0:T(8,128)(2,1)} collective-permute-done((bf16[2,2,24,1024]{3,2,1,0:T(8,128)(2,1)}, bf16[2,2,24,1024]{3,2,1,0:T(8,128)(2,1)}, u32[]{:S(2)}, u32[]{:S(2)}) %collective-permute-start.14) | collective-permute-done | bytes 196640 | tf_op jit(solution)/shard_map/ppermute | solution.py:1006
  58.8 2.1 pad_maximum_fusion.2.cot_ref
  61.8 8.3 %collective-permute-done.15.refs_3_ = bf16[2,2,24,1024]{3,2,1,0:T(8,128)(2,1)S(1)} collective-permute-done((bf16[2,2,24,1024]{3,2,1,0:T(8,128)(2,1)}, bf16[2,2,24,1024]{3,2,1,0:T(8,128)(2,1)S(1)}, u32[]{:S(2)}, u32[]{:S(2)}) %collective-permute-start.15) | collective-permute-done | bytes 196640 | tf_op jit(solution)/shard_map/ppermute | solution.py:1006
  70.7 2.2 join.3
  73.5 1.5 collective-permute-start.18
  75.1 12.7 %attend.1 = (bf16[256,384]{1,0:T(8,128)(2,1)}, bf16[1024,384]{1,0:T(8,128)(2,1)}, bf16[1024,384]{1,0:T(8,128)(2,1)}, f32[6,1024,256]{2,1,0:T(8,128)}, f32[256,38...) custom-call(s32[4]{0:T(128)} %get-tuple-element.316.meta_ref, ...), custom_call_target="tpu_custom_call" | custom-call | flops 1 | bytes 1 | tf_op jit(solution)/shard_map/attend/pallas_call | solution.py:328
  87.9 1.6 collective-permute-done.17.their_ref
  89.5 2.0 collective-permute-done.19.refs_2_
  94.2 1.5 collective-permute-start.22
  95.7 1.5 collective-permute-start.23
  100.0 4.9 %mix.1 = (f32[256,768]{1,0:T(8,128)}, bf16[256,768]{1,0:T(8,128)(2,1)}, bf16[768,256]{1,0:T(8,128)(2,1)}, bf16[768,256]{1,0:T(8,128)(2,1)}, bf16[768,768]{1,0:T(8,128)(2,1)}) custom-call(s32[9]{0:T(128)} %stack.201.meta_ref, f32[256,768]{1,0:T(8,128)} %pad_maximum_fusion.1.tokens_ref, bf16[256,384]{1,0:T(8,128)(2,1)} %get-tuple-element.185.own_ref, ...), custom_call_target="tpu_custom_call" | custom-call | flops 1 | bytes 1 | tf_op jit(solution)/shard_map/mix/pallas_call | solution.py:403
  107.3 3.0 %collective-permute-done.24.refs_8_ = bf16[4,64,768]{2,1,0:T(8,128)(2,1)} collective-permute-done((bf16[4,64,768]{2,1,0:T(8,128)(2,1)}, bf16[4,64,768]{2,1,0:T(8,128)(2,1)}, u32[]{:S(2)}, u32[]{:S(2)}) %collective-permute-start.24) | collective-permute-done | bytes 393248 | tf_op jit(solution)/shard_map/ppermute | solution.py:1006
  110.3 11.7 %feed.1 = (f32[256,768]{1,0:T(8,128)}, f32[256,768]{1,0:T(8,128)}, bf16[2,192,1024]{2,1,0:T(8,128)(2,1)}, bf16[2,192,1024]{2,1,0:T(8,128)(2,1)}, bf16[2,192,1024...) custom-call(s32[36]{0:T(128)} %stack.246.meta_ref, ...), custom_call_target="tpu_custom_call" | custom-call | flops 1 | bytes 1 | tf_op jit(solution)/shard_map/feed/pallas_call | solution.py:531
  123.8 2.4 %collective-permute-start.28 = (bf16[2,192,1024]{2,1,0:T(8,128)(2,1)}, bf16[2,192,1024]{2,1,0:T(8,128)(2,1)}, u32[]{:S(2)}, u32[]{:S(2)}) collective-permute-start(bf16[2,192,1024]{2,1,0:T(8,128)(2,1)} %get-tuple-element.228), channel_id=1, source_target_pairs={{0,24},{4,28},{8,16},{12,20},{16,8},{20,12},{24,0},{28,4},{1,25},{... | collective-permute-start | bytes 2359304 | tf_op jit(solution)/shard_map/ppermute | solution.py:1001
  127.1 3.7 %settle.1 = (f32[256,768]{1,0:T(8,128)}, bf16[256,384]{1,0:T(8,128)(2,1)}, f32[1,768]{1,0:T(1,128)}, bf16[256,768]{1,0:T(8,128)(2,1)}) custom-call(s32[1]{0:T(128)} %bitcast.core_ref.meta_ref, f32[256,768]{1,0:T(8,128)} %get-tuple-element.196.mixed_ref, f32[256,768]{1,0:T(8,128)} %pad_maximum_fusion.2.cot_ref, f32[256,768]{1,0:T(8,128)} %get-tuple-element.207.back_ref, ...), custom_call_target="tpu_custom_call" | custom-call | flops 1 | bytes 1 | tf_op jit(solution)/shard_map/settle/pallas_call | solution.py:593
  130.8 7.9 %retreat.1 = (bf16[256,384]{1,0:T(8,128)(2,1)}, bf16[1024,768]{1,0:T(8,128)(2,1)}, f32[3,8,128]{2,1,0:T(8,128)}) custom-call(s32[1]{0:T(128)} %bitcast.11.meta_ref, bf16[256,384]{1,0:T(8,128)(2,1)} %get-tuple-element.209.do_ref, f32[256,384]{1,0:T(8,128)} %get-tuple-element.210.o_ref, bf16[256,384]{1,0:T(8,128)(2,1)} %get-tuple-element.211.q_ref, ...), custom_call_target="tpu_custom_call" | custom-call | flops 1 | bytes 1 | tf_op jit(solution)/shard_map/retreat/pallas_call | solution.py:692
  138.7 7.3 %weight_grads.1 = (bf16[784,384]{1,0:T(8,128)(2,1)}, bf16[784,384]{1,0:T(8,128)(2,1)}, bf16[784,384]{1,0:T(8,128)(2,1)}, bf16[784,384]{1,0:T(8,128)(2,1)}) custom-call(s32[6]{0:T(128)} %stack.213.meta_ref, bf16[768,1024]{1,0:T(8,128)(2,1)} %get-tuple-element.197.turned_ref, bf16[256,384]{1,0:T(8,128)(2,1)} %get-tuple-element.230.dq_ref, ...), custom_call_target="tpu_custom_call" | custom-call | flops 1 | bytes 1 | tf_op jit(solution)/shard_map/weight_grads/pallas_call | solution.py:808
  146.0 5.9 %row_grads.1 = (bf16[4,128,768]{2,1,0:T(8,128)(2,1)}, bf16[4,128,768]{2,1,0:T(8,128)(2,1)}) custom-call(s32[6]{0:T(128)} %stack.213.meta_ref, bf16[256,384]{1,0:T(8,128)(2,1)} %get-tuple-element.230.dq_ref, bf16[1024,768]{1,0:T(8,128)(2,1)} %get-tuple-element.216.dkv_ref, bf16[4,192,384]{2,1,0:T(8,128)(2,1)} %bitcast.126, bf16[4,192,384]{2,1,0:T(8,128)(2,1)} %copy-done.3, ...), custom_call_target="tpu_custom_call" | custom-call | flops 1 | bytes 1 | tf_op jit(solution)/shard_map/row_grads/pallas_call | solution.py:856
  152.0 8.1 %collective-permute-done.27.refs_2_ = bf16[2,192,1024]{2,1,0:T(8,128)(2,1)} collective-permute-done((bf16[2,192,1024]{2,1,0:T(8,128)(2,1)}, bf16[2,192,1024]{2,1,0:T(8,128)(2,1)}, u32[]{:S(2)}, u32[]{:S(2)}) %collective-permute-start.27) | collective-permute-done | bytes 786464 | tf_op jit(solution)/shard_map/ppermute | solution.py:1001
  162.3 2.4 %collective-permute-start.33 = (bf16[784,384]{1,0:T(8,128)(2,1)}, bf16[784,384]{1,0:T(8,128)(2,1)}, u32[]{:S(2)}, u32[]{:S(2)}) collective-permute-start(bf16[784,384]{1,0:T(8,128)(2,1)} %get-tuple-element.235), channel_id=1, source_target_pairs={{0,24},{4,28},{8,16},{12,20},{16,8},{20,12},{24,0},{28,4},{1,25},{... | collective-permute-start | bytes 1806344 | tf_op jit(solution)/shard_map/ppermute | solution.py:1001
  164.7 2.8 %cut_plane.1 = (bf16[2,2,48,1024]{3,2,1,0:T(8,128)(2,1)}, bf16[2,2,48,1024]{3,2,1,0:T(8,128)(2,1)}) custom-call(s32[1]{0:T(128)} %bitcast.54.side_ref, bf16[2,192,1024]{2,1,0:T(8,128)(2,1)} %get-tuple-element.236.refs_0_, bf16[2,192,1024]{2,1,0:T(8,128)(2,1)} %collective-permute-done.26.refs_1_, bf16[2,192,1024]{2,1,0:T(8,128)(2,1)} %collective-permute-done.27.refs_2_, ...), custom_call_target="tpu_custom_call" | custom-call | flops 1 | bytes 1 | tf_op jit(solution)/shard_map/cut_plane/pallas_call | solution.py:886
  169.6 2.2 collective-permute-start.34
  172.4 14.3 %collective-permute-done.35 = bf16[1,4,64,768]{3,2,1,0:T(8,128)(2,1)S(1)} collective-permute-done((bf16[1,4,64,768]{3,2,1,0:T(8,128)(2,1)}, bf16[1,4,64,768]{3,2,1,0:T(8,128)(2,1)S(1)}, u32[]{:S(2)}, u32[]{:S(2)}) %collective-permute-start.35) | collective-permute-done | bytes 393248 | tf_op jit(solution)/shard_map/ppermute | solution.py:1068
  186.7 2.8 %collective-permute-done.34 = bf16[2,2,2,24,1024]{4,3,2,1,0:T(8,128)(2,1)} collective-permute-done((bf16[2,2,2,24,1024]{4,3,2,1,0:T(8,128)(2,1)}, bf16[2,2,2,24,1024]{4,3,2,1,0:T(8,128)(2,1)}, u32[]{:S(2)}, u32[]{:S(2)}) %collective-permute-start.34) | collective-permute-done | bytes 393248 | tf_op jit(solution)/shard_map/ppermute | solution.py:1068
  191.8 3.0 %sum_plane.1 = (bf16[208,384]{1,0:T(8,128)(2,1)}, bf16[208,384]{1,0:T(8,128)(2,1)}, bf16[208,384]{1,0:T(8,128)(2,1)}, bf16[208,384]{1,0:T(8,128)(2,1)}) custom-call(s32[4]{0:T(128)} %pad_add_fusion.2.order_ref, bf16[784,384]{1,0:T(8,128)(2,1)} %get-tuple-element.255.refs_0_, bf16[784,384]{1,0:T(8,128)(2,1)} %collective-permute-done.31.refs_1_, ...), custom_call_target="tpu_custom_call" | custom-call | flops 1 | bytes 1 | tf_op jit(solution)/shard_map/sum_plane/pallas_call | solution.py:922
  194.8 2.0 collective-permute-start.40
  196.8 2.4 %collective-permute-start.42 = (bf16[208,384]{1,0:T(8,128)(2,1)}, bf16[208,384]{1,0:T(8,128)(2,1)}, u32[]{:S(2)}, u32[]{:S(2)}) collective-permute-start(bf16[208,384]{1,0:T(8,128)(2,1)} %get-tuple-element.262), channel_id=1, source_target_pairs={{0,3},{1,0},{2,1},{3,2},{4,7},{5,4},{6,5},{7,6},{8,11},{9,8},{10,9... | collective-permute-start | bytes 479240 | tf_op jit(solution)/shard_map/ppermute | solution.py:1006
  202.2 2.8 %collective-permute-done.45 = bf16[2,64,768]{2,1,0:T(8,128)(2,1)S(1)} collective-permute-done((bf16[2,64,768]{2,1,0:T(8,128)(2,1)S(1)}, bf16[2,64,768]{2,1,0:T(8,128)(2,1)S(1)}, u32[]{:S(2)}, u32[]{:S(2)}) %collective-permute-start.45) | collective-permute-done | bytes 196640 | tf_op jit(solution)/shard_map/ppermute | solution.py:1001
  206.4 1.5 collective-permute-start.38
  209.1 2.0 fusion.8
  211.9 2.0 last_sum.1
  214.8 1.8 add_bitcast_fusion.1
  219.9 1.6 collective-permute-start.46
  224.0 2.3 %attention_update.1 = (f32[4,24,768]{2,1,0:T(8,128)}, f32[4,24,768]{2,1,0:T(8,128)}, f32[4,24,768]{2,1,0:T(8,128)}, bf16[4,24,768]{2,1,0:T(8,128)(2,1)}) custom-call(s32[1]{0:T(128)} %bitcast.core_ref.meta_ref, f32[208,384]{1,0:T(8,128)} %get-tuple-element.269.sum_ref, f32[88,384]{1,0:T(8,128)} %copy-done.37, f32[4,24,768]{2,1,0:T(8,128)} %weight_ref.1, ...), custom_call_target="tpu_custom_call" | custom-call | flops 1 | bytes 1 | tf_op jit(solution)/shard_map/attention_update/pallas_call | solution.py:983
  (222 shorter events, 49.5 us)
Async XLA Ops:
  0.7 3.3 %collective-permute-start.1 = (f32[128,768]{1,0:T(8,128)}, f32[128,768]{1,0:T(8,128)S(1)}, u32[]{:S(2)}, u32[]{:S(2)}) collective-permute-start(f32[128,768]{1,0:T(8,128)} %bitcast.137), channel_id=1, source_target_pairs={{0,4},{4,0},{8,12},{12,8},{16,20},{20,16},{24,28},{28,24},{1,5},{5... | collective-permute-start | bytes 1179656 | tf_op jit(solution)/shard_map/ppermute | solution.py:996
  1.2 2.8 %collective-permute-start = (f32[128,768]{1,0:T(8,128)}, f32[128,768]{1,0:T(8,128)S(1)}, u32[]{:S(2)}, u32[]{:S(2)}) collective-permute-start(f32[128,768]{1,0:T(8,128)} %bitcast.127), channel_id=1, source_target_pairs={{0,4},{4,0},{8,12},{12,8},{16,20},{20,16},{24,28},{28,24},{1,5},{5... | collective-permute-start | bytes 1179656 | tf_op jit(solution)/shard_map/ppermute | solution.py:996
  4.8 10.9 %collective-permute-start.2 = (bf16[1,208,768]{2,1,0:T(8,128)(2,1)}, bf16[1,208,768]{2,1,0:T(8,128)(2,1)S(1)}, u32[]{:S(2)}, u32[]{:S(2)}) collective-permute-start(bf16[1,208,768]{2,1,0:T(8,128)(2,1)} %bitcast.132), channel_id=1, source_target_pairs={{0,8},{4,12},{8,0},{12,4},{16,24},{20,28},{24,16},{28,20},{1,9},{5... | collective-permute-start | bytes 958472 | tf_op jit(solution)/shard_map/ppermute | solution.py:1001
  7.7 1.5 collective-permute-start.3
  7.7 1.6 collective-permute-start.4
  16.8 19.2 %collective-permute-start.5 = (bf16[2,208,768]{2,1,0:T(8,128)(2,1)S(1)}, bf16[2,208,768]{2,1,0:T(8,128)(2,1)S(1)}, u32[]{:S(2)}, u32[]{:S(2)}) collective-permute-start(bf16[2,208,768]{2,1,0:T(8,128)(2,1)S(1)} %pad_maximum_fusion.3), channel_id=1, source_target_pairs={{0,16},{4,20},{8,24},{12,28},{16,0},{20,4},{24,8},{28,12},{1,17},{... | collective-permute-start | bytes 1916936 | tf_op jit(solution)/shard_map/ppermute | solution.py:1001
  18.8 11.6 %collective-permute-start.8 = (bf16[4,2,24,384]{3,2,1,0:T(8,128)(2,1)}, bf16[4,2,24,384]{3,2,1,0:T(8,128)(2,1)S(1)}, u32[]{:S(2)}, u32[]{:S(2)}) collective-permute-start(bf16[4,2,24,384]{3,2,1,0:T(8,128)(2,1)} %fill.2.refs_0_), channel_id=1, source_target_pairs={{0,3},{1,0},{2,1},{3,2},{4,7},{5,4},{6,5},{7,6},{8,11},{9,8},{10,9... | collective-permute-start | bytes 442376 | tf_op jit(solution)/shard_map/ppermute | solution.py:1006
  22.4 12.2 %collective-permute-start.7 = (bf16[4,2,24,384]{3,2,1,0:T(8,128)(2,1)}, bf16[4,2,24,384]{3,2,1,0:T(8,128)(2,1)S(1)}, u32[]{:S(2)}, u32[]{:S(2)}) collective-permute-start(bf16[4,2,24,384]{3,2,1,0:T(8,128)(2,1)} %fill.2.refs_0_), channel_id=1, source_target_pairs={{0,2},{1,3},{2,0},{3,1},{4,6},{5,7},{6,4},{7,5},{8,10},{9,11},{10,... | collective-permute-start | bytes 442376 | tf_op jit(solution)/shard_map/ppermute | solution.py:1006
  22.4 12.2 %collective-permute-start.6 = (bf16[4,2,24,384]{3,2,1,0:T(8,128)(2,1)}, bf16[4,2,24,384]{3,2,1,0:T(8,128)(2,1)S(1)}, u32[]{:S(2)}, u32[]{:S(2)}) collective-permute-start(bf16[4,2,24,384]{3,2,1,0:T(8,128)(2,1)} %fill.2.refs_0_), channel_id=1, source_target_pairs={{0,1},{1,2},{2,3},{3,0},{4,5},{5,6},{6,7},{7,4},{8,9},{9,10},{10,1... | collective-permute-start | bytes 442376 | tf_op jit(solution)/shard_map/ppermute | solution.py:1006
  39.4 9.4 %collective-permute-start.9 = (bf16[4,144,768]{2,1,0:T(8,128)(2,1)S(1)}, bf16[4,144,768]{2,1,0:T(8,128)(2,1)}, u32[]{:S(2)}, u32[]{:S(2)}) collective-permute-start(bf16[4,144,768]{2,1,0:T(8,128)(2,1)S(1)} %slice.106.near_ref), channel_id=1, source_target_pairs={{0,4},{4,0},{8,12},{12,8},{16,20},{20,16},{24,28},{28,24},{1,5},{5... | collective-permute-start | bytes 2654216 | tf_op jit(solution)/shard_map/ppermute | solution.py:996
  39.4 9.4 %collective-permute-start.13 = (bf16[2,2,24,1024]{3,2,1,0:T(8,128)(2,1)}, bf16[2,2,24,1024]{3,2,1,0:T(8,128)(2,1)}, u32[]{:S(2)}, u32[]{:S(2)}) collective-permute-start(bf16[2,2,24,1024]{3,2,1,0:T(8,128)(2,1)} %fill.3.refs_0_), channel_id=1, source_target_pairs={{0,1},{1,2},{2,3},{3,0},{4,5},{5,6},{6,7},{7,4},{8,9},{9,10},{10,1... | collective-permute-start | bytes 589832 | tf_op jit(solution)/shard_map/ppermute | solution.py:1006
  40.0 32.9 %collective-permute-start.12 = (bf16[4,192,384]{2,1,0:T(8,128)(2,1)}, bf16[4,192,384]{2,1,0:T(8,128)(2,1)S(1)}, u32[]{:S(2)}, u32[]{:S(2)}) collective-permute-start(bf16[4,192,384]{2,1,0:T(8,128)(2,1)} %bitcast.121), channel_id=1, source_target_pairs={{0,24},{4,28},{8,16},{12,20},{16,8},{20,12},{24,0},{28,4},{1,25},{... | collective-permute-start | bytes 1769480 | tf_op jit(solution)/shard_map/ppermute | solution.py:1001
  41.5 31.4 %collective-permute-start.11 = (bf16[4,192,384]{2,1,0:T(8,128)(2,1)}, bf16[4,192,384]{2,1,0:T(8,128)(2,1)S(1)}, u32[]{:S(2)}, u32[]{:S(2)}) collective-permute-start(bf16[4,192,384]{2,1,0:T(8,128)(2,1)} %bitcast.122), channel_id=1, source_target_pairs={{0,16},{4,20},{8,24},{12,28},{16,0},{20,4},{24,8},{28,12},{1,17},{... | collective-permute-start | bytes 1769480 | tf_op jit(solution)/shard_map/ppermute | solution.py:1001
  43.0 29.9 %collective-permute-start.10 = (bf16[4,192,384]{2,1,0:T(8,128)(2,1)}, bf16[4,192,384]{2,1,0:T(8,128)(2,1)S(1)}, u32[]{:S(2)}, u32[]{:S(2)}) collective-permute-start(bf16[4,192,384]{2,1,0:T(8,128)(2,1)} %bitcast.123), channel_id=1, source_target_pairs={{0,8},{4,12},{8,0},{12,4},{16,24},{20,28},{24,16},{28,20},{1,9},{5... | collective-permute-start | bytes 1769480 | tf_op jit(solution)/shard_map/ppermute | solution.py:1001
  48.9 9.9 %collective-permute-start.14 = (bf16[2,2,24,1024]{3,2,1,0:T(8,128)(2,1)}, bf16[2,2,24,1024]{3,2,1,0:T(8,128)(2,1)}, u32[]{:S(2)}, u32[]{:S(2)}) collective-permute-start(bf16[2,2,24,1024]{3,2,1,0:T(8,128)(2,1)} %collective-permute-done.13.refs_1_), channel_id=1, source_target_pairs={{0,1},{1,2},{2,3},{3,0},{4,5},{5,6},{6,7},{7,4},{8,9},{9,10},{10,1... | collective-permute-start | bytes 589832 | tf_op jit(solution)/shard_map/ppermute | solution.py:1006
  48.9 24.1 %collective-permute-start.16 = (bf16[4,64,768]{2,1,0:T(8,128)(2,1)S(1)}, bf16[4,64,768]{2,1,0:T(8,128)(2,1)}, u32[]{:S(2)}, u32[]{:S(2)}) collective-permute-start(bf16[4,64,768]{2,1,0:T(8,128)(2,1)S(1)} %pad_maximum_fusion.4.refs_5_), channel_id=1, source_target_pairs={{0,1},{1,2},{2,3},{3,0},{4,5},{5,6},{6,7},{7,4},{8,9},{9,10},{10,1... | collective-permute-start | bytes 1179656 | tf_op jit(solution)/shard_map/ppermute | solution.py:1006
  58.8 11.3 %collective-permute-start.15 = (bf16[2,2,24,1024]{3,2,1,0:T(8,128)(2,1)}, bf16[2,2,24,1024]{3,2,1,0:T(8,128)(2,1)S(1)}, u32[]{:S(2)}, u32[]{:S(2)}) collective-permute-start(bf16[2,2,24,1024]{3,2,1,0:T(8,128)(2,1)} %collective-permute-done.14.refs_2_), channel_id=1, source_target_pairs={{0,1},{1,2},{2,3},{3,0},{4,5},{5,6},{6,7},{7,4},{8,9},{9,10},{10,1... | collective-permute-start | bytes 589832 | tf_op jit(solution)/shard_map/ppermute | solution.py:1006
  73.0 18.6 %collective-permute-start.19 = (bf16[2,192,1024]{2,1,0:T(8,128)(2,1)}, bf16[2,192,1024]{2,1,0:T(8,128)(2,1)S(1)}, u32[]{:S(2)}, u32[]{:S(2)}) collective-permute-start(bf16[2,192,1024]{2,1,0:T(8,128)(2,1)} %bitcast.129), channel_id=1, source_target_pairs={{0,16},{4,20},{8,24},{12,28},{16,0},{20,4},{24,8},{28,12},{1,17},{... | collective-permute-start | bytes 2359304 | tf_op jit(solution)/shard_map/ppermute | solution.py:1001
  73.5 18.2 %collective-permute-start.18 = (bf16[2,192,1024]{2,1,0:T(8,128)(2,1)}, bf16[2,192,1024]{2,1,0:T(8,128)(2,1)S(1)}, u32[]{:S(2)}, u32[]{:S(2)}) collective-permute-start(bf16[2,192,1024]{2,1,0:T(8,128)(2,1)} %bitcast.130), channel_id=1, source_target_pairs={{0,8},{4,12},{8,0},{12,4},{16,24},{20,28},{24,16},{28,20},{1,9},{5... | collective-permute-start | bytes 2359304 | tf_op jit(solution)/shard_map/ppermute | solution.py:1001
  75.0 14.5 %collective-permute-start.20 = (bf16[4,64,768]{2,1,0:T(8,128)(2,1)}, bf16[4,64,768]{2,1,0:T(8,128)(2,1)}, u32[]{:S(2)}, u32[]{:S(2)}) collective-permute-start(bf16[4,64,768]{2,1,0:T(8,128)(2,1)} %collective-permute-done.16.refs_6_), channel_id=1, source_target_pairs={{0,1},{1,2},{2,3},{3,0},{4,5},{5,6},{6,7},{7,4},{8,9},{9,10},{10,1... | collective-permute-start | bytes 1179656 | tf_op jit(solution)/shard_map/ppermute | solution.py:1006
  87.8 1.7 collective-permute-start.17
  94.2 5.0 %collective-permute-start.21 = (bf16[4,192,384]{2,1,0:T(8,128)(2,1)S(1)}, bf16[4,192,384]{2,1,0:T(8,128)(2,1)S(1)}, u32[]{:S(2)}, u32[]{:S(2)}) collective-permute-start(bf16[4,192,384]{2,1,0:T(8,128)(2,1)S(1)} %copy-done.23), channel_id=1, source_target_pairs={{0,4},{4,0},{8,12},{12,8},{16,20},{20,16},{24,28},{28,24},{1,5},{5... | collective-permute-start | bytes 1769480 | tf_op jit(solution)/shard_map/ppermute | solution.py:996
  94.2 11.7 %collective-permute-start.22 = (bf16[1,192,1024]{2,1,0:T(8,128)(2,1)}, bf16[1,192,1024]{2,1,0:T(8,128)(2,1)S(1)}, u32[]{:S(2)}, u32[]{:S(2)}) collective-permute-start(bf16[1,192,1024]{2,1,0:T(8,128)(2,1)} %slice.86), channel_id=1, source_target_pairs={{0,16},{4,20},{8,24},{12,28},{16,0},{20,4},{24,8},{28,12},{1,17},{... | collective-permute-start | bytes 1179656 | tf_op jit(solution)/shard_map/ppermute | solution.py:1001
  95.7 11.6 %collective-permute-start.23 = (bf16[1,192,1024]{2,1,0:T(8,128)(2,1)}, bf16[1,192,1024]{2,1,0:T(8,128)(2,1)}, u32[]{:S(2)}, u32[]{:S(2)}) collective-permute-start(bf16[1,192,1024]{2,1,0:T(8,128)(2,1)} %slice.87), channel_id=1, source_target_pairs={{0,8},{4,12},{8,0},{12,4},{16,24},{20,28},{24,16},{28,20},{1,9},{5... | collective-permute-start | bytes 1179656 | tf_op jit(solution)/shard_map/ppermute | solution.py:1001
  97.2 13.1 %collective-permute-start.24 = (bf16[4,64,768]{2,1,0:T(8,128)(2,1)}, bf16[4,64,768]{2,1,0:T(8,128)(2,1)}, u32[]{:S(2)}, u32[]{:S(2)}) collective-permute-start(bf16[4,64,768]{2,1,0:T(8,128)(2,1)} %collective-permute-done.20.refs_7_), channel_id=1, source_target_pairs={{0,1},{1,2},{2,3},{3,0},{4,5},{5,6},{6,7},{7,4},{8,9},{9,10},{10,1... | collective-permute-start | bytes 1179656 | tf_op jit(solution)/shard_map/ppermute | solution.py:1006
  122.0 4.2 %collective-permute-start.25 = (f32[256,768]{1,0:T(8,128)}, f32[256,768]{1,0:T(8,128)S(1)}, u32[]{:S(2)}, u32[]{:S(2)}) collective-permute-start(f32[256,768]{1,0:T(8,128)} %get-tuple-element.207.back_ref), channel_id=1, source_target_pairs={{0,4},{4,0},{8,12},{12,8},{16,20},{20,16},{24,28},{28,24},{1,5},{5... | collective-permute-start | bytes 2359304 | tf_op jit(solution)/shard_map/ppermute | solution.py:996
  122.7 29.3 %collective-permute-start.26 = (bf16[2,192,1024]{2,1,0:T(8,128)(2,1)}, bf16[2,192,1024]{2,1,0:T(8,128)(2,1)}, u32[]{:S(2)}, u32[]{:S(2)}) collective-permute-start(bf16[2,192,1024]{2,1,0:T(8,128)(2,1)} %get-tuple-element.226), channel_id=1, source_target_pairs={{0,8},{4,12},{8,0},{12,4},{16,24},{20,28},{24,16},{28,20},{1,9},{5... | collective-permute-start | bytes 2359304 | tf_op jit(solution)/shard_map/ppermute | solution.py:1001
  123.3 36.8 %collective-permute-start.27 = (bf16[2,192,1024]{2,1,0:T(8,128)(2,1)}, bf16[2,192,1024]{2,1,0:T(8,128)(2,1)}, u32[]{:S(2)}, u32[]{:S(2)}) collective-permute-start(bf16[2,192,1024]{2,1,0:T(8,128)(2,1)} %get-tuple-element.227), channel_id=1, source_target_pairs={{0,16},{4,20},{8,24},{12,28},{16,0},{20,4},{24,8},{28,12},{1,17},{... | collective-permute-start | bytes 2359304 | tf_op jit(solution)/shard_map/ppermute | solution.py:1001
  123.8 36.3 %collective-permute-start.28 = (bf16[2,192,1024]{2,1,0:T(8,128)(2,1)}, bf16[2,192,1024]{2,1,0:T(8,128)(2,1)}, u32[]{:S(2)}, u32[]{:S(2)}) collective-permute-start(bf16[2,192,1024]{2,1,0:T(8,128)(2,1)} %get-tuple-element.228), channel_id=1, source_target_pairs={{0,24},{4,28},{8,16},{12,20},{16,8},{20,12},{24,0},{28,4},{1,25},{... | collective-permute-start | bytes 2359304 | tf_op jit(solution)/shard_map/ppermute | solution.py:1001
  126.2 35.0 %collective-permute-start.29 = (bf16[2,4,64,768]{3,2,1,0:T(8,128)(2,1)}, bf16[2,4,64,768]{3,2,1,0:T(8,128)(2,1)S(1)}, u32[]{:S(2)}, u32[]{:S(2)}) collective-permute-start(bf16[2,4,64,768]{3,2,1,0:T(8,128)(2,1)} %get-tuple-element.229), channel_id=1, source_target_pairs={{0,2},{1,3},{2,0},{3,1},{4,6},{5,7},{6,4},{7,5},{8,10},{9,11},{10,... | collective-permute-start | bytes 2359304 | tf_op jit(solution)/shard_map/ppermute | solution.py:1068
  151.9 9.3 %collective-permute-start.30 = (bf16[4,128,768]{2,1,0:T(8,128)(2,1)}, bf16[4,128,768]{2,1,0:T(8,128)(2,1)S(1)}, u32[]{:S(2)}, u32[]{:S(2)}) collective-permute-start(bf16[4,128,768]{2,1,0:T(8,128)(2,1)} %get-tuple-element.231), channel_id=1, source_target_pairs={{0,4},{4,0},{8,12},{12,8},{16,20},{20,16},{24,28},{28,24},{1,5},{5... | collective-permute-start | bytes 2359304 | tf_op jit(solution)/shard_map/ppermute | solution.py:996
  161.2 28.3 %collective-permute-start.31 = (bf16[784,384]{1,0:T(8,128)(2,1)}, bf16[784,384]{1,0:T(8,128)(2,1)}, u32[]{:S(2)}, u32[]{:S(2)}) collective-permute-start(bf16[784,384]{1,0:T(8,128)(2,1)} %get-tuple-element.233), channel_id=1, source_target_pairs={{0,8},{4,12},{8,0},{12,4},{16,24},{20,28},{24,16},{28,20},{1,9},{5... | collective-permute-start | bytes 1806344 | tf_op jit(solution)/shard_map/ppermute | solution.py:1001
  161.7 28.5 %collective-permute-start.32 = (bf16[784,384]{1,0:T(8,128)(2,1)}, bf16[784,384]{1,0:T(8,128)(2,1)}, u32[]{:S(2)}, u32[]{:S(2)}) collective-permute-start(bf16[784,384]{1,0:T(8,128)(2,1)} %get-tuple-element.234), channel_id=1, source_target_pairs={{0,16},{4,20},{8,24},{12,28},{16,0},{20,4},{24,8},{28,12},{1,17},{... | collective-permute-start | bytes 1806344 | tf_op jit(solution)/shard_map/ppermute | solution.py:1001
  162.3 27.9 %collective-permute-start.33 = (bf16[784,384]{1,0:T(8,128)(2,1)}, bf16[784,384]{1,0:T(8,128)(2,1)}, u32[]{:S(2)}, u32[]{:S(2)}) collective-permute-start(bf16[784,384]{1,0:T(8,128)(2,1)} %get-tuple-element.235), channel_id=1, source_target_pairs={{0,24},{4,28},{8,16},{12,20},{16,8},{20,12},{24,0},{28,4},{1,25},{... | collective-permute-start | bytes 1806344 | tf_op jit(solution)/shard_map/ppermute | solution.py:1001
  167.5 22.7 %copy-start.27 = (bf16[2,2,48,1024]{3,2,1,0:T(8,128)(2,1)S(1)}, bf16[2,2,48,1024]{3,2,1,0:T(8,128)(2,1)}, u32[]{:S(2)}) copy-start(bf16[2,2,48,1024]{3,2,1,0:T(8,128)(2,1)} %get-tuple-element.252) | copy-start | bytes 1179652
  169.6 17.1 %collective-permute-start.35 = (bf16[1,4,64,768]{3,2,1,0:T(8,128)(2,1)}, bf16[1,4,64,768]{3,2,1,0:T(8,128)(2,1)S(1)}, u32[]{:S(2)}, u32[]{:S(2)}) collective-permute-start(bf16[1,4,64,768]{3,2,1,0:T(8,128)(2,1)} %constant_dynamic-slice_fusion.2), channel_id=1, source_target_pairs={{0,1},{1,0},{2,3},{3,2},{4,5},{5,4},{6,7},{7,6},{8,9},{9,8},{10,11... | collective-permute-start | bytes 1179656 | tf_op jit(solution)/shard_map/ppermute | solution.py:1068
  169.6 19.9 %collective-permute-start.34 = (bf16[2,2,2,24,1024]{4,3,2,1,0:T(8,128)(2,1)}, bf16[2,2,2,24,1024]{4,3,2,1,0:T(8,128)(2,1)}, u32[]{:S(2)}, u32[]{:S(2)}) collective-permute-start(bf16[2,2,2,24,1024]{4,3,2,1,0:T(8,128)(2,1)} %bitcast.55), channel_id=1, source_target_pairs={{0,2},{1,3},{2,0},{3,1},{4,6},{5,7},{6,4},{7,5},{8,10},{9,11},{10,... | collective-permute-start | bytes 1179656 | tf_op jit(solution)/shard_map/ppermute | solution.py:1068
  191.6 9.7 %collective-permute-start.37 = (bf16[2,2,1,24,1024]{4,3,2,1,0:T(8,128)(2,1)S(1)}, bf16[2,2,1,24,1024]{4,3,2,1,0:T(8,128)(2,1)S(1)}, u32[]{:S(2)}, u32[]{:S(2)}) collective-permute-start(bf16[2,2,1,24,1024]{4,3,2,1,0:T(8,128)(2,1)S(1)} %constant_dynamic-slice_fusion), channel_id=1, source_target_pairs={{0,1},{1,0},{2,3},{3,2},{4,5},{5,4},{6,7},{7,6},{8,9},{9,8},{10,11... | collective-permute-start | bytes 589832 | tf_op jit(solution)/shard_map/ppermute | solution.py:1068
  194.8 17.1 %collective-permute-start.40 = (bf16[208,384]{1,0:T(8,128)(2,1)}, bf16[208,384]{1,0:T(8,128)(2,1)}, u32[]{:S(2)}, u32[]{:S(2)}) collective-permute-start(bf16[208,384]{1,0:T(8,128)(2,1)} %get-tuple-element.260), channel_id=1, source_target_pairs={{0,1},{1,2},{2,3},{3,0},{4,5},{5,6},{6,7},{7,4},{8,9},{9,10},{10,1... | collective-permute-start | bytes 479240 | tf_op jit(solution)/shard_map/ppermute | solution.py:1006
  196.8 15.1 %collective-permute-start.41 = (bf16[208,384]{1,0:T(8,128)(2,1)}, bf16[208,384]{1,0:T(8,128)(2,1)}, u32[]{:S(2)}, u32[]{:S(2)}) collective-permute-start(bf16[208,384]{1,0:T(8,128)(2,1)} %get-tuple-element.261), channel_id=1, source_target_pairs={{0,2},{1,3},{2,0},{3,1},{4,6},{5,7},{6,4},{7,5},{8,10},{9,11},{10,... | collective-permute-start | bytes 479240 | tf_op jit(solution)/shard_map/ppermute | solution.py:1006
  196.8 15.1 %collective-permute-start.42 = (bf16[208,384]{1,0:T(8,128)(2,1)}, bf16[208,384]{1,0:T(8,128)(2,1)}, u32[]{:S(2)}, u32[]{:S(2)}) collective-permute-start(bf16[208,384]{1,0:T(8,128)(2,1)} %get-tuple-element.262), channel_id=1, source_target_pairs={{0,3},{1,0},{2,1},{3,2},{4,7},{5,4},{6,5},{7,6},{8,11},{9,8},{10,9... | collective-permute-start | bytes 479240 | tf_op jit(solution)/shard_map/ppermute | solution.py:1006
  199.2 5.7 %collective-permute-start.45 = (bf16[2,64,768]{2,1,0:T(8,128)(2,1)S(1)}, bf16[2,64,768]{2,1,0:T(8,128)(2,1)S(1)}, u32[]{:S(2)}, u32[]{:S(2)}) collective-permute-start(bf16[2,64,768]{2,1,0:T(8,128)(2,1)S(1)} %slice.97), channel_id=1, source_target_pairs={{0,16},{4,20},{8,24},{12,28},{16,0},{20,4},{24,8},{28,12},{1,17},{... | collective-permute-start | bytes 589832 | tf_op jit(solution)/shard_map/ppermute | solution.py:1001
  201.3 13.5 %collective-permute-start.36 = (f32[128,768]{1,0:T(8,128)}, f32[128,768]{1,0:T(8,128)}, u32[]{:S(2)}, u32[]{:S(2)}) collective-permute-start(f32[128,768]{1,0:T(8,128)} %constant_dynamic-slice_fusion.1), channel_id=1, source_target_pairs={{0,4},{4,0},{8,12},{12,8},{16,20},{20,16},{24,28},{28,24},{1,5},{5... | collective-permute-start | bytes 1179656 | tf_op jit(solution)/shard_map/ppermute | solution.py:996
  205.0 1.4 collective-permute-start.43
  206.4 11.5 %collective-permute-start.38 = (bf16[2,128,768]{2,1,0:T(8,128)(2,1)}, bf16[2,128,768]{2,1,0:T(8,128)(2,1)}, u32[]{:S(2)}, u32[]{:S(2)}) collective-permute-start(bf16[2,128,768]{2,1,0:T(8,128)(2,1)} %slice.91), channel_id=1, source_target_pairs={{0,8},{4,12},{8,0},{12,4},{16,24},{20,28},{24,16},{28,20},{1,9},{5... | collective-permute-start | bytes 1179656 | tf_op jit(solution)/shard_map/ppermute | solution.py:1001
  214.7 4.4 %collective-permute-start.44 = (f32[88,384]{1,0:T(8,128)}, f32[88,384]{1,0:T(8,128)S(1)}, u32[]{:S(2)}, u32[]{:S(2)}) collective-permute-start(f32[88,384]{1,0:T(8,128)} %get-tuple-element.270), channel_id=1, source_target_pairs={{0,4},{4,0},{8,12},{12,8},{16,20},{20,16},{24,28},{28,24},{1,5},{5... | collective-permute-start | bytes 405512 | tf_op jit(solution)/shard_map/ppermute | solution.py:996
  219.9 6.4 %collective-permute-start.46 = (bf16[1,64,768]{2,1,0:T(8,128)(2,1)S(1)}, bf16[1,64,768]{2,1,0:T(8,128)(2,1)S(1)}, u32[]{:S(2)}, u32[]{:S(2)}) collective-permute-start(bf16[1,64,768]{2,1,0:T(8,128)(2,1)S(1)} %slice.99), channel_id=1, source_target_pairs={{0,8},{4,12},{8,0},{12,4},{16,24},{20,28},{24,16},{28,20},{1,9},{5... | collective-permute-start | bytes 294920 | tf_op jit(solution)/shard_map/ppermute | solution.py:1001
  221.4 6.4 %collective-permute-start.39 = (bf16[1,128,768]{2,1,0:T(8,128)(2,1)S(1)}, bf16[1,128,768]{2,1,0:T(8,128)(2,1)S(1)}, u32[]{:S(2)}, u32[]{:S(2)}) collective-permute-start(bf16[1,128,768]{2,1,0:T(8,128)(2,1)S(1)} %get-tuple-element.304), channel_id=1, source_target_pairs={{0,16},{4,20},{8,24},{12,28},{16,0},{20,4},{24,8},{28,12},{1,17},{... | collective-permute-start | bytes 589832 | tf_op jit(solution)/shard_map/ppermute | solution.py:1001
  (49 other events, 321.5 us)
